TPU v7x, 32 devices: a whole 2x2x4 slice. The times are simulated.
32 devices in a mesh: dp: 8 (over y, x, core), tensor: 4 (over z).
Axes of the slice: x: 2, y: 2, z: 4, core: 2. Of those that a mesh axis runs over, the one named last changes fastest.
Arguments:
- subword_embedding_rows: bfloat16 [32000, 512], P('dp'), may hold values from -6 to 6
- entry_subword_index: int32 [512, 8], P(('dp', 'tensor')), may hold values from 0 to 31999
- entry_lengths: int32 [512], P(('dp', 'tensor')), may hold values from 1 to 8
- entry_counts: int32 [512], P(('dp', 'tensor')), may hold values from 1 to 131071, as said below
- encoder_triple: bfloat16 [512, 1536], replicated, may hold values from -0.25 to 0.25
- encoder_merge: bfloat16 [512, 512], replicated, may hold values from -0.5 to 0.5
- encoder_expand: bfloat16 [512, 2048], replicated, may hold values from -0.25 to 0.25
- encoder_reduce: bfloat16 [2048, 512], replicated, may hold values from -0.125 to 0.125
- embed_project: bfloat16 [512, 2048], replicated, may hold values from -0.25 to 0.25
- normone_gain: float32 [512], replicated, may hold values from 0.1 to 1.9
- normtwo_gain: float32 [512], replicated, may hold values from 0.1 to 1.9
- frozen_query: bfloat16 [2048, 2048], P('dp', 'tensor'), may hold values from -0.125 to 0.125
- frozen_key: bfloat16 [2048, 256], P('dp', 'tensor'), may hold values from -0.125 to 0.125
- frozen_value: bfloat16 [2048, 256], P('dp', 'tensor'), may hold values from -0.125 to 0.125
- frozen_output: bfloat16 [2048, 2048], P('dp', 'tensor'), may hold values from -1.5 to 1.5
- frozen_gate: bfloat16 [2048, 5632], P('dp', 'tensor'), may hold values from -0.125 to 0.125
- frozen_upward: bfloat16 [2048, 5632], P('dp', 'tensor'), may hold values from -0.125 to 0.125
- frozen_downward: bfloat16 [2048, 5632], P('dp', 'tensor'), may hold values from -0.078125 to 0.078125
- prenorm_gain: float32 [2048], replicated, may hold values from 0.1 to 1.9
- midnorm_gain: float32 [2048], replicated, may hold values from 0.1 to 1.9
- text_tokens: int32 [8192], P(('dp', 'tensor')), may hold values from 0 to 511
- cotangent: bfloat16 [8192, 2048], P(('dp', 'tensor')), may hold values from -6 to 6
Outputs:
- layer_output: bfloat16 [8192, 2048], P(('dp', 'tensor'))
- entry_vectors: bfloat16 [512, 2048], P(('dp', 'tensor'))
- subword_grad: float32 [32000, 512], P(('dp', 'tensor'))
- triple_grad: float32 [512, 1536], P(('dp', 'tensor'))
- merge_grad: float32 [512, 512], P(('dp', 'tensor'))
- expand_grad: float32 [512, 2048], P(('dp', 'tensor'))
- reduce_grad: float32 [2048, 512], P(('dp', 'tensor'))
- project_grad: float32 [512, 2048], P(('dp', 'tensor'))
- normone_grad: float32 [512], P(('dp', 'tensor'))
- normtwo_grad: float32 [512], P(('dp', 'tensor'))
Inputs may be any that keep to these rules, and one draw needn't show every extreme that they name: `entry_counts`: each entry's frequency lies between a power of two below 2^17 and twice it.
All inputs are finite; a program needn't handle non-finite values.
Results may differ from a plain program's by a relative error of at most 0.025.
Values may be sent and summed in bfloat16 or wider, within the bound.
No kernel may reach another device: no remote copies, remote signals or barrier semaphores. Data moves between devices by JAX's collectives and lax.ppermute only.
A program may use at most 256 MiB of HBM per device.

v0:
```python
from functools import partial

import jax
import jax.numpy as jnp
from jax import lax
from jax.sharding import PartitionSpec as P

HD = 64
HYPER_WIDTH = 512
EH = 8
EHD = 64
SUBWORD_SLOTS = 8


NEG = -1000000000.0
EPS = 1e-05
THETA = 10000.0


def layer_norm(values, gain):
    center = values - jnp.mean(values, axis=-1, keepdims=True)
    spread = jnp.mean(center * center, axis=-1, keepdims=True)
    return center * lax.rsqrt(spread + EPS) * gain


def rms_norm(values, gain):
    return values * lax.rsqrt(jnp.mean(values * values, axis=-1, keepdims=True) + EPS) * gain


def rope_tables(length, width):
    half_width = width // 2
    inverse = THETA ** (-(2.0 * jnp.arange(half_width, dtype=jnp.float32)) / width)
    angles = jnp.arange(length, dtype=jnp.float32)[:, None] * inverse[None, :]
    return (jnp.cos(angles), jnp.sin(angles))


def rotate(values, cosine, sine):
    half_width = values.shape[-1] // 2
    former = values[..., :half_width]
    latter = values[..., half_width:]
    return jnp.concatenate(
        [former * cosine - latter * sine, latter * cosine + former * sine], axis=-1
    )


def matmul(left, right):
    return jnp.dot(left, right, preferred_element_type=jnp.float32)


def times_trans(left, right):
    return lax.dot_general(
        left, right, (((1,), (1,)), ((), ())), preferred_element_type=jnp.float32
    )


def trans_times(left, right):
    return lax.dot_general(
        left, right, (((0,), (0,)), ((), ())), preferred_element_type=jnp.float32
    )


def row_sums(values, indices, row_count):
    inside = (indices >= 0) & (indices < row_count)
    picked = jnp.where(inside[:, None], values, 0.0)
    return jax.ops.segment_sum(picked, jnp.where(inside, indices, 0), num_segments=row_count)


def per_device(
    subword_embedding_rows,
    entry_subword_index,
    entry_lengths,
    entry_counts,
    encoder_triple,
    encoder_merge,
    encoder_expand,
    encoder_reduce,
    embed_project,
    normone_gain,
    normtwo_gain,
    frozen_query,
    frozen_key,
    frozen_value,
    frozen_output,
    frozen_gate,
    frozen_upward,
    frozen_downward,
    prenorm_gain,
    midnorm_gain,
    text_tokens,
    cotangent,
):
    bfloat = jnp.bfloat16
    single = jnp.float32
    gathered = (
        lax.all_gather(subword_embedding_rows, "dp", axis=0, tiled=True),
        lax.all_gather(frozen_query, "dp", axis=0, tiled=True),
        lax.all_gather(frozen_key, "dp", axis=0, tiled=True),
        lax.all_gather(frozen_value, "dp", axis=0, tiled=True),
        lax.all_gather(frozen_output, "dp", axis=0, tiled=True),
        lax.all_gather(frozen_gate, "dp", axis=0, tiled=True),
        lax.all_gather(frozen_upward, "dp", axis=0, tiled=True),
        lax.all_gather(frozen_downward, "dp", axis=0, tiled=True),
    )
    table = gathered[0]
    full_query, full_key, full_value, full_output, full_gate, full_upward, full_downward = gathered[
        1:
    ]
    entries = entry_subword_index.shape[0]
    flat_rows = entries * SUBWORD_SLOTS
    flat_ids = entry_subword_index.reshape(-1)
    rows_in = jnp.take(table, flat_ids, axis=0).astype(single)
    valid = jnp.arange(SUBWORD_SLOTS)[None, :] < entry_lengths[:, None]
    normed_one, norm_back_one = jax.vjp(layer_norm, rows_in, normone_gain)
    first_in = normed_one.astype(bfloat)
    triple = matmul(first_in, encoder_triple).astype(bfloat)
    enc_queries = triple[:, :HYPER_WIDTH].reshape(entries, SUBWORD_SLOTS, EH, EHD)
    enc_keys = triple[:, HYPER_WIDTH : 2 * HYPER_WIDTH].reshape(entries, SUBWORD_SLOTS, EH, EHD)
    enc_values = triple[:, 2 * HYPER_WIDTH :].reshape(entries, SUBWORD_SLOTS, EH, EHD)
    enc_scale = EHD ** (-0.5)
    enc_scores = (
        jnp.einsum("nqhd,nkhd->nhqk", enc_queries, enc_keys, preferred_element_type=single)
        * enc_scale
    )
    enc_scores = jnp.where(valid[:, None, None, :], enc_scores, NEG)
    enc_probs = jax.nn.softmax(enc_scores, axis=-1)
    enc_probs_low = enc_probs.astype(bfloat)
    enc_mixed = jnp.einsum(
        "nhqk,nkhd->nqhd", enc_probs_low, enc_values, preferred_element_type=single
    )
    enc_mixed = enc_mixed.reshape(flat_rows, HYPER_WIDTH).astype(bfloat)
    resid_one = rows_in + matmul(enc_mixed, encoder_merge)
    normed_two, norm_back_two = jax.vjp(layer_norm, resid_one, normtwo_gain)
    second_in = normed_two.astype(bfloat)
    expanded = matmul(second_in, encoder_expand)
    activated, gelu_back = jax.vjp(partial(jax.nn.gelu, approximate=False), expanded)
    activated_low = activated.astype(bfloat)
    resid_two = resid_one + matmul(activated_low, encoder_reduce)
    slot_counts = entry_lengths.astype(single)[:, None]
    pooled = (
        jnp.sum(
            jnp.where(
                valid[:, :, None], resid_two.reshape(entries, SUBWORD_SLOTS, HYPER_WIDTH), 0.0
            ),
            axis=1,
        )
        / slot_counts
    )
    pooled_low = pooled.astype(bfloat)
    vectors = matmul(pooled_low, embed_project).astype(bfloat)
    token_weight = (1.0 / jnp.log(1.0 + entry_counts.astype(single))).astype(bfloat)
    all_vectors, all_weights = (
        lax.all_gather(vectors, ("dp", "tensor"), axis=0, tiled=True),
        lax.all_gather(token_weight, ("dp", "tensor"), axis=0, tiled=True),
    )
    resid_in = jnp.take(all_vectors, text_tokens, axis=0).astype(single)
    row_weight = jnp.take(all_weights, text_tokens, axis=0).astype(single)
    pre_one, pre_back_one = jax.vjp(lambda values: rms_norm(values, prenorm_gain), resid_in)
    seq_one = lax.all_gather(pre_one.astype(bfloat), "tensor", axis=0, tiled=True)
    length = seq_one.shape[0]
    heads_here = full_query.shape[1] // HD
    groups_here = full_key.shape[1] // HD
    share = heads_here // groups_here
    cosine, sine = rope_tables(length, HD)

    def to_heads(values, count):
        return values.reshape(length, count, HD).transpose(1, 0, 2)

    def from_heads(values):
        return values.transpose(1, 0, 2).reshape(length, values.shape[0] * HD)

    lm_queries = rotate(to_heads(matmul(seq_one, full_query), heads_here), cosine, sine).astype(
        bfloat
    )
    lm_keys = rotate(to_heads(matmul(seq_one, full_key), groups_here), cosine, sine).astype(bfloat)
    lm_values = to_heads(matmul(seq_one, full_value), groups_here).astype(bfloat)
    block_rows = min(512, length)
    block_total = length // block_rows
    head_scale = HD ** (-0.5)

    def block_scores(block_idx):
        first = block_idx * block_rows
        key_end = first + block_rows
        query_block = lm_queries[:, first:key_end].reshape(groups_here, share, block_rows, HD)
        scores = (
            jnp.einsum(
                "cgqd,ckd->cgqk", query_block, lm_keys[:, :key_end], preferred_element_type=single
            )
            * head_scale
        )
        causal = (first + jnp.arange(block_rows))[:, None] >= jnp.arange(key_end)[None, :]
        return (query_block, jnp.where(causal, scores, NEG))

    outputs = []
    lse_list = []
    for block_idx in range(block_total):
        key_end = (block_idx + 1) * block_rows
        query_block, scores = block_scores(block_idx)
        largest = jnp.max(scores, axis=-1, keepdims=True)
        expon = jnp.exp(scores - largest)
        total = jnp.sum(expon, axis=-1, keepdims=True)
        lse_list.append(largest + jnp.log(total))
        probs_low = (expon / total).astype(bfloat)
        block_out = jnp.einsum(
            "cgqk,ckd->cgqd", probs_low, lm_values[:, :key_end], preferred_element_type=single
        )
        outputs.append(block_out.reshape(heads_here, block_rows, HD))
    lm_mixed = from_heads(jnp.concatenate(outputs, axis=1)).astype(bfloat)
    resid_mid = resid_in + lax.psum_scatter(
        times_trans(lm_mixed, full_output).astype(jnp.bfloat16),
        "tensor",
        scatter_dimension=0,
        tiled=True,
    ).astype(jnp.float32)
    pre_two, pre_back_two = jax.vjp(lambda values: rms_norm(values, midnorm_gain), resid_mid)
    seq_two = lax.all_gather(pre_two.astype(bfloat), "tensor", axis=0, tiled=True)
    gate_raw = matmul(seq_two, full_gate)
    upward_raw = matmul(seq_two, full_upward)
    swiglu, swiglu_back = jax.vjp(
        lambda gate, upward: jax.nn.silu(gate) * upward, gate_raw, upward_raw
    )
    swiglu_low = swiglu.astype(bfloat)
    layer_final = resid_mid + lax.psum_scatter(
        times_trans(swiglu_low, full_downward).astype(jnp.bfloat16),
        "tensor",
        scatter_dimension=0,
        tiled=True,
    ).astype(jnp.float32)
    back_weights = (
        lax.all_gather(frozen_query, "dp", axis=0, tiled=True),
        lax.all_gather(frozen_key, "dp", axis=0, tiled=True),
        lax.all_gather(frozen_value, "dp", axis=0, tiled=True),
        lax.all_gather(frozen_output, "dp", axis=0, tiled=True),
        lax.all_gather(frozen_gate, "dp", axis=0, tiled=True),
        lax.all_gather(frozen_upward, "dp", axis=0, tiled=True),
        lax.all_gather(frozen_downward, "dp", axis=0, tiled=True),
    )
    back_query, back_key, back_value, back_output, back_gate, back_upward, back_downward = (
        back_weights
    )
    out_cot = row_weight[:, None] * cotangent.astype(single)
    seq_down = lax.all_gather(out_cot.astype(bfloat), "tensor", axis=0, tiled=True)
    swiglu_grad = matmul(seq_down, back_downward)
    gate_grad, upward_grad = swiglu_back(swiglu_grad)
    gate_low = gate_grad.astype(bfloat)
    upward_low = upward_grad.astype(bfloat)
    norm_two_grad = lax.psum_scatter(
        (times_trans(gate_low, back_gate) + times_trans(upward_low, back_upward)).astype(
            jnp.bfloat16
        ),
        "tensor",
        scatter_dimension=0,
        tiled=True,
    ).astype(jnp.float32)
    mid_grad = out_cot + pre_back_two(norm_two_grad)[0]
    seq_mid = lax.all_gather(mid_grad.astype(bfloat), "tensor", axis=0, tiled=True)
    mixed_grad = to_heads(matmul(seq_mid, back_output).astype(bfloat), heads_here)
    query_parts = []
    key_acc = jnp.zeros((groups_here, length, HD), single)
    value_acc = jnp.zeros((groups_here, length, HD), single)
    for block_idx in range(block_total):
        first = block_idx * block_rows
        key_end = first + block_rows
        query_block, scores = block_scores(block_idx)
        probs = jnp.exp(scores - lse_list[block_idx])
        grad_block = mixed_grad[:, first:key_end].reshape(groups_here, share, block_rows, HD)
        prob_grad = jnp.einsum(
            "cgqd,ckd->cgqk", grad_block, lm_values[:, :key_end], preferred_element_type=single
        )
        delta = jnp.sum(probs * prob_grad, axis=-1, keepdims=True)
        score_grad = (probs * (prob_grad - delta)).astype(bfloat)
        block_query = jnp.einsum(
            "cgqk,ckd->cgqd", score_grad, lm_keys[:, :key_end], preferred_element_type=single
        )
        query_parts.append(block_query.reshape(heads_here, block_rows, HD) * head_scale)
        key_part = (
            jnp.einsum("cgqk,cgqd->ckd", score_grad, query_block, preferred_element_type=single)
            * head_scale
        )
        key_acc = key_acc.at[:, :key_end].add(key_part)
        value_part = jnp.einsum(
            "cgqk,cgqd->ckd", probs.astype(bfloat), grad_block, preferred_element_type=single
        )
        value_acc = value_acc.at[:, :key_end].add(value_part)
    query_grad = from_heads(rotate(jnp.concatenate(query_parts, axis=1), cosine, -sine)).astype(
        bfloat
    )
    key_grad = from_heads(rotate(key_acc, cosine, -sine)).astype(bfloat)
    value_grad = from_heads(value_acc).astype(bfloat)
    norm_one_grad = lax.psum_scatter(
        (
            times_trans(query_grad, back_query)
            + times_trans(key_grad, back_key)
            + times_trans(value_grad, back_value)
        ).astype(jnp.bfloat16),
        "tensor",
        scatter_dimension=0,
        tiled=True,
    ).astype(jnp.float32)
    input_grad = mid_grad + pre_back_one(norm_one_grad)[0]
    input_low = input_grad.astype(bfloat).astype(single)
    vector_grad = lax.psum_scatter(
        row_sums(input_low, text_tokens, lax.axis_size(("dp", "tensor")) * entries),
        ("dp", "tensor"),
        scatter_dimension=0,
        tiled=True,
    )
    vector_low = vector_grad.astype(bfloat)
    project_grad = trans_times(pooled_low, vector_low)
    pooled_grad = times_trans(vector_low, embed_project) / slot_counts
    grid_grad = jnp.where(valid[:, :, None], pooled_grad[:, None, :], 0.0).reshape(
        flat_rows, HYPER_WIDTH
    )
    reduce_in = grid_grad.astype(bfloat)
    reduce_grad = trans_times(activated_low, reduce_in)
    expand_in = gelu_back(times_trans(reduce_in, encoder_reduce))[0].astype(bfloat)
    expand_grad = trans_times(second_in, expand_in)
    resid_part, normtwo_grad = norm_back_two(times_trans(expand_in, encoder_expand))
    resid_one_grad = grid_grad + resid_part
    merge_in = resid_one_grad.astype(bfloat)
    merge_grad = trans_times(enc_mixed, merge_in)
    enc_mixed_grad = (
        times_trans(merge_in, encoder_merge).astype(bfloat).reshape(entries, SUBWORD_SLOTS, EH, EHD)
    )
    enc_prob_grad = jnp.einsum(
        "nqhd,nkhd->nhqk", enc_mixed_grad, enc_values, preferred_element_type=single
    )
    enc_delta = jnp.sum(enc_probs * enc_prob_grad, axis=-1, keepdims=True)
    enc_score_grad = (enc_probs * (enc_prob_grad - enc_delta)).astype(bfloat)
    enc_query_grad = (
        jnp.einsum("nhqk,nkhd->nqhd", enc_score_grad, enc_keys, preferred_element_type=single)
        * enc_scale
    )
    enc_key_grad = (
        jnp.einsum("nhqk,nqhd->nkhd", enc_score_grad, enc_queries, preferred_element_type=single)
        * enc_scale
    )
    enc_value_grad = jnp.einsum(
        "nhqk,nqhd->nkhd", enc_probs_low, enc_mixed_grad, preferred_element_type=single
    )
    triple_in = jnp.concatenate(
        [
            enc_query_grad.reshape(flat_rows, HYPER_WIDTH),
            enc_key_grad.reshape(flat_rows, HYPER_WIDTH),
            enc_value_grad.reshape(flat_rows, HYPER_WIDTH),
        ],
        axis=1,
    ).astype(bfloat)
    triple_grad = trans_times(first_in, triple_in)
    rows_part, normone_grad = norm_back_one(times_trans(triple_in, encoder_triple))
    rows_grad_low = (resid_one_grad + rows_part).astype(bfloat)
    table_rows = subword_embedding_rows.shape[0] // lax.axis_size("tensor")
    rows_low = rows_grad_low.astype(single)
    subword_grad = lax.psum_scatter(
        row_sums(rows_low, flat_ids, lax.axis_size(("dp", "tensor")) * table_rows),
        ("dp", "tensor"),
        scatter_dimension=0,
        tiled=True,
    )
    summed = (
        lax.psum_scatter(triple_grad, ("dp", "tensor"), scatter_dimension=0, tiled=True),
        lax.psum_scatter(merge_grad, ("dp", "tensor"), scatter_dimension=0, tiled=True),
        lax.psum_scatter(expand_grad, ("dp", "tensor"), scatter_dimension=0, tiled=True),
        lax.psum_scatter(reduce_grad, ("dp", "tensor"), scatter_dimension=0, tiled=True),
        lax.psum_scatter(project_grad, ("dp", "tensor"), scatter_dimension=0, tiled=True),
        lax.psum_scatter(normone_grad, ("dp", "tensor"), scatter_dimension=0, tiled=True),
        lax.psum_scatter(normtwo_grad, ("dp", "tensor"), scatter_dimension=0, tiled=True),
    )
    return (
        layer_final.astype(bfloat),
        vectors,
        subword_grad,
        summed[0],
        summed[1],
        summed[2],
        summed[3],
        summed[4],
        summed[5],
        summed[6],
    )


def solution(mesh):
    return jax.shard_map(
        per_device,
        mesh=mesh,
        in_specs=(
            P("dp", None),
            P(("dp", "tensor"), None),
            P(("dp", "tensor")),
            P(("dp", "tensor")),
            P(),
            P(),
            P(),
            P(),
            P(),
            P(),
            P(),
            P("dp", "tensor"),
            P("dp", "tensor"),
            P("dp", "tensor"),
            P("dp", "tensor"),
            P("dp", "tensor"),
            P("dp", "tensor"),
            P("dp", "tensor"),
            P(),
            P(),
            P(("dp", "tensor")),
            P(("dp", "tensor"), None),
        ),
        out_specs=(
            P(("dp", "tensor"), None),
            P(("dp", "tensor"), None),
            P(("dp", "tensor"), None),
            P(("dp", "tensor"), None),
            P(("dp", "tensor"), None),
            P(("dp", "tensor"), None),
            P(("dp", "tensor"), None),
            P(("dp", "tensor"), None),
            P(("dp", "tensor")),
            P(("dp", "tensor")),
        ),
        check_vma=False,
    )
```

profile of v0, /device:TPU:0, one launch (start us, length us, event | category | flops | bytes accessed | tf_op | source)
XLA Modules:
  0.0 3457.4 jit_solution(1992650504602529986)
XLA Ops:
  11.4 158.8 %all-gather.12.cloned.1.call-done = bf16[32000,512]{1,0:T(8,128)(2,1)} async-done(((bf16[4000,512]{1,0:T(8,128)(2,1)}), bf16[32000,512]{1,0:T(8,128)(2,1)}) %all-gather.12.cloned.1.call-update) | async-done | bytes 32768016 | tf_op jit(solution)/shard_map/all_gather | solution.py:95
  191.4 39.4 %all-reduce.2 = bf16[512]{0:T(512)(128)(2,1)S(1)} all-reduce(bf16[512]{0:T(512)(128)(2,1)S(1)} %dynamic-update-slice.10), channel_id=1, replica_groups=mesh['dp'=8,'tensor'=4] {'dp','tensor'}, use_global_device_ids=true, to_apply=%add.2 | all-reduce | flops 512 | bytes 2048
  234.0 13.7 all-gather.14.cloned.1.call-done
  278.1 55.5 %all-gather.16.cloned.1.call-done = bf16[1024,2048]{1,0:T(8,128)(2,1)} async-done(((bf16[256,2048]{1,0:T(8,128)(2,1)}), bf16[1024,2048]{1,0:T(8,128)(2,1)}) %all-gather.16.cloned.1.call-update) | async-done | bytes 4194320 | tf_op jit(solution)/shard_map/all_gather | solution.py:158
  338.4 23.4 all-gather.18.cloned.1.call-done
  402.5 72.3 %reduce-scatter.15.cloned.1.call-done = bf16[256,2048]{1,0:T(8,128)(2,1)} async-done(((bf16[1024,2048]{1,0:T(8,128)(2,1)}), bf16[256,2048]{1,0:T(8,128)(2,1)}) %reduce-scatter.15.cloned.1.call-update) | async-done | bytes 1048592 | tf_op jit(solution)/shard_map/reduce_scatter | solution.py:208
  480.1 77.6 %all-gather.30.cloned.1.call-done = bf16[1024,2048]{1,0:T(8,128)(2,1)} async-done(((bf16[256,2048]{1,0:T(8,128)(2,1)}), bf16[1024,2048]{1,0:T(8,128)(2,1)}) %all-gather.30.cloned.1.call-update) | async-done | bytes 4194320 | tf_op jit(solution)/shard_map/all_gather | solution.py:241
  557.7 43.9 %all-gather.28.cloned.1.call-done = bf16[2048,1408]{1,0:T(8,128)(2,1)} async-done(((bf16[256,1408]{1,0:T(8,128)(2,1)}), bf16[2048,1408]{1,0:T(8,128)(2,1)}) %all-gather.28.cloned.1.call-update) | async-done | bytes 5767184 | tf_op jit(solution)/shard_map/all_gather | solution.py:102
  601.6 12.1 fusion.185
  613.7 33.3 all-gather.24.cloned.1.call-done
  647.0 82.9 %all-gather.22.cloned.1.call-done = bf16[1024,2048]{1,0:T(8,128)(2,1)} async-done(((bf16[256,2048]{1,0:T(8,128)(2,1)}), bf16[1024,2048]{1,0:T(8,128)(2,1)}) %all-gather.22.cloned.1.call-update) | async-done | bytes 4194320 | tf_op jit(solution)/shard_map/all_gather | solution.py:215
  729.9 11.7 fusion.183
  741.5 32.2 all-gather.26.cloned.1.call-done
  773.8 11.8 fusion.184
  785.6 13.0 fusion.17
  798.6 14.6 add_convert_fusion.1
  813.4 12.9 convolution_convert_fusion
  826.3 63.9 %reduce-scatter.19.cloned.1.call-done = bf16[256,2048]{1,0:T(8,128)(2,1)} async-done(((bf16[1024,2048]{1,0:T(8,128)(2,1)}), bf16[256,2048]{1,0:T(8,128)(2,1)}) %reduce-scatter.19.cloned.1.call-update) | async-done | bytes 1048592 | tf_op jit(solution)/shard_map/reduce_scatter | solution.py:246
  892.5 77.4 %reduce-scatter.17.cloned.1.call-done = bf16[256,2048]{1,0:T(8,128)(2,1)} async-done(((bf16[1024,2048]{1,0:T(8,128)(2,1)}), bf16[256,2048]{1,0:T(8,128)(2,1)}) %reduce-scatter.17.cloned.1.call-update) | async-done | bytes 1048592 | tf_op jit(solution)/shard_map/reduce_scatter | solution.py:222
  974.6 81.3 %all-gather.32.cloned.1.call-done = bf16[1024,2048]{1,0:T(8,128)(2,1)} async-done(((bf16[256,2048]{1,0:T(8,128)(2,1)}), bf16[1024,2048]{1,0:T(8,128)(2,1)}) %all-gather.32.cloned.1.call-update) | async-done | bytes 4194320 | tf_op jit(solution)/shard_map/all_gather | solution.py:255
  1124.9 14.9 add_convert_fusion
  1140.4 74.9 %reduce-scatter.21.cloned.1.call-done = bf16[256,2048]{1,0:T(8,128)(2,1)} async-done(((bf16[1024,2048]{1,0:T(8,128)(2,1)}), bf16[256,2048]{1,0:T(8,128)(2,1)}) %reduce-scatter.21.cloned.1.call-update) | async-done | bytes 1048592 | tf_op jit(solution)/shard_map/reduce_scatter | solution.py:289
  1227.1 147.5 %reduce-scatter.23.cloned.1.call-done = f32[16,2048]{1,0:T(8,128)} async-done(((f32[512,2048]{1,0:T(8,128)}), f32[16,2048]{1,0:T(8,128)}) %reduce-scatter.23.cloned.1.call-update) | async-done | bytes 131088 | tf_op jit(solution)/shard_map/reduce_scatter | solution.py:301
  1413.3 20.8 broadcast_in_dim.216
  1434.1 15.9 scatter_fusion
  1450.7 37.8 %all-reduce.6 = (f32[512]{0:T(512)S(1)}, f32[512]{0:T(512)S(1)}) all-reduce(f32[512]{0:T(512)S(1)} %get-tuple-element.76, f32[512]{0:T(512)S(1)} %copy-done.99), channel_id=13, replica_groups=mesh['dp'=8,'tensor'=4] {'dp','tensor'}, use_global_device_ids=true, to_apply=%region_36.37.clone | all-reduce | flops 1024 | bytes 8192
  1489.7 27.6 reduce-scatter.27.cloned.1.call-done
  1517.3 104.9 %reduce-scatter.25.cloned.1.call-done = f32[16,1536]{1,0:T(8,128)} async-done(((f32[512,1536]{1,0:T(8,128)}), f32[16,1536]{1,0:T(8,128)}) %reduce-scatter.25.cloned.1.call-update) | async-done | bytes 98320 | tf_op jit(solution)/shard_map/reduce_scatter | solution.py:360
  1622.2 149.8 %reduce-scatter.29.cloned.1.call-done = f32[16,2048]{1,0:T(8,128)} async-done(((f32[512,2048]{1,0:T(8,128)}), f32[16,2048]{1,0:T(8,128)}) %reduce-scatter.29.cloned.1.call-update) | async-done | bytes 131088 | tf_op jit(solution)/shard_map/reduce_scatter | solution.py:362
  1772.0 148.9 %reduce-scatter.31.cloned.1.call-done = f32[64,512]{1,0:T(8,128)} async-done(((f32[2048,512]{1,0:T(8,128)}), f32[64,512]{1,0:T(8,128)}) %reduce-scatter.31.cloned.1.call-update) | async-done | bytes 131088 | tf_op jit(solution)/shard_map/reduce_scatter | solution.py:363
  1920.9 150.2 %reduce-scatter.33.cloned.1.call-done = f32[16,2048]{1,0:T(8,128)} async-done(((f32[512,2048]{1,0:T(8,128)}), f32[16,2048]{1,0:T(8,128)}) %reduce-scatter.33.cloned.1.call-update) | async-done | bytes 131088 | tf_op jit(solution)/shard_map/reduce_scatter | solution.py:364
  2071.2 1379.2 %reduce-scatter.35.cloned.1.call-done = f32[1000,512]{1,0:T(8,128)} async-done(((f32[32000,512]{1,0:T(8,128)}), f32[1000,512]{1,0:T(8,128)}) %reduce-scatter.35.cloned.1.call-update) | async-done | bytes 2048016
  (427 shorter events, 237.0 us)
Async XLA Ops:
  7.2 177.4 %copy-start = (bf16[512,2048]{1,0:T(8,128)(2,1)S(1)}, bf16[512,2048]{1,0:T(8,128)(2,1)}, u32[]{:S(2)}) copy-start(bf16[512,2048]{1,0:T(8,128)(2,1)} %param.40) | copy-start | bytes 6291460
  7.2 166.2 %copy-start.67 = (f32[512]{0:T(512)S(1)}, f32[512]{0:T(512)}, u32[]{:S(2)}) copy-start(f32[512]{0:T(512)} %param.43) | copy-start | bytes 6148
  7.2 162.9 %all-gather.12.cloned.1.call-start = ((), (), s32[]{:S(2)}) async-start(), calls=%async_computation.11 | async-start | bytes 36864000 | tf_op jit(solution)/shard_map/all_gather | solution.py:95
  7.9 239.8 %all-gather.14.cloned.1.call-start = ((), (), s32[]{:S(2)}) async-start(), calls=%async_computation.12 | async-start | bytes 2162688 | tf_op jit(solution)/shard_map/all_gather | solution.py:152
  9.6 179.5 %copy-start.102 = (f32[16]{0:T(128)}, f32[16]{0:T(128)S(1)}, u32[]{:S(2)}) copy-start(f32[16]{0:T(128)S(1)} %convert_element_type.210) | copy-start | bytes 196
  10.6 173.4 %copy-start.76 = (pred[128]{0:T(512)(128)(4,1)}, pred[128]{0:T(512)(128)(4,1)S(1)}, u32[]{:S(2)}) copy-start(pred[128]{0:T(512)(128)(4,1)S(1)} %get-tuple-element.102) | copy-start | bytes 388
  11.4 177.2 %copy-start.72 = (pred[16,8]{1,0:T(8,128)(4,1)}, pred[16,8]{1,0:T(8,128)(4,1)S(1)}, u32[]{:S(2)}) copy-start(pred[16,8]{1,0:T(8,128)(4,1)S(1)} %iota_compare_fusion.2) | copy-start | bytes 388
  191.1 142.5 %all-gather.16.cloned.1.call-start = ((), (), s32[]{:S(2)}) async-start(), calls=%async_computation.13 | async-start | bytes 5242880 | tf_op jit(solution)/shard_map/all_gather | solution.py:158
  251.9 717.9 %copy-start.3 = (bf16[256,2048]{1,0:T(8,128)(2,1)}, bf16[256,2048]{1,0:T(8,128)(2,1)S(1)}, u32[]{:S(2)}) copy-start(bf16[256,2048]{1,0:T(8,128)(2,1)S(1)} %gather_fusion.1) | copy-start | bytes 3145732
  253.8 108.0 %all-gather.18.cloned.1.call-start = ((), (), s32[]{:S(2)}) async-start(), calls=%async_computation.14 | async-start | bytes 2359296 | tf_op jit(solution)/shard_map/all_gather | solution.py:96
  254.4 137.1 %all-gather.20.cloned.1.call-start = ((), (), s32[]{:S(2)}) async-start(), calls=%async_computation.15 | async-start | bytes 2359296 | tf_op jit(solution)/shard_map/all_gather | solution.py:99
  255.0 219.7 %reduce-scatter.15.cloned.1.call-start = ((), (), s32[]{:S(2)}) async-start(), calls=%async_computation.16 | async-start | bytes 5242880 | tf_op jit(solution)/shard_map/reduce_scatter | solution.py:208
  380.1 686.9 %copy-start.43 = (bf16[1024,64]{0,1:T(8,128)(2,1)}, bf16[1024,64]{0,1:T(8,128)(2,1)S(1)}, u32[]{:S(2)}) copy-start(bf16[1024,64]{0,1:T(8,128)(2,1)S(1)} %convolution_convert_fusion.8) | copy-start | bytes 393220
  397.8 159.8 %all-gather.30.cloned.1.call-start = ((), (), s32[]{:S(2)}) async-start(), calls=%async_computation.22 | async-start | bytes 5242880 | tf_op jit(solution)/shard_map/all_gather | solution.py:241
  400.9 200.7 %all-gather.28.cloned.1.call-start = ((), (), s32[]{:S(2)}) async-start(), calls=%async_computation.20 | async-start | bytes 6488064 | tf_op jit(solution)/shard_map/all_gather | solution.py:102
  401.7 245.3 %all-gather.24.cloned.1.call-start = ((), (), s32[]{:S(2)}) async-start(), calls=%async_computation.18 | async-start | bytes 6488064 | tf_op jit(solution)/shard_map/all_gather | solution.py:100
  402.4 327.4 %all-gather.22.cloned.1.call-start = ((), (), s32[]{:S(2)}) async-start(), calls=%async_computation.17 | async-start | bytes 5242880 | tf_op jit(solution)/shard_map/all_gather | solution.py:215
  476.5 493.3 %copy-start.82 = (f32[256]{0:T(256)}, f32[256]{0:T(256)S(1)}, u32[]{:S(2)}) copy-start(f32[256]{0:T(256)S(1)} %fusion.145) | copy-start | bytes 3076
  479.3 294.5 %all-gather.26.cloned.1.call-start = ((), (), s32[]{:S(2)}) async-start(), calls=%async_computation.19 | async-start | bytes 6488064 | tf_op jit(solution)/shard_map/all_gather | solution.py:101
  480.0 410.2 %reduce-scatter.19.cloned.1.call-start = ((), (), s32[]{:S(2)}) async-start(), calls=%async_computation.23 | async-start | bytes 5242880 | tf_op jit(solution)/shard_map/reduce_scatter | solution.py:246
  813.3 156.5 %reduce-scatter.17.cloned.1.call-start = ((), (), s32[]{:S(2)}) async-start(), calls=%async_computation.21 | async-start | bytes 5242880 | tf_op jit(solution)/shard_map/reduce_scatter | solution.py:222
  826.3 229.6 %all-gather.32.cloned.1.call-start = ((), (), s32[]{:S(2)}) async-start(), calls=%async_computation.24 | async-start | bytes 5242880 | tf_op jit(solution)/shard_map/all_gather | solution.py:255
  974.5 240.8 %reduce-scatter.21.cloned.1.call-start = ((), (), s32[]{:S(2)}) async-start(), calls=%async_computation.25 | async-start | bytes 5242880 | tf_op jit(solution)/shard_map/reduce_scatter | solution.py:289
  1139.8 234.7 %reduce-scatter.23.cloned.1.call-start = ((), (), s32[]{:S(2)}) async-start(), calls=%async_computation.26 | async-start | bytes 4325376 | tf_op jit(solution)/shard_map/reduce_scatter | solution.py:301
  1226.3 153.4 %copy-start.9 = (f32[128,512]{1,0:T(8,128)S(1)}, f32[128,512]{1,0:T(8,128)}, u32[]{:S(2)}) copy-start(f32[128,512]{1,0:T(8,128)} %copy-done.8) | copy-start | bytes 786436
  1226.4 290.9 %reduce-scatter.27.cloned.1.call-start = ((), (), s32[]{:S(2)}) async-start(), calls=%async_computation.28 | async-start | bytes 1081344 | tf_op jit(solution)/shard_map/reduce_scatter | solution.py:361
  1227.1 155.8 %copy-start.86 = (pred[128]{0:T(512)(128)(4,1)}, pred[128]{0:T(512)(128)(4,1)S(1)}, u32[]{:S(2)}) copy-start(pred[128]{0:T(512)(128)(4,1)S(1)} %lt.89) | copy-start | bytes 388
  1382.9 239.3 %reduce-scatter.25.cloned.1.call-start = ((), (), s32[]{:S(2)}) async-start(), calls=%async_computation.27 | async-start | bytes 3244032 | tf_op jit(solution)/shard_map/reduce_scatter | solution.py:360
  1399.6 372.4 %reduce-scatter.29.cloned.1.call-start = ((), (), s32[]{:S(2)}) async-start(), calls=%async_computation.29 | async-start | bytes 4325376 | tf_op jit(solution)/shard_map/reduce_scatter | solution.py:362
  1403.8 517.1 %reduce-scatter.31.cloned.1.call-start = ((), (), s32[]{:S(2)}) async-start(), calls=%async_computation.30 | async-start | bytes 4325376 | tf_op jit(solution)/shard_map/reduce_scatter | solution.py:363
  1407.7 663.5 %reduce-scatter.33.cloned.1.call-start = ((), (), s32[]{:S(2)}) async-start(), calls=%async_computation.31 | async-start | bytes 4325376 | tf_op jit(solution)/shard_map/reduce_scatter | solution.py:364
  1410.6 2039.8 %reduce-scatter.35.cloned.1.call-start = ((), (), s32[]{:S(2)}) async-start(), calls=%async_computation.32 | async-start | bytes 67584000
  (118 other events, 2828.8 us)
Sparse Core Ops, SparseCore 0:
  9.9 160.1 all-gather.11
  191.2 56.4 all-gather.13
  253.9 79.6 all-gather.15
  335.3 26.4 all-gather.17
  363.5 27.8 all-gather.19
  397.9 76.7 reduce-scatter.14
  476.4 81.2 all-gather.29
  559.7 41.8 all-gather.27
  603.6 43.3 all-gather.23
  649.1 80.7 all-gather.21
  731.9 41.8 all-gather.25
  813.4 76.7 reduce-scatter.18
  892.5 77.2 reduce-scatter.16
  974.6 81.2 all-gather.31
  1140.0 75.2 reduce-scatter.20
  1226.5 148.0 reduce-scatter.22
  1383.0 134.2 reduce-scatter.26
  1524.0 98.0 reduce-scatter.24
  1625.1 146.8 reduce-scatter.28
  1774.8 146.0 reduce-scatter.30
  1923.9 147.2 reduce-scatter.32
  2074.2 1376.1 reduce-scatter.34
where the time goes:
time: 3470 us; the launch traced here: 3460 us
  waiting for transfers between devices  3010 us (87%)
  matrix products  211 us (6%)
  blocking collectives  97.1 us (3%)
  other arithmetic  75.7 us (2%)
  local copies, waits for them, and re-layouts  48.9 us (1%)
    unnamed x23, waiting for transfers between devices  1380 us
    all_gather x1, waiting for transfers between devices, per_device(): lax.all_gather(subword_embedding_rows, 'dp', axis=0, tiled=True)  159 us
    reduce_scatter x1, waiting for transfers between devices, per_device(): lax.psum_scatter(project_grad, ('dp', 'tensor'), scatter_dimension=0, til...  150 us
    reduce_scatter x1, waiting for transfers between devices, per_device(): lax.psum_scatter(expand_grad, ('dp', 'tensor'), scatter_dimension=0, tile...  150 us
    reduce_scatter x1, waiting for transfers between devices, per_device(): lax.psum_scatter(reduce_grad, ('dp', 'tensor'), scatter_dimension=0, tile...  149 us
    reduce_scatter x1, waiting for transfers between devices, per_device(): lax.psum_scatter(row_sums(input_low, text_tokens, lax.axis_size(('dp', 't...  147 us
    reduce_scatter x1, waiting for transfers between devices, per_device(): lax.psum_scatter(triple_grad, ('dp', 'tensor'), scatter_dimension=0, tile...  105 us
    all_gather x1, waiting for transfers between devices, per_device(): lax.all_gather(pre_two.astype(bfloat), 'tensor', axis=0, tiled=True)  82.9 us
  transfers between devices with their start and end apart: 22, of which 22 were waited for; matrix products, arithmetic and copies ran while one was open for 4% of the time, Pallas kernels for 0%

commit v1 on v0

v1 whole, which is shorter than its diff:
```python
from functools import partial

import jax
import jax.numpy as jnp
from jax import lax
from jax.sharding import PartitionSpec as P

HD = 64
HYPER_WIDTH = 512
EH = 8
EHD = 64
SUBWORD_SLOTS = 8


NEG = -1000000000.0
EPS = 1e-05
THETA = 10000.0


def layer_norm(values, gain):
    center = values - jnp.mean(values, axis=-1, keepdims=True)
    spread = jnp.mean(center * center, axis=-1, keepdims=True)
    return center * lax.rsqrt(spread + EPS) * gain


def rms_norm(values, gain):
    return values * lax.rsqrt(jnp.mean(values * values, axis=-1, keepdims=True) + EPS) * gain


def rope_tables(length, width):
    half_width = width // 2
    inverse = THETA ** (-(2.0 * jnp.arange(half_width, dtype=jnp.float32)) / width)
    angles = jnp.arange(length, dtype=jnp.float32)[:, None] * inverse[None, :]
    return (jnp.cos(angles), jnp.sin(angles))


def rotate(values, cosine, sine):
    half_width = values.shape[-1] // 2
    former = values[..., :half_width]
    latter = values[..., half_width:]
    return jnp.concatenate(
        [former * cosine - latter * sine, latter * cosine + former * sine], axis=-1
    )


def matmul(left, right):
    return jnp.dot(left, right, preferred_element_type=jnp.float32)


def times_trans(left, right):
    return lax.dot_general(
        left, right, (((1,), (1,)), ((), ())), preferred_element_type=jnp.float32
    )


def trans_times(left, right):
    return lax.dot_general(
        left, right, (((0,), (0,)), ((), ())), preferred_element_type=jnp.float32
    )


def ring(values, shift=1):
    size = lax.axis_size("tensor")
    return lax.ppermute(values, "tensor", [(i, (i + shift) % size) for i in range(size)])


def in_order(blocks, first):
    size = len(blocks)
    stacked = jnp.stack(blocks)
    return [
        lax.dynamic_index_in_dim(stacked, lax.rem(first - at + size, size), 0, keepdims=False)
        for at in range(size)
    ]


def per_device(
    subword_embedding_rows,
    entry_subword_index,
    entry_lengths,
    entry_counts,
    encoder_triple,
    encoder_merge,
    encoder_expand,
    encoder_reduce,
    embed_project,
    normone_gain,
    normtwo_gain,
    frozen_query,
    frozen_key,
    frozen_value,
    frozen_output,
    frozen_gate,
    frozen_upward,
    frozen_downward,
    prenorm_gain,
    midnorm_gain,
    text_tokens,
    cotangent,
):
    bfloat = jnp.bfloat16
    single = jnp.float32
    dp_size = lax.axis_size("dp")
    tensor_size = lax.axis_size("tensor")
    dp_at = lax.axis_index("dp")
    tensor_at = lax.axis_index("tensor")
    device_at = dp_at * tensor_size + tensor_at
    entries = entry_subword_index.shape[0]
    entry_total = entries * dp_size * tensor_size
    flat_rows = entries * SUBWORD_SLOTS
    table_rows = subword_embedding_rows.shape[0]
    model_width = embed_project.shape[1]

    with jax.named_scope("ids"):
        packed = jnp.concatenate([entry_subword_index, entry_counts[:, None]], axis=1)
        packed_dp = lax.all_gather(packed, "dp", axis=0, tiled=False)
        packed_all = lax.all_gather(
            jnp.concatenate([packed_dp.reshape(-1), text_tokens]), "tensor", axis=0, tiled=False
        )
    with jax.named_scope("qkv_weights"):
        frozen_triple = jnp.concatenate([frozen_query, frozen_key, frozen_value], axis=1)
        full_triple = lax.all_gather(frozen_triple, "dp", axis=0, tiled=True)
    with jax.named_scope("output_weights"):
        wide_output = lax.all_gather(frozen_output, "tensor", axis=1, tiled=True)
        full_output = lax.all_gather(wide_output, "dp", axis=0, tiled=True)
    with jax.named_scope("mlp_weights"):
        full_downward = lax.all_gather(frozen_downward, "dp", axis=0, tiled=True)
        full_gate = lax.all_gather(frozen_gate, "dp", axis=0, tiled=True)
        full_upward = lax.all_gather(frozen_upward, "dp", axis=0, tiled=True)
    with jax.named_scope("cot_ring"):
        cot_blocks = [cotangent]
        for _ in range(tensor_size - 1):
            cot_blocks.append(ring(cot_blocks[-1]))

    with jax.named_scope("lookup"):
        local_ids = packed_dp[:, :, :SUBWORD_SLOTS].reshape(-1) - dp_at * table_rows
        inside = (local_ids >= 0) & (local_ids < table_rows)
        served = jnp.take(
            subword_embedding_rows, jnp.clip(local_ids, 0, table_rows - 1), axis=0
        )
        served = jnp.where(inside[:, None], served, jnp.zeros((), bfloat))
        served = lax.all_to_all(
            served.reshape(dp_size, flat_rows, HYPER_WIDTH), "dp", 0, 0, tiled=True
        )
        rows_in = jnp.sum(served.astype(single), axis=0)

    with jax.named_scope("hyper_fwd"):
        valid = jnp.arange(SUBWORD_SLOTS)[None, :] < entry_lengths[:, None]
        normed_one, norm_back_one = jax.vjp(layer_norm, rows_in, normone_gain)
        first_in = normed_one.astype(bfloat)
        triple = matmul(first_in, encoder_triple).astype(bfloat)
        enc_queries = triple[:, :HYPER_WIDTH].reshape(entries, SUBWORD_SLOTS, EH, EHD)
        enc_keys = triple[:, HYPER_WIDTH : 2 * HYPER_WIDTH].reshape(
            entries, SUBWORD_SLOTS, EH, EHD
        )
        enc_values = triple[:, 2 * HYPER_WIDTH :].reshape(entries, SUBWORD_SLOTS, EH, EHD)
        enc_scale = EHD ** (-0.5)
        enc_scores = (
            jnp.einsum("nqhd,nkhd->nhqk", enc_queries, enc_keys, preferred_element_type=single)
            * enc_scale
        )
        enc_scores = jnp.where(valid[:, None, None, :], enc_scores, NEG)
        enc_probs = jax.nn.softmax(enc_scores, axis=-1)
        enc_probs_low = enc_probs.astype(bfloat)
        enc_mixed = jnp.einsum(
            "nhqk,nkhd->nqhd", enc_probs_low, enc_values, preferred_element_type=single
        )
        enc_mixed = enc_mixed.reshape(flat_rows, HYPER_WIDTH).astype(bfloat)
        resid_one = rows_in + matmul(enc_mixed, encoder_merge)
        normed_two, norm_back_two = jax.vjp(layer_norm, resid_one, normtwo_gain)
        second_in = normed_two.astype(bfloat)
        expanded = matmul(second_in, encoder_expand)
        activated, gelu_back = jax.vjp(partial(jax.nn.gelu, approximate=False), expanded)
        activated_low = activated.astype(bfloat)
        resid_two = resid_one + matmul(activated_low, encoder_reduce)
        slot_counts = entry_lengths.astype(single)[:, None]
        pooled = (
            jnp.sum(
                jnp.where(
                    valid[:, :, None],
                    resid_two.reshape(entries, SUBWORD_SLOTS, HYPER_WIDTH),
                    0.0,
                ),
                axis=1,
            )
            / slot_counts
        )
        pooled_low = pooled.astype(bfloat)
    with jax.named_scope("pooled_gather"):
        all_pooled = lax.all_gather(pooled_low, "tensor", axis=0, tiled=True)
        all_pooled = lax.all_gather(all_pooled, "dp", axis=0, tiled=True)

    with jax.named_scope("entry_vectors"):
        all_vectors = matmul(all_pooled, embed_project).astype(bfloat)
        vectors = lax.dynamic_slice_in_dim(all_vectors, device_at * entries, entries, 0)
        packed_ids = packed_all[:, : dp_size * entries * (SUBWORD_SLOTS + 1)].reshape(
            tensor_size, dp_size, entries, SUBWORD_SLOTS + 1
        )
        packed_ids = packed_ids.transpose(1, 0, 2, 3).reshape(entry_total, SUBWORD_SLOTS + 1)
        all_ids = packed_ids[:, :SUBWORD_SLOTS].reshape(-1)
        all_weights = (1.0 / jnp.log(1.0 + packed_ids[:, SUBWORD_SLOTS].astype(single))).astype(
            bfloat
        )
        seq_tokens = packed_all[:, dp_size * entries * (SUBWORD_SLOTS + 1) :].reshape(-1)
        length = seq_tokens.shape[0]
        rows_here = text_tokens.shape[0]
        seq_hot = (seq_tokens[:, None] == jnp.arange(entry_total)[None, :]).astype(bfloat)
        own_hot = (text_tokens[:, None] == jnp.arange(entry_total)[None, :]).astype(bfloat)
        seq_weight = matmul(seq_hot, all_weights[:, None])
        all_wide = all_vectors.astype(single)
        entry_normed, entry_norm_back = jax.vjp(
            lambda values: rms_norm(values, prenorm_gain), all_wide
        )
        entry_normed = entry_normed.astype(bfloat)
        entry_triple = matmul(entry_normed, full_triple)
        entry_high = entry_triple.astype(bfloat)
        entry_rest = (entry_triple - entry_high.astype(single)).astype(bfloat)
        seq_triple = matmul(seq_hot, entry_high) + matmul(seq_hot, entry_rest)
        resid_in = matmul(own_hot, all_vectors)

    heads_here = frozen_query.shape[1] // HD
    groups_here = frozen_key.shape[1] // HD
    query_width = frozen_query.shape[1]
    key_width = frozen_key.shape[1]
    share = heads_here // groups_here
    cosine, sine = rope_tables(length, HD)

    def to_heads(values, count):
        return values.reshape(length, count, HD).transpose(1, 0, 2)

    def from_heads(values):
        return values.transpose(1, 0, 2).reshape(length, values.shape[0] * HD)

    with jax.named_scope("attention_fwd"):
        lm_queries = rotate(
            to_heads(seq_triple[:, :query_width], heads_here), cosine, sine
        ).astype(bfloat)
        lm_keys = rotate(
            to_heads(seq_triple[:, query_width : query_width + key_width], groups_here),
            cosine,
            sine,
        ).astype(bfloat)
        lm_values = to_heads(seq_triple[:, query_width + key_width :], groups_here).astype(bfloat)
        block_rows = min(512, length)
        block_total = length // block_rows
        head_scale = HD ** (-0.5)

        def block_scores(block_idx):
            first = block_idx * block_rows
            key_end = first + block_rows
            query_block = lm_queries[:, first:key_end].reshape(groups_here, share, block_rows, HD)
            scores = (
                jnp.einsum(
                    "cgqd,ckd->cgqk",
                    query_block,
                    lm_keys[:, :key_end],
                    preferred_element_type=single,
                )
                * head_scale
            )
            causal = (first + jnp.arange(block_rows))[:, None] >= jnp.arange(key_end)[None, :]
            return (query_block, jnp.where(causal, scores, NEG))

        outputs = []
        lse_list = []
        for block_idx in range(block_total):
            key_end = (block_idx + 1) * block_rows
            query_block, scores = block_scores(block_idx)
            largest = jnp.max(scores, axis=-1, keepdims=True)
            expon = jnp.exp(scores - largest)
            total = jnp.sum(expon, axis=-1, keepdims=True)
            lse_list.append(largest + jnp.log(total))
            probs_low = (expon / total).astype(bfloat)
            block_out = jnp.einsum(
                "cgqk,ckd->cgqd", probs_low, lm_values[:, :key_end], preferred_element_type=single
            )
            outputs.append(block_out.reshape(heads_here, block_rows, HD))
        lm_mixed = from_heads(jnp.concatenate(outputs, axis=1)).astype(bfloat)
        own_mixed = lax.all_to_all(lm_mixed, "tensor", 0, 1, tiled=True)

    with jax.named_scope("attention_out"):
        resid_mid = resid_in + times_trans(own_mixed, full_output)
        pre_two, pre_back_two = jax.vjp(lambda values: rms_norm(values, midnorm_gain), resid_mid)

    with jax.named_scope("mlp_ring"):
        weight_blocks = seq_weight.reshape(tensor_size, rows_here, 1)
        block_at = [
            lax.rem(tensor_at - step + tensor_size, tensor_size) for step in range(tensor_size)
        ]
        out_cot = None
        seq_block = pre_two.astype(bfloat)
        carried = None
        own_part = None
        swiglu_blocks = []
        for step in range(tensor_size):
            now = seq_block
            if step < tensor_size - 1:
                seq_block = ring(seq_block)
            weight_block = lax.dynamic_index_in_dim(
                weight_blocks, block_at[step], 0, keepdims=False
            )
            cot_block = weight_block * cot_blocks[step].astype(single)
            if step == 0:
                out_cot = cot_block
            swiglu_grad = matmul(cot_block.astype(bfloat), full_downward)
            gate_raw = matmul(now, full_gate)
            upward_raw = matmul(now, full_upward)
            swiglu, swiglu_back = jax.vjp(
                lambda gate, upward: jax.nn.silu(gate) * upward, gate_raw, upward_raw
            )
            swiglu_blocks.append(swiglu.astype(bfloat))
            gate_grad, upward_grad = swiglu_back(swiglu_grad)
            part = times_trans(gate_grad.astype(bfloat), full_gate) + times_trans(
                upward_grad.astype(bfloat), full_upward
            )
            if step == 0:
                own_part = part
            else:
                if carried is not None:
                    part = part + carried.astype(single)
                carried = ring(part.astype(bfloat))
        norm_two_grad = own_part if carried is None else own_part + carried.astype(single)

    with jax.named_scope("layer_out"):
        swiglu_low = jnp.concatenate(in_order(swiglu_blocks, tensor_at), axis=0)
        layer_final = resid_mid + lax.psum_scatter(
            times_trans(swiglu_low, full_downward).astype(bfloat),
            "tensor",
            scatter_dimension=0,
            tiled=True,
        ).astype(single)

    with jax.named_scope("attention_bwd"):
        mid_grad = out_cot + pre_back_two(norm_two_grad)[0]
        mid_low = mid_grad.astype(bfloat)
        own_mixed_grad = matmul(mid_low, full_output).astype(bfloat)
        mixed_grad = to_heads(
            lax.all_to_all(own_mixed_grad, "tensor", 1, 0, tiled=True), heads_here
        )
        query_parts = []
        key_acc = jnp.zeros((groups_here, length, HD), single)
        value_acc = jnp.zeros((groups_here, length, HD), single)
        for block_idx in range(block_total):
            first = block_idx * block_rows
            key_end = first + block_rows
            query_block, scores = block_scores(block_idx)
            probs = jnp.exp(scores - lse_list[block_idx])
            grad_block = mixed_grad[:, first:key_end].reshape(groups_here, share, block_rows, HD)
            prob_grad = jnp.einsum(
                "cgqd,ckd->cgqk", grad_block, lm_values[:, :key_end], preferred_element_type=single
            )
            delta = jnp.sum(probs * prob_grad, axis=-1, keepdims=True)
            score_grad = (probs * (prob_grad - delta)).astype(bfloat)
            block_query = jnp.einsum(
                "cgqk,ckd->cgqd", score_grad, lm_keys[:, :key_end], preferred_element_type=single
            )
            query_parts.append(block_query.reshape(heads_here, block_rows, HD) * head_scale)
            key_part = (
                jnp.einsum("cgqk,cgqd->ckd", score_grad, query_block, preferred_element_type=single)
                * head_scale
            )
            key_acc = key_acc.at[:, :key_end].add(key_part)
            value_part = jnp.einsum(
                "cgqk,cgqd->ckd", probs.astype(bfloat), grad_block, preferred_element_type=single
            )
            value_acc = value_acc.at[:, :key_end].add(value_part)
        query_grad = from_heads(rotate(jnp.concatenate(query_parts, axis=1), cosine, -sine)).astype(
            bfloat
        )
        key_grad = from_heads(rotate(key_acc, cosine, -sine)).astype(bfloat)
        value_grad = from_heads(value_acc).astype(bfloat)
        triple_out = jnp.concatenate([query_grad, key_grad, value_grad], axis=1)

    with jax.named_scope("entry_bwd"):
        entry_out = trans_times(seq_hot, triple_out).astype(bfloat)
        entry_part = entry_norm_back(times_trans(entry_out, full_triple))[0]
        entry_part = (entry_part + trans_times(own_hot, mid_low)).astype(bfloat)
        project_part = trans_times(all_pooled, entry_part).astype(bfloat)
        pooled_part = times_trans(entry_part, embed_project)
        pooled_grad = lax.psum_scatter(pooled_part, "dp", scatter_dimension=0, tiled=True)
        pooled_grad = lax.psum_scatter(pooled_grad, "tensor", scatter_dimension=0, tiled=True)

    def summed(part):
        if part.ndim == 2:
            part = part.astype(bfloat)
        part = lax.psum_scatter(part, "dp", scatter_dimension=0, tiled=True)
        return lax.psum_scatter(part, "tensor", scatter_dimension=0, tiled=True).astype(single)

    with jax.named_scope("hyper_bwd"):
        project_grad = summed(project_part)
        pooled_grad = pooled_grad / slot_counts
        grid_grad = jnp.where(valid[:, :, None], pooled_grad[:, None, :], 0.0).reshape(
            flat_rows, HYPER_WIDTH
        )
        reduce_in = grid_grad.astype(bfloat)
        reduce_grad = trans_times(activated_low, reduce_in)
        expand_in = gelu_back(times_trans(reduce_in, encoder_reduce))[0].astype(bfloat)
        expand_grad = trans_times(second_in, expand_in)
        resid_part, normtwo_grad = norm_back_two(times_trans(expand_in, encoder_expand))
        resid_one_grad = grid_grad + resid_part
        merge_in = resid_one_grad.astype(bfloat)
        merge_grad = trans_times(enc_mixed, merge_in)
        enc_mixed_grad = (
            times_trans(merge_in, encoder_merge)
            .astype(bfloat)
            .reshape(entries, SUBWORD_SLOTS, EH, EHD)
        )
        enc_prob_grad = jnp.einsum(
            "nqhd,nkhd->nhqk", enc_mixed_grad, enc_values, preferred_element_type=single
        )
        enc_delta = jnp.sum(enc_probs * enc_prob_grad, axis=-1, keepdims=True)
        enc_score_grad = (enc_probs * (enc_prob_grad - enc_delta)).astype(bfloat)
        enc_query_grad = (
            jnp.einsum("nhqk,nkhd->nqhd", enc_score_grad, enc_keys, preferred_element_type=single)
            * enc_scale
        )
        enc_key_grad = (
            jnp.einsum(
                "nhqk,nqhd->nkhd", enc_score_grad, enc_queries, preferred_element_type=single
            )
            * enc_scale
        )
        enc_value_grad = jnp.einsum(
            "nhqk,nqhd->nkhd", enc_probs_low, enc_mixed_grad, preferred_element_type=single
        )
        triple_in = jnp.concatenate(
            [
                enc_query_grad.reshape(flat_rows, HYPER_WIDTH),
                enc_key_grad.reshape(flat_rows, HYPER_WIDTH),
                enc_value_grad.reshape(flat_rows, HYPER_WIDTH),
            ],
            axis=1,
        ).astype(bfloat)
        triple_grad = trans_times(first_in, triple_in)
        rows_part, normone_grad = norm_back_one(times_trans(triple_in, encoder_triple))
        rows_low = (resid_one_grad + rows_part).astype(bfloat)

    with jax.named_scope("grads_out"):
        all_rows = lax.all_gather(rows_low, "tensor", axis=0, tiled=True)
        all_rows = lax.all_gather(all_rows, "dp", axis=0, tiled=True)
        own_rows = table_rows // tensor_size
        row_hot = (
            (jnp.arange(own_rows) + device_at * own_rows)[:, None] == all_ids[None, :]
        ).astype(bfloat)
        subword_grad = matmul(row_hot, all_rows)
        reduce_grad = summed(reduce_grad)
        expand_grad = summed(expand_grad)
        merge_grad = summed(merge_grad)
        triple_grad = summed(triple_grad)
        gain_grads = summed(jnp.stack([normone_grad, normtwo_grad], axis=1).reshape(-1))
        gain_grads = gain_grads.reshape(-1, 2)
    return (
        layer_final.astype(bfloat),
        vectors,
        subword_grad,
        triple_grad,
        merge_grad,
        expand_grad,
        reduce_grad,
        project_grad,
        gain_grads[:, 0],
        gain_grads[:, 1],
    )


def solution(mesh):
    return jax.shard_map(
        per_device,
        mesh=mesh,
        in_specs=(
            P("dp", None),
            P(("dp", "tensor"), None),
            P(("dp", "tensor")),
            P(("dp", "tensor")),
            P(),
            P(),
            P(),
            P(),
            P(),
            P(),
            P(),
            P("dp", "tensor"),
            P("dp", "tensor"),
            P("dp", "tensor"),
            P("dp", "tensor"),
            P("dp", "tensor"),
            P("dp", "tensor"),
            P("dp", "tensor"),
            P(),
            P(),
            P(("dp", "tensor")),
            P(("dp", "tensor"), None),
        ),
        out_specs=(
            P(("dp", "tensor"), None),
            P(("dp", "tensor"), None),
            P(("dp", "tensor"), None),
            P(("dp", "tensor"), None),
            P(("dp", "tensor"), None),
            P(("dp", "tensor"), None),
            P(("dp", "tensor"), None),
            P(("dp", "tensor"), None),
            P(("dp", "tensor")),
            P(("dp", "tensor")),
        ),
        check_vma=False,
    )
```

time: 3470 us -> 1050 us (0.30)
  waiting for transfers between devices: 3010 us -> 575 us
    unnamed x23 -> x20, waiting for transfers between devices: 1380 us -> 2.17 us
    reduce_scatter x10 -> x13, waiting for transfers between devices: 1020 us -> 285 us  [the longest x5 181 us: summed(): part = lax.psum_scatter(part, 'dp', scatter_dimension=0, tiled=True)]
    all_gather x11 -> x7, waiting for transfers between devices: 607 us -> 93 us  [the longest x1 35.4 us: per_device(): all_rows = lax.all_gather(all_rows, 'dp', axis=0, tiled=True)]
    ppermute x0 -> x9, waiting for transfers between devices: none -> 132 us  [ring(): lax.ppermute(values, 'tensor', [(i, (i + shift) % size) for i in range(si...]
    all_gather x2 -> x5, blocking collectives: 19.9 us -> 83.4 us  [the longest x1 33 us: per_device(): lax.all_gather(jnp.concatenate([packed_dp.reshape(-1), text_tokens]), 'te...]
    all_to_all x0 -> x3, waiting for transfers between devices: none -> 62.8 us  [the longest x1 38 us: per_device(): own_mixed = lax.all_to_all(lm_mixed, 'tensor', 0, 1, tiled=True)]
    unnamed x2, blocking collectives: 77.2 us -> 24.4 us
    dot_general x12 -> x16, matrix products: 81.7 us -> 61.3 us  [times_trans(): lax.dot_general(left, right, (((1,), (1,)), ((), ())), preferred_element_...]
  transfers between devices with their start and end apart: 22 -> 32, of which waited for: 22 -> 20; matrix products, arithmetic and copies ran while one was open for 4% -> 19% of each run, Pallas kernels for 0% -> 0%
where the time goes in v1:
time: 1050 us; the launch traced here: 1040 us
  waiting for transfers between devices  575 us (55%)
  matrix products  214 us (20%)
  blocking collectives  108 us (10%)
  other arithmetic  48.3 us (5%)
  local copies, waits for them, and re-layouts  45.2 us (4%)
  starting transfers between devices  35.3 us (3%)
  between operations  18.5 us (2%)
    reduce_scatter x5, waiting for transfers between devices, summed(): part = lax.psum_scatter(part, 'dp', scatter_dimension=0, tiled=True)  181 us
    ppermute x9, waiting for transfers between devices, ring(): lax.ppermute(values, 'tensor', [(i, (i + shift) % size) for i in range(si...  132 us
    dot_general x24, matrix products, matmul(): return jnp.dot(left, right, preferred_element_type=jnp.float32)  72.9 us
    dot_general x16, matrix products, times_trans(): lax.dot_general(left, right, (((1,), (1,)), ((), ())), preferred_element_...  61.3 us
    reduce_scatter x5, waiting for transfers between devices, summed(): lax.psum_scatter(part, 'tensor', scatter_dimension=0, tiled=True)  48.8 us
    all_to_all x1, waiting for transfers between devices, per_device(): own_mixed = lax.all_to_all(lm_mixed, 'tensor', 0, 1, tiled=True)  38 us
    all_gather x1, waiting for transfers between devices, per_device(): all_rows = lax.all_gather(all_rows, 'dp', axis=0, tiled=True)  35.4 us
    reduce_scatter x1, waiting for transfers between devices, per_device(): lax.psum_scatter(pooled_part, 'dp', scatter_dimension=0, tiled=True)  34.5 us
  transfers between devices with their start and end apart: 32, of which 20 were waited for; matrix products, arithmetic and copies ran while one was open for 19% of the time, Pallas kernels for 0%

profile of v1, /device:TPU:0, one launch (start us, length us, event | category | flops | bytes accessed | tf_op | source)
XLA Modules:
  0.0 1044.3 jit_solution(343570049497847609)
XLA Ops:
  12.3 28.0 %all-gather.13.cloned.1.call-done = bf16[256,2048]{1,0:T(8,128)(2,1)} async-done(((bf16[256,512]{1,0:T(8,128)(2,1)}), bf16[256,2048]{1,0:T(8,128)(2,1)}) %all-gather.13.cloned.1.call-update) | async-done | bytes 1048592 | tf_op jit(solution)/shard_map/output_weights/all_gather | solution.py:123
  41.1 9.2 all-gather
  64.1 33.0 %all-gather.2 = s32[4,1,1408]{2,1,0:T(1,128)S(1)} all-gather(s32[1,1,1408]{2,1,0:T(1,128)S(1)} %reshape.824), channel_id=3, replica_groups=mesh['dp'=8,'tensor'=4] {'tensor'}, dimensions={0}, use_global_device_ids=true | all-gather | bytes 28160 | tf_op jit(solution)/shard_map/ids/all_gather | solution.py:116
  119.0 13.1 %all_gather.44 = bf16[64,512]{1,0:T(8,128)(2,1)S(1)} all-gather(bf16[16,512]{1,0:T(8,128)(2,1)S(1)} %divide_convert_fusion.8), channel_id=1, replica_groups=mesh['dp'=8,'tensor'=4] {'tensor'}, dimensions={0}, use_global_device_ids=true | all-gather | bytes 81920 | tf_op jit(solution)/shard_map/pooled_gather/all_gather | solution.py:189
  132.1 11.4 %all_gather.45 = bf16[512,512]{1,0:T(8,128)(2,1)S(1)} all-gather(bf16[64,512]{1,0:T(8,128)(2,1)S(1)} %all_gather.44), channel_id=1, replica_groups=mesh['dp'=8,'tensor'=4] {'dp'}, dimensions={0}, use_global_device_ids=true | all-gather | bytes 589824 | tf_op jit(solution)/shard_map/pooled_gather/all_gather | solution.py:190
  192.8 38.0 %all-to-all-done.1 = bf16[4,256,512]{1,2,0:T(8,128)(2,1)S(1)} async-done(((bf16[4,256,512]{1,2,0:T(8,128)(2,1)}), bf16[4,256,512]{1,2,0:T(8,128)(2,1)S(1)}, u32[]{:S(2)}, u32[]{:S(2)}) %all-to-all-start.1) | async-done | bytes 1048608 | tf_op jit(solution)/shard_map/attention_fwd/all_to_all | solution.py:278
  245.1 29.6 %all-gather.19.cloned.1.call-done = bf16[2048,1408]{1,0:T(8,128)(2,1)} async-done(((bf16[256,1408]{1,0:T(8,128)(2,1)}), bf16[2048,1408]{1,0:T(8,128)(2,1)}) %all-gather.19.cloned.1.call-update) | async-done | bytes 5767184 | tf_op jit(solution)/shard_map/mlp_weights/all_gather | solution.py:128
  288.9 18.5 %collective-permute-done.1 = bf16[256,2048]{1,0:T(8,128)(2,1)S(1)} collective-permute-done((bf16[256,2048]{1,0:T(8,128)(2,1)}, bf16[256,2048]{1,0:T(8,128)(2,1)S(1)}, u32[]{:S(2)}, u32[]{:S(2)}) %collective-permute-start.1) | collective-permute-done | bytes 1048608 | tf_op jit(solution)/shard_map/mlp_ring/ppermute | solution.py:64
  312.1 21.5 %collective-permute-done.2 = bf16[256,2048]{1,0:T(8,128)(2,1)S(1)} collective-permute-done((bf16[256,2048]{1,0:T(8,128)(2,1)S(1)}, bf16[256,2048]{1,0:T(8,128)(2,1)S(1)}, u32[]{:S(2)}, u32[]{:S(2)}) %collective-permute-start.2) | collective-permute-done | bytes 1048608 | tf_op jit(solution)/shard_map/mlp_ring/ppermute | solution.py:64
  341.2 8.3 convolution_convert_fusion
  372.9 41.5 %collective-permute-done.6 = bf16[256,2048]{1,0:T(8,128)(2,1)S(1)} collective-permute-done((bf16[256,2048]{1,0:T(8,128)(2,1)S(1)}, bf16[256,2048]{1,0:T(8,128)(2,1)S(1)}, u32[]{:S(2)}, u32[]{:S(2)}) %collective-permute-start.6) | collective-permute-done | bytes 1048608 | tf_op jit(solution)/shard_map/mlp_ring/ppermute | solution.py:64
  418.5 16.4 %collective-permute-start.7 = (bf16[256,2048]{1,0:T(8,128)(2,1)S(1)}, bf16[256,2048]{1,0:T(8,128)(2,1)S(1)}, u32[]{:S(2)}, u32[]{:S(2)}) collective-permute-start(bf16[256,2048]{1,0:T(8,128)(2,1)S(1)} %add_convert_fusion.1), channel_id=1, source_target_pairs={{0,1},{1,2},{2,3},{3,0},{4,5},{5,6},{6,7},{7,4},{8,9},{9,10},{10,1... | collective-permute-start | bytes 3145736 | tf_op jit(solution)/shard_map/mlp_ring/ppermute | solution.py:64
  441.7 27.7 %collective-permute-done.7 = bf16[256,2048]{1,0:T(8,128)(2,1)S(1)} collective-permute-done((bf16[256,2048]{1,0:T(8,128)(2,1)S(1)}, bf16[256,2048]{1,0:T(8,128)(2,1)S(1)}, u32[]{:S(2)}, u32[]{:S(2)}) %collective-permute-start.7) | collective-permute-done | bytes 1048608 | tf_op jit(solution)/shard_map/mlp_ring/ppermute | solution.py:64
  473.9 22.7 %collective-permute-done.8 = bf16[256,2048]{1,0:T(8,128)(2,1)S(1)} collective-permute-done((bf16[256,2048]{1,0:T(8,128)(2,1)S(1)}, bf16[256,2048]{1,0:T(8,128)(2,1)S(1)}, u32[]{:S(2)}, u32[]{:S(2)}) %collective-permute-start.8) | collective-permute-done | bytes 1048608 | tf_op jit(solution)/shard_map/mlp_ring/ppermute | solution.py:64
  516.1 24.8 %all-to-all-done.2 = bf16[256,4,512]{2,0,1:T(8,128)(2,1)S(1)} async-done(((bf16[256,4,512]{2,0,1:T(8,128)(2,1)}), bf16[256,4,512]{2,0,1:T(8,128)(2,1)S(1)}, u32[]{:S(2)}, u32[]{:S(2)}) %all-to-all-start.2) | async-done | bytes 1048608 | tf_op jit(solution)/shard_map/attention_bwd/all_to_all | solution.py:337
  550.0 9.3 multiply_reduce_fusion.1
  574.5 9.5 multiply_reduce_fusion
  588.6 8.0 multiply_convert_fusion
  603.0 8.1 fusion.20
  619.2 34.5 %reduce-scatter.16.cloned.1.call-done = f32[64,512]{1,0:T(8,128)} async-done(((f32[512,512]{1,0:T(8,128)}), f32[64,512]{1,0:T(8,128)}) %reduce-scatter.16.cloned.1.call-update) | async-done | bytes 131088 | tf_op jit(solution)/shard_map/entry_bwd/reduce_scatter | solution.py:379
  653.9 21.4 %reduce-scatter.18.cloned.1.call-done = f32[16,512]{1,0:T(8,128)} async-done(((f32[64,512]{1,0:T(8,128)}), f32[16,512]{1,0:T(8,128)}) %reduce-scatter.18.cloned.1.call-update) | async-done | bytes 32784 | tf_op jit(solution)/shard_map/entry_bwd/reduce_scatter | solution.py:380
  714.4 44.8 %reduce-scatter.36.cloned.1.call-done = bf16[64,2048]{1,0:T(8,128)(2,1)} async-done(((bf16[512,2048]{1,0:T(8,128)(2,1)}), bf16[64,2048]{1,0:T(8,128)(2,1)}) %reduce-scatter.36.cloned.1.call-update) | async-done | bytes 262160 | tf_op jit(solution)/shard_map/hyper_bwd/reduce_scatter | solution.py:385
  759.3 42.1 %reduce-scatter.20.cloned.1.call-done = bf16[64,1536]{1,0:T(8,128)(2,1)} async-done(((bf16[512,1536]{1,0:T(8,128)(2,1)}), bf16[64,1536]{1,0:T(8,128)(2,1)}) %reduce-scatter.20.cloned.1.call-update) | async-done | bytes 196624 | tf_op jit(solution)/shard_map/grads_out/reduce_scatter | solution.py:385
  801.5 44.5 %reduce-scatter.28.cloned.1.call-done = bf16[64,2048]{1,0:T(8,128)(2,1)} async-done(((bf16[512,2048]{1,0:T(8,128)(2,1)}), bf16[64,2048]{1,0:T(8,128)(2,1)}) %reduce-scatter.28.cloned.1.call-update) | async-done | bytes 262160 | tf_op jit(solution)/shard_map/grads_out/reduce_scatter | solution.py:385
  848.4 42.3 %reduce-scatter.32.cloned.1.call-done = bf16[256,512]{1,0:T(8,128)(2,1)} async-done(((bf16[2048,512]{1,0:T(8,128)(2,1)}), bf16[256,512]{1,0:T(8,128)(2,1)}) %reduce-scatter.32.cloned.1.call-update) | async-done | bytes 262160 | tf_op jit(solution)/shard_map/grads_out/reduce_scatter | solution.py:385
  890.9 16.6 %all_gather.54 = bf16[512,512]{1,0:T(8,128)(2,1)} all-gather(bf16[128,512]{1,0:T(8,128)(2,1)S(1)} %add_convert_fusion.6), channel_id=1, replica_groups=mesh['dp'=8,'tensor'=4] {'tensor'}, dimensions={0}, use_global_device_ids=true | all-gather | bytes 655360 | tf_op jit(solution)/shard_map/grads_out/all_gather | solution.py:438
  912.2 11.8 %all-reduce.2 = f32[1024]{0:T(1024)S(1)} all-reduce(f32[1024]{0:T(1024)S(1)} %reshape.811), channel_id=17, replica_groups=mesh['dp'=8,'tensor'=4] {'dp'}, use_global_device_ids=true, to_apply=%region_38.39.clone | all-reduce | flops 1024 | bytes 8192
  924.1 12.6 %all-reduce.3 = f32[128]{0:T(128)S(1)} all-reduce(f32[128]{0:T(128)S(1)} %dynamic-slice.41), channel_id=18, replica_groups=mesh['dp'=8,'tensor'=4] {'tensor'}, use_global_device_ids=true, to_apply=%region_39.40.clone | all-reduce | flops 128 | bytes 1024
  940.4 11.4 %reduce-scatter.22.cloned.1.call-done = bf16[16,1536]{1,0:T(8,128)(2,1)} async-done(((bf16[64,1536]{1,0:T(8,128)(2,1)}), bf16[16,1536]{1,0:T(8,128)(2,1)}) %reduce-scatter.22.cloned.1.call-update) | async-done | bytes 49168 | tf_op jit(solution)/shard_map/grads_out/reduce_scatter | solution.py:386
  953.3 18.7 %reduce-scatter.30.cloned.1.call-done = bf16[16,2048]{1,0:T(8,128)(2,1)} async-done(((bf16[64,2048]{1,0:T(8,128)(2,1)}), bf16[16,2048]{1,0:T(8,128)(2,1)}) %reduce-scatter.30.cloned.1.call-update) | async-done | bytes 65552 | tf_op jit(solution)/shard_map/grads_out/reduce_scatter | solution.py:386
  973.4 18.7 %reduce-scatter.34.cloned.1.call-done = bf16[64,512]{1,0:T(8,128)(2,1)} async-done(((bf16[256,512]{1,0:T(8,128)(2,1)}), bf16[64,512]{1,0:T(8,128)(2,1)}) %reduce-scatter.34.cloned.1.call-update) | async-done | bytes 65552 | tf_op jit(solution)/shard_map/grads_out/reduce_scatter | solution.py:386
  993.7 35.4 %all-gather.23.cloned.1.call-done = bf16[4096,512]{1,0:T(8,128)(2,1)} async-done(((bf16[512,512]{1,0:T(8,128)(2,1)}), bf16[4096,512]{1,0:T(8,128)(2,1)}) %all-gather.23.cloned.1.call-update) | async-done | bytes 4194320 | tf_op jit(solution)/shard_map/grads_out/all_gather | solution.py:439
  (542 shorter events, 292.4 us)
Async XLA Ops:
  7.2 33.1 %all-gather.13.cloned.1.call-start = ((), (), s32[]{:S(2)}) async-start(), calls=%async_computation.17 | async-start | bytes 1310720 | tf_op jit(solution)/shard_map/output_weights/all_gather | solution.py:123
  7.9 138.5 %all-gather.11.cloned.1.call-start = ((), (), s32[]{:S(2)}) async-start(), calls=%async_computation.16 | async-start | bytes 2949120 | tf_op jit(solution)/shard_map/qkv_weights/all_gather | solution.py:121
  11.5 175.3 %all-gather.21.cloned.1.call-start = ((), (), s32[]{:S(2)}) async-start(), calls=%async_computation.21 | async-start | bytes 6488064 | tf_op jit(solution)/shard_map/mlp_weights/all_gather | solution.py:126
  12.3 218.5 %all-gather.15.cloned.1.call-start = ((), (), s32[]{:S(2)}) async-start(), calls=%async_computation.18 | async-start | bytes 9437184 | tf_op jit(solution)/shard_map/output_weights/all_gather | solution.py:124
  40.3 200.0 %all-gather.17.cloned.1.call-start = ((), (), s32[]{:S(2)}) async-start(), calls=%async_computation.19 | async-start | bytes 6488064 | tf_op jit(solution)/shard_map/mlp_weights/all_gather | solution.py:127
  58.7 42.4 %all-to-all-start = ((bf16[8,128,512]{2,1,0:T(8,128)(2,1)}), bf16[8,128,512]{2,1,0:T(8,128)(2,1)S(1)}, u32[]{:S(2)}, u32[]{:S(2)}) async-start(bf16[8,128,512]{2,1,0:T(8,128)(2,1)} %select_select_fusion), calls=%async_computation | async-start | bytes 2097152 | tf_op jit(solution)/shard_map/lookup/all_to_all | solution.py:141
  62.3 212.3 %all-gather.19.cloned.1.call-start = ((), (), s32[]{:S(2)}) async-start(), calls=%async_computation.20 | async-start | bytes 6488064 | tf_op jit(solution)/shard_map/mlp_weights/all_gather | solution.py:128
  62.4 83.8 %collective-permute-start.3 = (bf16[256,2048]{1,0:T(8,128)(2,1)}, bf16[256,2048]{1,0:T(8,128)(2,1)}, u32[]{:S(2)}, u32[]{:S(2)}) collective-permute-start(bf16[256,2048]{1,0:T(8,128)(2,1)} %param.55), channel_id=1, source_target_pairs={{0,1},{1,2},{2,3},{3,0},{4,5},{5,6},{6,7},{7,4},{8,9},{9,10},{10,1... | collective-permute-start | bytes 3145736 | tf_op jit(solution)/shard_map/cot_ring/ppermute | solution.py:64
  146.2 38.7 %collective-permute-start.4 = (bf16[256,2048]{1,0:T(8,128)(2,1)}, bf16[256,2048]{1,0:T(8,128)(2,1)}, u32[]{:S(2)}, u32[]{:S(2)}) collective-permute-start(bf16[256,2048]{1,0:T(8,128)(2,1)} %collective-permute-done.3), channel_id=1, source_target_pairs={{0,1},{1,2},{2,3},{3,0},{4,5},{5,6},{6,7},{7,4},{8,9},{9,10},{10,1... | collective-permute-start | bytes 3145736 | tf_op jit(solution)/shard_map/cot_ring/ppermute | solution.py:64
  177.3 53.5 %all-to-all-start.1 = ((bf16[4,256,512]{1,2,0:T(8,128)(2,1)}), bf16[4,256,512]{1,2,0:T(8,128)(2,1)S(1)}, u32[]{:S(2)}, u32[]{:S(2)}) async-start(bf16[4,256,512]{1,2,0:T(8,128)(2,1)} %copy.86), calls=%async_computation.1 | async-start | bytes 2097152 | tf_op jit(solution)/shard_map/attention_fwd/all_to_all | solution.py:278
  182.3 317.7 %reduce-scatter.14.cloned.1.call-start = ((), (), s32[]{:S(2)}) async-start(), calls=%async_computation.22 | async-start | bytes 5242880 | tf_op jit(solution)/shard_map/layer_out/reduce_scatter | solution.py:325
  184.8 180.1 %collective-permute-start.5 = (bf16[256,2048]{1,0:T(8,128)(2,1)}, bf16[256,2048]{1,0:T(8,128)(2,1)}, u32[]{:S(2)}, u32[]{:S(2)}) collective-permute-start(bf16[256,2048]{1,0:T(8,128)(2,1)} %collective-permute-done.4), channel_id=1, source_target_pairs={{0,1},{1,2},{2,3},{3,0},{4,5},{5,6},{6,7},{7,4},{8,9},{9,10},{10,1... | collective-permute-start | bytes 3145736 | tf_op jit(solution)/shard_map/cot_ring/ppermute | solution.py:64
  240.1 39.9 %collective-permute-start = (bf16[256,2048]{1,0:T(8,128)(2,1)}, bf16[256,2048]{1,0:T(8,128)(2,1)}, u32[]{:S(2)}, u32[]{:S(2)}) collective-permute-start(bf16[256,2048]{1,0:T(8,128)(2,1)} %multiply_convert_fusion.5), channel_id=1, source_target_pairs={{0,1},{1,2},{2,3},{3,0},{4,5},{5,6},{6,7},{7,4},{8,9},{9,10},{10,1... | collective-permute-start | bytes 3145736 | tf_op jit(solution)/shard_map/mlp_ring/ppermute | solution.py:64
  280.0 27.4 %collective-permute-start.1 = (bf16[256,2048]{1,0:T(8,128)(2,1)}, bf16[256,2048]{1,0:T(8,128)(2,1)S(1)}, u32[]{:S(2)}, u32[]{:S(2)}) collective-permute-start(bf16[256,2048]{1,0:T(8,128)(2,1)} %collective-permute-done), channel_id=1, source_target_pairs={{0,1},{1,2},{2,3},{3,0},{4,5},{5,6},{6,7},{7,4},{8,9},{9,10},{10,1... | collective-permute-start | bytes 3145736 | tf_op jit(solution)/shard_map/mlp_ring/ppermute | solution.py:64
  307.4 26.3 %collective-permute-start.2 = (bf16[256,2048]{1,0:T(8,128)(2,1)S(1)}, bf16[256,2048]{1,0:T(8,128)(2,1)S(1)}, u32[]{:S(2)}, u32[]{:S(2)}) collective-permute-start(bf16[256,2048]{1,0:T(8,128)(2,1)S(1)} %collective-permute-done.1), channel_id=1, source_target_pairs={{0,1},{1,2},{2,3},{3,0},{4,5},{5,6},{6,7},{7,4},{8,9},{9,10},{10,1... | collective-permute-start | bytes 3145736 | tf_op jit(solution)/shard_map/mlp_ring/ppermute | solution.py:64
  364.9 49.5 %collective-permute-start.6 = (bf16[256,2048]{1,0:T(8,128)(2,1)S(1)}, bf16[256,2048]{1,0:T(8,128)(2,1)S(1)}, u32[]{:S(2)}, u32[]{:S(2)}) collective-permute-start(bf16[256,2048]{1,0:T(8,128)(2,1)S(1)} %fusion.30), channel_id=1, source_target_pairs={{0,1},{1,2},{2,3},{3,0},{4,5},{5,6},{6,7},{7,4},{8,9},{9,10},{10,1... | collective-permute-start | bytes 3145736 | tf_op jit(solution)/shard_map/mlp_ring/ppermute | solution.py:64
  418.5 50.9 %collective-permute-start.7 = (bf16[256,2048]{1,0:T(8,128)(2,1)S(1)}, bf16[256,2048]{1,0:T(8,128)(2,1)S(1)}, u32[]{:S(2)}, u32[]{:S(2)}) collective-permute-start(bf16[256,2048]{1,0:T(8,128)(2,1)S(1)} %add_convert_fusion.1), channel_id=1, source_target_pairs={{0,1},{1,2},{2,3},{3,0},{4,5},{5,6},{6,7},{7,4},{8,9},{9,10},{10,1... | collective-permute-start | bytes 3145736 | tf_op jit(solution)/shard_map/mlp_ring/ppermute | solution.py:64
  469.8 26.8 %collective-permute-start.8 = (bf16[256,2048]{1,0:T(8,128)(2,1)S(1)}, bf16[256,2048]{1,0:T(8,128)(2,1)S(1)}, u32[]{:S(2)}, u32[]{:S(2)}) collective-permute-start(bf16[256,2048]{1,0:T(8,128)(2,1)S(1)} %add_convert_fusion), channel_id=1, source_target_pairs={{0,1},{1,2},{2,3},{3,0},{4,5},{5,6},{6,7},{7,4},{8,9},{9,10},{10,1... | collective-permute-start | bytes 3145736 | tf_op jit(solution)/shard_map/mlp_ring/ppermute | solution.py:64
  512.2 28.6 %all-to-all-start.2 = ((bf16[256,4,512]{2,0,1:T(8,128)(2,1)}), bf16[256,4,512]{2,0,1:T(8,128)(2,1)S(1)}, u32[]{:S(2)}, u32[]{:S(2)}) async-start(bf16[256,4,512]{2,0,1:T(8,128)(2,1)} %bitcast.254), calls=%async_computation.3 | async-start | bytes 2097152 | tf_op jit(solution)/shard_map/attention_bwd/all_to_all | solution.py:337
  515.8 137.9 %reduce-scatter.16.cloned.1.call-start = ((), (), s32[]{:S(2)}) async-start(), calls=%async_computation.23 | async-start | bytes 1179648 | tf_op jit(solution)/shard_map/entry_bwd/reduce_scatter | solution.py:379
  619.1 56.1 %reduce-scatter.18.cloned.1.call-start = ((), (), s32[]{:S(2)}) async-start(), calls=%async_computation.24 | async-start | bytes 163840 | tf_op jit(solution)/shard_map/entry_bwd/reduce_scatter | solution.py:380
  653.7 60.6 %reduce-scatter.24.cloned.1.call-start = ((), (), s32[]{:S(2)}) async-start(), calls=%async_computation.28 | async-start | bytes 589824 | tf_op jit(solution)/shard_map/grads_out/reduce_scatter | solution.py:385
  681.8 77.4 %reduce-scatter.36.cloned.1.call-start = ((), (), s32[]{:S(2)}) async-start(), calls=%async_computation.34 | async-start | bytes 2359296 | tf_op jit(solution)/shard_map/hyper_bwd/reduce_scatter | solution.py:385
  686.3 115.1 %reduce-scatter.20.cloned.1.call-start = ((), (), s32[]{:S(2)}) async-start(), calls=%async_computation.26 | async-start | bytes 1769472 | tf_op jit(solution)/shard_map/grads_out/reduce_scatter | solution.py:385
  700.7 145.2 %reduce-scatter.28.cloned.1.call-start = ((), (), s32[]{:S(2)}) async-start(), calls=%async_computation.30 | async-start | bytes 2359296 | tf_op jit(solution)/shard_map/grads_out/reduce_scatter | solution.py:385
  704.0 186.7 %reduce-scatter.32.cloned.1.call-start = ((), (), s32[]{:S(2)}) async-start(), calls=%async_computation.32 | async-start | bytes 2359296 | tf_op jit(solution)/shard_map/grads_out/reduce_scatter | solution.py:385
  707.2 230.4 %reduce-scatter.26.cloned.1.call-start = ((), (), s32[]{:S(2)}) async-start(), calls=%async_computation.29 | async-start | bytes 81920 | tf_op jit(solution)/shard_map/grads_out/reduce_scatter | solution.py:386
  714.3 224.6 %reduce-scatter.38.cloned.1.call-start = ((), (), s32[]{:S(2)}) async-start(), calls=%async_computation.35 | async-start | bytes 327680 | tf_op jit(solution)/shard_map/hyper_bwd/reduce_scatter | solution.py:386
  759.2 192.6 %reduce-scatter.22.cloned.1.call-start = ((), (), s32[]{:S(2)}) async-start(), calls=%async_computation.27 | async-start | bytes 245760 | tf_op jit(solution)/shard_map/grads_out/reduce_scatter | solution.py:386
  801.4 170.5 %reduce-scatter.30.cloned.1.call-start = ((), (), s32[]{:S(2)}) async-start(), calls=%async_computation.31 | async-start | bytes 327680 | tf_op jit(solution)/shard_map/grads_out/reduce_scatter | solution.py:386
  846.0 146.2 %reduce-scatter.34.cloned.1.call-start = ((), (), s32[]{:S(2)}) async-start(), calls=%async_computation.33 | async-start | bytes 327680 | tf_op jit(solution)/shard_map/grads_out/reduce_scatter | solution.py:386
  890.7 138.4 %all-gather.23.cloned.1.call-start = ((), (), s32[]{:S(2)}) async-start(), calls=%async_computation.25 | async-start | bytes 4718592 | tf_op jit(solution)/shard_map/grads_out/all_gather | solution.py:439
  (145 other events, 1815.5 us)
Sparse Core Ops, SparseCore 0:
  9.6 30.6 all-gather.12
  42.2 37.2 all-gather.10
  81.3 46.9 all-gather.20
  130.0 54.3 all-gather.14
  186.2 43.3 all-gather.16
  231.3 43.3 all-gather.18
  349.7 102.5 reduce-scatter.13
  619.2 34.4 reduce-scatter.15
  656.0 19.1 reduce-scatter.17
  681.9 32.3 reduce-scatter.23
  717.9 41.2 reduce-scatter.35
  762.9 38.4 reduce-scatter.19
  804.7 41.1 reduce-scatter.27
  849.4 41.2 reduce-scatter.31
  892.8 19.1 reduce-scatter.25
  914.2 17.9 reduce-scatter.37
  934.2 17.5 reduce-scatter.21
  954.0 17.8 reduce-scatter.29
  974.2 17.9 reduce-scatter.33
  994.1 34.9 all-gather.22

commit v2 on v1

v2 whole, which is shorter than its diff:
```python
from functools import partial

import jax
import jax.numpy as jnp
from jax import lax
from jax.experimental import pallas as pl
from jax.experimental.pallas import tpu as pltpu
from jax.sharding import PartitionSpec as P

HD = 64
HYPER_WIDTH = 512
EH = 8
EHD = 64
SUBWORD_SLOTS = 8


NEG = -1000000000.0
EPS = 1e-05
THETA = 10000.0
VMEM_LIMIT = 62 * 1024 * 1024


def layer_norm(values, gain):
    center = values - jnp.mean(values, axis=-1, keepdims=True)
    spread = jnp.mean(center * center, axis=-1, keepdims=True)
    return center * lax.rsqrt(spread + EPS) * gain


def rms_norm(values, gain):
    return values * lax.rsqrt(jnp.mean(values * values, axis=-1, keepdims=True) + EPS) * gain


def rope_tables(length, width):
    half_width = width // 2
    inverse = THETA ** (-(2.0 * jnp.arange(half_width, dtype=jnp.float32)) / width)
    angles = jnp.arange(length, dtype=jnp.float32)[:, None] * inverse[None, :]
    return (jnp.cos(angles), jnp.sin(angles))


def rotate(values, cosine, sine):
    half_width = values.shape[-1] // 2
    former = values[..., :half_width]
    latter = values[..., half_width:]
    return jnp.concatenate(
        [former * cosine - latter * sine, latter * cosine + former * sine], axis=-1
    )


def matmul(left, right):
    return jnp.dot(left, right, preferred_element_type=jnp.float32)


def times_trans(left, right):
    return lax.dot_general(
        left, right, (((1,), (1,)), ((), ())), preferred_element_type=jnp.float32
    )


def trans_times(left, right):
    return lax.dot_general(
        left, right, (((0,), (0,)), ((), ())), preferred_element_type=jnp.float32
    )


def ring(values, shift=1):
    size = lax.axis_size("tensor")
    return lax.ppermute(values, "tensor", [(i, (i + shift) % size) for i in range(size)])


def tie(values, *others):
    return lax.optimization_barrier((values, *others))[0]


def tie_all(first, *values):
    return lax.optimization_barrier((*values, first))[:-1]


def in_order(blocks, first):
    size = len(blocks)
    stacked = jnp.stack(blocks)
    return [
        lax.dynamic_index_in_dim(stacked, lax.rem(first - at + size, size), 0, keepdims=False)
        for at in range(size)
    ]


def scatter_dp(values):
    size = lax.axis_size("dp")
    blocks = values.reshape(size, values.shape[0] // size, values.shape[1])
    blocks = lax.all_to_all(blocks, "dp", 0, 0, tiled=True)
    return jnp.sum(blocks.astype(jnp.float32), axis=0)


def from_all(values):
    return [values] + [ring(values, shift) for shift in range(1, lax.axis_size("tensor"))]


def rope_lanes(length):
    cosine, sine = rope_tables(length, HD)
    return (
        jnp.concatenate([cosine] * 4, axis=1),
        jnp.concatenate([-sine, sine, -sine, sine], axis=1),
    )


def swap(values):
    width = values.shape[1]
    lane = lax.broadcasted_iota(jnp.int32, values.shape, 1)
    ahead = pltpu.roll(values, width - HD // 2, 1)
    behind = pltpu.roll(values, HD // 2, 1)
    return jnp.where(lane % HD < HD // 2, ahead, behind)


def attention_operands(query_ref, pair_ref, cos_ref, sin_ref):
    bfloat = jnp.bfloat16
    cosine = cos_ref[...]
    sine = sin_ref[...]
    queries = query_ref[...]
    pair = pair_ref[...]
    queries = (queries * cosine + swap(queries) * sine).astype(bfloat)
    queries = queries * jnp.asarray(HD ** (-0.5), bfloat)
    keys = (pair * cosine + swap(pair) * sine).astype(bfloat)[:, :HD]
    return queries, keys, pair.astype(bfloat)[:, HD:]


def scores_by_key(keys, query_block, first):
    rows = query_block.shape[0]
    own = times_trans(keys[first : first + rows], query_block)
    key_at = lax.broadcasted_iota(jnp.int32, own.shape, 0)
    query_at = lax.broadcasted_iota(jnp.int32, own.shape, 1)
    parts = [jnp.where(query_at >= key_at, own, NEG)]
    if first > 0:
        parts.insert(0, times_trans(keys[:first], query_block))
    largest = parts[0].max(axis=0, keepdims=True)
    for part in parts[1:]:
        largest = jnp.maximum(largest, part.max(axis=0, keepdims=True))
    parts = [jnp.exp(part - largest) for part in parts]
    total = sum(part.sum(axis=0, keepdims=True) for part in parts)
    return parts, 1.0 / total


def attention_kernel(block_rows, query_ref, pair_ref, cos_ref, sin_ref, out_ref):
    queries, keys, values = attention_operands(query_ref, pair_ref, cos_ref, sin_ref)
    for first in range(0, queries.shape[0], block_rows):
        rows = slice(first, first + block_rows)
        heads = []
        for head in range(queries.shape[1] // HD):
            query_block = queries[rows, head * HD : (head + 1) * HD]
            parts, inverse = scores_by_key(keys, query_block, first)
            at = 0
            mixed = None
            for part in parts:
                here = trans_times(
                    values[at : at + part.shape[0]], (part * inverse).astype(jnp.bfloat16)
                )
                mixed = here if mixed is None else mixed + here
                at += part.shape[0]
            heads.append(mixed)
        out_ref[rows, :] = jnp.concatenate(heads, axis=0).T.astype(jnp.bfloat16)


def attention_back_kernel(
    block_rows, query_ref, pair_ref, cos_ref, sin_ref, grad_ref, query_out, pair_out, acc_ref
):
    bfloat = jnp.bfloat16
    queries, keys, values = attention_operands(query_ref, pair_ref, cos_ref, sin_ref)

    @pl.when(pl.program_id(0) == 0)
    def _():
        acc_ref[...] = jnp.zeros_like(acc_ref)

    for first in range(0, queries.shape[0], block_rows):
        rows = slice(first, first + block_rows)
        heads = []
        for head in range(queries.shape[1] // HD):
            lanes = slice(head * HD, (head + 1) * HD)
            query_block = queries[rows, lanes]
            grad_block = grad_ref[rows, lanes]
            parts, inverse = scores_by_key(keys, query_block, first)
            parts = [part * inverse for part in parts]
            at = 0
            prob_grads = []
            delta = 0.0
            for part in parts:
                prob_grad = times_trans(values[at : at + part.shape[0]], grad_block)
                delta = delta + (part * prob_grad).sum(axis=0, keepdims=True)
                prob_grads.append(prob_grad)
                at += part.shape[0]
            at = 0
            query_grad = None
            for part, prob_grad in zip(parts, prob_grads):
                here = slice(at, at + part.shape[0])
                score_grad = (part * (prob_grad - delta)).astype(bfloat)
                key_part = matmul(score_grad, query_block)
                value_part = matmul(part.astype(bfloat), grad_block)
                acc_ref[here, :] += jnp.concatenate([key_part, value_part], axis=1)
                query_part = trans_times(keys[here], score_grad)
                query_grad = query_part if query_grad is None else query_grad + query_part
                at += part.shape[0]
            heads.append(query_grad)
        grad = jnp.concatenate(heads, axis=0).T * HD ** (-0.5)
        grad = grad * cos_ref[rows, :] - swap(grad) * sin_ref[rows, :]
        query_out[rows, :] = grad.astype(bfloat)

    @pl.when(pl.program_id(0) == pl.num_programs(0) - 1)
    def _():
        total = acc_ref[...]
        turned = total * cos_ref[...] - swap(total) * sin_ref[...]
        lane = lax.broadcasted_iota(jnp.int32, total.shape, 1)
        pair_out[...] = jnp.where(lane < HD, turned, total).astype(bfloat)


def attention_specs(length, pairs):
    wide = 2 * HD
    return [
        pl.BlockSpec((length, wide), lambda at: (0, at)),
        pl.BlockSpec((length, wide), lambda at: (0, pairs)),
        pl.BlockSpec((length, wide), lambda at: (0, 0)),
        pl.BlockSpec((length, wide), lambda at: (0, 0)),
    ]


def attention(seq_triple, cosine, sine, query_width):
    length = seq_triple.shape[0]
    pairs = query_width // (2 * HD)
    return pl.pallas_call(
        partial(attention_kernel, min(256, length)),
        grid=(pairs,),
        in_specs=attention_specs(length, pairs),
        out_specs=pl.BlockSpec((length, 2 * HD), lambda at: (0, at)),
        out_shape=jax.ShapeDtypeStruct((length, query_width), jnp.bfloat16),
        compiler_params=pltpu.CompilerParams(vmem_limit_bytes=VMEM_LIMIT),
        name="attention",
    )(seq_triple, seq_triple, cosine, sine)


def attention_back(seq_triple, cosine, sine, mixed_grad):
    length, query_width = mixed_grad.shape
    pairs = query_width // (2 * HD)
    wide = 2 * HD
    return pl.pallas_call(
        partial(attention_back_kernel, min(256, length)),
        grid=(pairs,),
        in_specs=attention_specs(length, pairs)
        + [pl.BlockSpec((length, wide), lambda at: (0, at))],
        out_specs=[
            pl.BlockSpec((length, wide), lambda at: (0, at)),
            pl.BlockSpec((length, wide), lambda at: (0, 0)),
        ],
        out_shape=[
            jax.ShapeDtypeStruct((length, query_width), jnp.bfloat16),
            jax.ShapeDtypeStruct((length, wide), jnp.bfloat16),
        ],
        scratch_shapes=[pltpu.VMEM((length, wide), jnp.float32)],
        compiler_params=pltpu.CompilerParams(vmem_limit_bytes=VMEM_LIMIT),
        name="attention_back",
    )(seq_triple, seq_triple, cosine, sine, mixed_grad)


def mlp_kernel(
    query_width,
    unit_width,
    positions,
    resid_in_ref,
    swiglu_grad_ref,
    cot_ref,
    own_weight_ref,
    gain_ref,
    weights_ref,
    *refs,
):
    bfloat = jnp.bfloat16
    mixed_refs = refs[:positions]
    resid_ref, swiglu_ref, mid_ref, part_ref = refs[positions:]
    output_width = positions * query_width
    resid = resid_in_ref[...].astype(jnp.float32)
    for at, mixed_ref in enumerate(mixed_refs):
        columns = slice(at * query_width, (at + 1) * query_width)
        resid = resid + times_trans(mixed_ref[...], weights_ref[:, columns])
    resid_ref[...] = resid
    gain = gain_ref[...]
    spread = lax.rsqrt(jnp.mean(resid * resid, axis=1, keepdims=True) + EPS)
    normed = resid * spread
    seq_two = (normed * gain).astype(bfloat)
    gate_columns = slice(output_width, output_width + unit_width)
    upward_columns = slice(output_width + unit_width, output_width + 2 * unit_width)
    gate = matmul(seq_two, weights_ref[:, gate_columns])
    upward = matmul(seq_two, weights_ref[:, upward_columns])
    open_gate = jax.nn.sigmoid(gate)
    silu = gate * open_gate
    swiglu_ref[...] = (silu * upward).astype(bfloat)
    swiglu_grad = swiglu_grad_ref[...]
    slope = open_gate * (1.0 + gate * (1.0 - open_gate))
    gate_grad = (swiglu_grad * upward * slope).astype(bfloat)
    upward_grad = (swiglu_grad * silu).astype(bfloat)
    grad = times_trans(gate_grad, weights_ref[:, gate_columns])
    grad = grad + times_trans(upward_grad, weights_ref[:, upward_columns])
    grad = grad * gain
    grad = spread * (grad - normed * jnp.mean(grad * normed, axis=1, keepdims=True))
    grad = grad + own_weight_ref[...] * cot_ref[...].astype(jnp.float32)
    mid_low = grad.astype(bfloat)
    mid_ref[...] = mid_low
    part_ref[...] = matmul(mid_low, weights_ref[:, :output_width]).astype(bfloat)


def mlp(resid_in, swiglu_grad, cot, own_weight, gain, weights, mixed, rows_at, row_total):
    width = resid_in.shape[1]
    unit_width = swiglu_grad.shape[1]
    query_width = mixed[0].shape[1]
    block = min(256, row_total)
    offset = rows_at // block

    def rows_of(columns, shift):
        return pl.BlockSpec((block, columns), lambda at: (at + shift, 0))

    return pl.pallas_call(
        partial(mlp_kernel, query_width, unit_width, len(mixed)),
        grid=(row_total // block,),
        in_specs=[
            rows_of(width, offset),
            rows_of(unit_width, offset),
            rows_of(width, offset),
            rows_of(1, offset),
            pl.BlockSpec((1, width), lambda at: (0, 0)),
            pl.BlockSpec(weights.shape, lambda at: (0, 0), pipeline_mode=pl.Buffered(1)),
        ]
        + [rows_of(query_width, 0)] * len(mixed),
        out_specs=[
            rows_of(width, 0),
            rows_of(unit_width, 0),
            rows_of(width, 0),
            rows_of(query_width * len(mixed), 0),
        ],
        out_shape=[
            jax.ShapeDtypeStruct((row_total, width), jnp.float32),
            jax.ShapeDtypeStruct((row_total, unit_width), jnp.bfloat16),
            jax.ShapeDtypeStruct((row_total, width), jnp.bfloat16),
            jax.ShapeDtypeStruct((row_total, query_width * len(mixed)), jnp.bfloat16),
        ],
        compiler_params=pltpu.CompilerParams(vmem_limit_bytes=VMEM_LIMIT),
        name="mlp",
    )(resid_in, swiglu_grad, cot, own_weight, gain[None, :], weights, *mixed)


def hyper_heads(values):
    blocks = values.shape[0] // min(128, values.shape[0])
    return values.reshape(blocks, -1, EH, EHD).transpose(0, 2, 1, 3)


def hyper_rows(values):
    blocks, heads, rows, width = values.shape
    return values.transpose(0, 2, 1, 3).reshape(blocks * rows, heads * width)


def hyper_forward(rows_in, lengths, encoder_triple, encoder_merge, encoder_expand, encoder_reduce, gains):
    bfloat = jnp.bfloat16
    single = jnp.float32
    entries = lengths.shape[0]
    flat_rows = entries * SUBWORD_SLOTS
    valid = jnp.arange(SUBWORD_SLOTS)[None, :] < lengths[:, None]
    normed_one, norm_back_one = jax.vjp(layer_norm, rows_in, gains[0])
    first_in = normed_one.astype(bfloat)
    triple = matmul(first_in, encoder_triple).astype(bfloat)
    queries = hyper_heads(triple[:, :HYPER_WIDTH])
    keys = hyper_heads(triple[:, HYPER_WIDTH : 2 * HYPER_WIDTH])
    values = hyper_heads(triple[:, 2 * HYPER_WIDTH :])
    blocks, _, block_rows, _ = queries.shape
    scores = jnp.einsum("bhqd,bhkd->bhqk", queries, keys, preferred_element_type=single) * EHD ** (
        -0.5
    )
    at = jnp.arange(block_rows) // SUBWORD_SLOTS
    same = at[:, None] == at[None, :]
    open_slots = same[None] & valid.reshape(blocks, 1, block_rows)
    scores = jnp.where(open_slots[:, None], scores, NEG)
    probs = jax.nn.softmax(scores, axis=-1)
    probs_low = probs.astype(bfloat)
    mixed = jnp.einsum("bhqk,bhkd->bhqd", probs_low, values, preferred_element_type=single)
    mixed = hyper_rows(mixed.astype(bfloat))
    resid_one = rows_in + matmul(mixed, encoder_merge)
    normed_two, norm_back_two = jax.vjp(layer_norm, resid_one, gains[1])
    second_in = normed_two.astype(bfloat)
    expanded = matmul(second_in, encoder_expand)
    activated, gelu_back = jax.vjp(partial(jax.nn.gelu, approximate=False), expanded)
    activated_low = activated.astype(bfloat)

    def pool():
        resid_two = resid_one + matmul(activated_low, encoder_reduce)
        kept = jnp.where(
            valid[:, :, None], resid_two.reshape(entries, SUBWORD_SLOTS, HYPER_WIDTH), 0.0
        )
        return (jnp.sum(kept, axis=1) / lengths.astype(single)[:, None]).astype(bfloat)

    def backward(pooled_grad, share):
        pooled_grad = pooled_grad / lengths.astype(single)[:, None]
        grid_grad = jnp.where(valid[:, :, None], pooled_grad[:, None, :], 0.0).reshape(
            flat_rows, HYPER_WIDTH
        )
        reduce_in = grid_grad.astype(bfloat)
        reduce_grad = trans_times(share(activated_low), reduce_in)
        expand_in = gelu_back(times_trans(reduce_in, encoder_reduce))[0].astype(bfloat)
        expand_grad = trans_times(share(second_in), expand_in)
        resid_part, normtwo_grad = norm_back_two(times_trans(expand_in, encoder_expand))
        resid_one_grad = grid_grad + resid_part
        merge_in = resid_one_grad.astype(bfloat)
        merge_grad = trans_times(share(mixed), merge_in)
        mixed_grad = hyper_heads(times_trans(merge_in, encoder_merge).astype(bfloat))
        prob_grad = jnp.einsum("bhqd,bhkd->bhqk", mixed_grad, values, preferred_element_type=single)
        delta = jnp.sum(probs * prob_grad, axis=-1, keepdims=True)
        score_grad = (probs * (prob_grad - delta)).astype(bfloat)
        scale = EHD ** (-0.5)
        query_grad = (
            jnp.einsum("bhqk,bhkd->bhqd", score_grad, keys, preferred_element_type=single) * scale
        )
        key_grad = (
            jnp.einsum("bhqk,bhqd->bhkd", score_grad, queries, preferred_element_type=single)
            * scale
        )
        value_grad = jnp.einsum(
            "bhqk,bhqd->bhkd", probs_low, mixed_grad, preferred_element_type=single
        )
        triple_in = jnp.concatenate(
            [hyper_rows(grad.astype(bfloat)) for grad in (query_grad, key_grad, value_grad)], axis=1
        )
        triple_grad = trans_times(share(first_in), triple_in)
        rows_part, normone_grad = norm_back_one(times_trans(triple_in, encoder_triple))
        rows_low = (resid_one_grad + rows_part).astype(bfloat)
        return (
            rows_low,
            reduce_grad,
            expand_grad,
            merge_grad,
            triple_grad,
            normone_grad,
            normtwo_grad,
        )

    return pool, backward


def per_device(
    subword_embedding_rows,
    entry_subword_index,
    entry_lengths,
    entry_counts,
    encoder_triple,
    encoder_merge,
    encoder_expand,
    encoder_reduce,
    embed_project,
    normone_gain,
    normtwo_gain,
    frozen_query,
    frozen_key,
    frozen_value,
    frozen_output,
    frozen_gate,
    frozen_upward,
    frozen_downward,
    prenorm_gain,
    midnorm_gain,
    text_tokens,
    cotangent,
):
    bfloat = jnp.bfloat16
    single = jnp.float32
    dp_size = lax.axis_size("dp")
    tensor_size = lax.axis_size("tensor")
    dp_at = lax.axis_index("dp")
    tensor_at = lax.axis_index("tensor")
    device_at = dp_at * tensor_size + tensor_at
    entries = entry_subword_index.shape[0]
    entry_total = entries * dp_size * tensor_size
    flat_rows = entries * SUBWORD_SLOTS
    table_rows = subword_embedding_rows.shape[0]
    model_width = embed_project.shape[1]

    with jax.named_scope("ids"):
        packed = jnp.concatenate(
            [entry_subword_index, entry_counts[:, None], entry_lengths[:, None]], axis=1
        )
        packed_width = packed.shape[1]
        packed_dp = lax.all_gather(packed, "dp", axis=0, tiled=False)
    with jax.named_scope("first_weights"):
        first_weights = jnp.concatenate(
            [frozen_query, frozen_key, frozen_value, frozen_downward], axis=1
        )
        first_weights, cot_sent, output_sent = tie_all(
            packed_dp, first_weights, cotangent, frozen_output
        )
        first_weights = lax.all_gather(first_weights, "dp", axis=0, tiled=True)
        query_width = frozen_query.shape[1]
        key_width = frozen_key.shape[1]
        triple_width = query_width + 2 * key_width
        full_triple = first_weights[:, :triple_width]
        full_downward = first_weights[:, triple_width:]
    with jax.named_scope("output_weights"):
        output_blocks = from_all(output_sent)

    with jax.named_scope("lookup"):
        local_ids = packed_dp[:, :, :SUBWORD_SLOTS].reshape(-1) - dp_at * table_rows
        inside = (local_ids >= 0) & (local_ids < table_rows)
        served = jnp.take(subword_embedding_rows, jnp.clip(local_ids, 0, table_rows - 1), axis=0)
        served = jnp.where(inside[:, None], served, jnp.zeros((), bfloat))
        packed_all = from_all(
            tie(jnp.concatenate([packed_dp.reshape(-1), text_tokens]), served)
        )
        served_all = lax.all_to_all(
            served.reshape(dp_size, flat_rows, HYPER_WIDTH), "dp", 0, 0, tiled=True
        )
        rows_in = jnp.sum(served_all.astype(single), axis=0)
    with jax.named_scope("cot_ring"):
        cot_blocks = [cotangent]
        cot_blocks.append(ring(cot_sent))
        cot_blocks.append(ring(tie(cot_blocks[-1], served)))
    with jax.named_scope("second_weights"):
        second_weights = lax.all_gather(
            jnp.concatenate([*tie(output_blocks, served), frozen_gate, frozen_upward], axis=1),
            "dp",
            axis=0,
            tiled=True,
        )
    with jax.named_scope("hyper_wide"):
        rows_blocks = from_all(rows_in.astype(bfloat))

    encoders = (encoder_triple, encoder_merge, encoder_expand, encoder_reduce)
    gains = (normone_gain, normtwo_gain)
    with jax.named_scope("hyper_fwd"):
        pool, _ = hyper_forward(rows_in, entry_lengths, *encoders, gains)
        pooled_low = pool()
    with jax.named_scope("pooled_gather"):
        pooled_blocks = from_all(pooled_low)
        dp_pooled = jnp.concatenate(in_order(pooled_blocks, tensor_at), axis=0)
        all_pooled = lax.all_gather(dp_pooled, "dp", axis=0, tiled=True)
    with jax.named_scope("cot_ring"):
        cot_blocks.append(ring(tie(cot_blocks[-1], dp_pooled)))

    with jax.named_scope("entry_vectors"):
        all_vectors = matmul(all_pooled, embed_project).astype(bfloat)
        vectors = lax.dynamic_slice_in_dim(all_vectors, device_at * entries, entries, 0)
        packed_all = jnp.stack(in_order(packed_all, tensor_at))
        ids_size = dp_size * entries * packed_width
        packed_ids = packed_all[:, :ids_size].reshape(tensor_size, dp_size, entries, packed_width)
        lengths_wide = lax.dynamic_index_in_dim(packed_ids, dp_at, 1, keepdims=False)
        lengths_wide = lengths_wide[:, :, SUBWORD_SLOTS + 1].reshape(-1)
        packed_ids = packed_ids.transpose(1, 0, 2, 3).reshape(entry_total, packed_width)
        all_ids = packed_ids[:, :SUBWORD_SLOTS].reshape(-1)
        all_weights = (1.0 / jnp.log(1.0 + packed_ids[:, SUBWORD_SLOTS].astype(single))).astype(
            bfloat
        )
        seq_tokens = packed_all[:, ids_size:].reshape(-1)
        length = seq_tokens.shape[0]
        rows_here = text_tokens.shape[0]
        seq_hot = (seq_tokens[:, None] == jnp.arange(entry_total)[None, :]).astype(bfloat)
        seq_weight = matmul(seq_hot, all_weights[:, None])
        all_wide = all_vectors.astype(single)
        entry_normed, entry_norm_back = jax.vjp(
            lambda values: rms_norm(values, prenorm_gain), all_wide
        )
        entry_normed = entry_normed.astype(bfloat)
        entry_triple = matmul(entry_normed, full_triple)
        entry_high = entry_triple.astype(bfloat)
        entry_rest = (entry_triple - entry_high.astype(single)).astype(bfloat)
        seq_triple = matmul(seq_hot, entry_high) + matmul(seq_hot, entry_rest)

    cosine, sine = rope_lanes(length)
    with jax.named_scope("attention_fwd"):
        lm_mixed = attention(seq_triple, cosine, sine, query_width)
        block_rows = min(512, length)
        block_total = length // block_rows
        mixed_parts = [
            [lm_mixed[first : first + block_rows]] for first in range(0, length, block_rows)
        ]
    with jax.named_scope("mixed_ring"):
        mixed_parts[0][0] = tie(mixed_parts[0][0], cot_blocks[-1])
        late_hot, late_cot = tie_all(lm_mixed, seq_hot, cot_blocks)
        for parts in mixed_parts:
            for _ in range(tensor_size - 1):
                parts.append(ring(parts[-1]))
    with jax.named_scope("swiglu_grad"):
        seq_cot = jnp.concatenate(in_order(late_cot, tensor_at), axis=0)
        resid_in = matmul(late_hot, all_vectors).astype(bfloat)
        swiglu_grad = matmul((seq_weight * seq_cot.astype(single)).astype(bfloat), full_downward)
        own_rows_here = jnp.arange(length) // rows_here == tensor_at
        own_weight = jnp.where(own_rows_here[:, None], seq_weight, 0.0)

    with jax.named_scope("mlp"):
        resid_blocks = []
        swiglu_blocks = []
        mid_blocks = []
        mixed_grads = []
        for block_idx, parts in enumerate(mixed_parts):
            resid_mid, swiglu_low, mid_low, mixed_part = mlp(
                resid_in,
                swiglu_grad,
                seq_cot,
                own_weight,
                midnorm_gain,
                second_weights,
                parts,
                block_idx * block_rows,
                block_rows,
            )
            resid_blocks.append(resid_mid)
            swiglu_blocks.append(swiglu_low)
            mid_blocks.append(mid_low)
            carried = None
            for step in [*range(1, tensor_size), 0]:
                part = mixed_part[:, step * query_width : (step + 1) * query_width]
                if carried is not None:
                    part = (part.astype(single) + carried.astype(single)).astype(bfloat)
                if step > 0:
                    carried = ring(part)
            mixed_grads.append(part)

    with jax.named_scope("hyper_wide"):
        rows_wide = jnp.concatenate(in_order(rows_blocks, tensor_at), axis=0).astype(single)
        rows_wide = tie(rows_wide, mixed_parts[-1][0])
        _, hyper_backward = hyper_forward(rows_wide, lengths_wide, *encoders, gains)

    with jax.named_scope("layer_out"):
        layer_part = times_trans(jnp.concatenate(swiglu_blocks, axis=0), full_downward)
        layer_part, mixed_grads = lax.optimization_barrier((layer_part.astype(bfloat), mixed_grads))
        blocks_of = [
            lax.dynamic_slice_in_dim(
                block, lax.rem(tensor_at * rows_here, block_rows), rows_here, 0
            )
            for block in resid_blocks
        ]
        resid_own = blocks_of[0]
        for block_idx in range(1, block_total):
            resid_own = jnp.where(
                tensor_at * rows_here // block_rows == block_idx, blocks_of[block_idx], resid_own
            )
        layer_final = resid_own + lax.psum_scatter(
            layer_part, "tensor", scatter_dimension=0, tiled=True
        ).astype(single)
    with jax.named_scope("attention_bwd"):
        query_out, pair_out = attention_back(
            seq_triple, cosine, sine, jnp.concatenate(mixed_grads, axis=0)
        )
        triple_out = jnp.concatenate([query_out, pair_out], axis=1)

    with jax.named_scope("entry_bwd"):
        entry_out = trans_times(seq_hot, triple_out).astype(bfloat)
        entry_part = entry_norm_back(times_trans(entry_out, full_triple))[0]
        entry_part = entry_part + trans_times(seq_hot, jnp.concatenate(mid_blocks, axis=0))
        entry_part = entry_part.astype(bfloat)
        pooled_part = times_trans(entry_part, embed_project).astype(bfloat)
        pooled_part = tie(pooled_part, layer_final)
        pooled_part = scatter_dp(pooled_part).astype(bfloat)
        pooled_grad = sum(block.astype(single) for block in from_all(pooled_part))
        project_part = trans_times(all_pooled, tie(entry_part, pooled_part)).astype(bfloat)

    def share(values):
        rows, width = values.shape
        split = values.reshape(rows, dp_size, tensor_size, width // (dp_size * tensor_size))
        return lax.dynamic_index_in_dim(split, tensor_at, 2, keepdims=False).reshape(
            rows, width // tensor_size
        )

    with jax.named_scope("hyper_bwd"):
        project_grad = lax.psum_scatter(project_part, "dp", scatter_dimension=0, tiled=True)
        rows_low, reduce_grad, expand_grad, merge_grad, triple_grad, normone_grad, normtwo_grad = (
            hyper_backward(pooled_grad, share)
        )

    with jax.named_scope("grads_out"):
        all_rows = lax.all_gather(rows_low, "dp", axis=0, tiled=True)
        project_grad = tie(project_grad, rows_low)
        project_grad = project_grad.reshape(tensor_size, -1, model_width)
        project_grad = lax.all_to_all(project_grad, "tensor", 0, 0, tiled=True)
        project_grad = jnp.sum(project_grad.astype(single), axis=0)
        own_rows = table_rows // tensor_size
        row_hot = (
            (jnp.arange(own_rows) + device_at * own_rows)[:, None] == all_ids[None, :]
        ).astype(bfloat)
        subword_grad = matmul(row_hot, all_rows)

        depth = HYPER_WIDTH // (dp_size * tensor_size)
        deep = reduce_grad.shape[0] // dp_size // depth
        reduce_grad = reduce_grad.astype(bfloat).reshape(dp_size, deep, depth, HYPER_WIDTH)
        early = [reduce_grad[:, at] for at in range(deep)]
        early += [
            part.astype(bfloat).reshape(dp_size, depth, -1) for part in (expand_grad, merge_grad)
        ]
        early = jnp.concatenate(early, axis=2).reshape(dp_size * depth, -1)
        early = scatter_dp(early)
        gain_grads = share(jnp.stack([normone_grad, normtwo_grad])).transpose(1, 0)
        late = jnp.concatenate([triple_grad, jnp.pad(gain_grads, ((0, 0), (0, 126)))], axis=1)
        late = scatter_dp(late.astype(bfloat))
        reduce_width = deep * HYPER_WIDTH
        expand_width = expand_grad.shape[1]
        reduce_grad = early[:, :reduce_width].reshape(depth, deep, HYPER_WIDTH)
        reduce_grad = reduce_grad.transpose(1, 0, 2).reshape(deep * depth, HYPER_WIDTH)
        expand_grad = early[:, reduce_width : reduce_width + expand_width]
        merge_grad = early[:, reduce_width + expand_width :]
        grad_width = triple_grad.shape[1]
    return (
        layer_final.astype(bfloat),
        vectors,
        subword_grad,
        late[:, :grad_width],
        merge_grad,
        expand_grad,
        reduce_grad,
        project_grad,
        late[:, grad_width],
        late[:, grad_width + 1],
    )


def solution(mesh):
    return jax.shard_map(
        per_device,
        mesh=mesh,
        in_specs=(
            P("dp", None),
            P(("dp", "tensor"), None),
            P(("dp", "tensor")),
            P(("dp", "tensor")),
            P(),
            P(),
            P(),
            P(),
            P(),
            P(),
            P(),
            P("dp", "tensor"),
            P("dp", "tensor"),
            P("dp", "tensor"),
            P("dp", "tensor"),
            P("dp", "tensor"),
            P("dp", "tensor"),
            P("dp", "tensor"),
            P(),
            P(),
            P(("dp", "tensor")),
            P(("dp", "tensor"), None),
        ),
        out_specs=(
            P(("dp", "tensor"), None),
            P(("dp", "tensor"), None),
            P(("dp", "tensor"), None),
            P(("dp", "tensor"), None),
            P(("dp", "tensor"), None),
            P(("dp", "tensor"), None),
            P(("dp", "tensor"), None),
            P(("dp", "tensor"), None),
            P(("dp", "tensor")),
            P(("dp", "tensor")),
        ),
        check_vma=False,
    )
```

time: 1050 us -> 608 us (0.58)
  waiting for transfers between devices: 575 us -> 134 us
  Pallas kernels: 0 us -> 116 us
  matrix products: 214 us -> 124 us
  blocking collectives: 108 us -> 22 us
  local copies, waits for them, and re-layouts: 45.2 us -> 92.6 us
  starting transfers between devices: 35.3 us -> 62.8 us
  other arithmetic: 48.3 us -> 35.1 us
    reduce_scatter x13 -> x2, waiting for transfers between devices: 285 us -> 0.01 us  [the longest x1 0.01 us: per_device(): lax.psum_scatter(layer_part, 'tensor', scatter_dimension=0, tiled=True)]
    pallas_call x0 -> x4, Pallas kernels: none -> 116 us  [the longest x2 66.8 us: mlp(): pl.pallas_call(partial(mlp_kernel, query_width, unit_width, len(mixed)),...]
    all_gather x7 -> x3, waiting for transfers between devices: 93 us -> 0.02 us  [the longest x1 0.02 us: per_device(): first_weights = lax.all_gather(first_weights, 'dp', axis=0, tiled=True)]
    all_gather x4 -> x1, blocking collectives: 74.2 us -> 11.3 us  [per_device(): all_pooled = lax.all_gather(dp_pooled, 'dp', axis=0, tiled=True)]
    dot_general x18 -> x7, matrix products: 62 us -> 13.4 us  [the longest x1 3.28 us: backward(): jnp.einsum('bhqk,bhqd->bhkd', probs_low, mixed_grad, preferred_element_ty...]
    all_to_all x2 -> x4, waiting for transfers between devices: 62.8 us -> 25.1 us  [the longest x3 19.7 us: scatter_dp(): blocks = lax.all_to_all(blocks, 'dp', 0, 0, tiled=True)]
    ppermute x9 -> x30, waiting for transfers between devices: 132 us -> 101 us  [ring(): lax.ppermute(values, 'tensor', [(i, (i + shift) % size) for i in range(si...]
    dot_general x16 -> x7, matrix products: 61.3 us -> 31.7 us  [times_trans(): lax.dot_general(left, right, (((1,), (1,)), ((), ())), preferred_element_...]
  transfers between devices with their start and end apart: 32 -> 40, of which waited for: 20 -> 20; matrix products, arithmetic and copies ran while one was open for 19% -> 37% of each run, Pallas kernels for 0% -> 19%
where the time goes in v2:
time: 608 us; the launch traced here: 603 us
  waiting for transfers between devices  134 us (22%)
  matrix products  124 us (20%)
  Pallas kernels  116 us (19%)
  local copies, waits for them, and re-layouts  92.6 us (15%)
  starting transfers between devices  62.8 us (10%)
  other arithmetic  35.1 us (6%)
  blocking collectives  22 us (4%)
  between operations  15.5 us (3%)
    ppermute x30, waiting for transfers between devices, ring(): lax.ppermute(values, 'tensor', [(i, (i + shift) % size) for i in range(si...  101 us
    pallas_call x2, Pallas kernels, mlp(): pl.pallas_call(partial(mlp_kernel, query_width, unit_width, len(mixed)),...  66.8 us
    dot_general x14, matrix products, matmul(): return jnp.dot(left, right, preferred_element_type=jnp.float32)  58.2 us
    ppermute x30, starting transfers between devices, ring(): lax.ppermute(values, 'tensor', [(i, (i + shift) % size) for i in range(si...  41.3 us
    dot_general x7, matrix products, times_trans(): lax.dot_general(left, right, (((1,), (1,)), ((), ())), preferred_element_...  31.7 us
    pallas_call x1, Pallas kernels, attention_back(): pl.pallas_call(partial(attention_back_kernel, min(256, length)), grid=(pa...  30.3 us
    unnamed x153, local copies, waits for them, and re-layouts  21.7 us
    all_to_all x3, waiting for transfers between devices, scatter_dp(): blocks = lax.all_to_all(blocks, 'dp', 0, 0, tiled=True)  19.7 us
  transfers between devices with their start and end apart: 40, of which 20 were waited for; matrix products, arithmetic and copies ran while one was open for 37% of the time, Pallas kernels for 19%

profile of v2, /device:TPU:0, one launch (start us, length us, event | category | flops | bytes accessed | tf_op | source)
XLA Modules:
  0.0 602.5 jit_solution(2811812765521650812)
XLA Ops:
  9.6 10.7 %all-gather = s32[128,10]{1,0:T(8,128)S(1)} all-gather(s32[16,10]{1,0:T(8,128)S(1)} %pad_add_fusion.4), channel_id=2, replica_groups=mesh['dp'=8,'tensor'=4] {'dp'}, dimensions={0}, use_global_device_ids=true | all-gather | bytes 5760 | tf_op jit(solution)/shard_map/ids/all_gather | solution.py:482
  30.1 6.9 %gather_fusion = bf16[1024,512]{1,0:T(8,128)(2,1)S(1)} fusion(bf16[4000,512]{1,0:T(8,128)(2,1)} %param.22, s32[1024]{0:T(1024)S(1)} %broadcast_clamp_fusion), kind=kCustom, calls=%fused_computation | custom fusion | bytes 2101248 | tf_op jit(solution)/shard_map/lookup/jit(_take)/gather | solution.py:502
  41.5 6.0 collective-permute-done.9
  56.4 5.2 collective-permute-start
  82.1 8.1 %all-to-all-done = bf16[8,128,512]{2,1,0:T(8,128)(2,1)S(1)} async-done(((bf16[8,128,512]{2,1,0:T(8,128)(2,1)}), bf16[8,128,512]{2,1,0:T(8,128)(2,1)S(1)}, u32[]{:S(2)}, u32[]{:S(2)}) %all-to-all-start) | async-done | bytes 1048608 | tf_op jit(solution)/shard_map/lookup/all_to_all | solution.py:507
  95.1 5.3 fusion.65
  108.4 11.3 %all_gather.20 = bf16[512,512]{1,0:T(8,128)(2,1)S(1)} all-gather(bf16[64,512]{1,0:T(8,128)(2,1)S(1)} %pad_maximum_fusion.8), channel_id=1, replica_groups=mesh['dp'=8,'tensor'=4] {'dp'}, dimensions={0}, use_global_device_ids=true | all-gather | bytes 589824 | tf_op jit(solution)/shard_map/pooled_gather/all_gather | solution.py:533
  124.1 5.8 collective-permute-done.4
  138.4 18.8 %attention.1 = bf16[1024,512]{1,0:T(8,128)(2,1)} custom-call(f32[1024,640]{1,0:T(8,128)} %fusion.48.query_ref.pair_ref, f32[1024,640]{1,0:T(8,128)} %fusion.48.query_ref.pair_ref, f32[1024,128]{1,0:T(8,128)} %get-tuple-element.139.cos_ref, f32[1024,128]{1,0:T(8,128)} %get-tuple-element.140.sin_ref), custom_call_target="tpu_custom_call" | custom-call | tf_op jit(solution)/shard_map/attention_fwd/attention/pallas_call | solution.py:226
  162.3 12.9 %collective-permute-done.12.refs_1_ = bf16[512,512]{1,0:T(8,128)(2,1)S(1)} collective-permute-done((bf16[512,512]{1,0:T(8,128)(2,1)S(1)}, bf16[512,512]{1,0:T(8,128)(2,1)S(1)}, u32[]{:S(2)}, u32[]{:S(2)}) %collective-permute-start.12) | collective-permute-done | bytes 524320 | tf_op jit(solution)/shard_map/mixed_ring/ppermute | solution.py:67
  175.3 11.2 %collective-permute-done.15.refs_1_ = bf16[512,512]{1,0:T(8,128)(2,1)S(1)} collective-permute-done((bf16[512,512]{1,0:T(8,128)(2,1)S(1)}, bf16[512,512]{1,0:T(8,128)(2,1)S(1)}, u32[]{:S(2)}, u32[]{:S(2)}) %collective-permute-start.15) | collective-permute-done | bytes 524320 | tf_op jit(solution)/shard_map/mixed_ring/ppermute | solution.py:67
  186.5 11.8 %fusion.8.swiglu_grad_ref = f32[1024,1408]{1,0:T(8,128)} fusion(bf16[2048,2048]{1,0:T(8,128)(2,1)S(1)} %bitcast.289, f32[1024]{0:T(1024)S(1)} %bitcast.285, bf16[256,2048]{1,0:T(8,128)(2,1)S(1)} %get-tuple-element.89, bf16[256,2048]{1,0:T(8,128)(2,1)S(1)} %get-tuple-element.90, bf16[256,2048]{1,0:T(8,128)(2,1)S(1)} %get-tuple-element.91, ...), kind=kOutput, calls=%fused_computation.16 | convolution fusion | flops 5926551552 | bytes 15732736 | tf_op jit(solution)/shard_map/swiglu_grad/dot_general | solution.py:50
  203.7 5.4 collective-permute-done.16.refs_2_
  211.3 9.0 %collective-permute-done.14.refs_3_ = bf16[512,512]{1,0:T(8,128)(2,1)} collective-permute-done((bf16[512,512]{1,0:T(8,128)(2,1)S(1)}, bf16[512,512]{1,0:T(8,128)(2,1)}, u32[]{:S(2)}, u32[]{:S(2)}) %collective-permute-start.14) | collective-permute-done | bytes 524320 | tf_op jit(solution)/shard_map/mixed_ring/ppermute | solution.py:67
  220.3 33.4 %mlp.2 = (f32[512,2048]{1,0:T(8,128)}, bf16[512,1408]{1,0:T(8,128)(2,1)}, bf16[512,2048]{1,0:T(8,128)(2,1)}, bf16[512,2048]{1,0:T(8,128)(2,1)}) custom-call(bf16[1024,2048]{1,0:T(8,128)(2,1)} %convolution_convert_fusion.resid_in_ref, f32[1024,1408]{1,0:T(8,128)} %fusion.8.swiglu_grad_ref, bf16[1024,2048]{1,0:T(8,128)(2,1)} %pad_maximum_fusion.1.cot_ref, ...), custom_call_target="tpu_custom_call" | custom-call | tf_op jit(solution)/shard_map/mlp/mlp/pallas_call | solution.py:316
  255.8 33.4 %mlp.3 = (f32[512,2048]{1,0:T(8,128)}, bf16[512,1408]{1,0:T(8,128)(2,1)}, bf16[512,2048]{1,0:T(8,128)(2,1)}, bf16[512,2048]{1,0:T(8,128)(2,1)}) custom-call(bf16[1024,2048]{1,0:T(8,128)(2,1)} %convolution_convert_fusion.resid_in_ref, f32[1024,1408]{1,0:T(8,128)} %fusion.8.swiglu_grad_ref, bf16[1024,2048]{1,0:T(8,128)(2,1)} %pad_maximum_fusion.1.cot_ref, ...), custom_call_target="tpu_custom_call" | custom-call | tf_op jit(solution)/shard_map/mlp/mlp/pallas_call | solution.py:316
  294.9 12.2 %collective-permute-done.18 = bf16[512,512]{1,0:T(8,128)(2,1)S(1)} collective-permute-done((bf16[512,512]{1,0:T(8,128)(2,1)S(1)}, bf16[512,512]{1,0:T(8,128)(2,1)S(1)}, u32[]{:S(2)}, u32[]{:S(2)}) %collective-permute-start.18) | collective-permute-done | bytes 524320 | tf_op jit(solution)/shard_map/mlp/ppermute | solution.py:67
  307.4 11.0 %collective-permute-done.22 = bf16[512,512]{1,0:T(8,128)(2,1)S(1)} collective-permute-done((bf16[512,512]{1,0:T(8,128)(2,1)S(1)}, bf16[512,512]{1,0:T(8,128)(2,1)S(1)}, u32[]{:S(2)}, u32[]{:S(2)}) %collective-permute-start.22) | collective-permute-done | bytes 524320 | tf_op jit(solution)/shard_map/mlp/ppermute | solution.py:67
  319.6 10.0 %collective-permute-done.19 = bf16[512,512]{1,0:T(8,128)(2,1)S(1)} collective-permute-done((bf16[512,512]{1,0:T(8,128)(2,1)S(1)}, bf16[512,512]{1,0:T(8,128)(2,1)S(1)}, u32[]{:S(2)}, u32[]{:S(2)}) %collective-permute-start.19) | collective-permute-done | bytes 524320 | tf_op jit(solution)/shard_map/mlp/ppermute | solution.py:67
  331.0 11.7 %fusion.27 = bf16[1024,2048]{1,0:T(8,128)(2,1)} fusion(bf16[2048,2048]{1,0:T(8,128)(2,1)} %all-gather.5.cloned.1.call-done, bf16[512,1408]{1,0:T(8,128)(2,1)S(1)} %copy-done.61, bf16[512,1408]{1,0:T(8,128)(2,1)S(1)} %copy-done.62), kind=kOutput, calls=%fused_computation.47 | convolution fusion | flops 5913444352 | bytes 12845056 | tf_op jit(solution)/shard_map/layer_out/dot_general | solution.py:54
  355.9 8.0 %collective-permute-done.28 = bf16[128,512]{1,0:T(8,128)(2,1)S(1)} collective-permute-done((bf16[128,512]{1,0:T(8,128)(2,1)S(1)}, bf16[128,512]{1,0:T(8,128)(2,1)S(1)}, u32[]{:S(2)}, u32[]{:S(2)}) %collective-permute-start.28) | collective-permute-done | bytes 131104 | tf_op jit(solution)/shard_map/hyper_wide/ppermute | solution.py:67
  394.3 30.3 %attention_back.1 = (bf16[1024,512]{1,0:T(8,128)(2,1)}, bf16[1024,128]{1,0:T(8,128)(2,1)}) custom-call(f32[1024,640]{1,0:T(8,128)} %fusion.48.query_ref.pair_ref, f32[1024,640]{1,0:T(8,128)} %fusion.48.query_ref.pair_ref, f32[1024,128]{1,0:T(8,128)} %get-tuple-element.139.cos_ref, f32[1024,128]{1,0:T(8,128)} %get-tuple-element.140.sin_ref, ...), custom_call_target="tpu_custom_call" | custom-call | tf_op jit(solution)/shard_map/attention_bwd/attention_back/pallas_call | solution.py:241
  424.6 8.2 %fusion.16 = (f32[512]{0:T(512)S(1)}, f32[512,2048]{1,0:T(8,128)}) fusion(bf16[512,2048]{1,0:T(8,128)(2,1)} %get-tuple-element.126, f32[2048]{0:T(1024)S(1)} %copy-done.64, bf16[2048,2048]{1,0:T(8,128)(2,1)} %all-gather.5.cloned.1.call-done, bf16[1024,128]{1,0:T(8,128)(2,1)} %get-tuple-element.69, bf16[1024,512]{1,0:T(8,128)(2,1)} %get-tuple-element.68, ...), kind=kOutput, calls=%fused_computation.24 | convolution fusion | flops 2020933120 | bytes 10237952 | tf_op jit(solution)/shard_map/entry_bwd/dot_general | solution.py:54
  432.9 7.4 %fusion.11 = bf16[512,2048]{1,0:T(8,128)(2,1)S(1)} fusion(bf16[512,2048]{1,0:T(8,128)(2,1)} %get-tuple-element.126, f32[512,2048]{1,0:T(8,128)} %get-tuple-element.133, bf16[512,2048]{1,0:T(8,128)(2,1)} %get-tuple-element.71, bf16[512,2048]{1,0:T(8,128)(2,1)} %get-tuple-element.70, f32[512]{0:T(512)S(1)} %multiply_multiply_fusion.12, ...), kind=kOutput, calls=%fused_computation.19 | convolution fusion | flops 2164785152 | bytes 12599296 | tf_op jit(solution)/shard_map/entry_bwd/dot_general | solution.py:60
  447.7 5.5 all-to-all-start.1
  453.2 13.6 %multiply_convert_fusion.2 = (bf16[512,2048]{1,0:T(8,128)(2,1)}, f32[512,2048]{1,0:T(8,128)}, f32[512,2048]{1,0:T(8,128)}) fusion(bf16[512,512]{0,1:T(8,128)(2,1)S(1)} %copy-done.25, bf16[512,2048]{1,0:T(8,128)(2,1)} %param.28), kind=kOutput, calls=%fused_computation.31 | convolution fusion | flops 1141899264 | bytes 13107200 | tf_op jit(solution)/shard_map/hyper_wide/dot_general | solution.py:50
  467.0 7.6 %collective-permute-start.24 = (bf16[64,512]{1,0:T(8,128)(2,1)S(1)}, bf16[64,512]{1,0:T(8,128)(2,1)S(1)}, u32[]{:S(2)}, u32[]{:S(2)}) collective-permute-start(bf16[64,512]{1,0:T(8,128)(2,1)S(1)} %reduce_sum.268), channel_id=1, source_target_pairs={{0,1},{1,2},{2,3},{3,0},{4,5},{5,6},{6,7},{7,4},{8,9},{9,10},{10,1... | collective-permute-start | bytes 196616 | tf_op jit(solution)/shard_map/entry_bwd/ppermute | solution.py:67
  484.1 6.8 %add_convert_fusion = bf16[512,2048]{1,0:T(8,128)(2,1)S(1)} fusion(f32[512,2048]{1,0:T(8,128)} %get-tuple-element.85, f32[512,2048]{1,0:T(8,128)} %get-tuple-element.131, bf16[2048,512]{1,0:T(8,128)(2,1)} %param.29, f32[512,512]{0,1:T(8,128)S(1)} %copy.144, pred[512]{0:T(512)(128)(4,1)S(1)} %copy-done.47), kind=kOutput, calls=%fused_computation.32 | convolution fusion | flops 1088684032 | bytes 13632000 | tf_op jit(solution)/shard_map/hyper_bwd/dot_general | solution.py:54
  557.4 17.6 %all-to-all-done.3 = bf16[8,16,4608]{2,1,0:T(8,128)(2,1)S(1)} async-done(((bf16[8,16,4608]{2,1,0:T(8,128)(2,1)}), bf16[8,16,4608]{2,1,0:T(8,128)(2,1)S(1)}, u32[]{:S(2)}, u32[]{:S(2)}) %all-to-all-start.3) | async-done | bytes 1179680 | tf_op jit(solution)/shard_map/grads_out/all_to_all | solution.py:90
  575.8 4.6 all-to-all-start.4
  581.8 5.4 all-to-all-done.4
  587.9 7.9 %fusion.2 = f32[1000,512]{1,0:T(8,128)} fusion(bf16[4096,512]{0,1:T(8,128)(2,1)} %all-gather.9.cloned.1.call-done, s32[4096]{0:T(1024)S(1)} %eq.85, s32[1000]{0:T(1024)S(1)} %iota_add_fusion), kind=kOutput, calls=%fused_computation.3 | convolution fusion | flops 4198400000 | bytes 6262688 | tf_op jit(solution)/shard_map/grads_out/dot_general | solution.py:50
  (407 shorter events, 223.9 us)
Async XLA Ops:
  7.2 123.2 %all-gather.5.cloned.1.call-start = ((), (), s32[]{:S(2)}) async-start(), calls=%async_computation.7 | async-start | bytes 9437184 | tf_op jit(solution)/shard_map/first_weights/all_gather | solution.py:490
  25.2 195.1 %all-gather.7.cloned.1.call-start = ((), (), s32[]{:S(2)}) async-start(), calls=%async_computation.8 | async-start | bytes 22413312 | tf_op jit(solution)/shard_map/second_weights/all_gather | solution.py:516
  25.2 16.2 %collective-permute-start.10 = (bf16[256,512]{1,0:T(8,128)(2,1)}, bf16[256,512]{1,0:T(8,128)(2,1)}, u32[]{:S(2)}, u32[]{:S(2)}) collective-permute-start(bf16[256,512]{1,0:T(8,128)(2,1)} %param.36), channel_id=1, source_target_pairs={{0,2},{1,3},{2,0},{3,1},{4,6},{5,7},{6,4},{7,5},{8,10},{9,11},{10,... | collective-permute-start | bytes 786440 | tf_op jit(solution)/shard_map/output_weights/ppermute | solution.py:67
  27.9 13.6 %collective-permute-start.11 = (bf16[256,512]{1,0:T(8,128)(2,1)}, bf16[256,512]{1,0:T(8,128)(2,1)}, u32[]{:S(2)}, u32[]{:S(2)}) collective-permute-start(bf16[256,512]{1,0:T(8,128)(2,1)} %param.36), channel_id=1, source_target_pairs={{0,3},{1,0},{2,1},{3,2},{4,7},{5,4},{6,5},{7,6},{8,11},{9,8},{10,9... | collective-permute-start | bytes 786440 | tf_op jit(solution)/shard_map/output_weights/ppermute | solution.py:67
  29.2 18.2 %collective-permute-start.9 = (bf16[256,512]{1,0:T(8,128)(2,1)}, bf16[256,512]{1,0:T(8,128)(2,1)}, u32[]{:S(2)}, u32[]{:S(2)}) collective-permute-start(bf16[256,512]{1,0:T(8,128)(2,1)} %param.36), channel_id=1, source_target_pairs={{0,1},{1,2},{2,3},{3,0},{4,5},{5,6},{6,7},{7,4},{8,9},{9,10},{10,1... | collective-permute-start | bytes 786440 | tf_op jit(solution)/shard_map/output_weights/ppermute | solution.py:67
  56.4 21.9 %collective-permute-start = (s32[1536]{0:T(1024)S(1)}, s32[1536]{0:T(1024)S(1)}, u32[]{:S(2)}, u32[]{:S(2)}) collective-permute-start(s32[1536]{0:T(1024)S(1)} %pad_add_fusion.5), channel_id=1, source_target_pairs={{0,1},{1,2},{2,3},{3,0},{4,5},{5,6},{6,7},{7,4},{8,9},{9,10},{10,1... | collective-permute-start | bytes 18440 | tf_op jit(solution)/shard_map/lookup/ppermute | solution.py:67
  61.7 16.7 %collective-permute-start.1 = (s32[1536]{0:T(1024)S(1)}, s32[1536]{0:T(1024)S(1)}, u32[]{:S(2)}, u32[]{:S(2)}) collective-permute-start(s32[1536]{0:T(1024)S(1)} %pad_add_fusion.5), channel_id=1, source_target_pairs={{0,2},{1,3},{2,0},{3,1},{4,6},{5,7},{6,4},{7,5},{8,10},{9,11},{10,... | collective-permute-start | bytes 18440 | tf_op jit(solution)/shard_map/lookup/ppermute | solution.py:67
  63.7 14.7 %collective-permute-start.2 = (s32[1536]{0:T(1024)S(1)}, s32[1536]{0:T(1024)S(1)}, u32[]{:S(2)}, u32[]{:S(2)}) collective-permute-start(s32[1536]{0:T(1024)S(1)} %pad_add_fusion.5), channel_id=1, source_target_pairs={{0,3},{1,0},{2,1},{3,2},{4,7},{5,4},{6,5},{7,6},{8,11},{9,8},{10,9... | collective-permute-start | bytes 18440 | tf_op jit(solution)/shard_map/lookup/ppermute | solution.py:67
  68.0 22.1 %all-to-all-start = ((bf16[8,128,512]{2,1,0:T(8,128)(2,1)}), bf16[8,128,512]{2,1,0:T(8,128)(2,1)S(1)}, u32[]{:S(2)}, u32[]{:S(2)}) async-start(bf16[8,128,512]{2,1,0:T(8,128)(2,1)} %select_select_fusion), calls=%async_computation | async-start | bytes 2097152 | tf_op jit(solution)/shard_map/lookup/all_to_all | solution.py:507
  71.6 372.0 %reduce-scatter.3.cloned.1.call-start = ((), (), s32[]{:S(2)}) async-start(), calls=%async_computation.9 | async-start | bytes 5242880 | tf_op jit(solution)/shard_map/layer_out/reduce_scatter | solution.py:634
  71.7 34.2 %collective-permute-start.3 = (bf16[256,2048]{1,0:T(8,128)(2,1)}, bf16[256,2048]{1,0:T(8,128)(2,1)}, u32[]{:S(2)}, u32[]{:S(2)}) collective-permute-start(bf16[256,2048]{1,0:T(8,128)(2,1)} %param.43), channel_id=1, source_target_pairs={{0,1},{1,2},{2,3},{3,0},{4,5},{5,6},{6,7},{7,4},{8,9},{9,10},{10,1... | collective-permute-start | bytes 3145736 | tf_op jit(solution)/shard_map/cot_ring/ppermute | solution.py:67
  105.8 24.0 %collective-permute-start.4 = (bf16[256,2048]{1,0:T(8,128)(2,1)}, bf16[256,2048]{1,0:T(8,128)(2,1)}, u32[]{:S(2)}, u32[]{:S(2)}) collective-permute-start(bf16[256,2048]{1,0:T(8,128)(2,1)} %collective-permute-done.3), channel_id=1, source_target_pairs={{0,1},{1,2},{2,3},{3,0},{4,5},{5,6},{6,7},{7,4},{8,9},{9,10},{10,1... | collective-permute-start | bytes 3145736 | tf_op jit(solution)/shard_map/cot_ring/ppermute | solution.py:67
  129.9 27.4 %collective-permute-start.8 = (bf16[256,2048]{1,0:T(8,128)(2,1)}, bf16[256,2048]{1,0:T(8,128)(2,1)}, u32[]{:S(2)}, u32[]{:S(2)}) collective-permute-start(bf16[256,2048]{1,0:T(8,128)(2,1)} %collective-permute-done.4), channel_id=1, source_target_pairs={{0,1},{1,2},{2,3},{3,0},{4,5},{5,6},{6,7},{7,4},{8,9},{9,10},{10,1... | collective-permute-start | bytes 3145736 | tf_op jit(solution)/shard_map/cot_ring/ppermute | solution.py:67
  158.5 16.7 %collective-permute-start.12 = (bf16[512,512]{1,0:T(8,128)(2,1)S(1)}, bf16[512,512]{1,0:T(8,128)(2,1)S(1)}, u32[]{:S(2)}, u32[]{:S(2)}) collective-permute-start(bf16[512,512]{1,0:T(8,128)(2,1)S(1)} %get-tuple-element.96.refs_0_), channel_id=1, source_target_pairs={{0,1},{1,2},{2,3},{3,0},{4,5},{5,6},{6,7},{7,4},{8,9},{9,10},{10,1... | collective-permute-start | bytes 1572872 | tf_op jit(solution)/shard_map/mixed_ring/ppermute | solution.py:67
  158.6 27.9 %collective-permute-start.15 = (bf16[512,512]{1,0:T(8,128)(2,1)S(1)}, bf16[512,512]{1,0:T(8,128)(2,1)S(1)}, u32[]{:S(2)}, u32[]{:S(2)}) collective-permute-start(bf16[512,512]{1,0:T(8,128)(2,1)S(1)} %get-tuple-element.59.refs_0_), channel_id=1, source_target_pairs={{0,1},{1,2},{2,3},{3,0},{4,5},{5,6},{6,7},{7,4},{8,9},{9,10},{10,1... | collective-permute-start | bytes 1572872 | tf_op jit(solution)/shard_map/mixed_ring/ppermute | solution.py:67
  175.3 23.1 %collective-permute-start.13 = (bf16[512,512]{1,0:T(8,128)(2,1)S(1)}, bf16[512,512]{1,0:T(8,128)(2,1)S(1)}, u32[]{:S(2)}, u32[]{:S(2)}) collective-permute-start(bf16[512,512]{1,0:T(8,128)(2,1)S(1)} %collective-permute-done.12.refs_1_), channel_id=1, source_target_pairs={{0,1},{1,2},{2,3},{3,0},{4,5},{5,6},{6,7},{7,4},{8,9},{9,10},{10,1... | collective-permute-start | bytes 1572872 | tf_op jit(solution)/shard_map/mixed_ring/ppermute | solution.py:67
  186.5 22.6 %collective-permute-start.16 = (bf16[512,512]{1,0:T(8,128)(2,1)S(1)}, bf16[512,512]{1,0:T(8,128)(2,1)}, u32[]{:S(2)}, u32[]{:S(2)}) collective-permute-start(bf16[512,512]{1,0:T(8,128)(2,1)S(1)} %collective-permute-done.15.refs_1_), channel_id=1, source_target_pairs={{0,1},{1,2},{2,3},{3,0},{4,5},{5,6},{6,7},{7,4},{8,9},{9,10},{10,1... | collective-permute-start | bytes 1572872 | tf_op jit(solution)/shard_map/mixed_ring/ppermute | solution.py:67
  198.4 21.9 %collective-permute-start.14 = (bf16[512,512]{1,0:T(8,128)(2,1)S(1)}, bf16[512,512]{1,0:T(8,128)(2,1)}, u32[]{:S(2)}, u32[]{:S(2)}) collective-permute-start(bf16[512,512]{1,0:T(8,128)(2,1)S(1)} %collective-permute-done.13.refs_2_), channel_id=1, source_target_pairs={{0,1},{1,2},{2,3},{3,0},{4,5},{5,6},{6,7},{7,4},{8,9},{9,10},{10,1... | collective-permute-start | bytes 1572872 | tf_op jit(solution)/shard_map/mixed_ring/ppermute | solution.py:67
  209.1 46.7 %collective-permute-start.17 = (bf16[512,512]{1,0:T(8,128)(2,1)}, bf16[512,512]{1,0:T(8,128)(2,1)}, u32[]{:S(2)}, u32[]{:S(2)}) collective-permute-start(bf16[512,512]{1,0:T(8,128)(2,1)} %collective-permute-done.16.refs_2_), channel_id=1, source_target_pairs={{0,1},{1,2},{2,3},{3,0},{4,5},{5,6},{6,7},{7,4},{8,9},{9,10},{10,1... | collective-permute-start | bytes 1572872 | tf_op jit(solution)/shard_map/mixed_ring/ppermute | solution.py:67
  255.6 35.4 %collective-permute-start.21 = (bf16[512,512]{1,0:T(8,128)(2,1)}, bf16[512,512]{1,0:T(8,128)(2,1)}, u32[]{:S(2)}, u32[]{:S(2)}) collective-permute-start(bf16[512,512]{1,0:T(8,128)(2,1)} %slice.120), channel_id=1, source_target_pairs={{0,1},{1,2},{2,3},{3,0},{4,5},{5,6},{6,7},{7,4},{8,9},{9,10},{10,1... | collective-permute-start | bytes 1572872 | tf_op jit(solution)/shard_map/mlp/ppermute | solution.py:67
  290.4 16.7 %collective-permute-start.18 = (bf16[512,512]{1,0:T(8,128)(2,1)S(1)}, bf16[512,512]{1,0:T(8,128)(2,1)S(1)}, u32[]{:S(2)}, u32[]{:S(2)}) collective-permute-start(bf16[512,512]{1,0:T(8,128)(2,1)S(1)} %slice.116), channel_id=1, source_target_pairs={{0,1},{1,2},{2,3},{3,0},{4,5},{5,6},{6,7},{7,4},{8,9},{9,10},{10,1... | collective-permute-start | bytes 1572872 | tf_op jit(solution)/shard_map/mlp/ppermute | solution.py:67
  292.6 25.8 %collective-permute-start.22 = (bf16[512,512]{1,0:T(8,128)(2,1)S(1)}, bf16[512,512]{1,0:T(8,128)(2,1)S(1)}, u32[]{:S(2)}, u32[]{:S(2)}) collective-permute-start(bf16[512,512]{1,0:T(8,128)(2,1)S(1)} %add_convert_fusion.4), channel_id=1, source_target_pairs={{0,1},{1,2},{2,3},{3,0},{4,5},{5,6},{6,7},{7,4},{8,9},{9,10},{10,1... | collective-permute-start | bytes 1572872 | tf_op jit(solution)/shard_map/mlp/ppermute | solution.py:67
  307.3 22.3 %collective-permute-start.19 = (bf16[512,512]{1,0:T(8,128)(2,1)S(1)}, bf16[512,512]{1,0:T(8,128)(2,1)S(1)}, u32[]{:S(2)}, u32[]{:S(2)}) collective-permute-start(bf16[512,512]{1,0:T(8,128)(2,1)S(1)} %add_convert_fusion.7), channel_id=1, source_target_pairs={{0,1},{1,2},{2,3},{3,0},{4,5},{5,6},{6,7},{7,4},{8,9},{9,10},{10,1... | collective-permute-start | bytes 1572872 | tf_op jit(solution)/shard_map/mlp/ppermute | solution.py:67
  319.6 23.1 %collective-permute-start.23 = (bf16[512,512]{1,0:T(8,128)(2,1)S(1)}, bf16[512,512]{1,0:T(8,128)(2,1)S(1)}, u32[]{:S(2)}, u32[]{:S(2)}) collective-permute-start(bf16[512,512]{1,0:T(8,128)(2,1)S(1)} %add_convert_fusion.3), channel_id=1, source_target_pairs={{0,1},{1,2},{2,3},{3,0},{4,5},{5,6},{6,7},{7,4},{8,9},{9,10},{10,1... | collective-permute-start | bytes 1572872 | tf_op jit(solution)/shard_map/mlp/ppermute | solution.py:67
  330.6 13.8 %collective-permute-start.20 = (bf16[512,512]{1,0:T(8,128)(2,1)}, bf16[512,512]{1,0:T(8,128)(2,1)}, u32[]{:S(2)}, u32[]{:S(2)}) collective-permute-start(bf16[512,512]{1,0:T(8,128)(2,1)} %add_convert_fusion.6), channel_id=1, source_target_pairs={{0,1},{1,2},{2,3},{3,0},{4,5},{5,6},{6,7},{7,4},{8,9},{9,10},{10,1... | collective-permute-start | bytes 1572872 | tf_op jit(solution)/shard_map/mlp/ppermute | solution.py:67
  349.6 14.3 %collective-permute-start.28 = (bf16[128,512]{1,0:T(8,128)(2,1)S(1)}, bf16[128,512]{1,0:T(8,128)(2,1)S(1)}, u32[]{:S(2)}, u32[]{:S(2)}) collective-permute-start(bf16[128,512]{1,0:T(8,128)(2,1)S(1)} %get-tuple-element.106), channel_id=1, source_target_pairs={{0,2},{1,3},{2,0},{3,1},{4,6},{5,7},{6,4},{7,5},{8,10},{9,11},{10,... | collective-permute-start | bytes 393224 | tf_op jit(solution)/shard_map/hyper_wide/ppermute | solution.py:67
  447.7 19.2 %all-to-all-start.1 = ((bf16[8,64,512]{2,1,0:T(8,128)(2,1)}), bf16[8,64,512]{2,1,0:T(8,128)(2,1)S(1)}, u32[]{:S(2)}, u32[]{:S(2)}) async-start(bf16[8,64,512]{2,1,0:T(8,128)(2,1)} %bitcast.39), calls=%async_computation.2 | async-start | bytes 1048576 | tf_op jit(solution)/shard_map/entry_bwd/all_to_all | solution.py:90
  453.2 122.6 %reduce-scatter.5.cloned.1.call-start = ((), (), s32[]{:S(2)}) async-start(), calls=%async_computation.11 | async-start | bytes 2359296 | tf_op jit(solution)/shard_map/hyper_bwd/reduce_scatter | solution.py:662
  467.0 14.3 %collective-permute-start.24 = (bf16[64,512]{1,0:T(8,128)(2,1)S(1)}, bf16[64,512]{1,0:T(8,128)(2,1)S(1)}, u32[]{:S(2)}, u32[]{:S(2)}) collective-permute-start(bf16[64,512]{1,0:T(8,128)(2,1)S(1)} %reduce_sum.268), channel_id=1, source_target_pairs={{0,1},{1,2},{2,3},{3,0},{4,5},{5,6},{6,7},{7,4},{8,9},{9,10},{10,1... | collective-permute-start | bytes 196616 | tf_op jit(solution)/shard_map/entry_bwd/ppermute | solution.py:67
  481.2 106.7 %all-gather.9.cloned.1.call-start = ((), (), s32[]{:S(2)}) async-start(), calls=%async_computation.10 | async-start | bytes 4718592 | tf_op jit(solution)/shard_map/grads_out/all_gather | solution.py:668
  537.9 12.8 %all-to-all-start.2 = ((bf16[8,16,1664]{2,1,0:T(8,128)(2,1)}), bf16[8,16,1664]{2,1,0:T(8,128)(2,1)S(1)}, u32[]{:S(2)}, u32[]{:S(2)}) async-start(bf16[8,16,1664]{2,1,0:T(8,128)(2,1)} %pad_maximum_fusion.6), calls=%async_computation.3 | async-start | bytes 851968 | tf_op jit(solution)/shard_map/grads_out/all_to_all | solution.py:90
  550.7 24.4 %all-to-all-start.3 = ((bf16[8,16,4608]{2,1,0:T(8,128)(2,1)}), bf16[8,16,4608]{2,1,0:T(8,128)(2,1)S(1)}, u32[]{:S(2)}, u32[]{:S(2)}) async-start(bf16[8,16,4608]{2,1,0:T(8,128)(2,1)} %constant_dynamic-update-slice_fusion.9), calls=%async_computation.4 | async-start | bytes 2359296 | tf_op jit(solution)/shard_map/grads_out/all_to_all | solution.py:90
  (77 other events, 833.0 us)
Sparse Core Ops, SparseCore 0:
  25.3 58.1 all-gather.4
  85.3 113.1 all-gather.6
  346.7 80.6 reduce-scatter.2
  481.3 41.1 reduce-scatter.4
  526.5 45.3 all-gather.8

commit v3 on v2

v3 whole, which is shorter than its diff:
```python
import math
from functools import partial

import jax
import jax.numpy as jnp
from jax import lax
from jax.experimental import pallas as pl
from jax.experimental.pallas import tpu as pltpu
from jax.sharding import PartitionSpec as P

HD = 64
HYPER_WIDTH = 512
EH = 8
EHD = 64
SUBWORD_SLOTS = 8


NEG = -1000000000.0
EPS = 1e-05
THETA = 10000.0
VMEM_LIMIT = 62 * 1024 * 1024


def layer_norm(values, gain):
    center = values - jnp.mean(values, axis=-1, keepdims=True)
    spread = jnp.mean(center * center, axis=-1, keepdims=True)
    return center * lax.rsqrt(spread + EPS) * gain


def rms_norm(values, gain):
    return values * lax.rsqrt(jnp.mean(values * values, axis=-1, keepdims=True) + EPS) * gain


def rope_tables(length, width):
    half_width = width // 2
    inverse = THETA ** (-(2.0 * jnp.arange(half_width, dtype=jnp.float32)) / width)
    angles = jnp.arange(length, dtype=jnp.float32)[:, None] * inverse[None, :]
    return (jnp.cos(angles), jnp.sin(angles))


def rotate(values, cosine, sine):
    half_width = values.shape[-1] // 2
    former = values[..., :half_width]
    latter = values[..., half_width:]
    return jnp.concatenate(
        [former * cosine - latter * sine, latter * cosine + former * sine], axis=-1
    )


def matmul(left, right):
    return jnp.dot(left, right, preferred_element_type=jnp.float32)


def times_trans(left, right):
    return lax.dot_general(
        left, right, (((1,), (1,)), ((), ())), preferred_element_type=jnp.float32
    )


def trans_times(left, right):
    return lax.dot_general(
        left, right, (((0,), (0,)), ((), ())), preferred_element_type=jnp.float32
    )


def ring(values, shift=1):
    size = lax.axis_size("tensor")
    return lax.ppermute(values, "tensor", [(i, (i + shift) % size) for i in range(size)])


def tie(values, *others):
    return lax.optimization_barrier((values, *others))[0]


def tie_all(first, *values):
    return lax.optimization_barrier((*values, first))[:-1]


def in_order(blocks, first):
    size = len(blocks)
    stacked = jnp.stack(blocks)
    return [
        lax.dynamic_index_in_dim(stacked, lax.rem(first - at + size, size), 0, keepdims=False)
        for at in range(size)
    ]


def scatter_dp(values):
    size = lax.axis_size("dp")
    blocks = values.reshape(size, values.shape[0] // size, values.shape[1])
    blocks = lax.all_to_all(blocks, "dp", 0, 0, tiled=True)
    return jnp.sum(blocks.astype(jnp.float32), axis=0)


def from_all(values):
    return [values] + [ring(values, shift) for shift in range(1, lax.axis_size("tensor"))]


def cost(multiplies, values, transcendentals=0):
    return pl.CostEstimate(
        flops=2 * multiplies, bytes_accessed=values, transcendentals=transcendentals
    )


def rope_lanes(length):
    cosine, sine = rope_tables(length, HD)
    return (
        jnp.concatenate([cosine] * 4, axis=1),
        jnp.concatenate([-sine, sine, -sine, sine], axis=1),
    )


def swap(values):
    width = values.shape[1]
    lane = lax.broadcasted_iota(jnp.int32, values.shape, 1)
    ahead = pltpu.roll(values, width - HD // 2, 1)
    behind = pltpu.roll(values, HD // 2, 1)
    return jnp.where(lane % HD < HD // 2, ahead, behind)


def attention_operands(query_ref, pair_ref, cos_ref, sin_ref):
    bfloat = jnp.bfloat16
    cosine = cos_ref[...]
    sine = sin_ref[...]
    queries = query_ref[...]
    pair = pair_ref[...]
    queries = (queries * cosine + swap(queries) * sine).astype(bfloat)
    queries = queries * jnp.asarray(HD ** (-0.5), bfloat)
    keys = (pair * cosine + swap(pair) * sine).astype(bfloat)[:, :HD]
    return queries, keys, pair.astype(bfloat)[:, HD:]


def scores_by_key(keys, query_block, first):
    rows = query_block.shape[0]
    own = times_trans(keys[first : first + rows], query_block)
    key_at = lax.broadcasted_iota(jnp.int32, own.shape, 0)
    query_at = lax.broadcasted_iota(jnp.int32, own.shape, 1)
    parts = [jnp.where(query_at >= key_at, own, NEG)]
    if first > 0:
        parts.insert(0, times_trans(keys[:first], query_block))
    largest = parts[0].max(axis=0, keepdims=True)
    for part in parts[1:]:
        largest = jnp.maximum(largest, part.max(axis=0, keepdims=True))
    parts = [jnp.exp(part - largest) for part in parts]
    total = sum(part.sum(axis=0, keepdims=True) for part in parts)
    return parts, 1.0 / total


def attention_kernel(block_rows, base, query_ref, pair_ref, cos_ref, sin_ref, out_ref):
    queries, keys, values = attention_operands(query_ref, pair_ref, cos_ref, sin_ref)
    for first in range(base, queries.shape[0], block_rows):
        rows = slice(first, first + block_rows)
        heads = []
        for head in range(queries.shape[1] // HD):
            query_block = queries[rows, head * HD : (head + 1) * HD]
            parts, inverse = scores_by_key(keys, query_block, first)
            at = 0
            mixed = None
            for part in parts:
                here = trans_times(
                    values[at : at + part.shape[0]], (part * inverse).astype(jnp.bfloat16)
                )
                mixed = here if mixed is None else mixed + here
                at += part.shape[0]
            heads.append(mixed)
        out_rows = slice(first - base, first - base + block_rows)
        out_ref[out_rows, :] = jnp.concatenate(heads, axis=0).T.astype(jnp.bfloat16)


def attention_back_kernel(
    block_rows, base, query_ref, pair_ref, cos_ref, sin_ref, grad_ref, add_ref, query_out, pair_out, acc_ref
):
    bfloat = jnp.bfloat16
    queries, keys, values = attention_operands(query_ref, pair_ref, cos_ref, sin_ref)

    @pl.when(pl.program_id(0) == 0)
    def _():
        acc_ref[...] = jnp.zeros_like(acc_ref) if add_ref is None else add_ref[...]

    for first in range(base, queries.shape[0], block_rows):
        rows = slice(first, first + block_rows)
        out_rows = slice(first - base, first - base + block_rows)
        heads = []
        for head in range(queries.shape[1] // HD):
            lanes = slice(head * HD, (head + 1) * HD)
            query_block = queries[rows, lanes]
            grad_block = grad_ref[out_rows, lanes]
            parts, inverse = scores_by_key(keys, query_block, first)
            parts = [part * inverse for part in parts]
            at = 0
            prob_grads = []
            delta = 0.0
            for part in parts:
                prob_grad = times_trans(values[at : at + part.shape[0]], grad_block)
                delta = delta + (part * prob_grad).sum(axis=0, keepdims=True)
                prob_grads.append(prob_grad)
                at += part.shape[0]
            at = 0
            query_grad = None
            for part, prob_grad in zip(parts, prob_grads):
                here = slice(at, at + part.shape[0])
                score_grad = (part * (prob_grad - delta)).astype(bfloat)
                key_part = matmul(score_grad, query_block)
                value_part = matmul(part.astype(bfloat), grad_block)
                acc_ref[here, :] += jnp.concatenate([key_part, value_part], axis=1)
                query_part = trans_times(keys[here], score_grad)
                query_grad = query_part if query_grad is None else query_grad + query_part
                at += part.shape[0]
            heads.append(query_grad)
        grad = jnp.concatenate(heads, axis=0).T * HD ** (-0.5)
        grad = grad * cos_ref[rows, :] - swap(grad) * sin_ref[rows, :]
        query_out[out_rows, :] = grad.astype(bfloat)

    @pl.when(pl.program_id(0) == pl.num_programs(0) - 1)
    def _():
        total = acc_ref[...]
        if pair_out.dtype == jnp.float32:
            pair_out[...] = jnp.zeros_like(pair_out)
            pair_out[: total.shape[0], :] = total
            return
        turned = total * cos_ref[...] - swap(total) * sin_ref[...]
        lane = lax.broadcasted_iota(jnp.int32, total.shape, 1)
        pair_out[...] = jnp.where(lane < HD, turned, total).astype(bfloat)


def attention(seq_triple, cosine, sine, query_width, base, rows):
    pairs = query_width // (2 * HD)
    wide = 2 * HD
    keys = base + rows
    return pl.pallas_call(
        partial(attention_kernel, min(256, rows), base),
        grid=(pairs,),
        in_specs=[
            pl.BlockSpec((keys, wide), lambda at: (0, at)),
            pl.BlockSpec((keys, wide), lambda at: (0, pairs)),
            pl.BlockSpec((keys, wide), lambda at: (0, 0)),
            pl.BlockSpec((keys, wide), lambda at: (0, 0)),
        ],
        out_specs=pl.BlockSpec((rows, wide), lambda at: (0, at)),
        out_shape=jax.ShapeDtypeStruct((rows, query_width), jnp.bfloat16),
        cost_estimate=cost(
            8 * query_width * rows * keys, 6 * query_width * keys, query_width * keys * 10
        ),
        compiler_params=pltpu.CompilerParams(vmem_limit_bytes=VMEM_LIMIT),
        name="attention",
    )(seq_triple, seq_triple, cosine, sine)


def attention_back(seq_triple, cosine, sine, mixed_grad, base, before):
    length = seq_triple.shape[0]
    rows, query_width = mixed_grad.shape
    pairs = query_width // (2 * HD)
    wide = 2 * HD
    keys = base + rows
    last = keys == length
    specs = [
        pl.BlockSpec((keys, wide), lambda at: (0, at)),
        pl.BlockSpec((keys, wide), lambda at: (0, pairs)),
        pl.BlockSpec((keys, wide), lambda at: (0, 0)),
        pl.BlockSpec((keys, wide), lambda at: (0, 0)),
        pl.BlockSpec((rows, wide), lambda at: (0, at)),
    ]
    operands = [seq_triple, seq_triple, cosine, sine, mixed_grad]
    if before is not None:
        specs.append(pl.BlockSpec((keys, wide), lambda at: (0, 0)))
        operands.append(before)

    def kernel(*refs):
        given = refs[: len(operands)]
        add_ref = None if before is None else given[-1]
        attention_back_kernel(
            min(256, rows), base, *given[:5], add_ref, *refs[len(operands) :]
        )

    return pl.pallas_call(
        kernel,
        grid=(pairs,),
        in_specs=specs,
        out_specs=[
            pl.BlockSpec((rows, wide), lambda at: (0, at)),
            pl.BlockSpec((length, wide), lambda at: (0, 0)),
        ],
        out_shape=[
            jax.ShapeDtypeStruct((rows, query_width), jnp.bfloat16),
            jax.ShapeDtypeStruct((length, wide), jnp.bfloat16 if last else jnp.float32),
        ],
        cost_estimate=cost(
            20 * query_width * rows * keys, 8 * query_width * length, query_width * keys * 10
        ),
        scratch_shapes=[pltpu.VMEM((keys, wide), jnp.float32)],
        compiler_params=pltpu.CompilerParams(vmem_limit_bytes=VMEM_LIMIT),
        name="attention_back",
    )(*operands)


def unit_scale(values):
    spread = lax.rsqrt(jnp.mean(values * values, axis=1, keepdims=True) + EPS)
    return values * spread, spread


def one_hot(places, first, shape, axis):
    at = lax.broadcasted_iota(jnp.int32, shape, axis) + first
    return jnp.where(places == at, 1.0, 0.0).astype(jnp.bfloat16)


def entry_kernel(
    tokens_ref, pooled_ref, project_ref, gain_ref, triple_w_ref, vectors_ref, seq_ref
):
    bfloat = jnp.bfloat16
    step = pl.program_id(0)
    vectors = matmul(pooled_ref[...], project_ref[...]).astype(bfloat)
    vectors_ref[...] = vectors
    normed, _ = unit_scale(vectors.astype(jnp.float32))
    triple = matmul((normed * gain_ref[...]).astype(bfloat), triple_w_ref[...])
    high = triple.astype(bfloat)
    rest = (triple - high.astype(jnp.float32)).astype(bfloat)
    count = vectors.shape[0]
    hot = one_hot(tokens_ref[...], step * count, (seq_ref.shape[0], count), 1)
    picked = matmul(hot, high) + matmul(hot, rest)

    @pl.when(step == 0)
    def _():
        seq_ref[...] = picked

    @pl.when(step > 0)
    def _():
        seq_ref[...] += picked


def entry(tokens, pooled, project, gain, weights, triple_width):
    total, inner = pooled.shape
    length = tokens.shape[0]
    width = project.shape[1]
    block = min(512, total)

    def whole(shape):
        return pl.BlockSpec(shape, lambda at: (0, 0), pipeline_mode=pl.Buffered(1))

    return pl.pallas_call(
        entry_kernel,
        grid=(total // block,),
        in_specs=[
            whole((length, 1)),
            pl.BlockSpec((block, inner), lambda at: (at, 0)),
            whole(project.shape),
            whole((1, width)),
            whole((width, triple_width)),
        ],
        out_specs=[
            pl.BlockSpec((block, width), lambda at: (at, 0)),
            pl.BlockSpec((length, triple_width), lambda at: (0, 0)),
        ],
        out_shape=[
            jax.ShapeDtypeStruct((total, width), jnp.bfloat16),
            jax.ShapeDtypeStruct((length, triple_width), jnp.float32),
        ],
        cost_estimate=cost(
            total * width * (inner + triple_width) + 2 * length * total * triple_width,
            4 * width * (inner + triple_width),
        ),
        compiler_params=pltpu.CompilerParams(vmem_limit_bytes=VMEM_LIMIT),
        name="entry",
    )(tokens[:, None], pooled, project, gain[None, :], weights)


def entry_back_kernel(
    tokens_ref,
    vectors_ref,
    gain_ref,
    triple_w_ref,
    mid_ref,
    project_ref,
    pair_ref,
    *refs,
):
    bfloat = jnp.bfloat16
    query_refs = refs[:-2]
    entry_ref, pooled_ref = refs[-2:]
    count = vectors_ref.shape[0]
    length = tokens_ref.shape[1]
    hot = one_hot(tokens_ref[...], pl.program_id(0) * count, (count, length), 0)
    at = 0
    query_out = None
    for ref in query_refs:
        here = matmul(hot[:, at : at + ref.shape[0]], ref[...])
        query_out = here if query_out is None else query_out + here
        at += ref.shape[0]
    pair_out = matmul(hot, pair_ref[...])
    query_width = query_out.shape[1]
    grad = times_trans(query_out.astype(bfloat), triple_w_ref[:, :query_width])
    grad = grad + times_trans(pair_out.astype(bfloat), triple_w_ref[:, query_width:])
    grad = grad * gain_ref[...]
    normed, spread = unit_scale(vectors_ref[...].astype(jnp.float32))
    grad = spread * (grad - normed * jnp.mean(grad * normed, axis=1, keepdims=True))
    entry_grad = (grad + mid_ref[...]).astype(bfloat)
    entry_ref[...] = entry_grad
    pooled_ref[...] = times_trans(entry_grad, project_ref[...]).astype(bfloat)


def entry_back(tokens, vectors, gain, weights, mid_entries, project, pair_out, query_parts):
    total, width = vectors.shape
    length = tokens.shape[0]
    block = min(256, total)
    triple_width = query_parts[0].shape[1] + pair_out.shape[1]
    inner = project.shape[0]

    def whole(shape):
        return pl.BlockSpec(shape, lambda at: (0, 0), pipeline_mode=pl.Buffered(1))

    def rows_of(columns):
        return pl.BlockSpec((block, columns), lambda at: (at, 0))

    return pl.pallas_call(
        entry_back_kernel,
        grid=(total // block,),
        in_specs=[
            whole((1, length)),
            rows_of(width),
            whole((1, width)),
            whole((width, triple_width)),
            rows_of(width),
            whole(project.shape),
            whole(pair_out.shape),
        ]
        + [whole(part.shape) for part in query_parts],
        out_specs=[rows_of(width), rows_of(inner)],
        out_shape=[
            jax.ShapeDtypeStruct((total, width), jnp.bfloat16),
            jax.ShapeDtypeStruct((total, inner), jnp.bfloat16),
        ],
        cost_estimate=cost(
            total * (length * triple_width + width * (inner + triple_width)),
            4 * width * (inner + triple_width) + 8 * total * width,
        ),
        compiler_params=pltpu.CompilerParams(vmem_limit_bytes=VMEM_LIMIT),
        name="entry_back",
    )(tokens[None, :], vectors, gain[None, :], weights, mid_entries, project, pair_out, *query_parts)


def mlp_kernel(
    query_width,
    unit_width,
    positions,
    places_ref,
    resid_in_ref,
    swiglu_grad_ref,
    cot_ref,
    own_weight_ref,
    gain_ref,
    output_from,
    units_from,
    *refs,
):
    bfloat = jnp.bfloat16
    mixed_refs = refs[:positions]
    resid_ref, swiglu_ref, mid_ref, part_ref, output_ref, units_ref, arrived = refs[positions:]
    gate_columns = pl.ds(0, unit_width)
    upward_columns = pl.ds(unit_width, unit_width)
    copies = [
        pltpu.make_async_copy(output_from, output_ref, arrived.at[0]),
        pltpu.make_async_copy(
            units_from.at[:, gate_columns], units_ref.at[:, gate_columns], arrived.at[1]
        ),
        pltpu.make_async_copy(
            units_from.at[:, upward_columns], units_ref.at[:, upward_columns], arrived.at[2]
        ),
    ]

    def on_first(act):
        pl.when(pl.program_id(0) == 0)(act)

    @on_first
    def _():
        for copy in copies:
            copy.start()
        copies[0].wait()

    resid = resid_in_ref[...].astype(jnp.float32)
    for at, mixed_ref in enumerate(mixed_refs):
        columns = slice(at * query_width, (at + 1) * query_width)
        resid = resid + times_trans(mixed_ref[...], output_ref[:, columns])
    resid_ref[...] = resid
    gain = gain_ref[...]
    spread = lax.rsqrt(jnp.mean(resid * resid, axis=1, keepdims=True) + EPS)
    normed = resid * spread
    seq_two = (normed * gain).astype(bfloat)
    on_first(copies[1].wait)
    gate = matmul(seq_two, units_ref[:, gate_columns])
    on_first(copies[2].wait)
    upward = matmul(seq_two, units_ref[:, upward_columns])
    open_gate = jax.nn.sigmoid(gate)
    silu = gate * open_gate
    swiglu_ref[...] = (silu * upward).astype(bfloat)
    swiglu_grad = swiglu_grad_ref[...]
    slope = open_gate * (1.0 + gate * (1.0 - open_gate))
    gate_grad = (swiglu_grad * upward * slope).astype(bfloat)
    upward_grad = (swiglu_grad * silu).astype(bfloat)
    grad = times_trans(gate_grad, units_ref[:, gate_columns])
    grad = grad + times_trans(upward_grad, units_ref[:, upward_columns])
    grad = grad * gain
    grad = spread * (grad - normed * jnp.mean(grad * normed, axis=1, keepdims=True))
    grad = grad + own_weight_ref[...] * cot_ref[...].astype(jnp.float32)
    mid_low = grad.astype(bfloat)
    mid_ref[...] = mid_low
    for at in range(positions):
        columns = slice(at * query_width, (at + 1) * query_width)
        part_ref[places_ref[at]] = matmul(mid_low, output_ref[:, columns]).astype(bfloat)


def mlp(
    places, resid_in, swiglu_grad, cot, own_weight, gain, output_w, units_w, mixed, rows_at, row_total
):
    width = resid_in.shape[1]
    unit_width = swiglu_grad.shape[1]
    query_width = mixed[0].shape[1]
    block = min(256, row_total)
    offset = rows_at // block

    def rows_of(columns, shift):
        return pl.BlockSpec((block, columns), lambda at: (at + shift, 0))

    return pl.pallas_call(
        partial(mlp_kernel, query_width, unit_width, len(mixed)),
        grid=(row_total // block,),
        in_specs=[
            pl.BlockSpec(memory_space=pltpu.SMEM),
            rows_of(width, offset),
            rows_of(unit_width, offset),
            rows_of(width, offset),
            rows_of(1, offset),
            pl.BlockSpec((1, width), lambda at: (0, 0)),
            pl.BlockSpec(memory_space=pl.ANY),
            pl.BlockSpec(memory_space=pl.ANY),
        ]
        + [rows_of(query_width, 0)] * len(mixed),
        out_specs=[
            rows_of(width, 0),
            rows_of(unit_width, 0),
            rows_of(width, 0),
            pl.BlockSpec((len(mixed), block, query_width), lambda at: (0, at, 0)),
        ],
        out_shape=[
            jax.ShapeDtypeStruct((row_total, width), jnp.float32),
            jax.ShapeDtypeStruct((row_total, unit_width), jnp.bfloat16),
            jax.ShapeDtypeStruct((row_total, width), jnp.bfloat16),
            jax.ShapeDtypeStruct((len(mixed), row_total, query_width), jnp.bfloat16),
        ],
        cost_estimate=cost(
            2 * row_total * (output_w.size + units_w.size),
            2 * (output_w.size + units_w.size) + 16 * row_total * width,
        ),
        scratch_shapes=[
            pltpu.VMEM(output_w.shape, output_w.dtype),
            pltpu.VMEM(units_w.shape, units_w.dtype),
            pltpu.SemaphoreType.DMA((3,)),
        ],
        compiler_params=pltpu.CompilerParams(vmem_limit_bytes=VMEM_LIMIT),
        name="mlp",
    )(places, resid_in, swiglu_grad, cot, own_weight, gain[None, :], output_w, units_w, *mixed)


def centred(values):
    center = values - jnp.mean(values, axis=1, keepdims=True)
    spread = lax.rsqrt(jnp.mean(center * center, axis=1, keepdims=True) + EPS)
    return center * spread, spread


def centred_back(grad, normed, spread):
    return spread * (
        grad
        - jnp.mean(grad, axis=1, keepdims=True)
        - normed * jnp.mean(grad * normed, axis=1, keepdims=True)
    )


def slot_probs(triple_ref, rows, head, shut):
    wide = HYPER_WIDTH
    at = head * EHD
    queries = triple_ref[rows, at : at + EHD]
    keys = triple_ref[rows, wide + at : wide + at + EHD]
    values = triple_ref[rows, 2 * wide + at : 2 * wide + at + EHD]
    scores = jnp.where(shut, NEG, times_trans(keys, queries) * EHD ** (-0.5))
    parts = jnp.exp(scores - scores.max(axis=0, keepdims=True))
    return queries, keys, values, parts * (1.0 / parts.sum(axis=0, keepdims=True))


def slot_shut(open_ref, rows, count):
    key_entry = lax.broadcasted_iota(jnp.int32, (count, count), 0) // SUBWORD_SLOTS
    query_entry = lax.broadcasted_iota(jnp.int32, (count, count), 1) // SUBWORD_SLOTS
    return (key_entry != query_entry) | (open_ref[rows, :] == 0.0)


def hyper_wide_kernel(
    rows_ref,
    open_ref,
    gains_ref,
    triple_w_ref,
    merge_w_ref,
    expand_w_ref,
    reduce_w_ref,
    length_ref,
    first_ref,
    triple_ref,
    mixed_ref,
    resid_ref,
    second_ref,
    active_ref,
    slope_ref,
    pooled_ref,
):
    bfloat = jnp.bfloat16
    rows_in = rows_ref[...].astype(jnp.float32)
    first_in = (centred(rows_in)[0] * gains_ref[0:1, :]).astype(bfloat)
    first_ref[...] = first_in
    triple_ref[...] = matmul(first_in, triple_w_ref[...]).astype(bfloat)
    total = rows_in.shape[0]
    count = min(128, total)
    for first in range(0, total, count):
        rows = slice(first, first + count)
        shut = slot_shut(open_ref, rows, count)
        heads = []
        for head in range(EH):
            _, _, values, probs = slot_probs(triple_ref, rows, head, shut)
            heads.append(trans_times(values, probs.astype(bfloat)))
        mixed_ref[rows, :] = jnp.concatenate(heads, axis=0).T.astype(bfloat)
    resid_one = rows_in + matmul(mixed_ref[...], merge_w_ref[...])
    resid_ref[...] = resid_one
    second_in = (centred(resid_one)[0] * gains_ref[1:2, :]).astype(bfloat)
    second_ref[...] = second_in
    expanded = matmul(second_in, expand_w_ref[...])
    below = 0.5 * (1.0 + lax.erf(expanded * 0.5**0.5))
    active = (expanded * below).astype(bfloat)
    active_ref[...] = active
    resid_two = resid_one + matmul(active, reduce_w_ref[...])
    kept = jnp.where(open_ref[...] == 0.0, 0.0, resid_two)
    pooled = kept.reshape(total // SUBWORD_SLOTS, SUBWORD_SLOTS, kept.shape[1]).sum(axis=1)
    pooled_ref[...] = (pooled / length_ref[...]).astype(bfloat)
    bell = jnp.exp(-0.5 * expanded * expanded) * (2.0 * math.pi) ** (-0.5)
    slope_ref[...] = below + expanded * bell


def hyper_wide(rows_in, open_rows, gains, triple_w, merge_w, expand_w, reduce_w, lengths):
    total, width = rows_in.shape
    block = min(256, total)
    units = expand_w.shape[1]
    bfloat = jnp.bfloat16
    single = jnp.float32

    def rows_of(columns):
        return pl.BlockSpec((block, columns), lambda at: (at, 0))

    def whole(array):
        return pl.BlockSpec(array.shape, lambda at: (0, 0), pipeline_mode=pl.Buffered(1))

    outs = [
        (width, bfloat),
        (3 * width, bfloat),
        (width, bfloat),
        (width, single),
        (width, bfloat),
        (units, bfloat),
        (units, single),
    ]
    return pl.pallas_call(
        hyper_wide_kernel,
        grid=(total // block,),
        in_specs=[rows_of(width), rows_of(1)]
        + [whole(array) for array in (gains, triple_w, merge_w, expand_w, reduce_w)]
        + [pl.BlockSpec((block // SUBWORD_SLOTS, 1), lambda at: (at, 0))],
        out_specs=[rows_of(columns) for columns, _ in outs]
        + [pl.BlockSpec((block // SUBWORD_SLOTS, width), lambda at: (at, 0))],
        out_shape=[jax.ShapeDtypeStruct((total, columns), kind) for columns, kind in outs]
        + [jax.ShapeDtypeStruct((total // SUBWORD_SLOTS, width), bfloat)],
        cost_estimate=cost(16 * total * width * units, 12 * total * units),
        compiler_params=pltpu.CompilerParams(vmem_limit_bytes=VMEM_LIMIT),
        name="hyper_wide",
    )(rows_in, open_rows, gains, triple_w, merge_w, expand_w, reduce_w, lengths)


def hyper_back_units_kernel(
    dp_size,
    pooled_refs,
    scale_ref,
    gains_ref,
    resid_ref,
    slope_ref,
    mixed_share_ref,
    second_share_ref,
    active_share_ref,
    merge_w_ref,
    expand_w_ref,
    reduce_w_ref,
    resid_out,
    mixed_out,
    early_out,
    gains_out,
    reduce_acc,
    expand_acc,
    merge_acc,
):
    bfloat = jnp.bfloat16
    step = pl.program_id(0)
    total, width = resid_ref.shape
    pooled_grad = sum(ref[...].astype(jnp.float32) for ref in pooled_refs)
    grid_grad = jnp.broadcast_to(
        pooled_grad[:, None, :], (total // SUBWORD_SLOTS, SUBWORD_SLOTS, width)
    ).reshape(total, width)
    grid_grad = grid_grad * scale_ref[...]
    reduce_in = grid_grad.astype(bfloat)
    expand_in = times_trans(reduce_in, reduce_w_ref[...]) * slope_ref[...]
    expand_in = expand_in.astype(bfloat)
    second_grad = times_trans(expand_in, expand_w_ref[...])
    normed, spread = centred(resid_ref[...])
    gain_two = (second_grad * normed).sum(axis=0, keepdims=True)
    resid_grad = grid_grad + centred_back(second_grad * gains_ref[1:2, :], normed, spread)
    resid_out[...] = resid_grad
    merge_in = resid_grad.astype(bfloat)
    mixed_out[...] = times_trans(merge_in, merge_w_ref[...]).astype(bfloat)

    @pl.when(step == 0)
    def _():
        for ref in (reduce_acc, expand_acc, merge_acc, gains_out):
            ref[...] = jnp.zeros_like(ref)

    gains_out[0:1, :] += gain_two
    reduce_acc[...] += trans_times(active_share_ref[...], reduce_in)
    expand_acc[...] += trans_times(second_share_ref[...], expand_in)
    merge_acc[...] += trans_times(mixed_share_ref[...], merge_in)

    @pl.when(step == pl.num_programs(0) - 1)
    def _():
        depth = expand_acc.shape[0] // dp_size
        deep = reduce_acc.shape[0] // expand_acc.shape[0]
        reduced = reduce_acc[...].astype(bfloat).reshape(dp_size, deep, depth, width)
        for at in range(deep):
            early_out[:, at * width : (at + 1) * width] = reduced[:, at].reshape(
                dp_size * depth, width
            )
        units = expand_acc.shape[1]
        early_out[:, deep * width : deep * width + units] = expand_acc[...].astype(bfloat)
        early_out[:, deep * width + units :] = merge_acc[...].astype(bfloat)


def hyper_back_slots_kernel(
    resid_grad_ref,
    mixed_grad_ref,
    rows_ref,
    open_ref,
    gains_ref,
    triple_ref,
    first_share_ref,
    triple_w_ref,
    rows_out,
    late_out,
    gains_out,
    triple_acc,
    triple_in,
):
    bfloat = jnp.bfloat16
    step = pl.program_id(0)
    total, width = rows_ref.shape
    count = min(128, total)
    for first in range(0, total, count):
        rows = slice(first, first + count)
        shut = slot_shut(open_ref, rows, count)
        query_grads = []
        for head in range(EH):
            queries, keys, values, probs = slot_probs(triple_ref, rows, head, shut)
            at = head * EHD
            grad = mixed_grad_ref[rows, at : at + EHD]
            prob_grad = times_trans(values, grad)
            delta = (probs * prob_grad).sum(axis=0, keepdims=True)
            score_grad = (probs * (prob_grad - delta)).astype(bfloat)
            query_grads.append(trans_times(keys, score_grad))
            key_grad = matmul(score_grad, queries) * EHD ** (-0.5)
            value_grad = matmul(probs.astype(bfloat), grad)
            triple_in[rows, width + at : width + at + EHD] = key_grad.astype(bfloat)
            triple_in[rows, 2 * width + at : 2 * width + at + EHD] = value_grad.astype(bfloat)
        query_grad = jnp.concatenate(query_grads, axis=0).T * EHD ** (-0.5)
        triple_in[rows, :width] = query_grad.astype(bfloat)
    triple_grad = triple_in[...]
    first_grad = times_trans(triple_grad, triple_w_ref[...])
    normed, spread = centred(rows_ref[...].astype(jnp.float32))
    gain_one = (first_grad * normed).sum(axis=0, keepdims=True)
    rows_grad = resid_grad_ref[...] + centred_back(first_grad * gains_ref[0:1, :], normed, spread)
    rows_out[...] = rows_grad.astype(bfloat)

    @pl.when(step == 0)
    def _():
        triple_acc[...] = jnp.zeros_like(triple_acc)
        gains_out[...] = jnp.zeros_like(gains_out)

    gains_out[0:1, :] += gain_one
    triple_acc[...] += trans_times(first_share_ref[...], triple_grad)

    @pl.when(step == pl.num_programs(0) - 1)
    def _():
        late_out[...] = triple_acc[...].astype(bfloat)


def row_block(columns, rows):
    return pl.BlockSpec((rows, columns), lambda at: (at, 0))


def whole_block(shape):
    return pl.BlockSpec(shape, lambda at: (0, 0), pipeline_mode=pl.Buffered(1))


def hyper_back_units(dp_size, pooled, scale, gains, resid, slope, shares, weights):
    total, width = resid.shape
    block = min(256, total)
    units = slope.shape[1]
    share_width = shares[0].shape[1]
    deep = shares[2].shape[1] // share_width
    bfloat = jnp.bfloat16
    single = jnp.float32

    def kernel(*refs):
        hyper_back_units_kernel(dp_size, refs[: len(pooled)], *refs[len(pooled) :])

    early_width = deep * width + units + width
    return pl.pallas_call(
        kernel,
        grid=(total // block,),
        in_specs=[row_block(width, block // SUBWORD_SLOTS)] * len(pooled)
        + [row_block(1, block), whole_block(gains.shape)]
        + [row_block(width, block), row_block(units, block)]
        + [row_block(array.shape[1], block) for array in shares]
        + [whole_block(array.shape) for array in weights],
        out_specs=[
            row_block(width, block),
            row_block(width, block),
            pl.BlockSpec((share_width, early_width), lambda at: (0, 0)),
            pl.BlockSpec((8, width), lambda at: (0, 0)),
        ],
        out_shape=[
            jax.ShapeDtypeStruct((total, width), single),
            jax.ShapeDtypeStruct((total, width), bfloat),
            jax.ShapeDtypeStruct((share_width, early_width), bfloat),
            jax.ShapeDtypeStruct((8, width), single),
        ],
        scratch_shapes=[
            pltpu.VMEM((deep * share_width, width), single),
            pltpu.VMEM((share_width, units), single),
            pltpu.VMEM((share_width, width), single),
        ],
        cost_estimate=cost(12 * total * width * units, 6 * total * units),
        compiler_params=pltpu.CompilerParams(vmem_limit_bytes=VMEM_LIMIT),
        name="hyper_back_units",
    )(*pooled, scale, gains, resid, slope, *shares, *weights)


def hyper_back_slots(resid_grad, mixed_grad, rows_in, open_rows, gains, triple, first_share, weight):
    total, width = rows_in.shape
    block = min(256, total)
    share_width = first_share.shape[1]
    bfloat = jnp.bfloat16
    single = jnp.float32
    return pl.pallas_call(
        hyper_back_slots_kernel,
        grid=(total // block,),
        in_specs=[row_block(width, block)] * 3
        + [row_block(1, block), whole_block(gains.shape), row_block(3 * width, block)]
        + [row_block(share_width, block), whole_block(weight.shape)],
        out_specs=[
            row_block(width, block),
            pl.BlockSpec((share_width, 3 * width), lambda at: (0, 0)),
            pl.BlockSpec((8, width), lambda at: (0, 0)),
        ],
        out_shape=[
            jax.ShapeDtypeStruct((total, width), bfloat),
            jax.ShapeDtypeStruct((share_width, 3 * width), bfloat),
            jax.ShapeDtypeStruct((8, width), single),
        ],
        scratch_shapes=[
            pltpu.VMEM((share_width, 3 * width), single),
            pltpu.VMEM((block, 3 * width), bfloat),
        ],
        cost_estimate=cost(40 * total * width * width, 8 * total * width),
        compiler_params=pltpu.CompilerParams(vmem_limit_bytes=VMEM_LIMIT),
        name="hyper_back_slots",
    )(resid_grad, mixed_grad, rows_in, open_rows, gains, triple, first_share, weight)


def per_device(
    subword_embedding_rows,
    entry_subword_index,
    entry_lengths,
    entry_counts,
    encoder_triple,
    encoder_merge,
    encoder_expand,
    encoder_reduce,
    embed_project,
    normone_gain,
    normtwo_gain,
    frozen_query,
    frozen_key,
    frozen_value,
    frozen_output,
    frozen_gate,
    frozen_upward,
    frozen_downward,
    prenorm_gain,
    midnorm_gain,
    text_tokens,
    cotangent,
):
    bfloat = jnp.bfloat16
    single = jnp.float32
    dp_size = lax.axis_size("dp")
    tensor_size = lax.axis_size("tensor")
    dp_at = lax.axis_index("dp")
    tensor_at = lax.axis_index("tensor")
    device_at = dp_at * tensor_size + tensor_at
    entries = entry_subword_index.shape[0]
    entry_total = entries * dp_size * tensor_size
    flat_rows = entries * SUBWORD_SLOTS
    table_rows = subword_embedding_rows.shape[0]
    model_width = embed_project.shape[1]

    with jax.named_scope("ids"):
        packed = jnp.concatenate(
            [entry_subword_index, entry_counts[:, None], entry_lengths[:, None]], axis=1
        )
        packed_width = packed.shape[1]
        first_weights = jnp.concatenate(
            [frozen_query, frozen_key, frozen_value, frozen_downward], axis=1
        )
        packed_dp = lax.all_gather(tie(packed, first_weights), "dp", axis=0, tiled=False)
    with jax.named_scope("first_weights"):
        first_weights = lax.all_gather(first_weights, "dp", axis=0, tiled=True)
        query_width = frozen_query.shape[1]
        key_width = frozen_key.shape[1]
        triple_width = query_width + 2 * key_width
        full_triple = first_weights[:, :triple_width]
        full_downward = first_weights[:, triple_width:]
    with jax.named_scope("lookup"):
        local_ids = packed_dp[:, :, :SUBWORD_SLOTS].reshape(-1) - dp_at * table_rows
        inside = (local_ids >= 0) & (local_ids < table_rows)
        served = jnp.take(subword_embedding_rows, jnp.clip(local_ids, 0, table_rows - 1), axis=0)
        served = jnp.where(inside[:, None], served, jnp.zeros((), bfloat))
        served_all = lax.all_to_all(
            served.reshape(dp_size, flat_rows, HYPER_WIDTH), "dp", 0, 0, tiled=True
        )
        rows_in = jnp.sum(served_all.astype(single), axis=0)
    with jax.named_scope("cot_ring"):
        cot_blocks = [cotangent, ring(cotangent)]
        length = text_tokens.shape[0] * tensor_size
        cosine, sine = rope_lanes(length)
        rows_in = lax.optimization_barrier((rows_in, cot_blocks[-1], cosine, sine))
        rows_in, _, cosine, sine = rows_in
        cot_blocks.append(ring(cot_blocks[-1]))
        packed_all = from_all(
            tie(jnp.concatenate([packed_dp.reshape(-1), text_tokens]), cot_blocks[1])
        )
    with jax.named_scope("hyper_wide"):
        rows_blocks = from_all(rows_in.astype(bfloat))
    with jax.named_scope("second_weights"):
        second_weights = jnp.concatenate([frozen_gate, frozen_upward], axis=1)
        second_weights = lax.all_gather(
            tie(second_weights, served), "dp", axis=0, tiled=True
        )
    with jax.named_scope("hyper_wide"):
        rows_wide = jnp.concatenate(in_order(rows_blocks, tensor_at), axis=0)
        rows_wide, cot_blocks[2] = lax.optimization_barrier((rows_wide, cot_blocks[2]))
        packed_all = jnp.stack(in_order(packed_all, tensor_at))
        ids_size = dp_size * entries * packed_width
        packed_ids = packed_all[:, :ids_size].reshape(tensor_size, dp_size, entries, packed_width)
        lengths_wide = lax.dynamic_index_in_dim(packed_ids, dp_at, 1, keepdims=False)
        lengths_wide = lengths_wide[:, :, SUBWORD_SLOTS + 1].reshape(-1)
        valid_wide = jnp.arange(SUBWORD_SLOTS)[None, :] < lengths_wide[:, None]
        valid_wide = valid_wide.astype(single)
        counts_wide = lengths_wide.astype(single)[:, None]
        open_wide = valid_wide.reshape(-1, 1)
        scale_wide = (valid_wide / counts_wide).reshape(-1, 1)
        gain_pair = jnp.stack([normone_gain, normtwo_gain])
        encoders = (encoder_triple, encoder_merge, encoder_expand, encoder_reduce)
        first_in, triple, mixed, resid_one, second_in, activated, slope, dp_pooled = hyper_wide(
            rows_wide, open_wide, gain_pair, *encoders, counts_wide
        )
    with jax.named_scope("cot_ring"):
        cot_blocks.append(ring(cot_blocks[-1]))
        dp_pooled = tie(dp_pooled, cot_blocks[-1])
    with jax.named_scope("output_weights"):
        output_blocks = from_all(tie(frozen_output, dp_pooled))
    with jax.named_scope("pooled_gather"):
        all_pooled = lax.all_gather(dp_pooled, "dp", axis=0, tiled=True)
    with jax.named_scope("entry_vectors"):
        seq_tokens = packed_all[:, ids_size:].reshape(-1)
        all_vectors, seq_triple = entry(
            seq_tokens, all_pooled, embed_project, prenorm_gain, first_weights, triple_width
        )
    with jax.named_scope("output_weights"):
        output_weights = jnp.concatenate(tie(output_blocks, seq_triple), axis=1)
        output_weights = lax.all_gather(
            tie(output_weights, first_weights), "dp", axis=0, tiled=True
        )

    with jax.named_scope("attention_fwd"):
        block_rows = min(512, length)
        block_total = length // block_rows
        mixed_parts = []
        for first in range(0, length, block_rows):
            lm_mixed = attention(seq_triple, cosine, sine, query_width, first, block_rows)
            mixed_parts.append([lm_mixed])
            seq_triple = tie(seq_triple, lm_mixed)
    with jax.named_scope("mixed_ring"):
        late_ids, late_tokens, late_cot = tie_all(lm_mixed, packed_ids, seq_tokens, cot_blocks)
        for parts in mixed_parts:
            for _ in range(tensor_size - 1):
                parts.append(ring(parts[-1]))
    with jax.named_scope("swiglu_grad"):
        vectors = lax.dynamic_slice_in_dim(all_vectors, device_at * entries, entries, 0)
        late_ids = late_ids.transpose(1, 0, 2, 3).reshape(entry_total, packed_width)
        all_ids = late_ids[:, :SUBWORD_SLOTS].reshape(-1)
        all_weights = (1.0 / jnp.log(1.0 + late_ids[:, SUBWORD_SLOTS].astype(single))).astype(
            bfloat
        )
        rows_here = text_tokens.shape[0]
        seq_hot = (late_tokens[:, None] == jnp.arange(entry_total)[None, :]).astype(bfloat)
        seq_weight = matmul(seq_hot, all_weights[:, None])
        seq_cot = jnp.concatenate(in_order(late_cot, tensor_at), axis=0)
        resid_in = matmul(seq_hot, all_vectors).astype(bfloat)
        swiglu_grad = matmul((seq_weight * seq_cot.astype(single)).astype(bfloat), full_downward)
        own_rows_here = jnp.arange(length) // rows_here == tensor_at
        own_weight = jnp.where(own_rows_here[:, None], seq_weight, 0.0)

    def share(values):
        rows, width = values.shape
        split = values.reshape(rows, dp_size, tensor_size, width // (dp_size * tensor_size))
        return lax.dynamic_index_in_dim(split, tensor_at, 2, keepdims=False).reshape(
            rows, width // tensor_size
        )

    shares = [share(array) for array in tie((first_in, mixed, second_in, activated), lm_mixed)]

    with jax.named_scope("mlp"):
        places = lax.rem(tensor_at + tensor_size - jnp.arange(tensor_size), tensor_size)
        resid_blocks = []
        swiglu_blocks = []
        mid_blocks = []
        mixed_grads = []
        for block_idx, parts in enumerate(mixed_parts):
            last = block_idx == block_total - 1
            if block_idx == 0:
                mixed_parts = lax.optimization_barrier(mixed_parts)
                parts = mixed_parts[0]
            else:
                parts = mixed_parts[block_idx]
            if block_idx > 0:
                parts = tie(parts, mixed_part)
            resid_mid, swiglu_low, mid_low, mixed_part = mlp(
                jnp.arange(tensor_size) if last else places,
                resid_in,
                swiglu_grad,
                seq_cot,
                own_weight,
                midnorm_gain,
                output_weights,
                second_weights,
                parts,
                block_idx * block_rows,
                block_rows,
            )
            resid_blocks.append(resid_mid)
            swiglu_blocks.append(swiglu_low)
            mid_blocks.append(mid_low)
            if not last:
                mixed_grads.append(
                    lax.psum_scatter(
                        mixed_part.reshape(-1, query_width),
                        "tensor",
                        scatter_dimension=0,
                        tiled=True,
                    )
                )
                continue
            carried = None
            for step in [*range(1, tensor_size), 0]:
                part = mixed_part[step]
                if carried is not None:
                    part = (part.astype(single) + carried.astype(single)).astype(bfloat)
                if step == 2:
                    mid_entries = trans_times(seq_hot, jnp.concatenate(mid_blocks, axis=0))
                    part, mid_entries = lax.optimization_barrier((part, mid_entries))
                if step == 3:
                    layer_part = times_trans(jnp.concatenate(swiglu_blocks, axis=0), full_downward)
                    part, layer_part = lax.optimization_barrier((part, layer_part.astype(bfloat)))
                if step == 0:
                    pair_out = None
                    query_parts = []
                    for at, mixed_grad in enumerate(mixed_grads):
                        query_part, pair_out = attention_back(
                            seq_triple, cosine, sine, mixed_grad, at * block_rows, pair_out
                        )
                        query_parts.append(query_part)
                    part, pair_out = lax.optimization_barrier((part, pair_out))
                if step > 0:
                    carried = ring(part)
            last_grad = part

    with jax.named_scope("layer_out"):
        layer_part = tie(layer_part, last_grad)
        blocks_of = [
            lax.dynamic_slice_in_dim(
                block, lax.rem(tensor_at * rows_here, block_rows), rows_here, 0
            )
            for block in resid_blocks
        ]
        resid_own = blocks_of[0]
        for block_idx in range(1, block_total):
            resid_own = jnp.where(
                tensor_at * rows_here // block_rows == block_idx, blocks_of[block_idx], resid_own
            )
        layer_final = resid_own + lax.psum_scatter(
            layer_part, "tensor", scatter_dimension=0, tiled=True
        ).astype(single)
    with jax.named_scope("attention_bwd"):
        query_part, pair_out = attention_back(
            seq_triple, cosine, sine, last_grad, length - block_rows, pair_out
        )
        query_parts.append(query_part)

    with jax.named_scope("entry_bwd"):
        entry_part, pooled_part = entry_back(
            seq_tokens,
            all_vectors,
            prenorm_gain,
            first_weights,
            mid_entries,
            embed_project,
            pair_out,
            query_parts,
        )
        pooled_part = scatter_dp(pooled_part).astype(bfloat)
        pooled_grads = from_all(pooled_part)
        project_part = trans_times(all_pooled, entry_part).astype(bfloat)
        project_part = tie(project_part, pooled_part)

    with jax.named_scope("hyper_bwd"):
        project_grad = scatter_dp(project_part).astype(bfloat)
        resid_grad, mixed_grad, early, gain_two = hyper_back_units(
            dp_size,
            pooled_grads,
            scale_wide,
            gain_pair,
            resid_one,
            slope,
            shares[1:],
            encoders[1:],
        )
        resid_grad, early, project_grad = lax.optimization_barrier(
            (resid_grad, early, project_grad)
        )
        early = scatter_dp(early)
        rows_low, late, gain_one = hyper_back_slots(
            resid_grad,
            mixed_grad,
            rows_wide,
            open_wide,
            gain_pair,
            triple,
            shares[0],
            encoder_triple,
        )

    with jax.named_scope("grads_out"):
        rows_low, early = lax.optimization_barrier((rows_low, early))
        all_rows = lax.all_gather(rows_low, "dp", axis=0, tiled=True)
        late, project_grad = tie_all(rows_low, late, project_grad)
        project_grad = project_grad.reshape(tensor_size, -1, model_width)
        project_grad = lax.all_to_all(project_grad, "tensor", 0, 0, tiled=True)
        project_grad = jnp.sum(project_grad.astype(single), axis=0)
        own_rows = table_rows // tensor_size
        row_hot = (
            (jnp.arange(own_rows) + device_at * own_rows)[:, None] == all_ids[None, :]
        ).astype(bfloat)
        subword_grad = matmul(row_hot, all_rows)

        gain_grads = share(jnp.concatenate([gain_one[:1], gain_two[:1]], axis=0)).transpose(1, 0).astype(bfloat)
        late = jnp.concatenate([late, jnp.pad(gain_grads, ((0, 0), (0, 126)))], axis=1)
        late = scatter_dp(late)
        depth = early.shape[0]
        deep = encoder_reduce.shape[0] // HYPER_WIDTH
        reduce_width = deep * HYPER_WIDTH
        expand_width = encoder_expand.shape[1]
        reduce_grad = early[:, :reduce_width].reshape(depth, deep, HYPER_WIDTH)
        reduce_grad = reduce_grad.transpose(1, 0, 2).reshape(deep * depth, HYPER_WIDTH)
        expand_grad = early[:, reduce_width : reduce_width + expand_width]
        merge_grad = early[:, reduce_width + expand_width :]
        grad_width = encoder_triple.shape[1]
    return (
        layer_final.astype(bfloat),
        vectors,
        subword_grad,
        late[:, :grad_width],
        merge_grad,
        expand_grad,
        reduce_grad,
        project_grad,
        late[:, grad_width],
        late[:, grad_width + 1],
    )


def solution(mesh):
    return jax.shard_map(
        per_device,
        mesh=mesh,
        in_specs=(
            P("dp", None),
            P(("dp", "tensor"), None),
            P(("dp", "tensor")),
            P(("dp", "tensor")),
            P(),
            P(),
            P(),
            P(),
            P(),
            P(),
            P(),
            P("dp", "tensor"),
            P("dp", "tensor"),
            P("dp", "tensor"),
            P("dp", "tensor"),
            P("dp", "tensor"),
            P("dp", "tensor"),
            P("dp", "tensor"),
            P(),
            P(),
            P(("dp", "tensor")),
            P(("dp", "tensor"), None),
        ),
        out_specs=(
            P(("dp", "tensor"), None),
            P(("dp", "tensor"), None),
            P(("dp", "tensor"), None),
            P(("dp", "tensor"), None),
            P(("dp", "tensor"), None),
            P(("dp", "tensor"), None),
            P(("dp", "tensor"), None),
            P(("dp", "tensor"), None),
            P(("dp", "tensor")),
            P(("dp", "tensor")),
        ),
        check_vma=False,
    )
```

time: 608 us -> 537 us (0.88)
  matrix products: 124 us -> 47.4 us
  Pallas kernels: 116 us -> 181 us
  local copies, waits for them, and re-layouts: 92.6 us -> 34.5 us
  waiting for transfers between devices: 134 us -> 146 us
  other arithmetic: 35.1 us -> 27.9 us
  starting transfers between devices: 62.8 us -> 56.2 us
    pallas_call x2 -> x9, Pallas kernels: 49.2 us -> 116 us  [the longest x2 34.4 us: attention_back(): pl.pallas_call(kernel, grid=(pairs,), in_specs=specs, out_specs=[pl.Block...]
    dot_general x14 -> x4, matrix products: 58.2 us -> 24.6 us  [matmul(): return jnp.dot(left, right, preferred_element_type=jnp.float32)]
    reshape x14 -> x1, local copies, waits for them, and re-layouts: 28.2 us -> 0.17 us  [per_device(): late_ids = late_ids.transpose(1, 0, 2, 3).reshape(entry_total, packed_width)]
    dot_general x7 -> x1, matrix products: 31.7 us -> 11.7 us  [times_trans(): lax.dot_general(left, right, (((1,), (1,)), ((), ())), preferred_element_...]
    unnamed x153 -> x56, local copies, waits for them, and re-layouts: 21.7 us -> 3.67 us
    ppermute x30 -> x24, starting transfers between devices: 41.3 us -> 27.7 us  [ring(): lax.ppermute(values, 'tensor', [(i, (i + shift) % size) for i in range(si...]
    dot_general x7 -> x0, matrix products: 13.4 us -> none  [the longest x1 3.28 us: backward(): jnp.einsum('bhqk,bhqd->bhkd', probs_low, mixed_grad, preferred_element_ty...]
    all_to_all x1, waiting for transfers between devices: 8.06 us -> 15.1 us  [per_device(): lax.all_to_all(served.reshape(dp_size, flat_rows, HYPER_WIDTH), 'dp', 0,...]
  transfers between devices with their start and end apart: 40 -> 36, of which waited for: 20 -> 20; matrix products, arithmetic and copies ran while one was open for 37% -> 18% of each run, Pallas kernels for 19% -> 26%
where the time goes in v3:
time: 537 us; the launch traced here: 530 us
  Pallas kernels  181 us (34%)
  waiting for transfers between devices  146 us (27%)
  starting transfers between devices  56.2 us (10%)
  matrix products  47.4 us (9%)
  local copies, waits for them, and re-layouts  34.5 us (6%)
  other arithmetic  27.9 us (5%)
  blocking collectives  22.4 us (4%)
  between operations  15.2 us (3%)
    ppermute x24, waiting for transfers between devices, ring(): lax.ppermute(values, 'tensor', [(i, (i + shift) % size) for i in range(si...  106 us
    pallas_call x2, Pallas kernels, mlp(): pl.pallas_call(partial(mlp_kernel, query_width, unit_width, len(mixed)),...  64.7 us
    pallas_call x2, Pallas kernels, attention_back(): pl.pallas_call(kernel, grid=(pairs,), in_specs=specs, out_specs=[pl.Block...  34.4 us
    ppermute x24, starting transfers between devices, ring(): lax.ppermute(values, 'tensor', [(i, (i + shift) % size) for i in range(si...  27.7 us
    dot_general x4, matrix products, matmul(): return jnp.dot(left, right, preferred_element_type=jnp.float32)  24.6 us
    pallas_call x2, Pallas kernels, attention(): pl.pallas_call(partial(attention_kernel, min(256, rows), base), grid=(pai...  22.1 us
    all_to_all x4, waiting for transfers between devices, scatter_dp(): blocks = lax.all_to_all(blocks, 'dp', 0, 0, tiled=True)  17.7 us
    pallas_call x1, Pallas kernels, hyper_wide(): pl.pallas_call(hyper_wide_kernel, grid=(total // block,), in_specs=[rows_...  17.5 us
  transfers between devices with their start and end apart: 36, of which 20 were waited for; matrix products, arithmetic and copies ran while one was open for 18% of the time, Pallas kernels for 26%

profile of v3, /device:TPU:0, one launch (start us, length us, event | category | flops | bytes accessed | tf_op | source)
XLA Modules:
  0.0 529.9 jit_solution(8667201733006858954)
XLA Ops:
  18.2 9.2 %all-gather = s32[128,10]{1,0:T(8,128)S(1)} all-gather(s32[16,10]{1,0:T(8,128)S(1)} %pad_add_fusion.2), channel_id=2, replica_groups=mesh['dp'=8,'tensor'=4] {'dp'}, dimensions={0}, use_global_device_ids=true | all-gather | bytes 5760 | tf_op jit(solution)/shard_map/ids/all_gather | solution.py:930
  27.8 6.7 %gather_fusion = bf16[1024,512]{1,0:T(8,128)(2,1)S(1)} fusion(bf16[4000,512]{1,0:T(8,128)(2,1)} %param.22, s32[1024]{0:T(1024)S(1)} %broadcast_clamp_fusion), kind=kCustom, calls=%fused_computation | custom fusion | bytes 2101248 | tf_op jit(solution)/shard_map/lookup/jit(_take)/gather | solution.py:941
  48.7 15.1 %all-to-all-done = bf16[8,128,512]{2,1,0:T(8,128)(2,1)S(1)} async-done(((bf16[8,128,512]{2,1,0:T(8,128)(2,1)}), bf16[8,128,512]{2,1,0:T(8,128)(2,1)S(1)}, u32[]{:S(2)}, u32[]{:S(2)}) %all-to-all-start) | async-done | bytes 1048608 | tf_op jit(solution)/shard_map/lookup/all_to_all | solution.py:943
  78.4 18.3 %collective-permute-done.7 = bf16[256,2048]{1,0:T(8,128)(2,1)} collective-permute-done((bf16[256,2048]{1,0:T(8,128)(2,1)}, bf16[256,2048]{1,0:T(8,128)(2,1)}, u32[]{:S(2)}, u32[]{:S(2)}) %collective-permute-start.7) | collective-permute-done | bytes 1048608 | tf_op jit(solution)/shard_map/cot_ring/ppermute | solution.py:68
  99.4 17.5 %hyper_wide.1 = (bf16[512,512]{1,0:T(8,128)(2,1)}, bf16[512,1536]{1,0:T(8,128)(2,1)}, bf16[512,512]{1,0:T(8,128)(2,1)}, f32[512,512]{1,0:T(8,128)}, bf16[512,512...) custom-call(bf16[512,512]{1,0:T(8,128)(2,1)} %pad_maximum_fusion.7.rows_ref, ...), custom_call_target="tpu_custom_call" | custom-call | flops 17179869184 | bytes 12582912 | tf_op jit(solution)/shard_map/hyper_wide/hyper_wide/pallas_call | solution.py:664
  117.0 6.0 %collective-permute-done.8 = bf16[256,2048]{1,0:T(8,128)(2,1)} collective-permute-done((bf16[256,2048]{1,0:T(8,128)(2,1)}, bf16[256,2048]{1,0:T(8,128)(2,1)}, u32[]{:S(2)}, u32[]{:S(2)}) %collective-permute-start.8) | collective-permute-done | bytes 1048608 | tf_op jit(solution)/shard_map/cot_ring/ppermute | solution.py:68
  128.6 13.1 %all_gather.23.pooled_ref = bf16[512,512]{1,0:T(8,128)(2,1)} all-gather(bf16[64,512]{1,0:T(8,128)(2,1)} %get-tuple-element.100), channel_id=1, replica_groups=mesh['dp'=8,'tensor'=4] {'dp'}, dimensions={0}, use_global_device_ids=true | all-gather | bytes 589824 | tf_op jit(solution)/shard_map/pooled_gather/all_gather | solution.py:988
  141.7 9.1 %entry.1 = (bf16[512,2048]{1,0:T(8,128)(2,1)}, f32[1024,640]{1,0:T(8,128)}) custom-call(s32[1024,1]{1,0:T(8,128)} %bitcast.107, bf16[512,512]{1,0:T(8,128)(2,1)} %all_gather.23.pooled_ref, bf16[512,2048]{1,0:T(8,128)(2,1)} %project_ref.3, f32[1,2048]{1,0:T(1,128)} %bitcast.124, bf16[2048,2048]{1,0:T(8,128)(2,1)} %all-gather.6.cloned.1.call-done.triple_w_ref), custom_call_target="tpu_custom_call" | custom-call | flops 3758096384 | bytes 9437184 | tf_op jit(solution)/shard_map/entry_vectors/entry/pallas_call | solution.py:339
  153.6 8.9 %attention.2.refs_0_ = bf16[512,512]{1,0:T(8,128)(2,1)} custom-call(f32[1024,640]{1,0:T(8,128)} %get-tuple-element.141.query_ref.pair_ref.refs_0_.refs_1_, f32[1024,640]{1,0:T(8,128)} %get-tuple-element.141.query_ref.pair_ref.refs_0_.refs_1_, f32[1024,128]{1,0:T(8,128)} %get-tuple-element.102.cos_ref.refs_2_, f32[1024,128]{1,0:T(8,128)} %get-tuple-element.103.sin_ref.refs_3_), custom_call_target="tpu_custom_call" | custom-call | flops 2147483648 | bytes 1572864 | tf_op jit(solution)/shard_map/attention_fwd/attention/pallas_call | solution.py:230
  162.9 13.3 %attention.3.refs_0_ = bf16[512,512]{1,0:T(8,128)(2,1)} custom-call(f32[1024,640]{1,0:T(8,128)} %get-tuple-element.141.query_ref.pair_ref.refs_0_.refs_1_, f32[1024,640]{1,0:T(8,128)} %get-tuple-element.141.query_ref.pair_ref.refs_0_.refs_1_, f32[1024,128]{1,0:T(8,128)} %get-tuple-element.102.cos_ref.refs_2_, f32[1024,128]{1,0:T(8,128)} %get-tuple-element.103.sin_ref.refs_3_), custom_call_target="tpu_custom_call" | custom-call | flops 4294967296 | bytes 3145728 | tf_op jit(solution)/shard_map/attention_fwd/attention/pallas_call | solution.py:230
  181.8 10.8 %collective-permute-done.15.refs_1_ = bf16[512,512]{1,0:T(8,128)(2,1)} collective-permute-done((bf16[512,512]{1,0:T(8,128)(2,1)}, bf16[512,512]{1,0:T(8,128)(2,1)}, u32[]{:S(2)}, u32[]{:S(2)}) %collective-permute-start.15) | collective-permute-done | bytes 524320 | tf_op jit(solution)/shard_map/mixed_ring/ppermute | solution.py:68
  193.2 11.8 %fusion.6.swiglu_grad_ref = f32[1024,1408]{1,0:T(8,128)} fusion(bf16[2048,2048]{1,0:T(8,128)(2,1)S(1)} %bitcast.94, f32[1024]{0:T(1024)S(1)} %bitcast.129, bf16[256,2048]{1,0:T(8,128)(2,1)S(1)} %get-tuple-element.181, bf16[256,2048]{1,0:T(8,128)(2,1)S(1)} %get-tuple-element.182, bf16[256,2048]{1,0:T(8,128)(2,1)S(1)} %get-tuple-element.183, ...), kind=kOutput, calls=%fused_computation.8 | convolution fusion | flops 5926551552 | bytes 15732736 | tf_op jit(solution)/shard_map/swiglu_grad/dot_general | solution.py:51
  209.4 11.3 %collective-permute-done.13.refs_2_ = bf16[512,512]{1,0:T(8,128)(2,1)} collective-permute-done((bf16[512,512]{1,0:T(8,128)(2,1)}, bf16[512,512]{1,0:T(8,128)(2,1)}, u32[]{:S(2)}, u32[]{:S(2)}) %collective-permute-start.13) | collective-permute-done | bytes 524320 | tf_op jit(solution)/shard_map/mixed_ring/ppermute | solution.py:68
  226.4 5.6 %collective-permute-done.17.refs_3_ = bf16[512,512]{1,0:T(8,128)(2,1)S(1)} collective-permute-done((bf16[512,512]{1,0:T(8,128)(2,1)S(1)}, bf16[512,512]{1,0:T(8,128)(2,1)S(1)}, u32[]{:S(2)}, u32[]{:S(2)}) %collective-permute-start.17) | collective-permute-done | bytes 524320 | tf_op jit(solution)/shard_map/mixed_ring/ppermute | solution.py:68
  231.9 10.0 %collective-permute-done.14.refs_3_ = bf16[512,512]{1,0:T(8,128)(2,1)} collective-permute-done((bf16[512,512]{1,0:T(8,128)(2,1)}, bf16[512,512]{1,0:T(8,128)(2,1)}, u32[]{:S(2)}, u32[]{:S(2)}) %collective-permute-start.14) | collective-permute-done | bytes 524320 | tf_op jit(solution)/shard_map/mixed_ring/ppermute | solution.py:68
  241.9 32.2 %mlp.2 = (f32[512,2048]{1,0:T(8,128)}, bf16[512,1408]{1,0:T(8,128)(2,1)}, bf16[512,2048]{1,0:T(8,128)(2,1)}, bf16[4,512,512]{2,1,0:T(8,128)(2,1)}) custom-call(s32[4]{0:T(128)} %compare_select_fusion.2.places_ref, bf16[1024,2048]{1,0:T(8,128)(2,1)} %convolution_convert_fusion.resid_in_ref, f32[1024,1408]{1,0:T(8,128)} %fusion.6.swiglu_grad_ref, ...), custom_call_target="tpu_custom_call" | custom-call | flops 20401094656 | bytes 36700160 | tf_op jit(solution)/shard_map/mlp/mlp/pallas_call | solution.py:522
  275.1 32.5 %mlp.3 = (f32[512,2048]{1,0:T(8,128)}, bf16[512,1408]{1,0:T(8,128)(2,1)}, bf16[512,2048]{1,0:T(8,128)(2,1)}, bf16[4,512,512]{2,1,0:T(8,128)(2,1)}) custom-call(s32[4]{0:T(128)} %iota.46.places_ref, bf16[1024,2048]{1,0:T(8,128)(2,1)} %convolution_convert_fusion.resid_in_ref, f32[1024,1408]{1,0:T(8,128)} %fusion.6.swiglu_grad_ref, ...), custom_call_target="tpu_custom_call" | custom-call | flops 20401094656 | bytes 36700160 | tf_op jit(solution)/shard_map/mlp/mlp/pallas_call | solution.py:522
  308.8 6.9 %fusion.8.mid_ref = f32[512,2048]{1,0:T(8,128)} fusion(bf16[512,2048]{1,0:T(8,128)(2,1)} %get-tuple-element.135, bf16[512,2048]{1,0:T(8,128)(2,1)} %get-tuple-element.134, s32[1024]{0:T(1024)S(1)} %bitcast.128), kind=kOutput, calls=%fused_computation.12 | convolution fusion | flops 2156396544 | bytes 8392704 | tf_op jit(solution)/shard_map/mlp/dot_general | solution.py:61
  315.7 11.1 %collective-permute-done.18 = bf16[512,512]{1,0:T(8,128)(2,1)S(1)} collective-permute-done((bf16[512,512]{1,0:T(8,128)(2,1)S(1)}, bf16[512,512]{1,0:T(8,128)(2,1)S(1)}, u32[]{:S(2)}, u32[]{:S(2)}) %collective-permute-start.18) | collective-permute-done | bytes 524320 | tf_op jit(solution)/shard_map/mlp/ppermute | solution.py:68
  327.0 11.7 %fusion.13 = bf16[1024,2048]{1,0:T(8,128)(2,1)} fusion(bf16[2048,2048]{1,0:T(8,128)(2,1)} %all-gather.6.cloned.1.call-done.triple_w_ref, bf16[512,1408]{1,0:T(8,128)(2,1)S(1)} %copy-done.22, bf16[512,1408]{1,0:T(8,128)(2,1)S(1)} %copy-done.21), kind=kOutput, calls=%fused_computation.18 | convolution fusion | flops 5913444352 | bytes 12845056 | tf_op jit(solution)/shard_map/mlp/dot_general | solution.py:55
  342.3 14.1 %collective-permute-done.20 = bf16[512,512]{1,0:T(8,128)(2,1)S(1)} collective-permute-done((bf16[512,512]{1,0:T(8,128)(2,1)S(1)}, bf16[512,512]{1,0:T(8,128)(2,1)S(1)}, u32[]{:S(2)}, u32[]{:S(2)}) %collective-permute-start.20) | collective-permute-done | bytes 524320 | tf_op jit(solution)/shard_map/mlp/ppermute | solution.py:68
  357.3 12.7 %attention_back.2 = (bf16[512,512]{1,0:T(8,128)(2,1)}, f32[1024,128]{1,0:T(8,128)}) custom-call(f32[1024,640]{1,0:T(8,128)} %get-tuple-element.141.query_ref.pair_ref.refs_0_.refs_1_, f32[1024,640]{1,0:T(8,128)} %get-tuple-element.141.query_ref.pair_ref.refs_0_.refs_1_, f32[1024,128]{1,0:T(8,128)} %get-tuple-element.102.cos_ref.refs_2_, ...), custom_call_target="tpu_custom_call" | custom-call | flops 5368709120 | bytes 4194304 | tf_op jit(solution)/shard_map/mlp/attention_back/pallas_call | solution.py:275
  370.1 21.7 %attention_back.3 = (bf16[512,512]{1,0:T(8,128)(2,1)}, bf16[1024,128]{1,0:T(8,128)(2,1)}) custom-call(f32[1024,640]{1,0:T(8,128)} %get-tuple-element.141.query_ref.pair_ref.refs_0_.refs_1_, f32[1024,640]{1,0:T(8,128)} %get-tuple-element.141.query_ref.pair_ref.refs_0_.refs_1_, f32[1024,128]{1,0:T(8,128)} %get-tuple-element.102.cos_ref.refs_2_, ...), custom_call_target="tpu_custom_call" | custom-call | flops 10737418240 | bytes 4194304 | tf_op jit(solution)/shard_map/attention_bwd/attention_back/pallas_call | solution.py:275
  391.8 9.6 %entry_back.1 = (bf16[512,2048]{1,0:T(8,128)(2,1)}, bf16[512,512]{1,0:T(8,128)(2,1)}) custom-call(s32[1,1024]{1,0:T(1,128)} %bitcast.120, bf16[512,2048]{1,0:T(8,128)(2,1)} %get-tuple-element.106.vectors_ref, f32[1,2048]{1,0:T(1,128)} %bitcast.125, bf16[2048,2048]{1,0:T(8,128)(2,1)} %all-gather.6.cloned.1.call-done.triple_w_ref, f32[512,2048]{1,0:T(8,128)} %fusion.8.mid_ref, ...), custom_call_target="tpu_custom_call" | custom-call | flops 3087007744 | bytes 17825792 | tf_op jit(solution)/shard_map/entry_bwd/entry_back/pallas_call | solution.py:413
  409.3 5.5 %all-to-all-done.1 = bf16[8,64,512]{2,1,0:T(8,128)(2,1)S(1)} async-done(((bf16[8,64,512]{2,1,0:T(8,128)(2,1)}), bf16[8,64,512]{2,1,0:T(8,128)(2,1)S(1)}, u32[]{:S(2)}, u32[]{:S(2)}) %all-to-all-start.1) | async-done | bytes 524320 | tf_op jit(solution)/shard_map/entry_bwd/all_to_all | solution.py:91
  414.9 4.6 all-to-all-start.2
  428.8 7.7 %collective-permute-done.23.refs_3_ = bf16[64,512]{1,0:T(8,128)(2,1)S(1)} collective-permute-done((bf16[64,512]{1,0:T(8,128)(2,1)S(1)}, bf16[64,512]{1,0:T(8,128)(2,1)S(1)}, u32[]{:S(2)}, u32[]{:S(2)}) %collective-permute-start.23) | collective-permute-done | bytes 65568 | tf_op jit(solution)/shard_map/entry_bwd/ppermute | solution.py:68
  439.2 9.6 %hyper_back_units.1 = (f32[512,512]{1,0:T(8,128)}, bf16[512,512]{1,0:T(8,128)(2,1)}, bf16[128,4608]{1,0:T(8,128)(2,1)}, f32[8,512]{1,0:T(8,128)}) custom-call(bf16[64,512]{1,0:T(8,128)(2,1)} %copy-done.8, bf16[64,512]{1,0:T(8,128)(2,1)} %copy-done.20, bf16[64,512]{1,0:T(8,128)(2,1)} %copy-done.19, bf16[64,512]{1,0:T(8,128)(2,1)} %copy-done.18, ...), custom_call_target="tpu_custom_call" | custom-call | flops 12884901888 | bytes 6291456 | tf_op jit(solution)/shard_map/hyper_bwd/hyper_back_units/pallas_call | solution.py:822
  456.4 13.5 %hyper_back_slots.1 = (bf16[512,512]{1,0:T(8,128)(2,1)}, bf16[128,1536]{1,0:T(8,128)(2,1)}, f32[8,512]{1,0:T(8,128)}) custom-call(f32[512,512]{1,0:T(8,128)} %get-tuple-element.164.resid_grad_ref, bf16[512,512]{1,0:T(8,128)(2,1)} %get-tuple-element.165.mixed_grad_ref, bf16[512,512]{1,0:T(8,128)(2,1)} %pad_maximum_fusion.7.rows_ref, ...), custom_call_target="tpu_custom_call" | custom-call | flops 10737418240 | bytes 2097152 | tf_op jit(solution)/shard_map/hyper_bwd/hyper_back_slots/pallas_call | solution.py:859
  481.3 9.7 %all-to-all-done.4 = bf16[8,16,1664]{2,1,0:T(8,128)(2,1)S(1)} async-done(((bf16[8,16,1664]{2,1,0:T(8,128)(2,1)}), bf16[8,16,1664]{2,1,0:T(8,128)(2,1)S(1)}, u32[]{:S(2)}, u32[]{:S(2)}) %all-to-all-start.4) | async-done | bytes 426016 | tf_op jit(solution)/shard_map/grads_out/all_to_all | solution.py:91
  491.0 8.7 %all-to-all-start.5 = ((bf16[4,16,2048]{2,1,0:T(8,128)(2,1)}), bf16[4,16,2048]{2,1,0:T(8,128)(2,1)S(1)}, u32[]{:S(2)}, u32[]{:S(2)}) async-start(bf16[4,16,2048]{2,1,0:T(8,128)(2,1)} %bitcast.50), calls=%async_computation.7 | async-start | bytes 524288 | tf_op jit(solution)/shard_map/grads_out/all_to_all | solution.py:1173
  514.8 7.9 %fusion = f32[1000,512]{1,0:T(8,128)} fusion(bf16[4096,512]{1,0:T(8,128)(2,1)} %all-gather.12.cloned.1.call-done, s32[4096]{0:T(1024)S(1)} %eq.44, s32[1000]{0:T(1024)S(1)} %iota_add_fusion), kind=kOutput, calls=%fused_computation.1 | convolution fusion | flops 4198400000 | bytes 6262688 | tf_op jit(solution)/shard_map/grads_out/dot_general | solution.py:51
  (221 shorter events, 128.3 us)
Async XLA Ops:
  7.2 134.5 %all-gather.6.cloned.1.call-start = ((), (), s32[]{:S(2)}) async-start(), calls=%async_computation.8 | async-start | bytes 9437184 | tf_op jit(solution)/shard_map/first_weights/all_gather | solution.py:932
  12.2 229.7 %all-gather.10.cloned.1.call-start = ((), (), s32[]{:S(2)}) async-start(), calls=%async_computation.10 | async-start | bytes 12976128 | tf_op jit(solution)/shard_map/second_weights/all_gather | solution.py:961
  14.8 29.3 %collective-permute-start = (bf16[256,2048]{1,0:T(8,128)(2,1)S(1)}, bf16[256,2048]{1,0:T(8,128)(2,1)}, u32[]{:S(2)}, u32[]{:S(2)}) collective-permute-start(bf16[256,2048]{1,0:T(8,128)(2,1)S(1)} %copy-done.2), channel_id=1, source_target_pairs={{0,1},{1,2},{2,3},{3,0},{4,5},{5,6},{6,7},{7,4},{8,9},{9,10},{10,1... | collective-permute-start | bytes 3145736 | tf_op jit(solution)/shard_map/cot_ring/ppermute | solution.py:68
  35.8 28.0 %all-to-all-start = ((bf16[8,128,512]{2,1,0:T(8,128)(2,1)}), bf16[8,128,512]{2,1,0:T(8,128)(2,1)S(1)}, u32[]{:S(2)}, u32[]{:S(2)}) async-start(bf16[8,128,512]{2,1,0:T(8,128)(2,1)} %select_select_fusion), calls=%async_computation | async-start | bytes 2097152 | tf_op jit(solution)/shard_map/lookup/all_to_all | solution.py:943
  39.4 202.5 %all-gather.8.cloned.1.call-start = ((), (), s32[]{:S(2)}) async-start(), calls=%async_computation.9 | async-start | bytes 9437184 | tf_op jit(solution)/shard_map/output_weights/all_gather | solution.py:996
  44.1 22.7 %collective-permute-start.3 = (s32[1536]{0:T(1024)S(1)}, s32[1536]{0:T(1024)S(1)}, u32[]{:S(2)}, u32[]{:S(2)}) collective-permute-start(s32[1536]{0:T(1024)S(1)} %pad_add_fusion.3), channel_id=1, source_target_pairs={{0,3},{1,0},{2,1},{3,2},{4,7},{5,4},{6,5},{7,6},{8,11},{9,8},{10,9... | collective-permute-start | bytes 18440 | tf_op jit(solution)/shard_map/cot_ring/ppermute | solution.py:68
  46.3 24.3 %collective-permute-start.2 = (s32[1536]{0:T(1024)S(1)}, s32[1536]{0:T(1024)S(1)}, u32[]{:S(2)}, u32[]{:S(2)}) collective-permute-start(s32[1536]{0:T(1024)S(1)} %pad_add_fusion.3), channel_id=1, source_target_pairs={{0,2},{1,3},{2,0},{3,1},{4,6},{5,7},{6,4},{7,5},{8,10},{9,11},{10,... | collective-permute-start | bytes 18440 | tf_op jit(solution)/shard_map/cot_ring/ppermute | solution.py:68
  47.1 23.6 %collective-permute-start.1 = (s32[1536]{0:T(1024)S(1)}, s32[1536]{0:T(1024)S(1)}, u32[]{:S(2)}, u32[]{:S(2)}) collective-permute-start(s32[1536]{0:T(1024)S(1)} %pad_add_fusion.3), channel_id=1, source_target_pairs={{0,1},{1,2},{2,3},{3,0},{4,5},{5,6},{6,7},{7,4},{8,9},{9,10},{10,1... | collective-permute-start | bytes 18440 | tf_op jit(solution)/shard_map/cot_ring/ppermute | solution.py:68
  64.0 13.0 %collective-permute-start.5 = (bf16[128,512]{1,0:T(8,128)(2,1)S(1)}, bf16[128,512]{1,0:T(8,128)(2,1)S(1)}, u32[]{:S(2)}, u32[]{:S(2)}) collective-permute-start(bf16[128,512]{1,0:T(8,128)(2,1)S(1)} %convert_reduce_fusion.1), channel_id=1, source_target_pairs={{0,2},{1,3},{2,0},{3,1},{4,6},{5,7},{6,4},{7,5},{8,10},{9,11},{10,... | collective-permute-start | bytes 393224 | tf_op jit(solution)/shard_map/hyper_wide/ppermute | solution.py:68
  70.7 26.1 %collective-permute-start.7 = (bf16[256,2048]{1,0:T(8,128)(2,1)}, bf16[256,2048]{1,0:T(8,128)(2,1)}, u32[]{:S(2)}, u32[]{:S(2)}) collective-permute-start(bf16[256,2048]{1,0:T(8,128)(2,1)} %collective-permute-done), channel_id=1, source_target_pairs={{0,1},{1,2},{2,3},{3,0},{4,5},{5,6},{6,7},{7,4},{8,9},{9,10},{10,1... | collective-permute-start | bytes 3145736 | tf_op jit(solution)/shard_map/cot_ring/ppermute | solution.py:68
  96.8 26.2 %collective-permute-start.8 = (bf16[256,2048]{1,0:T(8,128)(2,1)}, bf16[256,2048]{1,0:T(8,128)(2,1)}, u32[]{:S(2)}, u32[]{:S(2)}) collective-permute-start(bf16[256,2048]{1,0:T(8,128)(2,1)} %collective-permute-done.7), channel_id=1, source_target_pairs={{0,1},{1,2},{2,3},{3,0},{4,5},{5,6},{6,7},{7,4},{8,9},{9,10},{10,1... | collective-permute-start | bytes 3145736 | tf_op jit(solution)/shard_map/cot_ring/ppermute | solution.py:68
  123.0 27.8 %collective-permute-start.11 = (bf16[256,512]{1,0:T(8,128)(2,1)S(1)}, bf16[256,512]{1,0:T(8,128)(2,1)S(1)}, u32[]{:S(2)}, u32[]{:S(2)}) collective-permute-start(bf16[256,512]{1,0:T(8,128)(2,1)S(1)} %copy-done.7), channel_id=1, source_target_pairs={{0,3},{1,0},{2,1},{3,2},{4,7},{5,4},{6,5},{7,6},{8,11},{9,8},{10,9... | collective-permute-start | bytes 786440 | tf_op jit(solution)/shard_map/output_weights/ppermute | solution.py:68
  123.0 27.8 %collective-permute-start.10 = (bf16[256,512]{1,0:T(8,128)(2,1)S(1)}, bf16[256,512]{1,0:T(8,128)(2,1)}, u32[]{:S(2)}, u32[]{:S(2)}) collective-permute-start(bf16[256,512]{1,0:T(8,128)(2,1)S(1)} %copy-done.7), channel_id=1, source_target_pairs={{0,2},{1,3},{2,0},{3,1},{4,6},{5,7},{6,4},{7,5},{8,10},{9,11},{10,... | collective-permute-start | bytes 786440 | tf_op jit(solution)/shard_map/output_weights/ppermute | solution.py:68
  126.5 24.3 %collective-permute-start.9 = (bf16[256,512]{1,0:T(8,128)(2,1)S(1)}, bf16[256,512]{1,0:T(8,128)(2,1)}, u32[]{:S(2)}, u32[]{:S(2)}) collective-permute-start(bf16[256,512]{1,0:T(8,128)(2,1)S(1)} %copy-done.7), channel_id=1, source_target_pairs={{0,1},{1,2},{2,3},{3,0},{4,5},{5,6},{6,7},{7,4},{8,9},{9,10},{10,1... | collective-permute-start | bytes 786440 | tf_op jit(solution)/shard_map/output_weights/ppermute | solution.py:68
  153.0 204.4 %reduce-scatter.3.cloned.1.call-start = ((), (), s32[]{:S(2)}) async-start(), calls=%async_computation.11 | async-start | bytes 2621440 | tf_op jit(solution)/shard_map/mlp/reduce_scatter | solution.py:1071
  162.4 30.2 %collective-permute-start.12 = (bf16[512,512]{1,0:T(8,128)(2,1)}, bf16[512,512]{1,0:T(8,128)(2,1)}, u32[]{:S(2)}, u32[]{:S(2)}) collective-permute-start(bf16[512,512]{1,0:T(8,128)(2,1)} %attention.2.refs_0_), channel_id=1, source_target_pairs={{0,1},{1,2},{2,3},{3,0},{4,5},{5,6},{6,7},{7,4},{8,9},{9,10},{10,1... | collective-permute-start | bytes 1572872 | tf_op jit(solution)/shard_map/mixed_ring/ppermute | solution.py:68
  176.2 16.4 %collective-permute-start.15 = (bf16[512,512]{1,0:T(8,128)(2,1)}, bf16[512,512]{1,0:T(8,128)(2,1)}, u32[]{:S(2)}, u32[]{:S(2)}) collective-permute-start(bf16[512,512]{1,0:T(8,128)(2,1)} %attention.3.refs_0_), channel_id=1, source_target_pairs={{0,1},{1,2},{2,3},{3,0},{4,5},{5,6},{6,7},{7,4},{8,9},{9,10},{10,1... | collective-permute-start | bytes 1572872 | tf_op jit(solution)/shard_map/mixed_ring/ppermute | solution.py:68
  192.6 16.8 %collective-permute-start.16 = (bf16[512,512]{1,0:T(8,128)(2,1)}, bf16[512,512]{1,0:T(8,128)(2,1)S(1)}, u32[]{:S(2)}, u32[]{:S(2)}) collective-permute-start(bf16[512,512]{1,0:T(8,128)(2,1)} %collective-permute-done.15.refs_1_), channel_id=1, source_target_pairs={{0,1},{1,2},{2,3},{3,0},{4,5},{5,6},{6,7},{7,4},{8,9},{9,10},{10,1... | collective-permute-start | bytes 1572872 | tf_op jit(solution)/shard_map/mixed_ring/ppermute | solution.py:68
  192.6 28.2 %collective-permute-start.13 = (bf16[512,512]{1,0:T(8,128)(2,1)}, bf16[512,512]{1,0:T(8,128)(2,1)}, u32[]{:S(2)}, u32[]{:S(2)}) collective-permute-start(bf16[512,512]{1,0:T(8,128)(2,1)} %collective-permute-done.12.refs_1_), channel_id=1, source_target_pairs={{0,1},{1,2},{2,3},{3,0},{4,5},{5,6},{6,7},{7,4},{8,9},{9,10},{10,1... | collective-permute-start | bytes 1572872 | tf_op jit(solution)/shard_map/mixed_ring/ppermute | solution.py:68
  209.4 22.5 %collective-permute-start.17 = (bf16[512,512]{1,0:T(8,128)(2,1)S(1)}, bf16[512,512]{1,0:T(8,128)(2,1)S(1)}, u32[]{:S(2)}, u32[]{:S(2)}) collective-permute-start(bf16[512,512]{1,0:T(8,128)(2,1)S(1)} %collective-permute-done.16.refs_2_), channel_id=1, source_target_pairs={{0,1},{1,2},{2,3},{3,0},{4,5},{5,6},{6,7},{7,4},{8,9},{9,10},{10,1... | collective-permute-start | bytes 1572872 | tf_op jit(solution)/shard_map/mixed_ring/ppermute | solution.py:68
  220.8 21.1 %collective-permute-start.14 = (bf16[512,512]{1,0:T(8,128)(2,1)}, bf16[512,512]{1,0:T(8,128)(2,1)}, u32[]{:S(2)}, u32[]{:S(2)}) collective-permute-start(bf16[512,512]{1,0:T(8,128)(2,1)} %collective-permute-done.13.refs_2_), channel_id=1, source_target_pairs={{0,1},{1,2},{2,3},{3,0},{4,5},{5,6},{6,7},{7,4},{8,9},{9,10},{10,1... | collective-permute-start | bytes 1572872 | tf_op jit(solution)/shard_map/mixed_ring/ppermute | solution.py:68
  274.1 233.0 %reduce-scatter.5.cloned.1.call-start = ((), (), s32[]{:S(2)}) async-start(), calls=%async_computation.12 | async-start | bytes 5242880 | tf_op jit(solution)/shard_map/layer_out/reduce_scatter | solution.py:1116
  308.7 18.1 %collective-permute-start.18 = (bf16[512,512]{1,0:T(8,128)(2,1)S(1)}, bf16[512,512]{1,0:T(8,128)(2,1)S(1)}, u32[]{:S(2)}, u32[]{:S(2)}) collective-permute-start(bf16[512,512]{1,0:T(8,128)(2,1)S(1)} %slice_bitcast_fusion), channel_id=1, source_target_pairs={{0,1},{1,2},{2,3},{3,0},{4,5},{5,6},{6,7},{7,4},{8,9},{9,10},{10,1... | collective-permute-start | bytes 1572872 | tf_op jit(solution)/shard_map/mlp/ppermute | solution.py:68
  326.9 15.0 %collective-permute-start.19 = (bf16[512,512]{1,0:T(8,128)(2,1)S(1)}, bf16[512,512]{1,0:T(8,128)(2,1)S(1)}, u32[]{:S(2)}, u32[]{:S(2)}) collective-permute-start(bf16[512,512]{1,0:T(8,128)(2,1)S(1)} %fusion.21), channel_id=1, source_target_pairs={{0,1},{1,2},{2,3},{3,0},{4,5},{5,6},{6,7},{7,4},{8,9},{9,10},{10,1... | collective-permute-start | bytes 1572872 | tf_op jit(solution)/shard_map/mlp/ppermute | solution.py:68
  342.1 14.3 %collective-permute-start.20 = (bf16[512,512]{1,0:T(8,128)(2,1)S(1)}, bf16[512,512]{1,0:T(8,128)(2,1)S(1)}, u32[]{:S(2)}, u32[]{:S(2)}) collective-permute-start(bf16[512,512]{1,0:T(8,128)(2,1)S(1)} %fusion.22), channel_id=1, source_target_pairs={{0,1},{1,2},{2,3},{3,0},{4,5},{5,6},{6,7},{7,4},{8,9},{9,10},{10,1... | collective-permute-start | bytes 1572872 | tf_op jit(solution)/shard_map/mlp/ppermute | solution.py:68
  401.4 13.4 %all-to-all-start.1 = ((bf16[8,64,512]{2,1,0:T(8,128)(2,1)}), bf16[8,64,512]{2,1,0:T(8,128)(2,1)S(1)}, u32[]{:S(2)}, u32[]{:S(2)}) async-start(bf16[8,64,512]{2,1,0:T(8,128)(2,1)} %bitcast.108), calls=%async_computation.3 | async-start | bytes 1048576 | tf_op jit(solution)/shard_map/entry_bwd/all_to_all | solution.py:91
  414.9 33.9 %all-to-all-start.2 = ((bf16[8,64,2048]{2,1,0:T(8,128)(2,1)}), bf16[8,64,2048]{2,1,0:T(8,128)(2,1)}, u32[]{:S(2)}, u32[]{:S(2)}) async-start(bf16[8,64,2048]{2,1,0:T(8,128)(2,1)} %bitcast.41), calls=%async_computation.4 | async-start | bytes 4194304 | tf_op jit(solution)/shard_map/hyper_bwd/all_to_all | solution.py:91
  425.7 12.8 %collective-permute-start.22 = (bf16[64,512]{1,0:T(8,128)(2,1)S(1)}, bf16[64,512]{1,0:T(8,128)(2,1)S(1)}, u32[]{:S(2)}, u32[]{:S(2)}) collective-permute-start(bf16[64,512]{1,0:T(8,128)(2,1)S(1)} %reduce_sum.61.refs_0_), channel_id=1, source_target_pairs={{0,2},{1,3},{2,0},{3,1},{4,6},{5,7},{6,4},{7,5},{8,10},{9,11},{10,... | collective-permute-start | bytes 196616 | tf_op jit(solution)/shard_map/entry_bwd/ppermute | solution.py:68
  451.6 20.8 %all-to-all-start.3 = ((bf16[8,16,4608]{2,1,0:T(8,128)(2,1)}), bf16[8,16,4608]{2,1,0:T(8,128)(2,1)S(1)}, u32[]{:S(2)}, u32[]{:S(2)}) async-start(bf16[8,16,4608]{2,1,0:T(8,128)(2,1)} %bitcast.100), calls=%async_computation.5 | async-start | bytes 2359296 | tf_op jit(solution)/shard_map/hyper_bwd/all_to_all | solution.py:91
  455.5 59.3 %all-gather.12.cloned.1.call-start = ((), (), s32[]{:S(2)}) async-start(), calls=%async_computation.13 | async-start | bytes 4718592 | tf_op jit(solution)/shard_map/grads_out/all_gather | solution.py:1170
  476.0 15.0 %all-to-all-start.4 = ((bf16[8,16,1664]{2,1,0:T(8,128)(2,1)}), bf16[8,16,1664]{2,1,0:T(8,128)(2,1)S(1)}, u32[]{:S(2)}, u32[]{:S(2)}) async-start(bf16[8,16,1664]{2,1,0:T(8,128)(2,1)} %bitcast.47), calls=%async_computation.6 | async-start | bytes 851968 | tf_op jit(solution)/shard_map/grads_out/all_to_all | solution.py:91
  491.0 15.4 %all-to-all-start.5 = ((bf16[4,16,2048]{2,1,0:T(8,128)(2,1)}), bf16[4,16,2048]{2,1,0:T(8,128)(2,1)S(1)}, u32[]{:S(2)}, u32[]{:S(2)}) async-start(bf16[4,16,2048]{2,1,0:T(8,128)(2,1)} %bitcast.50), calls=%async_computation.7 | async-start | bytes 524288 | tf_op jit(solution)/shard_map/grads_out/all_to_all | solution.py:1173
  (29 other events, 417.7 us)
Sparse Core Ops, SparseCore 0:
  12.3 65.8 all-gather.5
  80.1 69.1 all-gather.9
  153.1 53.0 all-gather.7
  274.3 42.6 reduce-scatter.2
  370.2 79.1 reduce-scatter.4
  472.7 42.1 all-gather.11

commit v4 on v3

--- a/solution.py
+++ b/solution.py
@@ -85,11 +85,14 @@
     ]
 
 
-def scatter_dp(values):
+def to_owners(values):
     size = lax.axis_size("dp")
     blocks = values.reshape(size, values.shape[0] // size, values.shape[1])
-    blocks = lax.all_to_all(blocks, "dp", 0, 0, tiled=True)
-    return jnp.sum(blocks.astype(jnp.float32), axis=0)
+    return lax.all_to_all(blocks, "dp", 0, 0, tiled=True)
+
+
+def scatter_dp(values):
+    return jnp.sum(to_owners(values).astype(jnp.float32), axis=0)
 
 
 def from_all(values):
@@ -368,13 +371,13 @@
     vectors_ref,
     gain_ref,
     triple_w_ref,
-    mid_ref,
     project_ref,
     pair_ref,
     *refs,
 ):
     bfloat = jnp.bfloat16
-    query_refs = refs[:-2]
+    half = (len(refs) - 2) // 2
+    mid_refs, query_refs = refs[:half], refs[half:-2]
     entry_ref, pooled_ref = refs[-2:]
     count = vectors_ref.shape[0]
     length = tokens_ref.shape[1]
@@ -392,12 +395,12 @@
     grad = grad * gain_ref[...]
     normed, spread = unit_scale(vectors_ref[...].astype(jnp.float32))
     grad = spread * (grad - normed * jnp.mean(grad * normed, axis=1, keepdims=True))
-    entry_grad = (grad + mid_ref[...]).astype(bfloat)
+    entry_grad = (grad + sum(ref[...] for ref in mid_refs)).astype(bfloat)
     entry_ref[...] = entry_grad
     pooled_ref[...] = times_trans(entry_grad, project_ref[...]).astype(bfloat)
 
 
-def entry_back(tokens, vectors, gain, weights, mid_entries, project, pair_out, query_parts):
+def entry_back(tokens, vectors, gain, weights, project, pair_out, mid_parts, query_parts):
     total, width = vectors.shape
     length = tokens.shape[0]
     block = min(256, total)
@@ -418,10 +421,10 @@
             rows_of(width),
             whole((1, width)),
             whole((width, triple_width)),
-            rows_of(width),
             whole(project.shape),
             whole(pair_out.shape),
         ]
+        + [rows_of(width)] * len(mid_parts)
         + [whole(part.shape) for part in query_parts],
         out_specs=[rows_of(width), rows_of(inner)],
         out_shape=[
@@ -434,36 +437,45 @@
         ),
         compiler_params=pltpu.CompilerParams(vmem_limit_bytes=VMEM_LIMIT),
         name="entry_back",
-    )(tokens[None, :], vectors, gain[None, :], weights, mid_entries, project, pair_out, *query_parts)
+    )(tokens[None, :], vectors, gain[None, :], weights, project, pair_out, *mid_parts, *query_parts)
 
 
 def mlp_kernel(
     query_width,
     unit_width,
     positions,
-    places_ref,
+    stacked,
+    plan_ref,
     resid_in_ref,
-    swiglu_grad_ref,
-    cot_ref,
+    weight_ref,
     own_weight_ref,
+    own_cot_ref,
     gain_ref,
     output_from,
     units_from,
     *refs,
 ):
     bfloat = jnp.bfloat16
-    mixed_refs = refs[:positions]
-    resid_ref, swiglu_ref, mid_ref, part_ref, output_ref, units_ref, arrived = refs[positions:]
-    gate_columns = pl.ds(0, unit_width)
-    upward_columns = pl.ds(unit_width, unit_width)
+    grads_from, mixed_refs, refs = refs[:positions], refs[positions : 2 * positions], refs[2 * positions :]
+    resid_ref, swiglu_ref, mid_ref, *refs = refs
+    part_refs, refs = refs[:-5], refs[-5:]
+    output_ref, units_ref, swiglu_grad_ref, arrived, grad_arrived = refs
+    grad_place = plan_ref[positions + pl.program_id(0)]
+    for at, grad_from in enumerate(grads_from):
+        copy = pltpu.make_async_copy(grad_from, swiglu_grad_ref, grad_arrived)
+        pl.when(grad_place == at)(copy.start)
+    gate_columns, upward_columns = [pl.ds(at * unit_width, unit_width) for at in range(2)]
+    output_columns = [pl.ds(at * query_width, query_width) for at in range(positions)]
     copies = [
-        pltpu.make_async_copy(output_from, output_ref, arrived.at[0]),
         pltpu.make_async_copy(
-            units_from.at[:, gate_columns], units_ref.at[:, gate_columns], arrived.at[1]
-        ),
+            output_from.at[:, columns], output_ref.at[:, columns], arrived.at[at]
+        )
+        for at, columns in enumerate(output_columns)
+    ] + [
         pltpu.make_async_copy(
-            units_from.at[:, upward_columns], units_ref.at[:, upward_columns], arrived.at[2]
-        ),
+            units_from.at[:, columns], units_ref.at[:, columns], arrived.at[positions + at]
+        )
+        for at, columns in enumerate((gate_columns, upward_columns))
     ]
 
     def on_first(act):
@@ -473,25 +485,26 @@
     def _():
         for copy in copies:
             copy.start()
-        copies[0].wait()
 
     resid = resid_in_ref[...].astype(jnp.float32)
     for at, mixed_ref in enumerate(mixed_refs):
-        columns = slice(at * query_width, (at + 1) * query_width)
+        on_first(copies[at].wait)
+        columns = output_columns[at]
         resid = resid + times_trans(mixed_ref[...], output_ref[:, columns])
     resid_ref[...] = resid
     gain = gain_ref[...]
     spread = lax.rsqrt(jnp.mean(resid * resid, axis=1, keepdims=True) + EPS)
     normed = resid * spread
     seq_two = (normed * gain).astype(bfloat)
-    on_first(copies[1].wait)
+    on_first(copies[positions].wait)
     gate = matmul(seq_two, units_ref[:, gate_columns])
-    on_first(copies[2].wait)
+    on_first(copies[positions + 1].wait)
     upward = matmul(seq_two, units_ref[:, upward_columns])
     open_gate = jax.nn.sigmoid(gate)
     silu = gate * open_gate
     swiglu_ref[...] = (silu * upward).astype(bfloat)
-    swiglu_grad = swiglu_grad_ref[...]
+    pltpu.make_async_copy(grads_from[0], swiglu_grad_ref, grad_arrived).wait()
+    swiglu_grad = weight_ref[...] * swiglu_grad_ref[...]
     slope = open_gate * (1.0 + gate * (1.0 - open_gate))
     gate_grad = (swiglu_grad * upward * slope).astype(bfloat)
     upward_grad = (swiglu_grad * silu).astype(bfloat)
@@ -499,64 +512,107 @@
     grad = grad + times_trans(upward_grad, units_ref[:, upward_columns])
     grad = grad * gain
     grad = spread * (grad - normed * jnp.mean(grad * normed, axis=1, keepdims=True))
-    grad = grad + own_weight_ref[...] * cot_ref[...].astype(jnp.float32)
+    grad = grad + own_weight_ref[...] * own_cot_ref[...].astype(jnp.float32)
     mid_low = grad.astype(bfloat)
     mid_ref[...] = mid_low
     for at in range(positions):
-        columns = slice(at * query_width, (at + 1) * query_width)
-        part_ref[places_ref[at]] = matmul(mid_low, output_ref[:, columns]).astype(bfloat)
+        columns = output_columns[at]
+        part = matmul(mid_low, output_ref[:, columns]).astype(bfloat)
+        if stacked:
+            part_refs[0][plan_ref[at]] = part
+        else:
+            part_refs[at][...] = part
 
 
 def mlp(
-    places, resid_in, swiglu_grad, cot, own_weight, gain, output_w, units_w, mixed, rows_at, row_total
+    plan,
+    block_idx,
+    row_total,
+    resid_in,
+    weight,
+    own_weight,
+    own_cot,
+    swiglu_grads,
+    gain,
+    output_w,
+    units_w,
+    mixed,
+    stacked,
 ):
     width = resid_in.shape[1]
-    unit_width = swiglu_grad.shape[1]
+    unit_width = units_w.shape[1] // 2
     query_width = mixed[0].shape[1]
-    block = min(256, row_total)
-    offset = rows_at // block
-
-    def rows_of(columns, shift):
-        return pl.BlockSpec((block, columns), lambda at: (at + shift, 0))
+    positions = len(mixed)
+    block = own_cot.shape[0]
+
+    def rows_of(columns, first=0):
+        return pl.BlockSpec((block, columns), lambda at, plan: (at + first, 0))
+
+    first = block_idx * row_total // block
+    part_shape = jax.ShapeDtypeStruct((row_total, query_width), jnp.bfloat16)
+    part_specs = [rows_of(query_width)] * positions
+    part_shapes = [part_shape] * positions
+    if stacked:
+        part_specs = [pl.BlockSpec((positions, block, query_width), lambda at, plan: (0, at, 0))]
+        part_shapes = [
+            jax.ShapeDtypeStruct((positions, row_total, query_width), jnp.bfloat16)
+        ]
+
+    def whole(shape):
+        return pl.BlockSpec(shape, lambda at, plan: (0, 0), pipeline_mode=pl.Buffered(1))
 
     return pl.pallas_call(
-        partial(mlp_kernel, query_width, unit_width, len(mixed)),
-        grid=(row_total // block,),
-        in_specs=[
-            pl.BlockSpec(memory_space=pltpu.SMEM),
-            rows_of(width, offset),
-            rows_of(unit_width, offset),
-            rows_of(width, offset),
-            rows_of(1, offset),
-            pl.BlockSpec((1, width), lambda at: (0, 0)),
-            pl.BlockSpec(memory_space=pl.ANY),
-            pl.BlockSpec(memory_space=pl.ANY),
-        ]
-        + [rows_of(query_width, 0)] * len(mixed),
-        out_specs=[
-            rows_of(width, 0),
-            rows_of(unit_width, 0),
-            rows_of(width, 0),
-            pl.BlockSpec((len(mixed), block, query_width), lambda at: (0, at, 0)),
-        ],
+        partial(mlp_kernel, query_width, unit_width, positions, stacked),
+        grid_spec=pltpu.PrefetchScalarGridSpec(
+            num_scalar_prefetch=1,
+            grid=(row_total // block,),
+            in_specs=[
+                rows_of(width, first),
+                rows_of(1, first),
+                rows_of(1, first),
+                whole((block, width)),
+                whole((1, width)),
+            ]
+            + [pl.BlockSpec(memory_space=pl.ANY)] * (2 + positions)
+            + [rows_of(query_width)] * positions,
+            out_specs=[
+                rows_of(width),
+                rows_of(unit_width),
+                rows_of(width),
+            ]
+            + part_specs,
+            scratch_shapes=[
+                pltpu.VMEM(output_w.shape, output_w.dtype),
+                pltpu.VMEM(units_w.shape, units_w.dtype),
+                pltpu.VMEM((block, unit_width), jnp.float32),
+                pltpu.SemaphoreType.DMA((positions + 2,)),
+                pltpu.SemaphoreType.DMA,
+            ],
+        ),
         out_shape=[
             jax.ShapeDtypeStruct((row_total, width), jnp.float32),
             jax.ShapeDtypeStruct((row_total, unit_width), jnp.bfloat16),
             jax.ShapeDtypeStruct((row_total, width), jnp.bfloat16),
-            jax.ShapeDtypeStruct((len(mixed), row_total, query_width), jnp.bfloat16),
-        ],
+        ]
+        + part_shapes,
         cost_estimate=cost(
-            2 * row_total * (output_w.size + units_w.size),
-            2 * (output_w.size + units_w.size) + 16 * row_total * width,
+            row_total * width * (2 * width + 4 * unit_width),
+            2 * width * (width + 2 * unit_width) + 16 * row_total * width,
         ),
-        scratch_shapes=[
-            pltpu.VMEM(output_w.shape, output_w.dtype),
-            pltpu.VMEM(units_w.shape, units_w.dtype),
-            pltpu.SemaphoreType.DMA((3,)),
-        ],
         compiler_params=pltpu.CompilerParams(vmem_limit_bytes=VMEM_LIMIT),
         name="mlp",
-    )(places, resid_in, swiglu_grad, cot, own_weight, gain[None, :], output_w, units_w, *mixed)
+    )(
+        plan,
+        resid_in,
+        weight,
+        own_weight,
+        own_cot,
+        gain[None, :],
+        output_w,
+        units_w,
+        *swiglu_grads,
+        *mixed,
+    )
 
 
 def centred(values):
@@ -933,8 +989,9 @@
         query_width = frozen_query.shape[1]
         key_width = frozen_key.shape[1]
         triple_width = query_width + 2 * key_width
-        full_triple = first_weights[:, :triple_width]
+        unit_width = frozen_gate.shape[1]
         full_downward = first_weights[:, triple_width:]
+        second_weights = jnp.concatenate([frozen_gate, frozen_upward], axis=1)
     with jax.named_scope("lookup"):
         local_ids = packed_dp[:, :, :SUBWORD_SLOTS].reshape(-1) - dp_at * table_rows
         inside = (local_ids >= 0) & (local_ids < table_rows)
@@ -948,22 +1005,18 @@
         cot_blocks = [cotangent, ring(cotangent)]
         length = text_tokens.shape[0] * tensor_size
         cosine, sine = rope_lanes(length)
-        rows_in = lax.optimization_barrier((rows_in, cot_blocks[-1], cosine, sine))
-        rows_in, _, cosine, sine = rows_in
         cot_blocks.append(ring(cot_blocks[-1]))
+        rows_in, cosine, sine, second_weights, *cot_blocks = lax.optimization_barrier(
+            (rows_in, cosine, sine, second_weights, *cot_blocks)
+        )
+        second_weights = lax.all_gather(second_weights, "dp", axis=0, tiled=True)
         packed_all = from_all(
             tie(jnp.concatenate([packed_dp.reshape(-1), text_tokens]), cot_blocks[1])
         )
     with jax.named_scope("hyper_wide"):
         rows_blocks = from_all(rows_in.astype(bfloat))
-    with jax.named_scope("second_weights"):
-        second_weights = jnp.concatenate([frozen_gate, frozen_upward], axis=1)
-        second_weights = lax.all_gather(
-            tie(second_weights, served), "dp", axis=0, tiled=True
-        )
     with jax.named_scope("hyper_wide"):
         rows_wide = jnp.concatenate(in_order(rows_blocks, tensor_at), axis=0)
-        rows_wide, cot_blocks[2] = lax.optimization_barrier((rows_wide, cot_blocks[2]))
         packed_all = jnp.stack(in_order(packed_all, tensor_at))
         ids_size = dp_size * entries * packed_width
         packed_ids = packed_all[:, :ids_size].reshape(tensor_size, dp_size, entries, packed_width)
@@ -979,39 +1032,31 @@
         first_in, triple, mixed, resid_one, second_in, activated, slope, dp_pooled = hyper_wide(
             rows_wide, open_wide, gain_pair, *encoders, counts_wide
         )
-    with jax.named_scope("cot_ring"):
-        cot_blocks.append(ring(cot_blocks[-1]))
-        dp_pooled = tie(dp_pooled, cot_blocks[-1])
     with jax.named_scope("output_weights"):
         output_blocks = from_all(tie(frozen_output, dp_pooled))
     with jax.named_scope("pooled_gather"):
         all_pooled = lax.all_gather(dp_pooled, "dp", axis=0, tiled=True)
+    with jax.named_scope("output_weights"):
+        output_weights = jnp.concatenate(output_blocks, axis=1)
+        output_weights, all_pooled = lax.optimization_barrier((output_weights, all_pooled))
+        output_weights = lax.all_gather(
+            tie(output_weights, first_weights), "dp", axis=0, tiled=True
+        )
+    with jax.named_scope("cot_ring"):
+        cot_blocks.append(ring(tie(cot_blocks[-1], all_pooled)))
     with jax.named_scope("entry_vectors"):
         seq_tokens = packed_all[:, ids_size:].reshape(-1)
         all_vectors, seq_triple = entry(
             seq_tokens, all_pooled, embed_project, prenorm_gain, first_weights, triple_width
         )
-    with jax.named_scope("output_weights"):
-        output_weights = jnp.concatenate(tie(output_blocks, seq_triple), axis=1)
-        output_weights = lax.all_gather(
-            tie(output_weights, first_weights), "dp", axis=0, tiled=True
-        )
 
     with jax.named_scope("attention_fwd"):
         block_rows = min(512, length)
         block_total = length // block_rows
-        mixed_parts = []
-        for first in range(0, length, block_rows):
-            lm_mixed = attention(seq_triple, cosine, sine, query_width, first, block_rows)
-            mixed_parts.append([lm_mixed])
-            seq_triple = tie(seq_triple, lm_mixed)
-    with jax.named_scope("mixed_ring"):
-        late_ids, late_tokens, late_cot = tie_all(lm_mixed, packed_ids, seq_tokens, cot_blocks)
-        for parts in mixed_parts:
-            for _ in range(tensor_size - 1):
-                parts.append(ring(parts[-1]))
-    with jax.named_scope("swiglu_grad"):
-        vectors = lax.dynamic_slice_in_dim(all_vectors, device_at * entries, entries, 0)
+        first_mixed = attention(seq_triple, cosine, sine, query_width, 0, block_rows)
+
+    with jax.named_scope("mlp_rows"):
+        late_ids, late_tokens = tie_all(first_mixed, packed_ids, seq_tokens)
         late_ids = late_ids.transpose(1, 0, 2, 3).reshape(entry_total, packed_width)
         all_ids = late_ids[:, :SUBWORD_SLOTS].reshape(-1)
         all_weights = (1.0 / jnp.log(1.0 + late_ids[:, SUBWORD_SLOTS].astype(single))).astype(
@@ -1020,11 +1065,25 @@
         rows_here = text_tokens.shape[0]
         seq_hot = (late_tokens[:, None] == jnp.arange(entry_total)[None, :]).astype(bfloat)
         seq_weight = matmul(seq_hot, all_weights[:, None])
-        seq_cot = jnp.concatenate(in_order(late_cot, tensor_at), axis=0)
-        resid_in = matmul(seq_hot, all_vectors).astype(bfloat)
-        swiglu_grad = matmul((seq_weight * seq_cot.astype(single)).astype(bfloat), full_downward)
         own_rows_here = jnp.arange(length) // rows_here == tensor_at
         own_weight = jnp.where(own_rows_here[:, None], seq_weight, 0.0)
+        resid_in = matmul(seq_hot, all_vectors).astype(bfloat)
+        per_block = block_rows // rows_here
+        vectors = lax.dynamic_slice_in_dim(all_vectors, device_at * entries, entries, 0)
+
+    with jax.named_scope("attention_fwd"):
+        seq_triple = tie(seq_triple, resid_in)
+        mixed_parts = [[first_mixed]]
+        for first in range(block_rows, length, block_rows):
+            lm_mixed = attention(seq_triple, cosine, sine, query_width, first, block_rows)
+            mixed_parts.append([lm_mixed])
+    with jax.named_scope("mixed_ring"):
+        for block_idx, parts in enumerate(mixed_parts):
+            last_part = ring(parts[0], tensor_size - 1)
+            parts.append(ring(parts[0]))
+            for step in range(2, tensor_size - 1):
+                parts.append(ring(parts[-1]))
+            parts.append(last_part)
 
     def share(values):
         rows, width = values.shape
@@ -1033,60 +1092,78 @@
             rows, width // tensor_size
         )
 
-    shares = [share(array) for array in tie((first_in, mixed, second_in, activated), lm_mixed)]
+    shares = [share(array) for array in (first_in, mixed, second_in, activated)]
+
+    with jax.named_scope("swiglu_grad"):
+        late_cots = tie(cot_blocks, lm_mixed)
+        swiglu_grads = [matmul(cot, full_downward) for cot in late_cots]
 
     with jax.named_scope("mlp"):
         places = lax.rem(tensor_at + tensor_size - jnp.arange(tensor_size), tensor_size)
         resid_blocks = []
-        swiglu_blocks = []
-        mid_blocks = []
+        layer_parts = []
+        mid_parts = []
         mixed_grads = []
         for block_idx, parts in enumerate(mixed_parts):
             last = block_idx == block_total - 1
+            rows = slice(block_idx * block_rows, (block_idx + 1) * block_rows)
             if block_idx == 0:
-                mixed_parts = lax.optimization_barrier(mixed_parts)
-                parts = mixed_parts[0]
+                near = [[later[1], later[-1]] for later in mixed_parts[1:]]
+                parts, near = lax.optimization_barrier((parts, near))
+                for later, (below, above) in zip(mixed_parts[1:], near):
+                    later[1], later[-1] = below, above
+                    for step in range(2, tensor_size - 1):
+                        later[step] = ring(later[step - 1])
             else:
-                parts = mixed_parts[block_idx]
-            if block_idx > 0:
-                parts = tie(parts, mixed_part)
-            resid_mid, swiglu_low, mid_low, mixed_part = mlp(
-                jnp.arange(tensor_size) if last else places,
+                parts, layer_parts, mid_parts = lax.optimization_barrier(
+                    (parts, layer_parts, mid_parts)
+                )
+            block_places = block_idx * per_block + jnp.arange(per_block)
+            block_places = lax.rem(tensor_at + tensor_size - block_places, tensor_size)
+            resid_mid, swiglu_low, mid_low, *mixed_part = mlp(
+                jnp.concatenate([places, block_places]),
+                block_idx,
+                block_rows,
                 resid_in,
-                swiglu_grad,
-                seq_cot,
+                seq_weight,
                 own_weight,
+                cotangent,
+                swiglu_grads,
                 midnorm_gain,
                 output_weights,
                 second_weights,
                 parts,
-                block_idx * block_rows,
-                block_rows,
+                not last,
             )
             resid_blocks.append(resid_mid)
-            swiglu_blocks.append(swiglu_low)
-            mid_blocks.append(mid_low)
             if not last:
                 mixed_grads.append(
                     lax.psum_scatter(
-                        mixed_part.reshape(-1, query_width),
+                        mixed_part[0].reshape(-1, query_width),
                         "tensor",
                         scatter_dimension=0,
                         tiled=True,
                     )
                 )
+                layer_parts.append(times_trans(swiglu_low, full_downward).astype(bfloat))
+                mid_parts.append(trans_times(seq_hot[rows], mid_low))
                 continue
             carried = None
             for step in [*range(1, tensor_size), 0]:
                 part = mixed_part[step]
-                if carried is not None:
-                    part = (part.astype(single) + carried.astype(single)).astype(bfloat)
                 if step == 2:
-                    mid_entries = trans_times(seq_hot, jnp.concatenate(mid_blocks, axis=0))
-                    part, mid_entries = lax.optimization_barrier((part, mid_entries))
+                    mid_parts.append(trans_times(seq_hot[rows], mid_low))
+                    carried, mid_parts = lax.optimization_barrier((carried, mid_parts))
                 if step == 3:
-                    layer_part = times_trans(jnp.concatenate(swiglu_blocks, axis=0), full_downward)
-                    part, layer_part = lax.optimization_barrier((part, layer_part.astype(bfloat)))
+                    layer_parts.append(times_trans(swiglu_low, full_downward).astype(bfloat))
+                    layer_cut = model_width * 5 // 8
+                    layer_halves = [
+                        jnp.concatenate([part[:, columns] for part in layer_parts], axis=0)
+                        for columns in (slice(None, layer_cut), slice(layer_cut, None))
+                    ]
+                    carried, layer_halves, shares = lax.optimization_barrier(
+                        (carried, layer_halves, shares)
+                    )
                 if step == 0:
                     pair_out = None
                     query_parts = []
@@ -1095,13 +1172,18 @@
                             seq_triple, cosine, sine, mixed_grad, at * block_rows, pair_out
                         )
                         query_parts.append(query_part)
-                    part, pair_out = lax.optimization_barrier((part, pair_out))
+                    carried, pair_out = lax.optimization_barrier((carried, pair_out))
+                if carried is not None:
+                    part = (part.astype(single) + carried.astype(single)).astype(bfloat)
                 if step > 0:
                     carried = ring(part)
             last_grad = part
 
     with jax.named_scope("layer_out"):
-        layer_part = tie(layer_part, last_grad)
+        layer_near, layer_far = layer_halves
+        layer_near = lax.psum_scatter(
+            tie(layer_near, last_grad), "tensor", scatter_dimension=0, tiled=True
+        )
         blocks_of = [
             lax.dynamic_slice_in_dim(
                 block, lax.rem(tensor_at * rows_here, block_rows), rows_here, 0
@@ -1113,9 +1195,6 @@
             resid_own = jnp.where(
                 tensor_at * rows_here // block_rows == block_idx, blocks_of[block_idx], resid_own
             )
-        layer_final = resid_own + lax.psum_scatter(
-            layer_part, "tensor", scatter_dimension=0, tiled=True
-        ).astype(single)
     with jax.named_scope("attention_bwd"):
         query_part, pair_out = attention_back(
             seq_triple, cosine, sine, last_grad, length - block_rows, pair_out
@@ -1128,18 +1207,26 @@
             all_vectors,
             prenorm_gain,
             first_weights,
-            mid_entries,
             embed_project,
             pair_out,
+            mid_parts,
             query_parts,
         )
-        pooled_part = scatter_dp(pooled_part).astype(bfloat)
+        project_part = trans_times(all_pooled, entry_part).astype(bfloat)
+        pooled_shares, project_part = lax.optimization_barrier(
+            (to_owners(pooled_part), project_part)
+        )
+        pooled_part = jnp.sum(pooled_shares.astype(single), axis=0).astype(bfloat)
         pooled_grads = from_all(pooled_part)
-        project_part = trans_times(all_pooled, entry_part).astype(bfloat)
-        project_part = tie(project_part, pooled_part)
 
     with jax.named_scope("hyper_bwd"):
-        project_grad = scatter_dp(project_part).astype(bfloat)
+        project_shares = to_owners(tie(project_part, pooled_grads[1]))
+    with jax.named_scope("layer_out"):
+        layer_far = lax.psum_scatter(
+            tie(layer_far, pooled_grads, layer_near), "tensor", scatter_dimension=0, tiled=True
+        )
+        layer_final = resid_own + jnp.concatenate([layer_near, layer_far], axis=1).astype(single)
+    with jax.named_scope("hyper_bwd"):
         resid_grad, mixed_grad, early, gain_two = hyper_back_units(
             dp_size,
             pooled_grads,
@@ -1150,10 +1237,10 @@
             shares[1:],
             encoders[1:],
         )
-        resid_grad, early, project_grad = lax.optimization_barrier(
-            (resid_grad, early, project_grad)
-        )
-        early = scatter_dp(early)
+        resid_grad, early, project_shares = lax.optimization_barrier(
+            (resid_grad, early, project_shares)
+        )
+        early = to_owners(early)
         rows_low, late, gain_one = hyper_back_slots(
             resid_grad,
             mixed_grad,
@@ -1166,7 +1253,11 @@
         )
 
     with jax.named_scope("grads_out"):
-        rows_low, early = lax.optimization_barrier((rows_low, early))
+        rows_low, early, project_shares = lax.optimization_barrier(
+            (rows_low, early, project_shares)
+        )
+        early = jnp.sum(early.astype(single), axis=0)
+        project_grad = jnp.sum(project_shares.astype(single), axis=0).astype(bfloat)
         all_rows = lax.all_gather(rows_low, "dp", axis=0, tiled=True)
         late, project_grad = tie_all(rows_low, late, project_grad)
         project_grad = project_grad.reshape(tensor_size, -1, model_width)

time: 537 us -> 504 us (0.939)
  waiting for transfers between devices: 146 us -> 90.5 us
  matrix products: 47.4 us -> 60.8 us
  local copies, waits for them, and re-layouts: 34.5 us -> 40.6 us
    ppermute x24, waiting for transfers between devices: 106 us -> 41.5 us  [ring(): lax.ppermute(values, 'tensor', [(i, (i + shift) % size) for i in range(si...]
    all_to_all x4, waiting for transfers between devices: 17.7 us -> 28.5 us  [to_owners(): return lax.all_to_all(blocks, 'dp', 0, 0, tiled=True)]
    dot_general x4 -> x7, matrix products: 24.6 us -> 34.4 us  [matmul(): return jnp.dot(left, right, preferred_element_type=jnp.float32)]
    dot_general x1 -> x2, matrix products: 11.7 us -> 13.8 us  [times_trans(): lax.dot_general(left, right, (((1,), (1,)), ((), ())), preferred_element_...]
    dot_general x2 -> x3, matrix products: 11.1 us -> 12.6 us  [trans_times(): lax.dot_general(left, right, (((0,), (0,)), ((), ())), preferred_element_...]
  transfers between devices with their start and end apart: 36 -> 37, of which waited for: 20 -> 19; matrix products, arithmetic and copies ran while one was open for 18% -> 22% of each run, Pallas kernels for 26% -> 37%
where the time goes in v4:
time: 504 us; the launch traced here: 495 us
  Pallas kernels  183 us (36%)
  waiting for transfers between devices  90.5 us (18%)
  matrix products  60.8 us (12%)
  starting transfers between devices  56.1 us (11%)
  local copies, waits for them, and re-layouts  40.6 us (8%)
  other arithmetic  25.9 us (5%)
  blocking collectives  22 us (4%)
  between operations  15.4 us (3%)
    pallas_call x2, Pallas kernels, mlp(): pl.pallas_call(partial(mlp_kernel, query_width, unit_width, positions, st...  64.7 us
    ppermute x24, waiting for transfers between devices, ring(): lax.ppermute(values, 'tensor', [(i, (i + shift) % size) for i in range(si...  41.5 us
    pallas_call x2, Pallas kernels, attention_back(): pl.pallas_call(kernel, grid=(pairs,), in_specs=specs, out_specs=[pl.Block...  34.4 us
    dot_general x7, matrix products, matmul(): return jnp.dot(left, right, preferred_element_type=jnp.float32)  34.4 us
    ppermute x24, starting transfers between devices, ring(): lax.ppermute(values, 'tensor', [(i, (i + shift) % size) for i in range(si...  32.4 us
    all_to_all x4, waiting for transfers between devices, to_owners(): return lax.all_to_all(blocks, 'dp', 0, 0, tiled=True)  28.5 us
    pallas_call x2, Pallas kernels, attention(): pl.pallas_call(partial(attention_kernel, min(256, rows), base), grid=(pai...  22.4 us
    pallas_call x1, Pallas kernels, hyper_wide(): pl.pallas_call(hyper_wide_kernel, grid=(total // block,), in_specs=[rows_...  18.5 us
  transfers between devices with their start and end apart: 37, of which 19 were waited for; matrix products, arithmetic and copies ran while one was open for 22% of the time, Pallas kernels for 37%

profile of v4, /device:TPU:0, one launch (start us, length us, event | category | flops | bytes accessed | tf_op | source)
XLA Modules:
  0.0 494.6 jit_solution(18126914137802176666)
XLA Ops:
  15.6 9.2 %all-gather = s32[128,10]{1,0:T(8,128)S(1)} all-gather(s32[16,10]{1,0:T(8,128)S(1)} %pad_add_fusion.2), channel_id=2, replica_groups=mesh['dp'=8,'tensor'=4] {'dp'}, dimensions={0}, use_global_device_ids=true | all-gather | bytes 5760 | tf_op jit(solution)/shard_map/ids/all_gather | solution.py:986
  25.2 6.7 %gather_fusion = bf16[1024,512]{1,0:T(8,128)(2,1)S(1)} fusion(bf16[4000,512]{1,0:T(8,128)(2,1)} %param.22, s32[1024]{0:T(1024)S(1)} %broadcast_clamp_fusion), kind=kCustom, calls=%fused_computation | custom fusion | bytes 2101248 | tf_op jit(solution)/shard_map/lookup/jit(_take)/gather | solution.py:998
  45.6 13.0 %all-to-all-done = bf16[8,128,512]{2,1,0:T(8,128)(2,1)S(1)} async-done(((bf16[8,128,512]{2,1,0:T(8,128)(2,1)}), bf16[8,128,512]{2,1,0:T(8,128)(2,1)S(1)}, u32[]{:S(2)}, u32[]{:S(2)}) %all-to-all-start) | async-done | bytes 1048608 | tf_op jit(solution)/shard_map/lookup/all_to_all | solution.py:1000
  58.7 8.1 %collective-permute-done.1 = bf16[256,2048]{1,0:T(8,128)(2,1)} collective-permute-done((bf16[256,2048]{1,0:T(8,128)(2,1)S(1)}, bf16[256,2048]{1,0:T(8,128)(2,1)}, u32[]{:S(2)}, u32[]{:S(2)}) %collective-permute-start.1) | collective-permute-done | bytes 1048608 | tf_op jit(solution)/shard_map/cot_ring/ppermute | solution.py:68
  82.0 18.5 %hyper_wide.1 = (bf16[512,512]{1,0:T(8,128)(2,1)}, bf16[512,1536]{1,0:T(8,128)(2,1)}, bf16[512,512]{1,0:T(8,128)(2,1)}, f32[512,512]{1,0:T(8,128)}, bf16[512,512...) custom-call(bf16[512,512]{1,0:T(8,128)(2,1)} %pad_maximum_fusion.7.rows_ref, ...), custom_call_target="tpu_custom_call" | custom-call | flops 17179869184 | bytes 12582912 | tf_op jit(solution)/shard_map/hyper_wide/hyper_wide/pallas_call | solution.py:720
  105.5 12.7 %all_gather.23.pooled_ref = bf16[512,512]{1,0:T(8,128)(2,1)} all-gather(bf16[64,512]{1,0:T(8,128)(2,1)} %get-tuple-element.106), channel_id=1, replica_groups=mesh['dp'=8,'tensor'=4] {'dp'}, dimensions={0}, use_global_device_ids=true | all-gather | bytes 589824 | tf_op jit(solution)/shard_map/pooled_gather/all_gather | solution.py:1038
  118.3 6.0 %collective-permute-done.9 = bf16[256,512]{1,0:T(8,128)(2,1)S(1)} collective-permute-done((bf16[256,512]{1,0:T(8,128)(2,1)S(1)}, bf16[256,512]{1,0:T(8,128)(2,1)S(1)}, u32[]{:S(2)}, u32[]{:S(2)}) %collective-permute-start.9) | collective-permute-done | bytes 262176 | tf_op jit(solution)/shard_map/output_weights/ppermute | solution.py:68
  128.6 9.2 %entry.1 = (bf16[512,2048]{1,0:T(8,128)(2,1)}, f32[1024,640]{1,0:T(8,128)}) custom-call(s32[1024,1]{1,0:T(8,128)} %bitcast.93, bf16[512,512]{1,0:T(8,128)(2,1)} %all_gather.23.pooled_ref, bf16[512,2048]{1,0:T(8,128)(2,1)} %project_ref.3, f32[1,2048]{1,0:T(1,128)} %bitcast.114, bf16[2048,2048]{1,0:T(8,128)(2,1)} %all-gather.6.cloned.1.call-done.triple_w_ref), custom_call_target="tpu_custom_call" | custom-call | flops 3758096384 | bytes 9437184 | tf_op jit(solution)/shard_map/entry_vectors/entry/pallas_call | solution.py:342
  137.9 8.9 %attention.2.refs_4_ = bf16[512,512]{1,0:T(8,128)(2,1)} custom-call(f32[1024,640]{1,0:T(8,128)} %get-tuple-element.121.query_ref.pair_ref.refs_0_.refs_1_, f32[1024,640]{1,0:T(8,128)} %get-tuple-element.121.query_ref.pair_ref.refs_0_.refs_1_, f32[1024,128]{1,0:T(8,128)} %get-tuple-element.110.cos_ref.refs_2_, f32[1024,128]{1,0:T(8,128)} %get-tuple-element.111.sin_ref.refs_3_), custom_call_target="tpu_custom_call" | custom-call | flops 2147483648 | bytes 1572864 | tf_op jit(solution)/shard_map/attention_fwd/attention/pallas_call | solution.py:233
  150.4 5.9 %convolution_convert_fusion.resid_in_ref = bf16[1024,2048]{1,0:T(8,128)(2,1)} fusion(bf16[512,2048]{1,0:T(8,128)(2,1)} %get-tuple-element.113.vectors_ref, s32[1024]{0:T(1024)S(1)} %bitcast.107), kind=kOutput, calls=%fused_computation.5 | convolution fusion | flops 2150105088 | bytes 6295552 | tf_op jit(solution)/shard_map/mlp_rows/dot_general | solution.py:51
  156.3 13.6 %attention.3.refs_4_ = bf16[512,512]{1,0:T(8,128)(2,1)} custom-call(f32[1024,640]{1,0:T(8,128)} %get-tuple-element.121.query_ref.pair_ref.refs_0_.refs_1_, f32[1024,640]{1,0:T(8,128)} %get-tuple-element.121.query_ref.pair_ref.refs_0_.refs_1_, f32[1024,128]{1,0:T(8,128)} %get-tuple-element.110.cos_ref.refs_2_, f32[1024,128]{1,0:T(8,128)} %get-tuple-element.111.sin_ref.refs_3_), custom_call_target="tpu_custom_call" | custom-call | flops 4294967296 | bytes 3145728 | tf_op jit(solution)/shard_map/attention_fwd/attention/pallas_call | solution.py:233
  177.6 5.7 %fusion.12.refs_0_ = f32[256,1408]{1,0:T(8,128)} fusion(bf16[256,2048]{1,0:T(8,128)(2,1)S(1)} %copy-done.27, bf16[2048,2048]{1,0:T(8,128)(2,1)} %all-gather.6.cloned.1.call-done.triple_w_ref), kind=kOutput, calls=%fused_computation.19 | convolution fusion | flops 1476395008 | bytes 8257536 | tf_op jit(solution)/shard_map/swiglu_grad/dot_general | solution.py:51
  183.3 5.8 %fusion.10.refs_1_ = f32[256,1408]{1,0:T(8,128)} fusion(bf16[256,2048]{1,0:T(8,128)(2,1)S(1)} %copy-done.29, bf16[2048,2048]{1,0:T(8,128)(2,1)} %all-gather.6.cloned.1.call-done.triple_w_ref), kind=kOutput, calls=%fused_computation.17 | convolution fusion | flops 1476395008 | bytes 8257536 | tf_op jit(solution)/shard_map/swiglu_grad/dot_general | solution.py:51
  189.2 4.2 fusion.8.refs_2_
  193.4 4.3 fusion.6.refs_3_
  201.5 8.2 %collective-permute-done.13.refs_6_ = bf16[512,512]{1,0:T(8,128)(2,1)} collective-permute-done((bf16[512,512]{1,0:T(8,128)(2,1)}, bf16[512,512]{1,0:T(8,128)(2,1)}, u32[]{:S(2)}, u32[]{:S(2)}) %collective-permute-start.13) | collective-permute-done | bytes 524320 | tf_op jit(solution)/shard_map/mixed_ring/ppermute | solution.py:68
  209.9 32.2 %mlp.2 = (f32[512,2048]{1,0:T(8,128)}, bf16[512,1408]{1,0:T(8,128)(2,1)}, bf16[512,2048]{1,0:T(8,128)(2,1)}, bf16[4,512,512]{2,1,0:T(8,128)(2,1)}) custom-call(s32[6]{0:T(128)} %get-tuple-element.209.plan_ref, bf16[1024,2048]{1,0:T(8,128)(2,1)} %convolution_convert_fusion.resid_in_ref, f32[1024,1]{1,0:T(8,128)} %copy.163.weight_ref, ...), custom_call_target="tpu_custom_call" | custom-call | flops 20401094656 | bytes 36700160 | tf_op jit(solution)/shard_map/mlp/mlp/pallas_call | solution.py:564
  243.5 7.4 %convolution_convert_fusion.3 = bf16[512,2048]{1,0:T(8,128)(2,1)} fusion(bf16[512,1408]{1,0:T(8,128)(2,1)S(1)} %copy-done.35, bf16[2048,2048]{1,0:T(8,128)(2,1)} %all-gather.6.cloned.1.call-done.triple_w_ref), kind=kOutput, calls=%fused_computation.8 | convolution fusion | flops 2953838592 | bytes 9306112 | tf_op jit(solution)/shard_map/mlp/dot_general | solution.py:55
  255.0 32.5 %mlp.3 = (f32[512,2048]{1,0:T(8,128)}, bf16[512,1408]{1,0:T(8,128)(2,1)}, bf16[512,2048]{1,0:T(8,128)(2,1)}, bf16[512,512]{1,0:T(8,128)(2,1)}, bf16[512,512]{1,0...) custom-call(s32[6]{0:T(128)} %get-tuple-element.208.plan_ref, ...), custom_call_target="tpu_custom_call" | custom-call | flops 20401094656 | bytes 36700160 | tf_op jit(solution)/shard_map/mlp/mlp/pallas_call | solution.py:564
  293.7 5.1 %fusion.17.refs_1_ = f32[512,2048]{1,0:T(8,128)} fusion(bf16[512,2048]{1,0:T(8,128)(2,1)} %get-tuple-element.143, pred[1024,512]{1,0:T(32,128)(4,1)S(1)} %iota_compare_fusion), kind=kOutput, calls=%fused_computation.34 | convolution fusion | flops 1073741824 | bytes 6553600 | tf_op jit(solution)/shard_map/mlp/dot_general | solution.py:61
  304.3 6.4 %convolution_convert_fusion.2 = bf16[512,2048]{1,0:T(8,128)(2,1)S(1)} fusion(bf16[512,1408]{1,0:T(8,128)(2,1)S(1)} %copy-done.34, bf16[2048,2048]{1,0:T(8,128)(2,1)} %all-gather.6.cloned.1.call-done.triple_w_ref), kind=kOutput, calls=%fused_computation.7 | convolution fusion | flops 2953838592 | bytes 9306112 | tf_op jit(solution)/shard_map/mlp/dot_general | solution.py:55
  318.2 12.7 %attention_back.2 = (bf16[512,512]{1,0:T(8,128)(2,1)}, f32[1024,128]{1,0:T(8,128)}) custom-call(f32[1024,640]{1,0:T(8,128)} %get-tuple-element.121.query_ref.pair_ref.refs_0_.refs_1_, f32[1024,640]{1,0:T(8,128)} %get-tuple-element.121.query_ref.pair_ref.refs_0_.refs_1_, f32[1024,128]{1,0:T(8,128)} %get-tuple-element.110.cos_ref.refs_2_, ...), custom_call_target="tpu_custom_call" | custom-call | flops 5368709120 | bytes 4194304 | tf_op jit(solution)/shard_map/mlp/attention_back/pallas_call | solution.py:278
  332.1 21.7 %attention_back.3 = (bf16[512,512]{1,0:T(8,128)(2,1)}, bf16[1024,128]{1,0:T(8,128)(2,1)}) custom-call(f32[1024,640]{1,0:T(8,128)} %get-tuple-element.121.query_ref.pair_ref.refs_0_.refs_1_, f32[1024,640]{1,0:T(8,128)} %get-tuple-element.121.query_ref.pair_ref.refs_0_.refs_1_, f32[1024,128]{1,0:T(8,128)} %get-tuple-element.110.cos_ref.refs_2_, ...), custom_call_target="tpu_custom_call" | custom-call | flops 10737418240 | bytes 4194304 | tf_op jit(solution)/shard_map/attention_bwd/attention_back/pallas_call | solution.py:278
  353.8 11.0 %entry_back.1 = (bf16[512,2048]{1,0:T(8,128)(2,1)}, bf16[512,512]{1,0:T(8,128)(2,1)}) custom-call(s32[1,1024]{1,0:T(1,128)} %bitcast.105, bf16[512,2048]{1,0:T(8,128)(2,1)} %get-tuple-element.113.vectors_ref, f32[1,2048]{1,0:T(1,128)} %bitcast.115, bf16[2048,2048]{1,0:T(8,128)(2,1)} %all-gather.6.cloned.1.call-done.triple_w_ref, ...), custom_call_target="tpu_custom_call" | custom-call | flops 3087007744 | bytes 17825792 | tf_op jit(solution)/shard_map/entry_bwd/entry_back/pallas_call | solution.py:416
  372.5 5.4 %all-to-all-done.1 = bf16[8,64,512]{2,1,0:T(8,128)(2,1)S(1)} async-done(((bf16[8,64,512]{2,1,0:T(8,128)(2,1)}), bf16[8,64,512]{2,1,0:T(8,128)(2,1)S(1)}, u32[]{:S(2)}, u32[]{:S(2)}) %all-to-all-start.1) | async-done | bytes 524320 | tf_op jit(solution)/shard_map/entry_bwd/all_to_all | solution.py:91
  389.8 4.6 all-to-all-start.2
  397.9 9.6 %hyper_back_units.1 = (f32[512,512]{1,0:T(8,128)}, bf16[512,512]{1,0:T(8,128)(2,1)}, bf16[128,4608]{1,0:T(8,128)(2,1)}, f32[8,512]{1,0:T(8,128)}) custom-call(bf16[64,512]{1,0:T(8,128)(2,1)} %copy-done.18, bf16[64,512]{1,0:T(8,128)(2,1)} %copy-done.33, bf16[64,512]{1,0:T(8,128)(2,1)} %copy-done.32, bf16[64,512]{1,0:T(8,128)(2,1)} %copy-done.31, ...), custom_call_target="tpu_custom_call" | custom-call | flops 12884901888 | bytes 6291456 | tf_op jit(solution)/shard_map/hyper_bwd/hyper_back_units/pallas_call | solution.py:878
  407.5 13.5 %all-to-all-done.2 = bf16[8,64,2048]{2,1,0:T(8,128)(2,1)} async-done(((bf16[8,64,2048]{2,1,0:T(8,128)(2,1)}), bf16[8,64,2048]{2,1,0:T(8,128)(2,1)}, u32[]{:S(2)}, u32[]{:S(2)}) %all-to-all-start.2) | async-done | bytes 2097184 | tf_op jit(solution)/shard_map/hyper_bwd/all_to_all | solution.py:91
  425.4 13.5 %hyper_back_slots.1 = (bf16[512,512]{1,0:T(8,128)(2,1)}, bf16[128,1536]{1,0:T(8,128)(2,1)}, f32[8,512]{1,0:T(8,128)}) custom-call(f32[512,512]{1,0:T(8,128)} %get-tuple-element.179.resid_grad_ref, bf16[512,512]{1,0:T(8,128)(2,1)} %get-tuple-element.180.mixed_grad_ref, bf16[512,512]{1,0:T(8,128)(2,1)} %pad_maximum_fusion.7.rows_ref, ...), custom_call_target="tpu_custom_call" | custom-call | flops 10737418240 | bytes 2097152 | tf_op jit(solution)/shard_map/hyper_bwd/hyper_back_slots/pallas_call | solution.py:915
  452.2 7.2 %all-to-all-done.4 = bf16[8,16,1664]{2,1,0:T(8,128)(2,1)S(1)} async-done(((bf16[8,16,1664]{2,1,0:T(8,128)(2,1)}), bf16[8,16,1664]{2,1,0:T(8,128)(2,1)S(1)}, u32[]{:S(2)}, u32[]{:S(2)}) %all-to-all-start.4) | async-done | bytes 426016 | tf_op jit(solution)/shard_map/grads_out/all_to_all | solution.py:91
  459.4 4.8 all-to-all-start.5
  479.4 7.9 %fusion = f32[1000,512]{1,0:T(8,128)} fusion(bf16[4096,512]{1,0:T(8,128)(2,1)} %all-gather.12.cloned.1.call-done, s32[4096]{0:T(1024)S(1)} %eq.44, s32[1000]{0:T(1024)S(1)} %iota_add_fusion), kind=kOutput, calls=%fused_computation.1 | convolution fusion | flops 4198400000 | bytes 6262688 | tf_op jit(solution)/shard_map/grads_out/dot_general | solution.py:51
  (264 shorter events, 143.6 us)
Async XLA Ops:
  7.2 118.2 %all-gather.6.cloned.1.call-start = ((), (), s32[]{:S(2)}) async-start(), calls=%async_computation.9 | async-start | bytes 9437184 | tf_op jit(solution)/shard_map/first_weights/all_gather | solution.py:988
  12.2 28.3 %collective-permute-start = (bf16[256,2048]{1,0:T(8,128)(2,1)S(1)}, bf16[256,2048]{1,0:T(8,128)(2,1)S(1)}, u32[]{:S(2)}, u32[]{:S(2)}) collective-permute-start(bf16[256,2048]{1,0:T(8,128)(2,1)S(1)} %copy-done.26), channel_id=1, source_target_pairs={{0,1},{1,2},{2,3},{3,0},{4,5},{5,6},{6,7},{7,4},{8,9},{9,10},{10,1... | collective-permute-start | bytes 3145736 | tf_op jit(solution)/shard_map/cot_ring/ppermute | solution.py:68
  33.2 25.4 %all-to-all-start = ((bf16[8,128,512]{2,1,0:T(8,128)(2,1)}), bf16[8,128,512]{2,1,0:T(8,128)(2,1)S(1)}, u32[]{:S(2)}, u32[]{:S(2)}) async-start(bf16[8,128,512]{2,1,0:T(8,128)(2,1)} %select_select_fusion), calls=%async_computation | async-start | bytes 2097152 | tf_op jit(solution)/shard_map/lookup/all_to_all | solution.py:1000
  36.7 173.2 %all-gather.10.cloned.1.call-start = ((), (), s32[]{:S(2)}) async-start(), calls=%async_computation.11 | async-start | bytes 12976128 | tf_op jit(solution)/shard_map/cot_ring/all_gather | solution.py:1012
  40.5 26.4 %collective-permute-start.1 = (bf16[256,2048]{1,0:T(8,128)(2,1)S(1)}, bf16[256,2048]{1,0:T(8,128)(2,1)}, u32[]{:S(2)}, u32[]{:S(2)}) collective-permute-start(bf16[256,2048]{1,0:T(8,128)(2,1)S(1)} %collective-permute-done), channel_id=1, source_target_pairs={{0,1},{1,2},{2,3},{3,0},{4,5},{5,6},{6,7},{7,4},{8,9},{9,10},{10,1... | collective-permute-start | bytes 3145736 | tf_op jit(solution)/shard_map/cot_ring/ppermute | solution.py:68
  66.9 143.0 %all-gather.8.cloned.1.call-start = ((), (), s32[]{:S(2)}) async-start(), calls=%async_computation.10 | async-start | bytes 9437184 | tf_op jit(solution)/shard_map/output_weights/all_gather | solution.py:1042
  67.2 9.4 %collective-permute-start.3 = (s32[1536]{0:T(1024)S(1)}, s32[1536]{0:T(1024)S(1)}, u32[]{:S(2)}, u32[]{:S(2)}) collective-permute-start(s32[1536]{0:T(1024)S(1)} %pad_add_fusion.3), channel_id=1, source_target_pairs={{0,2},{1,3},{2,0},{3,1},{4,6},{5,7},{6,4},{7,5},{8,10},{9,11},{10,... | collective-permute-start | bytes 18440 | tf_op jit(solution)/shard_map/cot_ring/ppermute | solution.py:68
  67.3 9.3 %collective-permute-start.2 = (s32[1536]{0:T(1024)S(1)}, s32[1536]{0:T(1024)S(1)}, u32[]{:S(2)}, u32[]{:S(2)}) collective-permute-start(s32[1536]{0:T(1024)S(1)} %pad_add_fusion.3), channel_id=1, source_target_pairs={{0,1},{1,2},{2,3},{3,0},{4,5},{5,6},{6,7},{7,4},{8,9},{9,10},{10,1... | collective-permute-start | bytes 18440 | tf_op jit(solution)/shard_map/cot_ring/ppermute | solution.py:68
  69.8 11.2 %collective-permute-start.6 = (bf16[128,512]{1,0:T(8,128)(2,1)S(1)}, bf16[128,512]{1,0:T(8,128)(2,1)S(1)}, u32[]{:S(2)}, u32[]{:S(2)}) collective-permute-start(bf16[128,512]{1,0:T(8,128)(2,1)S(1)} %convert_reduce_fusion.1), channel_id=1, source_target_pairs={{0,2},{1,3},{2,0},{3,1},{4,6},{5,7},{6,4},{7,5},{8,10},{9,11},{10,... | collective-permute-start | bytes 393224 | tf_op jit(solution)/shard_map/hyper_wide/ppermute | solution.py:68
  72.7 8.3 %collective-permute-start.5 = (bf16[128,512]{1,0:T(8,128)(2,1)S(1)}, bf16[128,512]{1,0:T(8,128)(2,1)S(1)}, u32[]{:S(2)}, u32[]{:S(2)}) collective-permute-start(bf16[128,512]{1,0:T(8,128)(2,1)S(1)} %convert_reduce_fusion.1), channel_id=1, source_target_pairs={{0,1},{1,2},{2,3},{3,0},{4,5},{5,6},{6,7},{7,4},{8,9},{9,10},{10,1... | collective-permute-start | bytes 393224 | tf_op jit(solution)/shard_map/hyper_wide/ppermute | solution.py:68
  100.6 17.7 %collective-permute-start.10 = (bf16[256,512]{1,0:T(8,128)(2,1)S(1)}, bf16[256,512]{1,0:T(8,128)(2,1)S(1)}, u32[]{:S(2)}, u32[]{:S(2)}) collective-permute-start(bf16[256,512]{1,0:T(8,128)(2,1)S(1)} %copy-done.16), channel_id=1, source_target_pairs={{0,3},{1,0},{2,1},{3,2},{4,7},{5,4},{6,5},{7,6},{8,11},{9,8},{10,9... | collective-permute-start | bytes 786440 | tf_op jit(solution)/shard_map/output_weights/ppermute | solution.py:68
  102.5 21.8 %collective-permute-start.9 = (bf16[256,512]{1,0:T(8,128)(2,1)S(1)}, bf16[256,512]{1,0:T(8,128)(2,1)S(1)}, u32[]{:S(2)}, u32[]{:S(2)}) collective-permute-start(bf16[256,512]{1,0:T(8,128)(2,1)S(1)} %copy-done.16), channel_id=1, source_target_pairs={{0,2},{1,3},{2,0},{3,1},{4,6},{5,7},{6,4},{7,5},{8,10},{9,11},{10,... | collective-permute-start | bytes 786440 | tf_op jit(solution)/shard_map/output_weights/ppermute | solution.py:68
  104.0 20.2 %collective-permute-start.8 = (bf16[256,512]{1,0:T(8,128)(2,1)S(1)}, bf16[256,512]{1,0:T(8,128)(2,1)S(1)}, u32[]{:S(2)}, u32[]{:S(2)}) collective-permute-start(bf16[256,512]{1,0:T(8,128)(2,1)S(1)} %copy-done.16), channel_id=1, source_target_pairs={{0,1},{1,2},{2,3},{3,0},{4,5},{5,6},{6,7},{7,4},{8,9},{9,10},{10,1... | collective-permute-start | bytes 786440 | tf_op jit(solution)/shard_map/output_weights/ppermute | solution.py:68
  125.5 192.7 %reduce-scatter.4.cloned.1.call-start = ((), (), s32[]{:S(2)}) async-start(), calls=%async_computation.12 | async-start | bytes 2621440 | tf_op jit(solution)/shard_map/mlp/reduce_scatter | solution.py:1141
  128.6 48.6 %collective-permute-start.11 = (bf16[256,2048]{1,0:T(8,128)(2,1)}, bf16[256,2048]{1,0:T(8,128)(2,1)}, u32[]{:S(2)}, u32[]{:S(2)}) collective-permute-start(bf16[256,2048]{1,0:T(8,128)(2,1)} %collective-permute-done.1), channel_id=1, source_target_pairs={{0,1},{1,2},{2,3},{3,0},{4,5},{5,6},{6,7},{7,4},{8,9},{9,10},{10,1... | collective-permute-start | bytes 3145736 | tf_op jit(solution)/shard_map/cot_ring/ppermute | solution.py:68
  146.7 50.9 %collective-permute-start.14 = (bf16[512,512]{1,0:T(8,128)(2,1)}, bf16[512,512]{1,0:T(8,128)(2,1)}, u32[]{:S(2)}, u32[]{:S(2)}) collective-permute-start(bf16[512,512]{1,0:T(8,128)(2,1)} %attention.2.refs_4_), channel_id=1, source_target_pairs={{0,3},{1,0},{2,1},{3,2},{4,7},{5,4},{6,5},{7,6},{8,11},{9,8},{10,9... | collective-permute-start | bytes 1572872 | tf_op jit(solution)/shard_map/mixed_ring/ppermute | solution.py:68
  150.4 43.0 %collective-permute-start.12 = (bf16[512,512]{1,0:T(8,128)(2,1)}, bf16[512,512]{1,0:T(8,128)(2,1)}, u32[]{:S(2)}, u32[]{:S(2)}) collective-permute-start(bf16[512,512]{1,0:T(8,128)(2,1)} %attention.2.refs_4_), channel_id=1, source_target_pairs={{0,1},{1,2},{2,3},{3,0},{4,5},{5,6},{6,7},{7,4},{8,9},{9,10},{10,1... | collective-permute-start | bytes 1572872 | tf_op jit(solution)/shard_map/mixed_ring/ppermute | solution.py:68
  169.9 27.8 %collective-permute-start.16 = (bf16[512,512]{1,0:T(8,128)(2,1)}, bf16[512,512]{1,0:T(8,128)(2,1)}, u32[]{:S(2)}, u32[]{:S(2)}) collective-permute-start(bf16[512,512]{1,0:T(8,128)(2,1)} %attention.3.refs_4_), channel_id=1, source_target_pairs={{0,3},{1,0},{2,1},{3,2},{4,7},{5,4},{6,5},{7,6},{8,11},{9,8},{10,9... | collective-permute-start | bytes 1572872 | tf_op jit(solution)/shard_map/mixed_ring/ppermute | solution.py:68
  173.7 27.9 %collective-permute-start.15 = (bf16[512,512]{1,0:T(8,128)(2,1)}, bf16[512,512]{1,0:T(8,128)(2,1)}, u32[]{:S(2)}, u32[]{:S(2)}) collective-permute-start(bf16[512,512]{1,0:T(8,128)(2,1)} %attention.3.refs_4_), channel_id=1, source_target_pairs={{0,1},{1,2},{2,3},{3,0},{4,5},{5,6},{6,7},{7,4},{8,9},{9,10},{10,1... | collective-permute-start | bytes 1572872 | tf_op jit(solution)/shard_map/mixed_ring/ppermute | solution.py:68
  193.4 16.3 %collective-permute-start.13 = (bf16[512,512]{1,0:T(8,128)(2,1)}, bf16[512,512]{1,0:T(8,128)(2,1)}, u32[]{:S(2)}, u32[]{:S(2)}) collective-permute-start(bf16[512,512]{1,0:T(8,128)(2,1)} %collective-permute-done.12.refs_5_), channel_id=1, source_target_pairs={{0,1},{1,2},{2,3},{3,0},{4,5},{5,6},{6,7},{7,4},{8,9},{9,10},{10,1... | collective-permute-start | bytes 1572872 | tf_op jit(solution)/shard_map/mixed_ring/ppermute | solution.py:68
  209.7 44.4 %collective-permute-start.17 = (bf16[512,512]{1,0:T(8,128)(2,1)}, bf16[512,512]{1,0:T(8,128)(2,1)S(1)}, u32[]{:S(2)}, u32[]{:S(2)}) collective-permute-start(bf16[512,512]{1,0:T(8,128)(2,1)} %collective-permute-done.15.refs_5_), channel_id=1, source_target_pairs={{0,1},{1,2},{2,3},{3,0},{4,5},{5,6},{6,7},{7,4},{8,9},{9,10},{10,1... | collective-permute-start | bytes 1572872 | tf_op jit(solution)/shard_map/mlp/ppermute | solution.py:68
  242.1 147.0 %reduce-scatter.6.cloned.1.call-start = ((), (), s32[]{:S(2)}) async-start(), calls=%async_computation.13 | async-start | bytes 3276800 | tf_op jit(solution)/shard_map/layer_out/reduce_scatter | solution.py:1184
  287.5 14.2 %collective-permute-start.18 = (bf16[512,512]{1,0:T(8,128)(2,1)}, bf16[512,512]{1,0:T(8,128)(2,1)}, u32[]{:S(2)}, u32[]{:S(2)}) collective-permute-start(bf16[512,512]{1,0:T(8,128)(2,1)} %get-tuple-element.141), channel_id=1, source_target_pairs={{0,1},{1,2},{2,3},{3,0},{4,5},{5,6},{6,7},{7,4},{8,9},{9,10},{10,1... | collective-permute-start | bytes 1572872 | tf_op jit(solution)/shard_map/mlp/ppermute | solution.py:68
  303.6 13.2 %collective-permute-start.19 = (bf16[512,512]{1,0:T(8,128)(2,1)}, bf16[512,512]{1,0:T(8,128)(2,1)}, u32[]{:S(2)}, u32[]{:S(2)}) collective-permute-start(bf16[512,512]{1,0:T(8,128)(2,1)} %add_convert_fusion.3), channel_id=1, source_target_pairs={{0,1},{1,2},{2,3},{3,0},{4,5},{5,6},{6,7},{7,4},{8,9},{9,10},{10,1... | collective-permute-start | bytes 1572872 | tf_op jit(solution)/shard_map/mlp/ppermute | solution.py:68
  318.0 13.1 %collective-permute-start.20 = (bf16[512,512]{1,0:T(8,128)(2,1)S(1)}, bf16[512,512]{1,0:T(8,128)(2,1)S(1)}, u32[]{:S(2)}, u32[]{:S(2)}) collective-permute-start(bf16[512,512]{1,0:T(8,128)(2,1)S(1)} %add_convert_fusion.2), channel_id=1, source_target_pairs={{0,1},{1,2},{2,3},{3,0},{4,5},{5,6},{6,7},{7,4},{8,9},{9,10},{10,1... | collective-permute-start | bytes 1572872 | tf_op jit(solution)/shard_map/mlp/ppermute | solution.py:68
  364.8 13.2 %all-to-all-start.1 = ((bf16[8,64,512]{2,1,0:T(8,128)(2,1)}), bf16[8,64,512]{2,1,0:T(8,128)(2,1)S(1)}, u32[]{:S(2)}, u32[]{:S(2)}) async-start(bf16[8,64,512]{2,1,0:T(8,128)(2,1)} %bitcast.92), calls=%async_computation.3 | async-start | bytes 1048576 | tf_op jit(solution)/shard_map/entry_bwd/all_to_all | solution.py:91
  368.3 103.4 %reduce-scatter.8.cloned.1.call-start = ((), (), s32[]{:S(2)}) async-start(), calls=%async_computation.14 | async-start | bytes 1966080 | tf_op jit(solution)/shard_map/layer_out/reduce_scatter | solution.py:1225
  389.8 31.2 %all-to-all-start.2 = ((bf16[8,64,2048]{2,1,0:T(8,128)(2,1)}), bf16[8,64,2048]{2,1,0:T(8,128)(2,1)}, u32[]{:S(2)}, u32[]{:S(2)}) async-start(bf16[8,64,2048]{2,1,0:T(8,128)(2,1)} %bitcast.32), calls=%async_computation.5 | async-start | bytes 4194304 | tf_op jit(solution)/shard_map/hyper_bwd/all_to_all | solution.py:91
  421.0 20.3 %all-to-all-start.3 = ((bf16[8,16,4608]{2,1,0:T(8,128)(2,1)}), bf16[8,16,4608]{2,1,0:T(8,128)(2,1)S(1)}, u32[]{:S(2)}, u32[]{:S(2)}) async-start(bf16[8,16,4608]{2,1,0:T(8,128)(2,1)} %bitcast.86), calls=%async_computation.6 | async-start | bytes 2359296 | tf_op jit(solution)/shard_map/hyper_bwd/all_to_all | solution.py:91
  424.6 54.8 %all-gather.12.cloned.1.call-start = ((), (), s32[]{:S(2)}) async-start(), calls=%async_computation.15 | async-start | bytes 4718592 | tf_op jit(solution)/shard_map/grads_out/all_gather | solution.py:1261
  447.0 12.4 %all-to-all-start.4 = ((bf16[8,16,1664]{2,1,0:T(8,128)(2,1)}), bf16[8,16,1664]{2,1,0:T(8,128)(2,1)S(1)}, u32[]{:S(2)}, u32[]{:S(2)}) async-start(bf16[8,16,1664]{2,1,0:T(8,128)(2,1)} %bitcast.36), calls=%async_computation.7 | async-start | bytes 851968 | tf_op jit(solution)/shard_map/grads_out/all_to_all | solution.py:91
  459.4 11.6 %all-to-all-start.5 = ((bf16[4,16,2048]{2,1,0:T(8,128)(2,1)}), bf16[4,16,2048]{2,1,0:T(8,128)(2,1)S(1)}, u32[]{:S(2)}, u32[]{:S(2)}) async-start(bf16[4,16,2048]{2,1,0:T(8,128)(2,1)} %bitcast.39), calls=%async_computation.8 | async-start | bytes 524288 | tf_op jit(solution)/shard_map/grads_out/all_to_all | solution.py:1264
  (47 other events, 394.9 us)
Sparse Core Ops, SparseCore 0:
  12.3 63.2 all-gather.5
  77.5 68.3 all-gather.9
  147.8 54.3 all-gather.7
  242.2 44.8 reduce-scatter.3
  332.2 53.6 reduce-scatter.5
  389.3 35.8 reduce-scatter.7
  441.4 37.8 all-gather.11

commit v5 on v4

--- a/solution.py
+++ b/solution.py
@@ -141,37 +141,39 @@
     parts = [jnp.where(query_at >= key_at, own, NEG)]
     if first > 0:
         parts.insert(0, times_trans(keys[:first], query_block))
-    largest = parts[0].max(axis=0, keepdims=True)
-    for part in parts[1:]:
-        largest = jnp.maximum(largest, part.max(axis=0, keepdims=True))
-    parts = [jnp.exp(part - largest) for part in parts]
-    total = sum(part.sum(axis=0, keepdims=True) for part in parts)
-    return parts, 1.0 / total
-
-
-def attention_kernel(block_rows, base, query_ref, pair_ref, cos_ref, sin_ref, out_ref):
+    return parts
+
+
+def attention_kernel(
+    block_rows, base, query_ref, pair_ref, cos_ref, sin_ref, out_ref, total_ref
+):
     queries, keys, values = attention_operands(query_ref, pair_ref, cos_ref, sin_ref)
     for first in range(base, queries.shape[0], block_rows):
         rows = slice(first, first + block_rows)
         heads = []
         for head in range(queries.shape[1] // HD):
             query_block = queries[rows, head * HD : (head + 1) * HD]
-            parts, inverse = scores_by_key(keys, query_block, first)
+            parts = scores_by_key(keys, query_block, first)
+            largest = parts[0].max(axis=0, keepdims=True)
+            for part in parts[1:]:
+                largest = jnp.maximum(largest, part.max(axis=0, keepdims=True))
+            parts = [jnp.exp(part - largest) for part in parts]
+            total = sum(part.sum(axis=0, keepdims=True) for part in parts)
             at = 0
             mixed = None
             for part in parts:
-                here = trans_times(
-                    values[at : at + part.shape[0]], (part * inverse).astype(jnp.bfloat16)
-                )
+                here = trans_times(values[at : at + part.shape[0]], part.astype(jnp.bfloat16))
                 mixed = here if mixed is None else mixed + here
                 at += part.shape[0]
+            mixed = mixed * (1.0 / total)
+            out_rows = slice(first - base, first - base + block_rows)
+            total_ref[0, head : head + 1, out_rows] = largest + jnp.log(total)
             heads.append(mixed)
-        out_rows = slice(first - base, first - base + block_rows)
         out_ref[out_rows, :] = jnp.concatenate(heads, axis=0).T.astype(jnp.bfloat16)
 
 
 def attention_back_kernel(
-    block_rows, base, query_ref, pair_ref, cos_ref, sin_ref, grad_ref, add_ref, query_out, pair_out, acc_ref
+    block_rows, base, query_ref, pair_ref, cos_ref, sin_ref, grad_ref, mixed_ref, total_ref, add_ref, query_out, pair_out, acc_ref
 ):
     bfloat = jnp.bfloat16
     queries, keys, values = attention_operands(query_ref, pair_ref, cos_ref, sin_ref)
@@ -183,20 +185,23 @@
     for first in range(base, queries.shape[0], block_rows):
         rows = slice(first, first + block_rows)
         out_rows = slice(first - base, first - base + block_rows)
+        deltas = mixed_ref[out_rows, :].astype(jnp.float32) * grad_ref[out_rows, :].astype(
+            jnp.float32
+        )
+        deltas = deltas.T
         heads = []
         for head in range(queries.shape[1] // HD):
             lanes = slice(head * HD, (head + 1) * HD)
             query_block = queries[rows, lanes]
             grad_block = grad_ref[out_rows, lanes]
-            parts, inverse = scores_by_key(keys, query_block, first)
-            parts = [part * inverse for part in parts]
+            parts = scores_by_key(keys, query_block, first)
+            row_total = total_ref[0, head : head + 1, out_rows]
+            parts = [jnp.exp(part - row_total) for part in parts]
+            delta = deltas[head * HD : (head + 1) * HD].sum(axis=0, keepdims=True)
             at = 0
             prob_grads = []
-            delta = 0.0
             for part in parts:
-                prob_grad = times_trans(values[at : at + part.shape[0]], grad_block)
-                delta = delta + (part * prob_grad).sum(axis=0, keepdims=True)
-                prob_grads.append(prob_grad)
+                prob_grads.append(times_trans(values[at : at + part.shape[0]], grad_block))
                 at += part.shape[0]
             at = 0
             query_grad = None
@@ -239,8 +244,14 @@
             pl.BlockSpec((keys, wide), lambda at: (0, 0)),
             pl.BlockSpec((keys, wide), lambda at: (0, 0)),
         ],
-        out_specs=pl.BlockSpec((rows, wide), lambda at: (0, at)),
-        out_shape=jax.ShapeDtypeStruct((rows, query_width), jnp.bfloat16),
+        out_specs=[
+            pl.BlockSpec((rows, wide), lambda at: (0, at)),
+            pl.BlockSpec((1, 8, rows), lambda at: (at, 0, 0)),
+        ],
+        out_shape=[
+            jax.ShapeDtypeStruct((rows, query_width), jnp.bfloat16),
+            jax.ShapeDtypeStruct((pairs, 8, rows), jnp.float32),
+        ],
         cost_estimate=cost(
             8 * query_width * rows * keys, 6 * query_width * keys, query_width * keys * 10
         ),
@@ -249,7 +260,7 @@
     )(seq_triple, seq_triple, cosine, sine)
 
 
-def attention_back(seq_triple, cosine, sine, mixed_grad, base, before):
+def attention_back(seq_triple, cosine, sine, mixed_grad, mixed, totals, base, before):
     length = seq_triple.shape[0]
     rows, query_width = mixed_grad.shape
     pairs = query_width // (2 * HD)
@@ -262,8 +273,10 @@
         pl.BlockSpec((keys, wide), lambda at: (0, 0)),
         pl.BlockSpec((keys, wide), lambda at: (0, 0)),
         pl.BlockSpec((rows, wide), lambda at: (0, at)),
+        pl.BlockSpec((rows, wide), lambda at: (0, at)),
+        pl.BlockSpec((1, 8, rows), lambda at: (at, 0, 0)),
     ]
-    operands = [seq_triple, seq_triple, cosine, sine, mixed_grad]
+    operands = [seq_triple, seq_triple, cosine, sine, mixed_grad, mixed, totals]
     if before is not None:
         specs.append(pl.BlockSpec((keys, wide), lambda at: (0, 0)))
         operands.append(before)
@@ -272,7 +285,7 @@
         given = refs[: len(operands)]
         add_ref = None if before is None else given[-1]
         attention_back_kernel(
-            min(256, rows), base, *given[:5], add_ref, *refs[len(operands) :]
+            min(256, rows), base, *given[:7], add_ref, *refs[len(operands) :]
         )
 
     return pl.pallas_call(
@@ -438,6 +451,43 @@
         compiler_params=pltpu.CompilerParams(vmem_limit_bytes=VMEM_LIMIT),
         name="entry_back",
     )(tokens[None, :], vectors, gain[None, :], weights, project, pair_out, *mid_parts, *query_parts)
+
+
+def swiglu_grad_kernel(first, *refs):
+    positions = (len(refs) - 3) // 3
+    grads_from, weights_from = refs[:positions], refs[positions]
+    outs = refs[positions + 1 : 2 * positions + 1]
+    weights_ref, cots, arrived = refs[-positions - 2], refs[-positions - 1 : -1], refs[-1]
+    unit_width = weights_ref.shape[1]
+    copies = [
+        pltpu.make_async_copy(
+            weights_from.at[:, pl.ds(first, unit_width)], weights_ref, arrived.at[positions]
+        )
+    ]
+    for at in range(positions):
+        copies.append(pltpu.make_async_copy(grads_from[at], cots[at], arrived.at[at]))
+    for copy in copies:
+        copy.start()
+    copies[0].wait()
+    for at in range(positions):
+        copies[at + 1].wait()
+        outs[at][...] = matmul(cots[at][...], weights_ref[...])
+
+
+def swiglu_products(cots, weights, first, unit_width):
+    rows, width = cots[0].shape
+    return pl.pallas_call(
+        partial(swiglu_grad_kernel, first),
+        in_specs=[pl.BlockSpec(memory_space=pl.ANY)] * (len(cots) + 1),
+        out_specs=[pl.BlockSpec(memory_space=pltpu.VMEM)] * len(cots),
+        out_shape=[jax.ShapeDtypeStruct((rows, unit_width), jnp.float32)] * len(cots),
+        scratch_shapes=[pltpu.VMEM((width, unit_width), weights.dtype)]
+        + [pltpu.VMEM((rows, width), cots[0].dtype)] * len(cots)
+        + [pltpu.SemaphoreType.DMA((len(cots) + 1,))],
+        cost_estimate=cost(len(cots) * rows * width * unit_width, 4 * width * unit_width),
+        compiler_params=pltpu.CompilerParams(vmem_limit_bytes=VMEM_LIMIT),
+        name="swiglu_products",
+    )(*cots, weights)
 
 
 def mlp_kernel(
@@ -1053,7 +1103,9 @@
     with jax.named_scope("attention_fwd"):
         block_rows = min(512, length)
         block_total = length // block_rows
-        first_mixed = attention(seq_triple, cosine, sine, query_width, 0, block_rows)
+        first_mixed, first_totals = attention(
+            seq_triple, cosine, sine, query_width, 0, block_rows
+        )
 
     with jax.named_scope("mlp_rows"):
         late_ids, late_tokens = tie_all(first_mixed, packed_ids, seq_tokens)
@@ -1075,7 +1127,9 @@
         seq_triple = tie(seq_triple, resid_in)
         mixed_parts = [[first_mixed]]
         for first in range(block_rows, length, block_rows):
-            lm_mixed = attention(seq_triple, cosine, sine, query_width, first, block_rows)
+            lm_mixed, last_totals = attention(
+                seq_triple, cosine, sine, query_width, first, block_rows
+            )
             mixed_parts.append([lm_mixed])
     with jax.named_scope("mixed_ring"):
         for block_idx, parts in enumerate(mixed_parts):
@@ -1085,18 +1139,24 @@
                 parts.append(ring(parts[-1]))
             parts.append(last_part)
 
-    def share(values):
+    def share_slice(values):
         rows, width = values.shape
         split = values.reshape(rows, dp_size, tensor_size, width // (dp_size * tensor_size))
         return lax.dynamic_index_in_dim(split, tensor_at, 2, keepdims=False).reshape(
             rows, width // tensor_size
         )
 
-    shares = [share(array) for array in (first_in, mixed, second_in, activated)]
+    def share(values, position):
+        width = values.shape[1]
+        depth = width // (dp_size * tensor_size)
+        row = lax.broadcasted_iota(jnp.int32, (width, width // tensor_size), 0)
+        column = lax.broadcasted_iota(jnp.int32, (width, width // tensor_size), 1)
+        held = (column // depth * tensor_size + position) * depth + column % depth
+        return matmul(values, (row == held).astype(bfloat)).astype(bfloat)
 
     with jax.named_scope("swiglu_grad"):
-        late_cots = tie(cot_blocks, lm_mixed)
-        swiglu_grads = [matmul(cot, full_downward) for cot in late_cots]
+        late_cots = tie(cot_blocks, lm_mixed, mixed_parts[0][1])
+        swiglu_grads = swiglu_products(late_cots, first_weights, triple_width, unit_width)
 
     with jax.named_scope("mlp"):
         places = lax.rem(tensor_at + tensor_size - jnp.arange(tensor_size), tensor_size)
@@ -1109,7 +1169,17 @@
             rows = slice(block_idx * block_rows, (block_idx + 1) * block_rows)
             if block_idx == 0:
                 near = [[later[1], later[-1]] for later in mixed_parts[1:]]
-                parts, near = lax.optimization_barrier((parts, near))
+                late_core = tie(lax.rem(dp_at, 2), lm_mixed)
+                pooled_pairs = all_pooled.reshape(entry_total, dp_size // 2, 2, -1)
+                pooled_kept, pooled_sent = [
+                    lax.dynamic_index_in_dim(pooled_pairs, at, 2, keepdims=False).reshape(
+                        entry_total, -1
+                    )
+                    for at in (late_core, 1 - late_core)
+                ]
+                parts, near, pooled_kept, pooled_sent = lax.optimization_barrier(
+                    (parts, near, pooled_kept, pooled_sent)
+                )
                 for later, (below, above) in zip(mixed_parts[1:], near):
                     later[1], later[-1] = below, above
                     for step in range(2, tensor_size - 1):
@@ -1154,9 +1224,14 @@
                 if step == 2:
                     mid_parts.append(trans_times(seq_hot[rows], mid_low))
                     carried, mid_parts = lax.optimization_barrier((carried, mid_parts))
+                    swiglu_low = tie(swiglu_low, carried)
                 if step == 3:
                     layer_parts.append(times_trans(swiglu_low, full_downward).astype(bfloat))
-                    layer_cut = model_width * 5 // 8
+                    late_position = tie(tensor_at, mid_parts)
+                    shares = [
+                        share_slice(array) for array in (first_in, mixed, second_in)
+                    ] + [share(activated, late_position)]
+                    layer_cut = model_width // 2
                     layer_halves = [
                         jnp.concatenate([part[:, columns] for part in layer_parts], axis=0)
                         for columns in (slice(None, layer_cut), slice(layer_cut, None))
@@ -1169,7 +1244,14 @@
                     query_parts = []
                     for at, mixed_grad in enumerate(mixed_grads):
                         query_part, pair_out = attention_back(
-                            seq_triple, cosine, sine, mixed_grad, at * block_rows, pair_out
+                            seq_triple,
+                            cosine,
+                            sine,
+                            mixed_grad,
+                            first_mixed,
+                            first_totals,
+                            at * block_rows,
+                            pair_out,
                         )
                         query_parts.append(query_part)
                     carried, pair_out = lax.optimization_barrier((carried, pair_out))
@@ -1197,7 +1279,14 @@
             )
     with jax.named_scope("attention_bwd"):
         query_part, pair_out = attention_back(
-            seq_triple, cosine, sine, last_grad, length - block_rows, pair_out
+            seq_triple,
+            cosine,
+            sine,
+            last_grad,
+            lm_mixed,
+            last_totals,
+            length - block_rows,
+            pair_out,
         )
         query_parts.append(query_part)
 
@@ -1212,7 +1301,10 @@
             mid_parts,
             query_parts,
         )
-        project_part = trans_times(all_pooled, entry_part).astype(bfloat)
+        project_sent = trans_times(pooled_sent, entry_part).astype(bfloat)
+        project_kept = trans_times(pooled_kept, entry_part)
+        project_sent = lax.ppermute(project_sent, "dp", [(i, i ^ 1) for i in range(dp_size)])
+        project_part = (project_kept + project_sent.astype(single)).astype(bfloat)
         pooled_shares, project_part = lax.optimization_barrier(
             (to_owners(pooled_part), project_part)
         )
@@ -1220,7 +1312,14 @@
         pooled_grads = from_all(pooled_part)
 
     with jax.named_scope("hyper_bwd"):
-        project_shares = to_owners(tie(project_part, pooled_grads[1]))
+        project_shares = lax.all_to_all(
+            project_part.reshape(dp_size // 2, -1, model_width),
+            "dp",
+            0,
+            0,
+            axis_index_groups=[list(range(first, dp_size, 2)) for first in range(2)],
+            tiled=True,
+        )
     with jax.named_scope("layer_out"):
         layer_far = lax.psum_scatter(
             tie(layer_far, pooled_grads, layer_near), "tensor", scatter_dimension=0, tiled=True
@@ -1269,7 +1368,10 @@
         ).astype(bfloat)
         subword_grad = matmul(row_hot, all_rows)
 
-        gain_grads = share(jnp.concatenate([gain_one[:1], gain_two[:1]], axis=0)).transpose(1, 0).astype(bfloat)
+        gain_grads = jnp.concatenate([gain_one[:1], gain_two[:1]], axis=0)
+        gain_grads = gain_grads.reshape(2, dp_size, tensor_size, -1)
+        gain_grads = lax.dynamic_index_in_dim(gain_grads, tensor_at, 2, keepdims=False)
+        gain_grads = gain_grads.reshape(2, -1).transpose(1, 0).astype(bfloat)
         late = jnp.concatenate([late, jnp.pad(gain_grads, ((0, 0), (0, 126)))], axis=1)
         late = scatter_dp(late)
         depth = early.shape[0]

time: 504 us -> 493 us (0.978)
  matrix products: 60.8 us -> 45.1 us
  starting transfers between devices: 56.1 us -> 65.5 us
    dot_general x7 -> x4, matrix products: 34.4 us -> 18.2 us  [matmul(): return jnp.dot(left, right, preferred_element_type=jnp.float32)]
    pallas_call x0 -> x1, Pallas kernels: none -> 11.4 us  [swiglu_products(): pl.pallas_call(partial(swiglu_grad_kernel, first), in_specs=[pl.BlockSpec...]
    ppermute x24, starting transfers between devices: 32.4 us -> 42.8 us  [ring(): lax.ppermute(values, 'tensor', [(i, (i + shift) % size) for i in range(si...]
    all_to_all x4 -> x3, waiting for transfers between devices: 28.5 us -> 18.2 us  [to_owners(): return lax.all_to_all(blocks, 'dp', 0, 0, tiled=True)]
    pallas_call x2, Pallas kernels: 34.4 us -> 25.4 us  [attention_back(): pl.pallas_call(kernel, grid=(pairs,), in_specs=specs, out_specs=[pl.Block...]
    ppermute x24, waiting for transfers between devices: 41.5 us -> 47.1 us  [ring(): lax.ppermute(values, 'tensor', [(i, (i + shift) % size) for i in range(si...]
    all_to_all x4 -> x3, starting transfers between devices: 15.1 us -> 10.5 us  [to_owners(): return lax.all_to_all(blocks, 'dp', 0, 0, tiled=True)]
    dot_general x3 -> x4, matrix products: 12.6 us -> 13 us  [trans_times(): lax.dot_general(left, right, (((0,), (0,)), ((), ())), preferred_element_...]
  transfers between devices with their start and end apart: 37 -> 38, of which waited for: 19 -> 18; matrix products, arithmetic and copies ran while one was open for 22% -> 18% of each run, Pallas kernels for 37% -> 38%
where the time goes in v5:
time: 493 us; the launch traced here: 484 us
  Pallas kernels  184 us (37%)
  waiting for transfers between devices  91 us (18%)
  starting transfers between devices  65.5 us (13%)
  matrix products  45.1 us (9%)
  local copies, waits for them, and re-layouts  36.3 us (7%)
  other arithmetic  26.3 us (5%)
  blocking collectives  20.1 us (4%)
  between operations  15.4 us (3%)
    pallas_call x2, Pallas kernels, mlp(): pl.pallas_call(partial(mlp_kernel, query_width, unit_width, positions, st...  64.7 us
    ppermute x24, waiting for transfers between devices, ring(): lax.ppermute(values, 'tensor', [(i, (i + shift) % size) for i in range(si...  47.1 us
    ppermute x24, starting transfers between devices, ring(): lax.ppermute(values, 'tensor', [(i, (i + shift) % size) for i in range(si...  42.8 us
    pallas_call x2, Pallas kernels, attention_back(): pl.pallas_call(kernel, grid=(pairs,), in_specs=specs, out_specs=[pl.Block...  25.4 us
    pallas_call x2, Pallas kernels, attention(): pl.pallas_call(partial(attention_kernel, min(256, rows), base), grid=(pai...  20.6 us
    pallas_call x1, Pallas kernels, hyper_wide(): pl.pallas_call(hyper_wide_kernel, grid=(total // block,), in_specs=[rows_...  18.5 us
    all_to_all x3, waiting for transfers between devices, to_owners(): return lax.all_to_all(blocks, 'dp', 0, 0, tiled=True)  18.2 us
    dot_general x4, matrix products, matmul(): return jnp.dot(left, right, preferred_element_type=jnp.float32)  18.2 us
  transfers between devices with their start and end apart: 38, of which 18 were waited for; matrix products, arithmetic and copies ran while one was open for 18% of the time, Pallas kernels for 38%

profile of v5, /device:TPU:0, one launch (start us, length us, event | category | flops | bytes accessed | tf_op | source)
XLA Modules:
  0.0 483.7 jit_solution(17812441959062599488)
XLA Ops:
  15.6 9.2 %all-gather = s32[128,10]{1,0:T(8,128)S(1)} all-gather(s32[16,10]{1,0:T(8,128)S(1)} %pad_add_fusion.2), channel_id=2, replica_groups=mesh['dp'=8,'tensor'=4] {'dp'}, dimensions={0}, use_global_device_ids=true | all-gather | bytes 5760 | tf_op jit(solution)/shard_map/ids/all_gather | solution.py:1036
  25.2 6.7 %gather_fusion = bf16[1024,512]{1,0:T(8,128)(2,1)S(1)} fusion(bf16[4000,512]{1,0:T(8,128)(2,1)} %param.22, s32[1024]{0:T(1024)S(1)} %broadcast_clamp_fusion), kind=kCustom, calls=%fused_computation | custom fusion | bytes 2101248 | tf_op jit(solution)/shard_map/lookup/jit(_take)/gather | solution.py:1048
  45.6 13.0 %all-to-all-done = bf16[8,128,512]{2,1,0:T(8,128)(2,1)S(1)} async-done(((bf16[8,128,512]{2,1,0:T(8,128)(2,1)}), bf16[8,128,512]{2,1,0:T(8,128)(2,1)S(1)}, u32[]{:S(2)}, u32[]{:S(2)}) %all-to-all-start) | async-done | bytes 1048608 | tf_op jit(solution)/shard_map/lookup/all_to_all | solution.py:1050
  58.7 8.1 %collective-permute-done.1.refs_2_ = bf16[256,2048]{1,0:T(8,128)(2,1)} collective-permute-done((bf16[256,2048]{1,0:T(8,128)(2,1)S(1)}, bf16[256,2048]{1,0:T(8,128)(2,1)}, u32[]{:S(2)}, u32[]{:S(2)}) %collective-permute-start.1) | collective-permute-done | bytes 1048608 | tf_op jit(solution)/shard_map/cot_ring/ppermute | solution.py:68
  72.7 3.8 collective-permute-start.7
  82.0 18.5 %hyper_wide.1 = (bf16[512,512]{1,0:T(8,128)(2,1)}, bf16[512,1536]{1,0:T(8,128)(2,1)}, bf16[512,512]{1,0:T(8,128)(2,1)}, f32[512,512]{1,0:T(8,128)}, bf16[512,512...) custom-call(bf16[512,512]{1,0:T(8,128)(2,1)} %pad_maximum_fusion.7.rows_ref, ...), custom_call_target="tpu_custom_call" | custom-call | flops 17179869184 | bytes 12582912 | tf_op jit(solution)/shard_map/hyper_wide/hyper_wide/pallas_call | solution.py:770
  105.6 10.9 %all_gather.23.pooled_ref = bf16[512,512]{1,0:T(8,128)(2,1)S(1)} all-gather(bf16[64,512]{1,0:T(8,128)(2,1)} %get-tuple-element.118), channel_id=1, replica_groups=mesh['dp'=8,'tensor'=4] {'dp'}, dimensions={0}, use_global_device_ids=true | all-gather | bytes 589824 | tf_op jit(solution)/shard_map/pooled_gather/all_gather | solution.py:1088
  116.5 7.8 %collective-permute-done.9 = bf16[256,512]{1,0:T(8,128)(2,1)S(1)} collective-permute-done((bf16[256,512]{1,0:T(8,128)(2,1)S(1)}, bf16[256,512]{1,0:T(8,128)(2,1)S(1)}, u32[]{:S(2)}, u32[]{:S(2)}) %collective-permute-start.9) | collective-permute-done | bytes 262176 | tf_op jit(solution)/shard_map/output_weights/ppermute | solution.py:68
  131.3 9.1 %entry.1 = (bf16[512,2048]{1,0:T(8,128)(2,1)}, f32[1024,640]{1,0:T(8,128)}) custom-call(s32[1024,1]{1,0:T(8,128)} %bitcast.91, bf16[512,512]{1,0:T(8,128)(2,1)} %copy-done.4, bf16[512,2048]{1,0:T(8,128)(2,1)} %project_ref.3, f32[1,2048]{1,0:T(1,128)} %bitcast.112, bf16[2048,2048]{1,0:T(8,128)(2,1)} %all-gather.6.cloned.1.call-done.triple_w_ref.refs_4_), custom_call_target="tpu_custom_call" | custom-call | flops 3758096384 | bytes 9437184 | tf_op jit(solution)/shard_map/entry_vectors/entry/pallas_call | solution.py:355
  140.5 8.2 %attention.2 = (bf16[512,512]{1,0:T(8,128)(2,1)}, f32[4,8,512]{2,1,0:T(8,128)}) custom-call(f32[1024,640]{1,0:T(8,128)} %get-tuple-element.134.query_ref.pair_ref.refs_0_.refs_1_, f32[1024,640]{1,0:T(8,128)} %get-tuple-element.134.query_ref.pair_ref.refs_0_.refs_1_, f32[1024,128]{1,0:T(8,128)} %get-tuple-element.122.cos_ref.refs_2_, ...), custom_call_target="tpu_custom_call" | custom-call | flops 2147483648 | bytes 1572864 | tf_op jit(solution)/shard_map/attention_fwd/attention/pallas_call | solution.py:238
  152.4 5.9 %convolution_convert_fusion.resid_in_ref = bf16[1024,2048]{1,0:T(8,128)(2,1)} fusion(bf16[512,2048]{1,0:T(8,128)(2,1)} %get-tuple-element.126.vectors_ref, s32[1024]{0:T(1024)S(1)} %bitcast.105), kind=kOutput, calls=%fused_computation.11 | convolution fusion | flops 2150105088 | bytes 6295552 | tf_op jit(solution)/shard_map/mlp_rows/dot_general | solution.py:51
  158.4 12.4 %attention.3 = (bf16[512,512]{1,0:T(8,128)(2,1)}, f32[4,8,512]{2,1,0:T(8,128)}) custom-call(f32[1024,640]{1,0:T(8,128)} %get-tuple-element.134.query_ref.pair_ref.refs_0_.refs_1_, f32[1024,640]{1,0:T(8,128)} %get-tuple-element.134.query_ref.pair_ref.refs_0_.refs_1_, f32[1024,128]{1,0:T(8,128)} %get-tuple-element.122.cos_ref.refs_2_, ...), custom_call_target="tpu_custom_call" | custom-call | flops 4294967296 | bytes 3145728 | tf_op jit(solution)/shard_map/attention_fwd/attention/pallas_call | solution.py:238
  170.8 3.8 collective-permute-start.16
  174.6 13.2 %collective-permute-start.15 = (bf16[512,512]{1,0:T(8,128)(2,1)}, bf16[512,512]{1,0:T(8,128)(2,1)}, u32[]{:S(2)}, u32[]{:S(2)}) collective-permute-start(bf16[512,512]{1,0:T(8,128)(2,1)} %get-tuple-element.153.refs_4_.refs_5_), channel_id=1, source_target_pairs={{0,1},{1,2},{2,3},{3,0},{4,5},{5,6},{6,7},{7,4},{8,9},{9,10},{10,1... | collective-permute-start | bytes 1572872 | tf_op jit(solution)/shard_map/mixed_ring/ppermute | solution.py:68
  191.5 11.4 %swiglu_products.1 = (f32[256,1408]{1,0:T(8,128)}, f32[256,1408]{1,0:T(8,128)}, f32[256,1408]{1,0:T(8,128)}, f32[256,1408]{1,0:T(8,128)}) custom-call(bf16[256,2048]{1,0:T(8,128)(2,1)} %own_cot_ref.3, bf16[256,2048]{1,0:T(8,128)(2,1)} %copy-done.31, bf16[256,2048]{1,0:T(8,128)(2,1)} %collective-permute-done.1.refs_2_, ...), custom_call_target="tpu_custom_call" | custom-call | flops 5905580032 | bytes 11534336 | tf_op jit(solution)/shard_map/swiglu_grad/swiglu_products/pallas_call | solution.py:479
  204.8 7.5 %collective-permute-done.13.refs_6_ = bf16[512,512]{1,0:T(8,128)(2,1)S(1)} collective-permute-done((bf16[512,512]{1,0:T(8,128)(2,1)}, bf16[512,512]{1,0:T(8,128)(2,1)S(1)}, u32[]{:S(2)}, u32[]{:S(2)}) %collective-permute-start.13) | collective-permute-done | bytes 524320 | tf_op jit(solution)/shard_map/mixed_ring/ppermute | solution.py:68
  213.1 32.1 %mlp.2 = (f32[512,2048]{1,0:T(8,128)}, bf16[512,1408]{1,0:T(8,128)(2,1)}, bf16[512,2048]{1,0:T(8,128)(2,1)}, bf16[4,512,512]{2,1,0:T(8,128)(2,1)}) custom-call(s32[6]{0:T(128)} %get-tuple-element.239.plan_ref, bf16[1024,2048]{1,0:T(8,128)(2,1)} %convolution_convert_fusion.resid_in_ref, f32[1024,1]{1,0:T(8,128)} %copy.159.weight_ref, ...), custom_call_target="tpu_custom_call" | custom-call | flops 20401094656 | bytes 36700160 | tf_op jit(solution)/shard_map/mlp/mlp/pallas_call | solution.py:614
  246.6 7.4 %fusion.9 = bf16[512,2048]{1,0:T(8,128)(2,1)} fusion(bf16[512,1408]{1,0:T(8,128)(2,1)S(1)} %copy-done.40, bf16[2048,2048]{1,0:T(8,128)(2,1)} %all-gather.6.cloned.1.call-done.triple_w_ref.refs_4_), kind=kOutput, calls=%fused_computation.12 | convolution fusion | flops 2953838592 | bytes 9306112 | tf_op jit(solution)/shard_map/mlp/dot_general | solution.py:55
  258.2 32.6 %mlp.3 = (f32[512,2048]{1,0:T(8,128)}, bf16[512,1408]{1,0:T(8,128)(2,1)}, bf16[512,2048]{1,0:T(8,128)(2,1)}, bf16[512,512]{1,0:T(8,128)(2,1)}, bf16[512,512]{1,0...) custom-call(s32[6]{0:T(128)} %get-tuple-element.238.plan_ref, ...), custom_call_target="tpu_custom_call" | custom-call | flops 20401094656 | bytes 36700160 | tf_op jit(solution)/shard_map/mlp/mlp/pallas_call | solution.py:614
  297.5 7.5 %collective-permute-done.18 = bf16[512,512]{1,0:T(8,128)(2,1)S(1)} collective-permute-done((bf16[512,512]{1,0:T(8,128)(2,1)}, bf16[512,512]{1,0:T(8,128)(2,1)S(1)}, u32[]{:S(2)}, u32[]{:S(2)}) %collective-permute-start.18) | collective-permute-done | bytes 524320 | tf_op jit(solution)/shard_map/mlp/ppermute | solution.py:68
  305.7 6.6 %fusion.12 = bf16[512,2048]{1,0:T(8,128)(2,1)S(1)} fusion(bf16[512,1408]{1,0:T(8,128)(2,1)S(1)} %copy-done.39, bf16[2048,2048]{1,0:T(8,128)(2,1)} %all-gather.6.cloned.1.call-done.triple_w_ref.refs_4_), kind=kOutput, calls=%fused_computation.13 | convolution fusion | flops 2953838592 | bytes 9306112 | tf_op jit(solution)/shard_map/mlp/dot_general | solution.py:55
  321.0 9.9 %attention_back.2 = (bf16[512,512]{1,0:T(8,128)(2,1)}, f32[1024,128]{1,0:T(8,128)}) custom-call(f32[1024,640]{1,0:T(8,128)} %get-tuple-element.134.query_ref.pair_ref.refs_0_.refs_1_, f32[1024,640]{1,0:T(8,128)} %get-tuple-element.134.query_ref.pair_ref.refs_0_.refs_1_, f32[1024,128]{1,0:T(8,128)} %get-tuple-element.122.cos_ref.refs_2_, ...), custom_call_target="tpu_custom_call" | custom-call | flops 5368709120 | bytes 4194304 | tf_op jit(solution)/shard_map/mlp/attention_back/pallas_call | solution.py:291
  336.2 15.5 %attention_back.3 = (bf16[512,512]{1,0:T(8,128)(2,1)}, bf16[1024,128]{1,0:T(8,128)(2,1)}) custom-call(f32[1024,640]{1,0:T(8,128)} %get-tuple-element.134.query_ref.pair_ref.refs_0_.refs_1_, f32[1024,640]{1,0:T(8,128)} %get-tuple-element.134.query_ref.pair_ref.refs_0_.refs_1_, f32[1024,128]{1,0:T(8,128)} %get-tuple-element.122.cos_ref.refs_2_, ...), custom_call_target="tpu_custom_call" | custom-call | flops 10737418240 | bytes 4194304 | tf_op jit(solution)/shard_map/attention_bwd/attention_back/pallas_call | solution.py:291
  351.7 11.0 %entry_back.1 = (bf16[512,2048]{1,0:T(8,128)(2,1)}, bf16[512,512]{1,0:T(8,128)(2,1)}) custom-call(s32[1,1024]{1,0:T(1,128)} %bitcast.103, bf16[512,2048]{1,0:T(8,128)(2,1)} %get-tuple-element.126.vectors_ref, f32[1,2048]{1,0:T(1,128)} %bitcast.113, bf16[2048,2048]{1,0:T(8,128)(2,1)} %all-gather.6.cloned.1.call-done.triple_w_ref.refs_4_, ...), custom_call_target="tpu_custom_call" | custom-call | flops 3087007744 | bytes 17825792 | tf_op jit(solution)/shard_map/entry_bwd/entry_back/pallas_call | solution.py:429
  372.8 6.5 %all-to-all-done.1 = bf16[8,64,512]{2,1,0:T(8,128)(2,1)S(1)} async-done(((bf16[8,64,512]{2,1,0:T(8,128)(2,1)}), bf16[8,64,512]{2,1,0:T(8,128)(2,1)S(1)}, u32[]{:S(2)}, u32[]{:S(2)}) %all-to-all-start.1) | async-done | bytes 524320 | tf_op jit(solution)/shard_map/entry_bwd/all_to_all | solution.py:91
  393.0 9.6 %hyper_back_units.1 = (f32[512,512]{1,0:T(8,128)}, bf16[512,512]{1,0:T(8,128)(2,1)}, bf16[128,4608]{1,0:T(8,128)(2,1)}, f32[8,512]{1,0:T(8,128)}) custom-call(bf16[64,512]{1,0:T(8,128)(2,1)} %copy-done.19, bf16[64,512]{1,0:T(8,128)(2,1)} %copy-done.36, bf16[64,512]{1,0:T(8,128)(2,1)} %copy-done.35, bf16[64,512]{1,0:T(8,128)(2,1)} %copy-done.34, ...), custom_call_target="tpu_custom_call" | custom-call | flops 12884901888 | bytes 6291456 | tf_op jit(solution)/shard_map/hyper_bwd/hyper_back_units/pallas_call | solution.py:928
  410.6 13.6 %hyper_back_slots.1 = (bf16[512,512]{1,0:T(8,128)(2,1)}, bf16[128,1536]{1,0:T(8,128)(2,1)}, f32[8,512]{1,0:T(8,128)}) custom-call(f32[512,512]{1,0:T(8,128)} %get-tuple-element.203.resid_grad_ref, bf16[512,512]{1,0:T(8,128)(2,1)} %get-tuple-element.204.mixed_grad_ref, bf16[512,512]{1,0:T(8,128)(2,1)} %pad_maximum_fusion.7.rows_ref, ...), custom_call_target="tpu_custom_call" | custom-call | flops 10737418240 | bytes 2097152 | tf_op jit(solution)/shard_map/hyper_bwd/hyper_back_slots/pallas_call | solution.py:965
  436.7 9.4 %all-to-all-done.4 = bf16[8,16,1664]{2,1,0:T(8,128)(2,1)S(1)} async-done(((bf16[8,16,1664]{2,1,0:T(8,128)(2,1)}), bf16[8,16,1664]{2,1,0:T(8,128)(2,1)S(1)}, u32[]{:S(2)}, u32[]{:S(2)}) %all-to-all-start.4) | async-done | bytes 426016 | tf_op jit(solution)/shard_map/grads_out/all_to_all | solution.py:91
  446.2 4.7 all-to-all-start.5
  458.3 3.8 add_convert_fusion
  462.1 6.4 %all-gather.12.cloned.1.call-done = bf16[4096,512]{1,0:T(8,128)(2,1)} async-done(((bf16[512,512]{1,0:T(8,128)(2,1)}), bf16[4096,512]{1,0:T(8,128)(2,1)}) %all-gather.12.cloned.1.call-update) | async-done | bytes 4194320 | tf_op jit(solution)/shard_map/grads_out/all_gather | solution.py:1360
  468.5 7.9 %fusion = f32[1000,512]{1,0:T(8,128)} fusion(bf16[4096,512]{1,0:T(8,128)(2,1)} %all-gather.12.cloned.1.call-done, s32[4096]{0:T(1024)S(1)} %eq.50, s32[1000]{0:T(1024)S(1)} %iota_add_fusion), kind=kOutput, calls=%fused_computation.1 | convolution fusion | flops 4198400000 | bytes 6262688 | tf_op jit(solution)/shard_map/grads_out/dot_general | solution.py:51
  (267 shorter events, 134.3 us)
Async XLA Ops:
  7.2 118.2 %all-gather.6.cloned.1.call-start = ((), (), s32[]{:S(2)}) async-start(), calls=%async_computation.9 | async-start | bytes 9437184 | tf_op jit(solution)/shard_map/first_weights/all_gather | solution.py:1038
  12.2 28.3 %collective-permute-start = (bf16[256,2048]{1,0:T(8,128)(2,1)S(1)}, bf16[256,2048]{1,0:T(8,128)(2,1)S(1)}, u32[]{:S(2)}, u32[]{:S(2)}) collective-permute-start(bf16[256,2048]{1,0:T(8,128)(2,1)S(1)} %copy-done.30), channel_id=1, source_target_pairs={{0,1},{1,2},{2,3},{3,0},{4,5},{5,6},{6,7},{7,4},{8,9},{9,10},{10,1... | collective-permute-start | bytes 3145736 | tf_op jit(solution)/shard_map/cot_ring/ppermute | solution.py:68
  33.2 25.4 %all-to-all-start = ((bf16[8,128,512]{2,1,0:T(8,128)(2,1)}), bf16[8,128,512]{2,1,0:T(8,128)(2,1)S(1)}, u32[]{:S(2)}, u32[]{:S(2)}) async-start(bf16[8,128,512]{2,1,0:T(8,128)(2,1)} %select_select_fusion), calls=%async_computation | async-start | bytes 2097152 | tf_op jit(solution)/shard_map/lookup/all_to_all | solution.py:1050
  36.7 176.4 %all-gather.10.cloned.1.call-start = ((), (), s32[]{:S(2)}) async-start(), calls=%async_computation.11 | async-start | bytes 12976128 | tf_op jit(solution)/shard_map/cot_ring/all_gather | solution.py:1062
  40.5 26.4 %collective-permute-start.1 = (bf16[256,2048]{1,0:T(8,128)(2,1)S(1)}, bf16[256,2048]{1,0:T(8,128)(2,1)}, u32[]{:S(2)}, u32[]{:S(2)}) collective-permute-start(bf16[256,2048]{1,0:T(8,128)(2,1)S(1)} %collective-permute-done.refs_1_), channel_id=1, source_target_pairs={{0,1},{1,2},{2,3},{3,0},{4,5},{5,6},{6,7},{7,4},{8,9},{9,10},{10,1... | collective-permute-start | bytes 3145736 | tf_op jit(solution)/shard_map/cot_ring/ppermute | solution.py:68
  66.9 146.2 %all-gather.8.cloned.1.call-start = ((), (), s32[]{:S(2)}) async-start(), calls=%async_computation.10 | async-start | bytes 9437184 | tf_op jit(solution)/shard_map/output_weights/all_gather | solution.py:1092
  67.2 9.4 %collective-permute-start.3 = (s32[1536]{0:T(1024)S(1)}, s32[1536]{0:T(1024)S(1)}, u32[]{:S(2)}, u32[]{:S(2)}) collective-permute-start(s32[1536]{0:T(1024)S(1)} %pad_add_fusion.3), channel_id=1, source_target_pairs={{0,2},{1,3},{2,0},{3,1},{4,6},{5,7},{6,4},{7,5},{8,10},{9,11},{10,... | collective-permute-start | bytes 18440 | tf_op jit(solution)/shard_map/cot_ring/ppermute | solution.py:68
  67.3 9.3 %collective-permute-start.2 = (s32[1536]{0:T(1024)S(1)}, s32[1536]{0:T(1024)S(1)}, u32[]{:S(2)}, u32[]{:S(2)}) collective-permute-start(s32[1536]{0:T(1024)S(1)} %pad_add_fusion.3), channel_id=1, source_target_pairs={{0,1},{1,2},{2,3},{3,0},{4,5},{5,6},{6,7},{7,4},{8,9},{9,10},{10,1... | collective-permute-start | bytes 18440 | tf_op jit(solution)/shard_map/cot_ring/ppermute | solution.py:68
  69.8 11.2 %collective-permute-start.6 = (bf16[128,512]{1,0:T(8,128)(2,1)S(1)}, bf16[128,512]{1,0:T(8,128)(2,1)S(1)}, u32[]{:S(2)}, u32[]{:S(2)}) collective-permute-start(bf16[128,512]{1,0:T(8,128)(2,1)S(1)} %convert_reduce_fusion.1), channel_id=1, source_target_pairs={{0,2},{1,3},{2,0},{3,1},{4,6},{5,7},{6,4},{7,5},{8,10},{9,11},{10,... | collective-permute-start | bytes 393224 | tf_op jit(solution)/shard_map/hyper_wide/ppermute | solution.py:68
  72.7 8.3 %collective-permute-start.5 = (bf16[128,512]{1,0:T(8,128)(2,1)S(1)}, bf16[128,512]{1,0:T(8,128)(2,1)S(1)}, u32[]{:S(2)}, u32[]{:S(2)}) collective-permute-start(bf16[128,512]{1,0:T(8,128)(2,1)S(1)} %convert_reduce_fusion.1), channel_id=1, source_target_pairs={{0,1},{1,2},{2,3},{3,0},{4,5},{5,6},{6,7},{7,4},{8,9},{9,10},{10,1... | collective-permute-start | bytes 393224 | tf_op jit(solution)/shard_map/hyper_wide/ppermute | solution.py:68
  100.6 15.9 %collective-permute-start.10 = (bf16[256,512]{1,0:T(8,128)(2,1)S(1)}, bf16[256,512]{1,0:T(8,128)(2,1)S(1)}, u32[]{:S(2)}, u32[]{:S(2)}) collective-permute-start(bf16[256,512]{1,0:T(8,128)(2,1)S(1)} %copy-done.17), channel_id=1, source_target_pairs={{0,3},{1,0},{2,1},{3,2},{4,7},{5,4},{6,5},{7,6},{8,11},{9,8},{10,9... | collective-permute-start | bytes 786440 | tf_op jit(solution)/shard_map/output_weights/ppermute | solution.py:68
  102.5 21.8 %collective-permute-start.9 = (bf16[256,512]{1,0:T(8,128)(2,1)S(1)}, bf16[256,512]{1,0:T(8,128)(2,1)S(1)}, u32[]{:S(2)}, u32[]{:S(2)}) collective-permute-start(bf16[256,512]{1,0:T(8,128)(2,1)S(1)} %copy-done.17), channel_id=1, source_target_pairs={{0,2},{1,3},{2,0},{3,1},{4,6},{5,7},{6,4},{7,5},{8,10},{9,11},{10,... | collective-permute-start | bytes 786440 | tf_op jit(solution)/shard_map/output_weights/ppermute | solution.py:68
  104.0 20.2 %collective-permute-start.8 = (bf16[256,512]{1,0:T(8,128)(2,1)S(1)}, bf16[256,512]{1,0:T(8,128)(2,1)S(1)}, u32[]{:S(2)}, u32[]{:S(2)}) collective-permute-start(bf16[256,512]{1,0:T(8,128)(2,1)S(1)} %copy-done.17), channel_id=1, source_target_pairs={{0,1},{1,2},{2,3},{3,0},{4,5},{5,6},{6,7},{7,4},{8,9},{9,10},{10,1... | collective-permute-start | bytes 786440 | tf_op jit(solution)/shard_map/output_weights/ppermute | solution.py:68
  125.5 195.5 %reduce-scatter.4.cloned.1.call-start = ((), (), s32[]{:S(2)}) async-start(), calls=%async_computation.12 | async-start | bytes 2621440 | tf_op jit(solution)/shard_map/mlp/reduce_scatter | solution.py:1211
  131.3 60.2 %collective-permute-start.11 = (bf16[256,2048]{1,0:T(8,128)(2,1)}, bf16[256,2048]{1,0:T(8,128)(2,1)}, u32[]{:S(2)}, u32[]{:S(2)}) collective-permute-start(bf16[256,2048]{1,0:T(8,128)(2,1)} %collective-permute-done.1.refs_2_), channel_id=1, source_target_pairs={{0,1},{1,2},{2,3},{3,0},{4,5},{5,6},{6,7},{7,4},{8,9},{9,10},{10,1... | collective-permute-start | bytes 3145736 | tf_op jit(solution)/shard_map/cot_ring/ppermute | solution.py:68
  148.6 54.2 %collective-permute-start.14 = (bf16[512,512]{1,0:T(8,128)(2,1)}, bf16[512,512]{1,0:T(8,128)(2,1)}, u32[]{:S(2)}, u32[]{:S(2)}) collective-permute-start(bf16[512,512]{1,0:T(8,128)(2,1)} %get-tuple-element.147.refs_4_.refs_5_), channel_id=1, source_target_pairs={{0,3},{1,0},{2,1},{3,2},{4,7},{5,4},{6,5},{7,6},{8,11},{9,8},{10,9... | collective-permute-start | bytes 1572872 | tf_op jit(solution)/shard_map/mixed_ring/ppermute | solution.py:68
  152.4 39.0 %collective-permute-start.12 = (bf16[512,512]{1,0:T(8,128)(2,1)}, bf16[512,512]{1,0:T(8,128)(2,1)}, u32[]{:S(2)}, u32[]{:S(2)}) collective-permute-start(bf16[512,512]{1,0:T(8,128)(2,1)} %get-tuple-element.147.refs_4_.refs_5_), channel_id=1, source_target_pairs={{0,1},{1,2},{2,3},{3,0},{4,5},{5,6},{6,7},{7,4},{8,9},{9,10},{10,1... | collective-permute-start | bytes 1572872 | tf_op jit(solution)/shard_map/mixed_ring/ppermute | solution.py:68
  170.8 32.1 %collective-permute-start.16 = (bf16[512,512]{1,0:T(8,128)(2,1)}, bf16[512,512]{1,0:T(8,128)(2,1)}, u32[]{:S(2)}, u32[]{:S(2)}) collective-permute-start(bf16[512,512]{1,0:T(8,128)(2,1)} %get-tuple-element.153.refs_4_.refs_5_), channel_id=1, source_target_pairs={{0,3},{1,0},{2,1},{3,2},{4,7},{5,4},{6,5},{7,6},{8,11},{9,8},{10,9... | collective-permute-start | bytes 1572872 | tf_op jit(solution)/shard_map/mixed_ring/ppermute | solution.py:68
  174.6 30.2 %collective-permute-start.15 = (bf16[512,512]{1,0:T(8,128)(2,1)}, bf16[512,512]{1,0:T(8,128)(2,1)}, u32[]{:S(2)}, u32[]{:S(2)}) collective-permute-start(bf16[512,512]{1,0:T(8,128)(2,1)} %get-tuple-element.153.refs_4_.refs_5_), channel_id=1, source_target_pairs={{0,1},{1,2},{2,3},{3,0},{4,5},{5,6},{6,7},{7,4},{8,9},{9,10},{10,1... | collective-permute-start | bytes 1572872 | tf_op jit(solution)/shard_map/mixed_ring/ppermute | solution.py:68
  191.4 20.9 %collective-permute-start.13 = (bf16[512,512]{1,0:T(8,128)(2,1)}, bf16[512,512]{1,0:T(8,128)(2,1)S(1)}, u32[]{:S(2)}, u32[]{:S(2)}) collective-permute-start(bf16[512,512]{1,0:T(8,128)(2,1)} %collective-permute-done.12.refs_5_), channel_id=1, source_target_pairs={{0,1},{1,2},{2,3},{3,0},{4,5},{5,6},{6,7},{7,4},{8,9},{9,10},{10,1... | collective-permute-start | bytes 1572872 | tf_op jit(solution)/shard_map/mixed_ring/ppermute | solution.py:68
  213.1 44.2 %collective-permute-start.17 = (bf16[512,512]{1,0:T(8,128)(2,1)}, bf16[512,512]{1,0:T(8,128)(2,1)S(1)}, u32[]{:S(2)}, u32[]{:S(2)}) collective-permute-start(bf16[512,512]{1,0:T(8,128)(2,1)} %collective-permute-done.15.refs_5_), channel_id=1, source_target_pairs={{0,1},{1,2},{2,3},{3,0},{4,5},{5,6},{6,7},{7,4},{8,9},{9,10},{10,1... | collective-permute-start | bytes 1572872 | tf_op jit(solution)/shard_map/mlp/ppermute | solution.py:68
  245.3 141.5 %reduce-scatter.6.cloned.1.call-start = ((), (), s32[]{:S(2)}) async-start(), calls=%async_computation.13 | async-start | bytes 2621440 | tf_op jit(solution)/shard_map/layer_out/reduce_scatter | solution.py:1266
  290.8 14.2 %collective-permute-start.18 = (bf16[512,512]{1,0:T(8,128)(2,1)}, bf16[512,512]{1,0:T(8,128)(2,1)S(1)}, u32[]{:S(2)}, u32[]{:S(2)}) collective-permute-start(bf16[512,512]{1,0:T(8,128)(2,1)} %get-tuple-element.160), channel_id=1, source_target_pairs={{0,1},{1,2},{2,3},{3,0},{4,5},{5,6},{6,7},{7,4},{8,9},{9,10},{10,1... | collective-permute-start | bytes 1572872 | tf_op jit(solution)/shard_map/mlp/ppermute | solution.py:68
  305.2 14.2 %collective-permute-start.19 = (bf16[512,512]{1,0:T(8,128)(2,1)S(1)}, bf16[512,512]{1,0:T(8,128)(2,1)}, u32[]{:S(2)}, u32[]{:S(2)}) collective-permute-start(bf16[512,512]{1,0:T(8,128)(2,1)S(1)} %add_convert_fusion.3), channel_id=1, source_target_pairs={{0,1},{1,2},{2,3},{3,0},{4,5},{5,6},{6,7},{7,4},{8,9},{9,10},{10,1... | collective-permute-start | bytes 1572872 | tf_op jit(solution)/shard_map/mlp/ppermute | solution.py:68
  320.6 13.6 %collective-permute-start.20 = (bf16[512,512]{1,0:T(8,128)(2,1)S(1)}, bf16[512,512]{1,0:T(8,128)(2,1)}, u32[]{:S(2)}, u32[]{:S(2)}) collective-permute-start(bf16[512,512]{1,0:T(8,128)(2,1)S(1)} %add_convert_fusion.2), channel_id=1, source_target_pairs={{0,1},{1,2},{2,3},{3,0},{4,5},{5,6},{6,7},{7,4},{8,9},{9,10},{10,1... | collective-permute-start | bytes 1572872 | tf_op jit(solution)/shard_map/mlp/ppermute | solution.py:68
  366.1 13.2 %all-to-all-start.1 = ((bf16[8,64,512]{2,1,0:T(8,128)(2,1)}), bf16[8,64,512]{2,1,0:T(8,128)(2,1)S(1)}, u32[]{:S(2)}, u32[]{:S(2)}) async-start(bf16[8,64,512]{2,1,0:T(8,128)(2,1)} %bitcast.32), calls=%async_computation.3 | async-start | bytes 1048576 | tf_op jit(solution)/shard_map/entry_bwd/all_to_all | solution.py:91
  369.6 88.6 %reduce-scatter.8.cloned.1.call-start = ((), (), s32[]{:S(2)}) async-start(), calls=%async_computation.14 | async-start | bytes 2621440 | tf_op jit(solution)/shard_map/layer_out/reduce_scatter | solution.py:1324
  389.4 15.8 %all-to-all-start.2 = ((bf16[4,64,2048]{2,1,0:T(8,128)(2,1)}), bf16[4,64,2048]{2,1,0:T(8,128)(2,1)S(1)}, u32[]{:S(2)}, u32[]{:S(2)}) async-start(bf16[4,64,2048]{2,1,0:T(8,128)(2,1)} %bitcast.33), calls=%async_computation.5 | async-start | bytes 2097152 | tf_op jit(solution)/shard_map/hyper_bwd/all_to_all | solution.py:1315
  406.2 20.3 %all-to-all-start.3 = ((bf16[8,16,4608]{2,1,0:T(8,128)(2,1)}), bf16[8,16,4608]{2,1,0:T(8,128)(2,1)S(1)}, u32[]{:S(2)}, u32[]{:S(2)}) async-start(bf16[8,16,4608]{2,1,0:T(8,128)(2,1)} %bitcast.83), calls=%async_computation.6 | async-start | bytes 2359296 | tf_op jit(solution)/shard_map/hyper_bwd/all_to_all | solution.py:91
  409.8 58.7 %all-gather.12.cloned.1.call-start = ((), (), s32[]{:S(2)}) async-start(), calls=%async_computation.15 | async-start | bytes 4718592 | tf_op jit(solution)/shard_map/grads_out/all_gather | solution.py:1360
  431.6 14.6 %all-to-all-start.4 = ((bf16[8,16,1664]{2,1,0:T(8,128)(2,1)}), bf16[8,16,1664]{2,1,0:T(8,128)(2,1)S(1)}, u32[]{:S(2)}, u32[]{:S(2)}) async-start(bf16[8,16,1664]{2,1,0:T(8,128)(2,1)} %bitcast.37), calls=%async_computation.7 | async-start | bytes 851968 | tf_op jit(solution)/shard_map/grads_out/all_to_all | solution.py:91
  446.2 11.4 %all-to-all-start.5 = ((bf16[4,16,2048]{2,1,0:T(8,128)(2,1)}), bf16[4,16,2048]{2,1,0:T(8,128)(2,1)S(1)}, u32[]{:S(2)}, u32[]{:S(2)}) async-start(bf16[4,16,2048]{2,1,0:T(8,128)(2,1)} %bitcast.40), calls=%async_computation.8 | async-start | bytes 524288 | tf_op jit(solution)/shard_map/grads_out/all_to_all | solution.py:1363
  (48 other events, 399.0 us)
Sparse Core Ops, SparseCore 0:
  12.3 63.2 all-gather.5
  77.5 68.3 all-gather.9
  147.8 54.3 all-gather.7
  245.4 44.9 reduce-scatter.3
  336.3 41.5 reduce-scatter.5
  387.0 42.0 reduce-scatter.7
  431.1 37.3 all-gather.11

commit v6 on v5

--- a/solution.py
+++ b/solution.py
@@ -408,7 +408,7 @@
     grad = grad * gain_ref[...]
     normed, spread = unit_scale(vectors_ref[...].astype(jnp.float32))
     grad = spread * (grad - normed * jnp.mean(grad * normed, axis=1, keepdims=True))
-    entry_grad = (grad + sum(ref[...] for ref in mid_refs)).astype(bfloat)
+    entry_grad = (grad + sum(ref[...].astype(jnp.float32) for ref in mid_refs)).astype(bfloat)
     entry_ref[...] = entry_grad
     pooled_ref[...] = times_trans(entry_grad, project_ref[...]).astype(bfloat)
 
@@ -742,7 +742,7 @@
     pooled = kept.reshape(total // SUBWORD_SLOTS, SUBWORD_SLOTS, kept.shape[1]).sum(axis=1)
     pooled_ref[...] = (pooled / length_ref[...]).astype(bfloat)
     bell = jnp.exp(-0.5 * expanded * expanded) * (2.0 * math.pi) ** (-0.5)
-    slope_ref[...] = below + expanded * bell
+    slope_ref[...] = (below + expanded * bell).astype(bfloat)
 
 
 def hyper_wide(rows_in, open_rows, gains, triple_w, merge_w, expand_w, reduce_w, lengths):
@@ -765,7 +765,7 @@
         (width, single),
         (width, bfloat),
         (units, bfloat),
-        (units, single),
+        (units, bfloat),
     ]
     return pl.pallas_call(
         hyper_wide_kernel,
@@ -813,7 +813,7 @@
     ).reshape(total, width)
     grid_grad = grid_grad * scale_ref[...]
     reduce_in = grid_grad.astype(bfloat)
-    expand_in = times_trans(reduce_in, reduce_w_ref[...]) * slope_ref[...]
+    expand_in = times_trans(reduce_in, reduce_w_ref[...]) * slope_ref[...].astype(jnp.float32)
     expand_in = expand_in.astype(bfloat)
     second_grad = times_trans(expand_in, expand_w_ref[...])
     normed, spread = centred(resid_ref[...])
@@ -1216,13 +1216,13 @@
                     )
                 )
                 layer_parts.append(times_trans(swiglu_low, full_downward).astype(bfloat))
-                mid_parts.append(trans_times(seq_hot[rows], mid_low))
+                mid_parts.append(trans_times(seq_hot[rows], mid_low).astype(bfloat))
                 continue
             carried = None
             for step in [*range(1, tensor_size), 0]:
                 part = mixed_part[step]
                 if step == 2:
-                    mid_parts.append(trans_times(seq_hot[rows], mid_low))
+                    mid_parts.append(trans_times(seq_hot[rows], mid_low).astype(bfloat))
                     carried, mid_parts = lax.optimization_barrier((carried, mid_parts))
                     swiglu_low = tie(swiglu_low, carried)
                 if step == 3:

time: 493 us -> 492 us (level)
  no operation moved by 1% of the time
where the time goes in v6:
time: 492 us; the launch traced here: 482 us
  Pallas kernels  182 us (37%)
  waiting for transfers between devices  90.7 us (18%)
  starting transfers between devices  66.8 us (14%)
  matrix products  43.9 us (9%)
  local copies, waits for them, and re-layouts  36.3 us (7%)
  other arithmetic  26.2 us (5%)
  blocking collectives  20.2 us (4%)
  between operations  15.4 us (3%)
    pallas_call x2, Pallas kernels, mlp(): pl.pallas_call(partial(mlp_kernel, query_width, unit_width, positions, st...  64.8 us
    ppermute x24, waiting for transfers between devices, ring(): lax.ppermute(values, 'tensor', [(i, (i + shift) % size) for i in range(si...  47.8 us
    ppermute x24, starting transfers between devices, ring(): lax.ppermute(values, 'tensor', [(i, (i + shift) % size) for i in range(si...  42.7 us
    pallas_call x2, Pallas kernels, attention_back(): pl.pallas_call(kernel, grid=(pairs,), in_specs=specs, out_specs=[pl.Block...  25.4 us
    pallas_call x2, Pallas kernels, attention(): pl.pallas_call(partial(attention_kernel, min(256, rows), base), grid=(pai...  20.6 us
    pallas_call x1, Pallas kernels, hyper_wide(): pl.pallas_call(hyper_wide_kernel, grid=(total // block,), in_specs=[rows_...  18.4 us
    dot_general x4, matrix products, matmul(): return jnp.dot(left, right, preferred_element_type=jnp.float32)  18.2 us
    all_to_all x3, waiting for transfers between devices, to_owners(): return lax.all_to_all(blocks, 'dp', 0, 0, tiled=True)  17.7 us
  transfers between devices with their start and end apart: 38, of which 18 were waited for; matrix products, arithmetic and copies ran while one was open for 18% of the time, Pallas kernels for 38%

profile of v6, /device:TPU:0, one launch (start us, length us, event | category | flops | bytes accessed | tf_op | source)
XLA Modules:
  0.0 481.8 jit_solution(13401194963533983062)
XLA Ops:
  15.6 9.2 %all-gather = s32[128,10]{1,0:T(8,128)S(1)} all-gather(s32[16,10]{1,0:T(8,128)S(1)} %pad_add_fusion.2), channel_id=2, replica_groups=mesh['dp'=8,'tensor'=4] {'dp'}, dimensions={0}, use_global_device_ids=true | all-gather | bytes 5760 | tf_op jit(solution)/shard_map/ids/all_gather | solution.py:1036
  25.2 6.7 %gather_fusion = bf16[1024,512]{1,0:T(8,128)(2,1)S(1)} fusion(bf16[4000,512]{1,0:T(8,128)(2,1)} %param.22, s32[1024]{0:T(1024)S(1)} %broadcast_clamp_fusion), kind=kCustom, calls=%fused_computation | custom fusion | bytes 2101248 | tf_op jit(solution)/shard_map/lookup/jit(_take)/gather | solution.py:1048
  45.6 13.0 %all-to-all-done = bf16[8,128,512]{2,1,0:T(8,128)(2,1)S(1)} async-done(((bf16[8,128,512]{2,1,0:T(8,128)(2,1)}), bf16[8,128,512]{2,1,0:T(8,128)(2,1)S(1)}, u32[]{:S(2)}, u32[]{:S(2)}) %all-to-all-start) | async-done | bytes 1048608 | tf_op jit(solution)/shard_map/lookup/all_to_all | solution.py:1050
  58.7 8.1 %collective-permute-done.1.refs_2_ = bf16[256,2048]{1,0:T(8,128)(2,1)} collective-permute-done((bf16[256,2048]{1,0:T(8,128)(2,1)S(1)}, bf16[256,2048]{1,0:T(8,128)(2,1)}, u32[]{:S(2)}, u32[]{:S(2)}) %collective-permute-start.1) | collective-permute-done | bytes 1048608 | tf_op jit(solution)/shard_map/cot_ring/ppermute | solution.py:68
  72.7 3.8 collective-permute-start.7
  82.0 18.4 %hyper_wide.1 = (bf16[512,512]{1,0:T(8,128)(2,1)}, bf16[512,1536]{1,0:T(8,128)(2,1)}, bf16[512,512]{1,0:T(8,128)(2,1)}, f32[512,512]{1,0:T(8,128)}, bf16[512,512...) custom-call(bf16[512,512]{1,0:T(8,128)(2,1)} %pad_maximum_fusion.7.rows_ref, ...), custom_call_target="tpu_custom_call" | custom-call | flops 17179869184 | bytes 12582912 | tf_op jit(solution)/shard_map/hyper_wide/hyper_wide/pallas_call | solution.py:770
  105.4 10.9 %all_gather.23.pooled_ref = bf16[512,512]{1,0:T(8,128)(2,1)S(1)} all-gather(bf16[64,512]{1,0:T(8,128)(2,1)} %get-tuple-element.118), channel_id=1, replica_groups=mesh['dp'=8,'tensor'=4] {'dp'}, dimensions={0}, use_global_device_ids=true | all-gather | bytes 589824 | tf_op jit(solution)/shard_map/pooled_gather/all_gather | solution.py:1088
  116.3 7.8 %collective-permute-done.9 = bf16[256,512]{1,0:T(8,128)(2,1)S(1)} collective-permute-done((bf16[256,512]{1,0:T(8,128)(2,1)S(1)}, bf16[256,512]{1,0:T(8,128)(2,1)S(1)}, u32[]{:S(2)}, u32[]{:S(2)}) %collective-permute-start.9) | collective-permute-done | bytes 262176 | tf_op jit(solution)/shard_map/output_weights/ppermute | solution.py:68
  131.1 9.2 %entry.1 = (bf16[512,2048]{1,0:T(8,128)(2,1)}, f32[1024,640]{1,0:T(8,128)}) custom-call(s32[1024,1]{1,0:T(8,128)} %bitcast.91, bf16[512,512]{1,0:T(8,128)(2,1)} %copy-done.2, bf16[512,2048]{1,0:T(8,128)(2,1)} %project_ref.3, f32[1,2048]{1,0:T(1,128)} %bitcast.112, bf16[2048,2048]{1,0:T(8,128)(2,1)} %all-gather.6.cloned.1.call-done.triple_w_ref.refs_4_), custom_call_target="tpu_custom_call" | custom-call | flops 3758096384 | bytes 9437184 | tf_op jit(solution)/shard_map/entry_vectors/entry/pallas_call | solution.py:355
  140.2 8.2 %attention.2 = (bf16[512,512]{1,0:T(8,128)(2,1)}, f32[4,8,512]{2,1,0:T(8,128)}) custom-call(f32[1024,640]{1,0:T(8,128)} %get-tuple-element.134.query_ref.pair_ref.refs_0_.refs_1_, f32[1024,640]{1,0:T(8,128)} %get-tuple-element.134.query_ref.pair_ref.refs_0_.refs_1_, f32[1024,128]{1,0:T(8,128)} %get-tuple-element.122.cos_ref.refs_2_, ...), custom_call_target="tpu_custom_call" | custom-call | flops 2147483648 | bytes 1572864 | tf_op jit(solution)/shard_map/attention_fwd/attention/pallas_call | solution.py:238
  152.2 6.0 %convolution_convert_fusion.resid_in_ref = bf16[1024,2048]{1,0:T(8,128)(2,1)} fusion(bf16[512,2048]{1,0:T(8,128)(2,1)} %get-tuple-element.126.vectors_ref, s32[1024]{0:T(1024)S(1)} %bitcast.105), kind=kOutput, calls=%fused_computation.11 | convolution fusion | flops 2150105088 | bytes 6295552 | tf_op jit(solution)/shard_map/mlp_rows/dot_general | solution.py:51
  158.1 12.4 %attention.3 = (bf16[512,512]{1,0:T(8,128)(2,1)}, f32[4,8,512]{2,1,0:T(8,128)}) custom-call(f32[1024,640]{1,0:T(8,128)} %get-tuple-element.134.query_ref.pair_ref.refs_0_.refs_1_, f32[1024,640]{1,0:T(8,128)} %get-tuple-element.134.query_ref.pair_ref.refs_0_.refs_1_, f32[1024,128]{1,0:T(8,128)} %get-tuple-element.122.cos_ref.refs_2_, ...), custom_call_target="tpu_custom_call" | custom-call | flops 4294967296 | bytes 3145728 | tf_op jit(solution)/shard_map/attention_fwd/attention/pallas_call | solution.py:238
  170.6 3.8 collective-permute-start.16
  174.4 13.2 %collective-permute-start.15 = (bf16[512,512]{1,0:T(8,128)(2,1)}, bf16[512,512]{1,0:T(8,128)(2,1)}, u32[]{:S(2)}, u32[]{:S(2)}) collective-permute-start(bf16[512,512]{1,0:T(8,128)(2,1)} %get-tuple-element.153.refs_4_.refs_5_), channel_id=1, source_target_pairs={{0,1},{1,2},{2,3},{3,0},{4,5},{5,6},{6,7},{7,4},{8,9},{9,10},{10,1... | collective-permute-start | bytes 1572872 | tf_op jit(solution)/shard_map/mixed_ring/ppermute | solution.py:68
  191.3 11.3 %swiglu_products.1 = (f32[256,1408]{1,0:T(8,128)}, f32[256,1408]{1,0:T(8,128)}, f32[256,1408]{1,0:T(8,128)}, f32[256,1408]{1,0:T(8,128)}) custom-call(bf16[256,2048]{1,0:T(8,128)(2,1)} %own_cot_ref.3, bf16[256,2048]{1,0:T(8,128)(2,1)} %copy-done.30, bf16[256,2048]{1,0:T(8,128)(2,1)} %collective-permute-done.1.refs_2_, ...), custom_call_target="tpu_custom_call" | custom-call | flops 5905580032 | bytes 11534336 | tf_op jit(solution)/shard_map/swiglu_grad/swiglu_products/pallas_call | solution.py:479
  204.6 7.5 %collective-permute-done.13.refs_6_ = bf16[512,512]{1,0:T(8,128)(2,1)S(1)} collective-permute-done((bf16[512,512]{1,0:T(8,128)(2,1)}, bf16[512,512]{1,0:T(8,128)(2,1)S(1)}, u32[]{:S(2)}, u32[]{:S(2)}) %collective-permute-start.13) | collective-permute-done | bytes 524320 | tf_op jit(solution)/shard_map/mixed_ring/ppermute | solution.py:68
  212.9 32.2 %mlp.2 = (f32[512,2048]{1,0:T(8,128)}, bf16[512,1408]{1,0:T(8,128)(2,1)}, bf16[512,2048]{1,0:T(8,128)(2,1)}, bf16[4,512,512]{2,1,0:T(8,128)(2,1)}) custom-call(s32[6]{0:T(128)} %get-tuple-element.239.plan_ref, bf16[1024,2048]{1,0:T(8,128)(2,1)} %convolution_convert_fusion.resid_in_ref, f32[1024,1]{1,0:T(8,128)} %copy.159.weight_ref, ...), custom_call_target="tpu_custom_call" | custom-call | flops 20401094656 | bytes 36700160 | tf_op jit(solution)/shard_map/mlp/mlp/pallas_call | solution.py:614
  246.4 7.5 %fusion.9 = bf16[512,2048]{1,0:T(8,128)(2,1)} fusion(bf16[512,1408]{1,0:T(8,128)(2,1)S(1)} %copy-done.41, bf16[2048,2048]{1,0:T(8,128)(2,1)} %all-gather.6.cloned.1.call-done.triple_w_ref.refs_4_), kind=kOutput, calls=%fused_computation.14 | convolution fusion | flops 2953838592 | bytes 9306112 | tf_op jit(solution)/shard_map/mlp/dot_general | solution.py:55
  257.3 32.6 %mlp.3 = (f32[512,2048]{1,0:T(8,128)}, bf16[512,1408]{1,0:T(8,128)(2,1)}, bf16[512,2048]{1,0:T(8,128)(2,1)}, bf16[512,512]{1,0:T(8,128)(2,1)}, bf16[512,512]{1,0...) custom-call(s32[6]{0:T(128)} %get-tuple-element.238.plan_ref, ...), custom_call_target="tpu_custom_call" | custom-call | flops 20401094656 | bytes 36700160 | tf_op jit(solution)/shard_map/mlp/mlp/pallas_call | solution.py:614
  296.1 8.0 %collective-permute-done.18 = bf16[512,512]{1,0:T(8,128)(2,1)S(1)} collective-permute-done((bf16[512,512]{1,0:T(8,128)(2,1)}, bf16[512,512]{1,0:T(8,128)(2,1)S(1)}, u32[]{:S(2)}, u32[]{:S(2)}) %collective-permute-start.18) | collective-permute-done | bytes 524320 | tf_op jit(solution)/shard_map/mlp/ppermute | solution.py:68
  304.9 6.6 %fusion.12 = bf16[512,2048]{1,0:T(8,128)(2,1)S(1)} fusion(bf16[512,1408]{1,0:T(8,128)(2,1)S(1)} %copy-done.40, bf16[2048,2048]{1,0:T(8,128)(2,1)} %all-gather.6.cloned.1.call-done.triple_w_ref.refs_4_), kind=kOutput, calls=%fused_computation.15 | convolution fusion | flops 2953838592 | bytes 9306112 | tf_op jit(solution)/shard_map/mlp/dot_general | solution.py:55
  320.0 9.9 %attention_back.2 = (bf16[512,512]{1,0:T(8,128)(2,1)}, f32[1024,128]{1,0:T(8,128)}) custom-call(f32[1024,640]{1,0:T(8,128)} %get-tuple-element.134.query_ref.pair_ref.refs_0_.refs_1_, f32[1024,640]{1,0:T(8,128)} %get-tuple-element.134.query_ref.pair_ref.refs_0_.refs_1_, f32[1024,128]{1,0:T(8,128)} %get-tuple-element.122.cos_ref.refs_2_, ...), custom_call_target="tpu_custom_call" | custom-call | flops 5368709120 | bytes 4194304 | tf_op jit(solution)/shard_map/mlp/attention_back/pallas_call | solution.py:291
  335.4 15.5 %attention_back.3 = (bf16[512,512]{1,0:T(8,128)(2,1)}, bf16[1024,128]{1,0:T(8,128)(2,1)}) custom-call(f32[1024,640]{1,0:T(8,128)} %get-tuple-element.134.query_ref.pair_ref.refs_0_.refs_1_, f32[1024,640]{1,0:T(8,128)} %get-tuple-element.134.query_ref.pair_ref.refs_0_.refs_1_, f32[1024,128]{1,0:T(8,128)} %get-tuple-element.122.cos_ref.refs_2_, ...), custom_call_target="tpu_custom_call" | custom-call | flops 10737418240 | bytes 4194304 | tf_op jit(solution)/shard_map/attention_bwd/attention_back/pallas_call | solution.py:291
  350.8 9.9 %entry_back.1 = (bf16[512,2048]{1,0:T(8,128)(2,1)}, bf16[512,512]{1,0:T(8,128)(2,1)}) custom-call(s32[1,1024]{1,0:T(1,128)} %bitcast.103, bf16[512,2048]{1,0:T(8,128)(2,1)} %get-tuple-element.126.vectors_ref, f32[1,2048]{1,0:T(1,128)} %bitcast.113, bf16[2048,2048]{1,0:T(8,128)(2,1)} %all-gather.6.cloned.1.call-done.triple_w_ref.refs_4_, ...), custom_call_target="tpu_custom_call" | custom-call | flops 3087007744 | bytes 17825792 | tf_op jit(solution)/shard_map/entry_bwd/entry_back/pallas_call | solution.py:429
  370.9 6.5 %all-to-all-done.1 = bf16[8,64,512]{2,1,0:T(8,128)(2,1)S(1)} async-done(((bf16[8,64,512]{2,1,0:T(8,128)(2,1)}), bf16[8,64,512]{2,1,0:T(8,128)(2,1)S(1)}, u32[]{:S(2)}, u32[]{:S(2)}) %all-to-all-start.1) | async-done | bytes 524320 | tf_op jit(solution)/shard_map/entry_bwd/all_to_all | solution.py:91
  391.0 9.3 %hyper_back_units.1 = (f32[512,512]{1,0:T(8,128)}, bf16[512,512]{1,0:T(8,128)(2,1)}, bf16[128,4608]{1,0:T(8,128)(2,1)}, f32[8,512]{1,0:T(8,128)}) custom-call(bf16[64,512]{1,0:T(8,128)(2,1)} %copy-done.17, bf16[64,512]{1,0:T(8,128)(2,1)} %copy-done.35, bf16[64,512]{1,0:T(8,128)(2,1)} %copy-done.34, bf16[64,512]{1,0:T(8,128)(2,1)} %copy-done.33, ...), custom_call_target="tpu_custom_call" | custom-call | flops 12884901888 | bytes 6291456 | tf_op jit(solution)/shard_map/hyper_bwd/hyper_back_units/pallas_call | solution.py:928
  408.1 13.5 %hyper_back_slots.1 = (bf16[512,512]{1,0:T(8,128)(2,1)}, bf16[128,1536]{1,0:T(8,128)(2,1)}, f32[8,512]{1,0:T(8,128)}) custom-call(f32[512,512]{1,0:T(8,128)} %get-tuple-element.203.resid_grad_ref, bf16[512,512]{1,0:T(8,128)(2,1)} %get-tuple-element.204.mixed_grad_ref, bf16[512,512]{1,0:T(8,128)(2,1)} %pad_maximum_fusion.7.rows_ref, ...), custom_call_target="tpu_custom_call" | custom-call | flops 10737418240 | bytes 2097152 | tf_op jit(solution)/shard_map/hyper_bwd/hyper_back_slots/pallas_call | solution.py:965
  434.3 8.9 %all-to-all-done.4 = bf16[8,16,1664]{2,1,0:T(8,128)(2,1)S(1)} async-done(((bf16[8,16,1664]{2,1,0:T(8,128)(2,1)}), bf16[8,16,1664]{2,1,0:T(8,128)(2,1)S(1)}, u32[]{:S(2)}, u32[]{:S(2)}) %all-to-all-start.4) | async-done | bytes 426016 | tf_op jit(solution)/shard_map/grads_out/all_to_all | solution.py:91
  443.2 6.0 %all-to-all-start.5 = ((bf16[4,16,2048]{2,1,0:T(8,128)(2,1)}), bf16[4,16,2048]{2,1,0:T(8,128)(2,1)S(1)}, u32[]{:S(2)}, u32[]{:S(2)}) async-start(bf16[4,16,2048]{2,1,0:T(8,128)(2,1)} %bitcast.40), calls=%async_computation.8 | async-start | bytes 524288 | tf_op jit(solution)/shard_map/grads_out/all_to_all | solution.py:1363
  456.6 3.8 add_convert_fusion
  460.4 6.2 %all-gather.12.cloned.1.call-done = bf16[4096,512]{1,0:T(8,128)(2,1)} async-done(((bf16[512,512]{1,0:T(8,128)(2,1)}), bf16[4096,512]{1,0:T(8,128)(2,1)}) %all-gather.12.cloned.1.call-update) | async-done | bytes 4194320 | tf_op jit(solution)/shard_map/grads_out/all_gather | solution.py:1360
  466.6 7.9 %fusion = f32[1000,512]{1,0:T(8,128)} fusion(bf16[4096,512]{1,0:T(8,128)(2,1)} %all-gather.12.cloned.1.call-done, s32[4096]{0:T(1024)S(1)} %eq.50, s32[1000]{0:T(1024)S(1)} %iota_add_fusion), kind=kOutput, calls=%fused_computation.1 | convolution fusion | flops 4198400000 | bytes 6262688 | tf_op jit(solution)/shard_map/grads_out/dot_general | solution.py:51
  (269 shorter events, 132.7 us)
Async XLA Ops:
  7.2 118.0 %all-gather.6.cloned.1.call-start = ((), (), s32[]{:S(2)}) async-start(), calls=%async_computation.9 | async-start | bytes 9437184 | tf_op jit(solution)/shard_map/first_weights/all_gather | solution.py:1038
  12.2 28.3 %collective-permute-start = (bf16[256,2048]{1,0:T(8,128)(2,1)S(1)}, bf16[256,2048]{1,0:T(8,128)(2,1)S(1)}, u32[]{:S(2)}, u32[]{:S(2)}) collective-permute-start(bf16[256,2048]{1,0:T(8,128)(2,1)S(1)} %copy-done.29), channel_id=1, source_target_pairs={{0,1},{1,2},{2,3},{3,0},{4,5},{5,6},{6,7},{7,4},{8,9},{9,10},{10,1... | collective-permute-start | bytes 3145736 | tf_op jit(solution)/shard_map/cot_ring/ppermute | solution.py:68
  33.2 25.4 %all-to-all-start = ((bf16[8,128,512]{2,1,0:T(8,128)(2,1)}), bf16[8,128,512]{2,1,0:T(8,128)(2,1)S(1)}, u32[]{:S(2)}, u32[]{:S(2)}) async-start(bf16[8,128,512]{2,1,0:T(8,128)(2,1)} %select_select_fusion), calls=%async_computation | async-start | bytes 2097152 | tf_op jit(solution)/shard_map/lookup/all_to_all | solution.py:1050
  36.7 176.1 %all-gather.10.cloned.1.call-start = ((), (), s32[]{:S(2)}) async-start(), calls=%async_computation.11 | async-start | bytes 12976128 | tf_op jit(solution)/shard_map/cot_ring/all_gather | solution.py:1062
  40.5 26.4 %collective-permute-start.1 = (bf16[256,2048]{1,0:T(8,128)(2,1)S(1)}, bf16[256,2048]{1,0:T(8,128)(2,1)}, u32[]{:S(2)}, u32[]{:S(2)}) collective-permute-start(bf16[256,2048]{1,0:T(8,128)(2,1)S(1)} %collective-permute-done.refs_1_), channel_id=1, source_target_pairs={{0,1},{1,2},{2,3},{3,0},{4,5},{5,6},{6,7},{7,4},{8,9},{9,10},{10,1... | collective-permute-start | bytes 3145736 | tf_op jit(solution)/shard_map/cot_ring/ppermute | solution.py:68
  66.9 146.0 %all-gather.8.cloned.1.call-start = ((), (), s32[]{:S(2)}) async-start(), calls=%async_computation.10 | async-start | bytes 9437184 | tf_op jit(solution)/shard_map/output_weights/all_gather | solution.py:1092
  67.2 9.4 %collective-permute-start.3 = (s32[1536]{0:T(1024)S(1)}, s32[1536]{0:T(1024)S(1)}, u32[]{:S(2)}, u32[]{:S(2)}) collective-permute-start(s32[1536]{0:T(1024)S(1)} %pad_add_fusion.3), channel_id=1, source_target_pairs={{0,2},{1,3},{2,0},{3,1},{4,6},{5,7},{6,4},{7,5},{8,10},{9,11},{10,... | collective-permute-start | bytes 18440 | tf_op jit(solution)/shard_map/cot_ring/ppermute | solution.py:68
  67.3 9.3 %collective-permute-start.2 = (s32[1536]{0:T(1024)S(1)}, s32[1536]{0:T(1024)S(1)}, u32[]{:S(2)}, u32[]{:S(2)}) collective-permute-start(s32[1536]{0:T(1024)S(1)} %pad_add_fusion.3), channel_id=1, source_target_pairs={{0,1},{1,2},{2,3},{3,0},{4,5},{5,6},{6,7},{7,4},{8,9},{9,10},{10,1... | collective-permute-start | bytes 18440 | tf_op jit(solution)/shard_map/cot_ring/ppermute | solution.py:68
  69.8 11.2 %collective-permute-start.6 = (bf16[128,512]{1,0:T(8,128)(2,1)S(1)}, bf16[128,512]{1,0:T(8,128)(2,1)S(1)}, u32[]{:S(2)}, u32[]{:S(2)}) collective-permute-start(bf16[128,512]{1,0:T(8,128)(2,1)S(1)} %convert_reduce_fusion.1), channel_id=1, source_target_pairs={{0,2},{1,3},{2,0},{3,1},{4,6},{5,7},{6,4},{7,5},{8,10},{9,11},{10,... | collective-permute-start | bytes 393224 | tf_op jit(solution)/shard_map/hyper_wide/ppermute | solution.py:68
  72.7 8.3 %collective-permute-start.5 = (bf16[128,512]{1,0:T(8,128)(2,1)S(1)}, bf16[128,512]{1,0:T(8,128)(2,1)S(1)}, u32[]{:S(2)}, u32[]{:S(2)}) collective-permute-start(bf16[128,512]{1,0:T(8,128)(2,1)S(1)} %convert_reduce_fusion.1), channel_id=1, source_target_pairs={{0,1},{1,2},{2,3},{3,0},{4,5},{5,6},{6,7},{7,4},{8,9},{9,10},{10,1... | collective-permute-start | bytes 393224 | tf_op jit(solution)/shard_map/hyper_wide/ppermute | solution.py:68
  100.4 15.9 %collective-permute-start.10 = (bf16[256,512]{1,0:T(8,128)(2,1)S(1)}, bf16[256,512]{1,0:T(8,128)(2,1)S(1)}, u32[]{:S(2)}, u32[]{:S(2)}) collective-permute-start(bf16[256,512]{1,0:T(8,128)(2,1)S(1)} %copy-done.15), channel_id=1, source_target_pairs={{0,3},{1,0},{2,1},{3,2},{4,7},{5,4},{6,5},{7,6},{8,11},{9,8},{10,9... | collective-permute-start | bytes 786440 | tf_op jit(solution)/shard_map/output_weights/ppermute | solution.py:68
  102.3 21.8 %collective-permute-start.9 = (bf16[256,512]{1,0:T(8,128)(2,1)S(1)}, bf16[256,512]{1,0:T(8,128)(2,1)S(1)}, u32[]{:S(2)}, u32[]{:S(2)}) collective-permute-start(bf16[256,512]{1,0:T(8,128)(2,1)S(1)} %copy-done.15), channel_id=1, source_target_pairs={{0,2},{1,3},{2,0},{3,1},{4,6},{5,7},{6,4},{7,5},{8,10},{9,11},{10,... | collective-permute-start | bytes 786440 | tf_op jit(solution)/shard_map/output_weights/ppermute | solution.py:68
  103.9 20.2 %collective-permute-start.8 = (bf16[256,512]{1,0:T(8,128)(2,1)S(1)}, bf16[256,512]{1,0:T(8,128)(2,1)S(1)}, u32[]{:S(2)}, u32[]{:S(2)}) collective-permute-start(bf16[256,512]{1,0:T(8,128)(2,1)S(1)} %copy-done.15), channel_id=1, source_target_pairs={{0,1},{1,2},{2,3},{3,0},{4,5},{5,6},{6,7},{7,4},{8,9},{9,10},{10,1... | collective-permute-start | bytes 786440 | tf_op jit(solution)/shard_map/output_weights/ppermute | solution.py:68
  125.2 194.8 %reduce-scatter.4.cloned.1.call-start = ((), (), s32[]{:S(2)}) async-start(), calls=%async_computation.12 | async-start | bytes 2621440 | tf_op jit(solution)/shard_map/mlp/reduce_scatter | solution.py:1211
  131.0 60.2 %collective-permute-start.11 = (bf16[256,2048]{1,0:T(8,128)(2,1)}, bf16[256,2048]{1,0:T(8,128)(2,1)}, u32[]{:S(2)}, u32[]{:S(2)}) collective-permute-start(bf16[256,2048]{1,0:T(8,128)(2,1)} %collective-permute-done.1.refs_2_), channel_id=1, source_target_pairs={{0,1},{1,2},{2,3},{3,0},{4,5},{5,6},{6,7},{7,4},{8,9},{9,10},{10,1... | collective-permute-start | bytes 3145736 | tf_op jit(solution)/shard_map/cot_ring/ppermute | solution.py:68
  148.4 54.1 %collective-permute-start.14 = (bf16[512,512]{1,0:T(8,128)(2,1)}, bf16[512,512]{1,0:T(8,128)(2,1)}, u32[]{:S(2)}, u32[]{:S(2)}) collective-permute-start(bf16[512,512]{1,0:T(8,128)(2,1)} %get-tuple-element.147.refs_4_.refs_5_), channel_id=1, source_target_pairs={{0,3},{1,0},{2,1},{3,2},{4,7},{5,4},{6,5},{7,6},{8,11},{9,8},{10,9... | collective-permute-start | bytes 1572872 | tf_op jit(solution)/shard_map/mixed_ring/ppermute | solution.py:68
  152.2 39.0 %collective-permute-start.12 = (bf16[512,512]{1,0:T(8,128)(2,1)}, bf16[512,512]{1,0:T(8,128)(2,1)}, u32[]{:S(2)}, u32[]{:S(2)}) collective-permute-start(bf16[512,512]{1,0:T(8,128)(2,1)} %get-tuple-element.147.refs_4_.refs_5_), channel_id=1, source_target_pairs={{0,1},{1,2},{2,3},{3,0},{4,5},{5,6},{6,7},{7,4},{8,9},{9,10},{10,1... | collective-permute-start | bytes 1572872 | tf_op jit(solution)/shard_map/mixed_ring/ppermute | solution.py:68
  170.6 32.0 %collective-permute-start.16 = (bf16[512,512]{1,0:T(8,128)(2,1)}, bf16[512,512]{1,0:T(8,128)(2,1)}, u32[]{:S(2)}, u32[]{:S(2)}) collective-permute-start(bf16[512,512]{1,0:T(8,128)(2,1)} %get-tuple-element.153.refs_4_.refs_5_), channel_id=1, source_target_pairs={{0,3},{1,0},{2,1},{3,2},{4,7},{5,4},{6,5},{7,6},{8,11},{9,8},{10,9... | collective-permute-start | bytes 1572872 | tf_op jit(solution)/shard_map/mixed_ring/ppermute | solution.py:68
  174.4 30.2 %collective-permute-start.15 = (bf16[512,512]{1,0:T(8,128)(2,1)}, bf16[512,512]{1,0:T(8,128)(2,1)}, u32[]{:S(2)}, u32[]{:S(2)}) collective-permute-start(bf16[512,512]{1,0:T(8,128)(2,1)} %get-tuple-element.153.refs_4_.refs_5_), channel_id=1, source_target_pairs={{0,1},{1,2},{2,3},{3,0},{4,5},{5,6},{6,7},{7,4},{8,9},{9,10},{10,1... | collective-permute-start | bytes 1572872 | tf_op jit(solution)/shard_map/mixed_ring/ppermute | solution.py:68
  191.2 20.9 %collective-permute-start.13 = (bf16[512,512]{1,0:T(8,128)(2,1)}, bf16[512,512]{1,0:T(8,128)(2,1)S(1)}, u32[]{:S(2)}, u32[]{:S(2)}) collective-permute-start(bf16[512,512]{1,0:T(8,128)(2,1)} %collective-permute-done.12.refs_5_), channel_id=1, source_target_pairs={{0,1},{1,2},{2,3},{3,0},{4,5},{5,6},{6,7},{7,4},{8,9},{9,10},{10,1... | collective-permute-start | bytes 1572872 | tf_op jit(solution)/shard_map/mixed_ring/ppermute | solution.py:68
  212.9 43.7 %collective-permute-start.17 = (bf16[512,512]{1,0:T(8,128)(2,1)}, bf16[512,512]{1,0:T(8,128)(2,1)S(1)}, u32[]{:S(2)}, u32[]{:S(2)}) collective-permute-start(bf16[512,512]{1,0:T(8,128)(2,1)} %collective-permute-done.15.refs_5_), channel_id=1, source_target_pairs={{0,1},{1,2},{2,3},{3,0},{4,5},{5,6},{6,7},{7,4},{8,9},{9,10},{10,1... | collective-permute-start | bytes 1572872 | tf_op jit(solution)/shard_map/mlp/ppermute | solution.py:68
  245.1 139.8 %reduce-scatter.6.cloned.1.call-start = ((), (), s32[]{:S(2)}) async-start(), calls=%async_computation.13 | async-start | bytes 2621440 | tf_op jit(solution)/shard_map/layer_out/reduce_scatter | solution.py:1266
  290.0 14.1 %collective-permute-start.18 = (bf16[512,512]{1,0:T(8,128)(2,1)}, bf16[512,512]{1,0:T(8,128)(2,1)S(1)}, u32[]{:S(2)}, u32[]{:S(2)}) collective-permute-start(bf16[512,512]{1,0:T(8,128)(2,1)} %get-tuple-element.160), channel_id=1, source_target_pairs={{0,1},{1,2},{2,3},{3,0},{4,5},{5,6},{6,7},{7,4},{8,9},{9,10},{10,1... | collective-permute-start | bytes 1572872 | tf_op jit(solution)/shard_map/mlp/ppermute | solution.py:68
  304.2 14.3 %collective-permute-start.19 = (bf16[512,512]{1,0:T(8,128)(2,1)S(1)}, bf16[512,512]{1,0:T(8,128)(2,1)}, u32[]{:S(2)}, u32[]{:S(2)}) collective-permute-start(bf16[512,512]{1,0:T(8,128)(2,1)S(1)} %add_convert_fusion.3), channel_id=1, source_target_pairs={{0,1},{1,2},{2,3},{3,0},{4,5},{5,6},{6,7},{7,4},{8,9},{9,10},{10,1... | collective-permute-start | bytes 1572872 | tf_op jit(solution)/shard_map/mlp/ppermute | solution.py:68
  319.7 13.6 %collective-permute-start.20 = (bf16[512,512]{1,0:T(8,128)(2,1)S(1)}, bf16[512,512]{1,0:T(8,128)(2,1)}, u32[]{:S(2)}, u32[]{:S(2)}) collective-permute-start(bf16[512,512]{1,0:T(8,128)(2,1)S(1)} %add_convert_fusion.2), channel_id=1, source_target_pairs={{0,1},{1,2},{2,3},{3,0},{4,5},{5,6},{6,7},{7,4},{8,9},{9,10},{10,1... | collective-permute-start | bytes 1572872 | tf_op jit(solution)/shard_map/mlp/ppermute | solution.py:68
  364.2 13.2 %all-to-all-start.1 = ((bf16[8,64,512]{2,1,0:T(8,128)(2,1)}), bf16[8,64,512]{2,1,0:T(8,128)(2,1)S(1)}, u32[]{:S(2)}, u32[]{:S(2)}) async-start(bf16[8,64,512]{2,1,0:T(8,128)(2,1)} %bitcast.32), calls=%async_computation.3 | async-start | bytes 1048576 | tf_op jit(solution)/shard_map/entry_bwd/all_to_all | solution.py:91
  367.7 88.9 %reduce-scatter.8.cloned.1.call-start = ((), (), s32[]{:S(2)}) async-start(), calls=%async_computation.14 | async-start | bytes 2621440 | tf_op jit(solution)/shard_map/layer_out/reduce_scatter | solution.py:1324
  387.5 15.3 %all-to-all-start.2 = ((bf16[4,64,2048]{2,1,0:T(8,128)(2,1)}), bf16[4,64,2048]{2,1,0:T(8,128)(2,1)S(1)}, u32[]{:S(2)}, u32[]{:S(2)}) async-start(bf16[4,64,2048]{2,1,0:T(8,128)(2,1)} %bitcast.33), calls=%async_computation.5 | async-start | bytes 2097152 | tf_op jit(solution)/shard_map/hyper_bwd/all_to_all | solution.py:1315
  403.8 20.3 %all-to-all-start.3 = ((bf16[8,16,4608]{2,1,0:T(8,128)(2,1)}), bf16[8,16,4608]{2,1,0:T(8,128)(2,1)S(1)}, u32[]{:S(2)}, u32[]{:S(2)}) async-start(bf16[8,16,4608]{2,1,0:T(8,128)(2,1)} %bitcast.83), calls=%async_computation.6 | async-start | bytes 2359296 | tf_op jit(solution)/shard_map/hyper_bwd/all_to_all | solution.py:91
  407.3 59.3 %all-gather.12.cloned.1.call-start = ((), (), s32[]{:S(2)}) async-start(), calls=%async_computation.15 | async-start | bytes 4718592 | tf_op jit(solution)/shard_map/grads_out/all_gather | solution.py:1360
  429.1 14.1 %all-to-all-start.4 = ((bf16[8,16,1664]{2,1,0:T(8,128)(2,1)}), bf16[8,16,1664]{2,1,0:T(8,128)(2,1)S(1)}, u32[]{:S(2)}, u32[]{:S(2)}) async-start(bf16[8,16,1664]{2,1,0:T(8,128)(2,1)} %bitcast.37), calls=%async_computation.7 | async-start | bytes 851968 | tf_op jit(solution)/shard_map/grads_out/all_to_all | solution.py:91
  443.2 12.7 %all-to-all-start.5 = ((bf16[4,16,2048]{2,1,0:T(8,128)(2,1)}), bf16[4,16,2048]{2,1,0:T(8,128)(2,1)S(1)}, u32[]{:S(2)}, u32[]{:S(2)}) async-start(bf16[4,16,2048]{2,1,0:T(8,128)(2,1)} %bitcast.40), calls=%async_computation.8 | async-start | bytes 524288 | tf_op jit(solution)/shard_map/grads_out/all_to_all | solution.py:1363
  (49 other events, 401.1 us)
Sparse Core Ops, SparseCore 0:
  12.3 63.2 all-gather.5
  77.5 68.3 all-gather.9
  147.8 54.0 all-gather.7
  245.2 44.9 reduce-scatter.3
  335.5 41.4 reduce-scatter.5
  385.0 42.0 reduce-scatter.7
  429.2 37.4 all-gather.11
